TPU v7x, 32 devices: a whole 2x2x4 slice. The times are simulated.
32 devices in a mesh: groups: 2 (over y), sy: 4 (over z), sx: 2 (over core), ta: 2 (over x).
Axes of the slice: x: 2, y: 2, z: 4, core: 2. Of those that a mesh axis runs over, the one named last changes fastest.
Arguments:
- state_field: bfloat16 [8, 64, 32, 384], P(('groups', 'ta'), 'sy', 'sx'), parts along dimension 0, may hold values from -80 to 80
- outlier_flags: int32 [8, 64, 32], P(('groups', 'ta'), 'sy', 'sx'), parts along dimension 0, may hold values 0 or 1
- window_shift: int32 [2], replicated, may hold values from 1 to 8, as said below
- layer_norm_gain: float32 [384], replicated, may hold values from 0.1 to 1.9
- qkv_weight: bfloat16 [384, 1152], replicated, may hold values from -0.3125 to 0.3125
- out_weight: bfloat16 [384, 384], replicated, may hold values from -1.25 to 1.25
- position_bias: float32 [6, 2883], replicated, may hold values from -4 to 300
- cotangent: bfloat16 [8, 64, 32, 384], P(('groups', 'ta'), 'sy', 'sx'), parts along dimension 0, may hold values from -6 to 6
Outputs:
- update: bfloat16 [8, 64, 32, 384], P(('groups', 'ta'), 'sy', 'sx'), parts along dimension 0
- field_grad: bfloat16 [8, 64, 32, 384], P(('groups', 'ta'), 'sy', 'sx'), parts along dimension 0
- qkv_grad: float32 [768, 1152], P('groups'), parts along dimension 0
- out_grad: float32 [768, 384], P('groups'), parts along dimension 0
- norm_gain_gradient: float32 [768], P('groups'), parts along dimension 0
There are 2 independent parts, one for each index of `groups`. A program takes and returns all parts, laid end to end along the dimension named above; an argument that names none is the same for every part. Nothing has to cross between parts.
Inputs may be any that keep to these rules, and one draw needn't show every extreme that they name: `window_shift`: one of the two shifts equals 8, the other is smaller.
All inputs are finite; a program needn't handle non-finite values. No bound on the sum of `outlier_flags` on one device may be relied on, other than what follows from the above.
Results may differ from a plain program's by a relative error of at most 0.011.
Values may be sent and summed in bfloat16 or wider, within the bound.
No kernel may reach another device: no remote copies, remote signals or barrier semaphores. Data moves between devices by JAX's collectives and lax.ppermute only.
A program may use at most 256 MiB of HBM per device.

v0:
```python
import functools
import math

import jax
import jax.numpy as jnp
from jax import lax
from jax.experimental import pallas as pl
from jax.experimental.pallas import tpu as pltpu
from jax.sharding import PartitionSpec as P

MODEL_WIDTH = 384
HEADS = 6
HEAD_WIDTH = 64
RIM = 8
SIDE = 16
TOKENS = 512
HALF = 256
EPS = 1e-05
LOG2E = math.log2(math.e)
VMEM_LIMIT = 48 * 1024 * 1024

bf16 = jnp.bfloat16
f32 = jnp.float32


def nn(a, b):
    return lax.dot_general(a, b, (((1,), (0,)), ((), ())), preferred_element_type=f32)


def nt(a, b):
    return lax.dot_general(a, b, (((1,), (1,)), ((), ())), preferred_element_type=f32)


def tn(a, b):
    return lax.dot_general(a, b, (((0,), (0,)), ((), ())), preferred_element_type=f32)


def iota(shape, dim):
    return lax.broadcasted_iota(jnp.int32, shape, dim)


def prepare_kernel(strips, cot, out_weight, qkv_weight, bias_blocks, d_context_t, qkv_weight_t):
    lane = iota((SIDE, TOKENS), 1)
    for entry in range(HEADS * 3):
        even = jnp.broadcast_to(strips[2 * entry : 2 * entry + 1, :], (SIDE, TOKENS))
        odd = jnp.broadcast_to(strips[2 * entry + 1 : 2 * entry + 2, :], (SIDE, TOKENS))
        even = pltpu.roll(even, TOKENS - 15, 1, stride=1, stride_axis=0)
        odd = pltpu.roll(odd, 1, 1, stride=1, stride_axis=0)
        rows = jnp.where(lane % 32 < 16, even, odd) * LOG2E
        for row in range(SIDE):
            first = (15 - row) * SIDE
            bias_blocks[entry, row * SIDE : (row + 1) * SIDE, :] = rows[:, first : first + HALF]
    d_context_t[...] = nt(out_weight[...], cot[...]).astype(bf16)
    qkv_weight_t[...] = qkv_weight[...].T


def source_onehots(row_shift, col_shift, sign):
    token = iota((HALF, 1), 0)
    row = token // SIDE + sign * row_shift
    col = token % SIDE + sign * col_shift
    if sign > 0:
        row_out, col_out = row >= SIDE, col >= SIDE
        near_row, near_col = row - SIDE, col - SIDE
    else:
        row_out, col_out = row < 0, col < 0
        near_row, near_col = row + RIM, col + RIM
    inner = jnp.where(row_out | col_out, -1, row * SIDE + col)
    rows = jnp.where(row_out & ~col_out, near_row * SIDE + col, -1)
    cols = jnp.where(col_out & ~row_out, row * RIM + near_col, -1)
    corner = jnp.where(row_out & col_out, near_row * RIM + near_col, -1)
    return [
        (iota((HALF, count), 1) == place).astype(f32).astype(bf16)
        for place, count in ((inner, HALF), (rows, 128), (cols, 128), (corner, 64))
    ]


def flag_strip(flags, first, count, width):
    total = count * width
    repeat = (iota((width, total), 1) % width == iota((width, total), 0)).astype(f32).astype(bf16)
    spread = nn(flags[first : first + count, :], repeat)
    keep = iota((count, total), 1) // width == iota((count, total), 0)
    strip = jnp.sum(jnp.where(keep, spread, 0.0), 0, keepdims=True)
    return jnp.broadcast_to(strip, (128, total)).astype(bf16)


def attention_kernel(
    shift,
    inner,
    rows,
    cols,
    corner,
    inner_flags,
    gain,
    qkv_weight,
    qkv_weight_t,
    out_weight,
    cot,
    d_context_t,
    bias_blocks,
    update,
    grads,
    d_rolled,
    penalty,
    context_t,
    d_qkv,
):
    onehots = source_onehots(shift[0], shift[1], 1)
    rolled = []
    on_diagonal = iota((HALF, HALF), 0) == iota((HALF, HALF), 1)
    for t in range(2):
        parts = (
            inner[t * 256 : t * 256 + 256, :],
            rows[t * 128 : t * 128 + 128, :],
            cols[t * 128 : t * 128 + 128, :],
            corner[t * 64 : t * 64 + 64, :],
        )
        rolled.append(sum(nn(hot, part) for hot, part in zip(onehots, parts)))
        strips = (
            flag_strip(inner_flags, t * 16, 16, 16),
            flag_strip(rows[256:272, :16], t * 8, 8, 16),
            flag_strip(cols[256:288, :8], t * 16, 16, 8),
            flag_strip(corner[128:144, :8], t * 8, 8, 8),
        )
        marks = sum(nt(hot, strip) for hot, strip in zip(onehots, strips))
        column = jnp.where(marks > 0.5, -1e30, 0.0)
        wide = jnp.concatenate([column, column], 1)
        own = jnp.where(on_diagonal, 0.0, wide)
        penalty[t * HALF : (t + 1) * HALF, t * HALF : (t + 1) * HALF] = own
        penalty[t * HALF : (t + 1) * HALF, (1 - t) * HALF : (2 - t) * HALF] = wide
    rolled = jnp.concatenate(rolled, 0)
    centred = rolled - jnp.mean(rolled, -1, keepdims=True)
    inv_std = lax.rsqrt(jnp.mean(centred * centred, -1, keepdims=True) + EPS)
    xhat = centred * inv_std
    normed = (xhat * gain[...]).astype(bf16)
    normed_t = normed.T
    qkv_t = nt(qkv_weight_t[...], normed).astype(bf16)
    kv = nn(normed, qkv_weight[:, MODEL_WIDTH:]).astype(bf16)
    scale = LOG2E * HEAD_WIDTH ** (-0.5)
    zeros = jnp.zeros((HEAD_WIDTH, TOKENS), bf16)
    for pair in range(HEADS // 2):
        key_pair = kv[:, pair * 128 : pair * 128 + 128]
        value_pair = kv[:, MODEL_WIDTH + pair * 128 : MODEL_WIDTH + pair * 128 + 128]
        d_pair = [[], [], []]
        for side in range(2):
            head = 2 * pair + side
            at = head * HEAD_WIDTH
            q_t = qkv_t[at : at + HEAD_WIDTH, :]
            k_t = qkv_t[MODEL_WIDTH + at : MODEL_WIDTH + at + HEAD_WIDTH, :]
            v_t = qkv_t[2 * MODEL_WIDTH + at : 2 * MODEL_WIDTH + at + HEAD_WIDTH, :]
            d_t = d_context_t[at : at + HEAD_WIDTH, :]
            d_eighth = d_t * 0.125
            q_wide = jnp.concatenate([q_t, zeros] if side == 0 else [zeros, q_t], 0)
            d_wide = jnp.concatenate([d_eighth, zeros] if side == 0 else [zeros, d_eighth], 0)
            dq_parts = []
            dk_parts = [0.0, 0.0]
            dv_parts = [0.0, 0.0]
            for b in range(2):
                lanes = slice(b * HALF, (b + 1) * HALF)
                scores = nn(key_pair, q_wide[:, lanes])
                d_probs = nn(value_pair, d_wide[:, lanes])
                halves = [slice(a * HALF, (a + 1) * HALF) for a in range(2)]
                s = [
                    scores[halves[a]] * scale
                    + bias_blocks[head * 3 + b - a + 1]
                    + penalty[halves[a], lanes]
                    for a in range(2)
                ]
                top = jnp.maximum(
                    jnp.max(s[0], 0, keepdims=True), jnp.max(s[1], 0, keepdims=True)
                )
                e = [jnp.exp2(s[a] - top) for a in range(2)]
                total = jnp.sum(e[0], 0, keepdims=True) + jnp.sum(e[1], 0, keepdims=True)
                inverse = 1.0 / total
                p = [e[a] * inverse for a in range(2)]
                pb = [p[a].astype(bf16) for a in range(2)]
                context_t[at : at + HEAD_WIDTH, lanes] = (
                    nn(v_t[:, :HALF], pb[0]) + nn(v_t[:, HALF:], pb[1])
                ).astype(bf16)
                dp = [d_probs[halves[a]] for a in range(2)]
                delta = jnp.sum(p[0] * dp[0], 0, keepdims=True) + jnp.sum(
                    p[1] * dp[1], 0, keepdims=True
                )
                ds = [(p[a] * (dp[a] - delta)).astype(bf16) for a in range(2)]
                dq_parts.append(nn(k_t[:, :HALF], ds[0]) + nn(k_t[:, HALF:], ds[1]))
                for a in range(2):
                    dk_parts[a] = dk_parts[a] + nt(q_t[:, lanes], ds[a])
                    dv_parts[a] = dv_parts[a] + nt(d_t[:, lanes], pb[a])
            for kind, pieces in enumerate((dq_parts, dk_parts, dv_parts)):
                d_pair[kind].append(jnp.concatenate(pieces, 1).astype(bf16))
        for kind in range(3):
            first = kind * MODEL_WIDTH + pair * 128
            d_qkv[:, first : first + 128] = jnp.concatenate(d_pair[kind], 0).T
    update[...] = tn(context_t[...], out_weight[...]).astype(bf16)
    grads[:MODEL_WIDTH, :] = nn(context_t[...], cot[...]).astype(bf16)
    d_rows = d_qkv[...]
    for kind in range(3):
        columns = d_rows[:, kind * MODEL_WIDTH : (kind + 1) * MODEL_WIDTH]
        first = (kind + 1) * MODEL_WIDTH
        grads[first : first + MODEL_WIDTH, :] = nn(normed_t, columns).astype(bf16)
    d_xhat = nn(d_rows, qkv_weight_t[...]) * gain[...]
    d_rolled[...] = (
        inv_std
        * (
            d_xhat
            - jnp.mean(d_xhat, -1, keepdims=True)
            - xhat * jnp.mean(d_xhat * xhat, -1, keepdims=True)
        )
    ).astype(bf16)


def unroll_kernel(shift, inner, rows, cols, corner, field_grad):
    onehots = source_onehots(shift[0], shift[1], -1)
    for t in range(2):
        parts = (
            inner[t * 256 : t * 256 + 256, :],
            rows[t * 128 : t * 128 + 128, :],
            cols[t * 128 : t * 128 + 128, :],
            corner[t * 64 : t * 64 + 64, :],
        )
        field_grad[t * 256 : t * 256 + 256, :] = sum(
            nn(hot, part) for hot, part in zip(onehots, parts)
        ).astype(bf16)


def in_vmem(count):
    return [pl.BlockSpec(memory_space=pltpu.VMEM)] * count


def local_call(kernel, shapes, inputs, scratch=(), scalars=0):
    return pl.pallas_call(
        kernel,
        out_shape=[jax.ShapeDtypeStruct(shape, dtype) for shape, dtype in shapes],
        in_specs=[pl.BlockSpec(memory_space=pltpu.SMEM)] * scalars
        + in_vmem(len(inputs) - scalars),
        out_specs=in_vmem(len(shapes)),
        scratch_shapes=list(scratch),
        compiler_params=pltpu.CompilerParams(vmem_limit_bytes=VMEM_LIMIT),
    )(*inputs)


def passed_along(block, axis, distance):
    count = lax.axis_size(axis)
    return lax.ppermute(block, axis, [((i - distance) % count, i) for i in range(count)])


def scatter_sum(block, axis):
    count = lax.axis_size(axis)
    me = lax.axis_index(axis)
    share = block.shape[0] // count
    pick = lambda owner: lax.dynamic_slice_in_dim(block, owner * share, share, 0)
    arrived = [
        passed_along(pick(lax.rem(me + step, count)), axis, step) for step in range(1, count)
    ]
    total = pick(me).astype(f32)
    for piece in arrived:
        total = total + piece.astype(f32)
    return total.astype(bf16)


def gather_shares(block, axis):
    count = lax.axis_size(axis)
    me = lax.axis_index(axis)
    share = block.shape[0]
    pieces = [passed_along(block, axis, step) for step in range(count - 1, 0, -1)] + [block]
    ring = jnp.concatenate(pieces + pieces[:-1], 0)
    return lax.dynamic_slice_in_dim(ring, (count - 1 - me) * share, count * share, 0)


def shards(
    state_field,
    outlier_flags,
    window_shift,
    layer_norm_gain,
    qkv_weight,
    out_weight,
    position_bias,
    cotangent,
):
    width = MODEL_WIDTH
    marks = outlier_flags.astype(bf16)
    pad_marks = lambda m: jnp.pad(m, ((0, 0), (0, width - m.shape[1])))
    row_message = jnp.concatenate(
        [
            state_field[:, :RIM].reshape(2 * RIM * SIDE, width),
            pad_marks(marks[:, :RIM].reshape(2 * RIM, SIDE)),
        ],
        0,
    )
    col_message = jnp.concatenate(
        [
            state_field[:, :, :RIM].reshape(2 * SIDE * RIM, width),
            pad_marks(marks[:, :, :RIM].reshape(2 * SIDE, RIM)),
        ],
        0,
    )
    rows = passed_along(row_message, "sy", -1)
    cols = passed_along(col_message, "sx", -1)
    strips = position_bias[:, ::-1].reshape(HEADS, 3, 31, 31)
    strips = jnp.pad(strips, ((0, 0), (0, 0), (0, 1), (0, 1)))
    strips = strips.reshape(HEADS, 3, 16, 2, 32).transpose(0, 1, 3, 2, 4).reshape(36, TOKENS)
    cot_rows = cotangent.reshape(TOKENS, width)
    bias_blocks, d_context_t, qkv_weight_t = local_call(
        prepare_kernel,
        [((18, HALF, HALF), f32), ((width, TOKENS), bf16), ((3 * width, width), bf16)],
        [strips, cot_rows, out_weight, qkv_weight],
    )
    corner_message = jnp.concatenate(
        [
            rows[: 2 * RIM * SIDE].reshape(2 * RIM, SIDE, width)[:, :RIM].reshape(-1, width),
            rows[2 * RIM * SIDE :],
        ],
        0,
    )
    corner = passed_along(corner_message, "sx", -1)
    gain = layer_norm_gain.reshape(1, width)
    update, grads, d_rolled = local_call(
        attention_kernel,
        [((TOKENS, width), bf16), ((4 * width, width), bf16), ((TOKENS, width), bf16)],
        [
            window_shift,
            state_field.reshape(TOKENS, width),
            rows,
            cols,
            corner,
            marks.reshape(2 * SIDE, SIDE),
            gain,
            qkv_weight,
            qkv_weight_t,
            out_weight,
            cot_rows,
            d_context_t,
            bias_blocks,
        ],
        scratch=[
            pltpu.VMEM((TOKENS, TOKENS), f32),
            pltpu.VMEM((width, TOKENS), bf16),
            pltpu.VMEM((TOKENS, 3 * width), bf16),
        ],
        scalars=1,
    )
    grid = d_rolled.reshape(2, SIDE, SIDE, width)
    below = passed_along(grid[:, RIM:].reshape(-1, width), "sy", 1)
    beside = passed_along(grid[:, :, RIM:].reshape(-1, width), "sx", 1)
    across = passed_along(
        below.reshape(2 * RIM, SIDE, width)[:, RIM:].reshape(-1, width), "sx", 1
    )
    axes = ("sx", "ta", "sy")
    for axis in axes:
        grads = scatter_sum(grads, axis)
    for axis in reversed(axes):
        grads = gather_shares(grads, axis)
    (field_grad,) = local_call(
        unroll_kernel,
        [((TOKENS, width), bf16)],
        [window_shift, d_rolled, below, beside, across],
        scalars=1,
    )
    tiles = lax.axis_size("sy") * lax.axis_size("sx") * lax.axis_size("ta")
    grads = grads.astype(f32) / tiles
    out_grad = grads[:width]
    qkv_grad = jnp.concatenate([grads[width * k : width * (k + 1)] for k in (1, 2, 3)], 1)
    gain_grad = jnp.sum(qkv_grad * qkv_weight.astype(f32), 1) / layer_norm_gain
    shape = state_field.shape
    return (update.reshape(shape), field_grad.reshape(shape), qkv_grad, out_grad, gain_grad)


def solution(mesh):
    in_specs = (
        P(("groups", "ta"), "sy", "sx", None),
        P(("groups", "ta"), "sy", "sx"),
        P(),
        P(),
        P(),
        P(),
        P(),
        P(("groups", "ta"), "sy", "sx", None),
    )
    out_specs = (
        P(("groups", "ta"), "sy", "sx", None),
        P(("groups", "ta"), "sy", "sx", None),
        P("groups", None),
        P("groups", None),
        P("groups"),
    )
    return jax.shard_map(shards, mesh=mesh, in_specs=in_specs, out_specs=out_specs, check_vma=False)
```

profile of v0, /device:TPU:1, one launch (start us, length us, event | category | flops | bytes accessed | tf_op | source)
XLA Modules:
  0.0 97.2 jit_solution(5261828727511184995)
XLA Ops:
  2.4 4.2 %collective-permute-start = (bf16[272,384]{1,0:T(8,128)(2,1)S(1)}, bf16[272,384]{1,0:T(8,128)(2,1)S(1)}, u32[]{:S(2)}, u32[]{:S(2)}) collective-permute-start(bf16[272,384]{1,0:T(8,128)(2,1)S(1)} %fusion.7), channel_id=1, source_target_pairs={{4,0},{8,4},{12,8},{0,12},{5,1},{9,5},{13,9},{1,13},{6,2},{10,6},{... | collective-permute-start | bytes 626696 | tf_op jit(solution)/shard_map/ppermute | solution.py:243
  8.6 1.8 %collective-permute-done.rows = bf16[272,384]{1,0:T(8,128)(2,1)S(1)} collective-permute-done((bf16[272,384]{1,0:T(8,128)(2,1)S(1)}, bf16[272,384]{1,0:T(8,128)(2,1)S(1)}, u32[]{:S(2)}, u32[]{:S(2)}) %collective-permute-start) | collective-permute-done | bytes 208928 | tf_op jit(solution)/shard_map/ppermute | solution.py:243
  10.5 1.6 %collective-permute-start.2 = (bf16[144,384]{1,0:T(8,128)(2,1)S(1)}, bf16[144,384]{1,0:T(8,128)(2,1)S(1)}, u32[]{:S(2)}, u32[]{:S(2)}) collective-permute-start(bf16[144,384]{1,0:T(8,128)(2,1)S(1)} %pad_maximum_fusion.1), channel_id=1, source_target_pairs={{2,0},{0,2},{3,1},{1,3},{6,4},{4,6},{7,5},{5,7},{10,8},{8,10},{11,... | collective-permute-start | bytes 331784 | tf_op jit(solution)/shard_map/ppermute | solution.py:243
  12.1 1.6 %reverse = f32[6,2944]{1,0:T(8,128)S(1)} reverse(f32[6,2944]{1,0:T(8,128)S(1)} %bitcast.41), dimensions={1} | reverse | bytes 141312
  14.4 4.8 %shard_map.119 = (f32[18,256,256]{2,1,0:T(8,128)}, bf16[384,512]{1,0:T(8,128)(2,1)S(1)}, bf16[1152,384]{1,0:T(8,128)(2,1)S(1)}) custom-call(f32[36,512]{1,0:T(8,128)S(1)} %reshape.81.strips, bf16[512,384]{1,0:T(8,128)(2,1)S(1)} %bitcast.27, bf16[384,384]{1,0:T(8,128)(2,1)S(1)} %copy-done.3, bf16[384,1152]{1,0:T(8,128)(2,1)S(1)} %copy-done), custom_call_target="tpu_custom_call" | custom-call | tf_op jit(solution)/shard_map/pallas_call | solution.py:230
  22.4 14.6 %shard_map.120 = (bf16[512,384]{1,0:T(8,128)(2,1)}, bf16[1536,384]{1,0:T(8,128)(2,1)S(1)}, bf16[512,384]{1,0:T(8,128)(2,1)S(1)}) custom-call(s32[2]{0:T(128)S(1)} %copy-done.10, bf16[512,384]{1,0:T(8,128)(2,1)S(1)} %bitcast.26, bf16[272,384]{1,0:T(8,128)(2,1)S(1)} %copy-done.5, bf16[288,384]{1,0:T(8,128)(2,1)S(1)} %copy-done.7, ...), custom_call_target="tpu_custom_call" | custom-call | tf_op jit(solution)/shard_map/pallas_call | solution.py:230
  37.2 2.1 %collective-permute-done.6 = bf16[768,384]{1,0:T(8,128)(2,1)} collective-permute-done((bf16[768,384]{1,0:T(8,128)(2,1)S(1)}, bf16[768,384]{1,0:T(8,128)(2,1)}, u32[]{:S(2)}, u32[]{:S(2)}) %collective-permute-start.6) | collective-permute-done | bytes 589856 | tf_op jit(solution)/shard_map/ppermute | solution.py:243
  39.3 1.2 %add_convert_fusion = bf16[768,384]{1,0:T(8,128)(2,1)S(1)} fusion(bf16[768,384]{1,0:T(8,128)(2,1)} %collective-permute-done.6, bf16[1536,384]{1,0:T(8,128)(2,1)S(1)} %get-tuple-element.16, s32[]{:T(128)S(6)} %select_n.33), kind=kLoop, calls=%fused_computation.8 | loop fusion | flops 1179648 | bytes 1769476 | tf_op jit(solution)/shard_map/convert_element_type | solution.py:257
  40.5 1.3 %collective-permute-start.7 = (bf16[384,384]{1,0:T(8,128)(2,1)S(1)}, bf16[384,384]{1,0:T(8,128)(2,1)S(1)}, u32[]{:S(2)}, u32[]{:S(2)}) collective-permute-start(bf16[384,384]{1,0:T(8,128)(2,1)S(1)} %constant_dynamic-slice_fusion.4), channel_id=1, source_target_pairs={{1,0},{0,1},{3,2},{2,3},{5,4},{4,5},{7,6},{6,7},{9,8},{8,9},{11,10... | collective-permute-start | bytes 884744 | tf_op jit(solution)/shard_map/ppermute | solution.py:243
  41.8 7.3 %collective-permute-done.7 = bf16[384,384]{1,0:T(8,128)(2,1)S(1)} collective-permute-done((bf16[384,384]{1,0:T(8,128)(2,1)S(1)}, bf16[384,384]{1,0:T(8,128)(2,1)S(1)}, u32[]{:S(2)}, u32[]{:S(2)}) %collective-permute-start.7) | collective-permute-done | bytes 294944 | tf_op jit(solution)/shard_map/ppermute | solution.py:243
  49.2 4.0 %collective-permute-start.10 = (bf16[96,384]{1,0:T(8,128)(2,1)S(1)}, bf16[96,384]{1,0:T(8,128)(2,1)S(1)}, u32[]{:S(2)}, u32[]{:S(2)}) collective-permute-start(bf16[96,384]{1,0:T(8,128)(2,1)S(1)} %get-tuple-element.24), channel_id=1, source_target_pairs={{4,0},{8,4},{12,8},{0,12},{5,1},{9,5},{13,9},{1,13},{6,2},{10,6},{... | collective-permute-start | bytes 221192 | tf_op jit(solution)/shard_map/ppermute | solution.py:243
  53.6 1.0 %collective-permute-done.10 = bf16[96,384]{1,0:T(8,128)(2,1)S(1)} collective-permute-done((bf16[96,384]{1,0:T(8,128)(2,1)S(1)}, bf16[96,384]{1,0:T(8,128)(2,1)S(1)}, u32[]{:S(2)}, u32[]{:S(2)}) %collective-permute-start.10) | collective-permute-done | bytes 73760 | tf_op jit(solution)/shard_map/ppermute | solution.py:243
  54.6 6.0 %collective-permute-done.9 = bf16[96,384]{1,0:T(8,128)(2,1)S(1)} collective-permute-done((bf16[96,384]{1,0:T(8,128)(2,1)S(1)}, bf16[96,384]{1,0:T(8,128)(2,1)S(1)}, u32[]{:S(2)}, u32[]{:S(2)}) %collective-permute-start.9) | collective-permute-done | bytes 73760 | tf_op jit(solution)/shard_map/ppermute | solution.py:243
  61.8 1.4 %collective-permute-start.13 = (bf16[96,384]{1,0:T(8,128)(2,1)S(1)}, bf16[96,384]{1,0:T(8,128)(2,1)S(1)}, u32[]{:S(2)}, u32[]{:S(2)}) collective-permute-start(bf16[96,384]{1,0:T(8,128)(2,1)S(1)} %add_convert_fusion.2), channel_id=1, source_target_pairs={{12,0},{0,4},{4,8},{8,12},{13,1},{1,5},{5,9},{9,13},{14,2},{2,6},{... | collective-permute-start | bytes 221192 | tf_op jit(solution)/shard_map/ppermute | solution.py:243
  64.0 2.1 %collective-permute-done.12 = bf16[96,384]{1,0:T(8,128)(2,1)S(1)} collective-permute-done((bf16[96,384]{1,0:T(8,128)(2,1)S(1)}, bf16[96,384]{1,0:T(8,128)(2,1)S(1)}, u32[]{:S(2)}, u32[]{:S(2)}) %collective-permute-start.12) | collective-permute-done | bytes 73760 | tf_op jit(solution)/shard_map/ppermute | solution.py:243
  66.1 2.2 %collective-permute-done.13 = bf16[96,384]{1,0:T(8,128)(2,1)S(1)} collective-permute-done((bf16[96,384]{1,0:T(8,128)(2,1)S(1)}, bf16[96,384]{1,0:T(8,128)(2,1)S(1)}, u32[]{:S(2)}, u32[]{:S(2)}) %collective-permute-start.13) | collective-permute-done | bytes 73760 | tf_op jit(solution)/shard_map/ppermute | solution.py:243
  68.4 1.3 %collective-permute-start.14 = (bf16[384,384]{1,0:T(8,128)(2,1)S(1)}, bf16[384,384]{1,0:T(8,128)(2,1)S(1)}, u32[]{:S(2)}, u32[]{:S(2)}) collective-permute-start(bf16[384,384]{1,0:T(8,128)(2,1)S(1)} %constant_dynamic-slice_fusion), channel_id=1, source_target_pairs={{1,0},{0,1},{3,2},{2,3},{5,4},{4,5},{7,6},{6,7},{9,8},{8,9},{11,10... | collective-permute-start | bytes 884744 | tf_op jit(solution)/shard_map/ppermute | solution.py:243
  69.7 4.8 %collective-permute-done.14 = bf16[384,384]{1,0:T(8,128)(2,1)S(1)} collective-permute-done((bf16[384,384]{1,0:T(8,128)(2,1)S(1)}, bf16[384,384]{1,0:T(8,128)(2,1)S(1)}, u32[]{:S(2)}, u32[]{:S(2)}) %collective-permute-start.14) | collective-permute-done | bytes 294944 | tf_op jit(solution)/shard_map/ppermute | solution.py:243
  74.5 1.4 %fusion.3 = bf16[768,384]{1,0:T(8,128)(2,1)S(1)} fusion(s32[]{:T(128)S(6)} %select_n.42, bf16[384,384]{1,0:T(8,128)(2,1)S(1)} %collective-permute-done.14, bf16[384,384]{1,0:T(8,128)(2,1)S(1)} %constant_dynamic-slice_fusion), kind=kLoop, calls=%fused_computation.13 | loop fusion | flops 1769472 | bytes 1179652 | tf_op jit(solution)/shard_map/concatenate | solution.py:265
  76.0 3.4 %collective-permute-start.15 = (bf16[768,384]{1,0:T(8,128)(2,1)S(1)}, bf16[768,384]{1,0:T(8,128)(2,1)S(1)}, u32[]{:S(2)}, u32[]{:S(2)}) collective-permute-start(bf16[768,384]{1,0:T(8,128)(2,1)S(1)} %fusion.3), channel_id=1, source_target_pairs={{2,0},{0,2},{3,1},{1,3},{6,4},{4,6},{7,5},{5,7},{10,8},{8,10},{11,... | collective-permute-start | bytes 1769480 | tf_op jit(solution)/shard_map/ppermute | solution.py:243
  79.6 8.2 %collective-permute-done.3.rows = bf16[256,384]{1,0:T(8,128)(2,1)S(1)} collective-permute-done((bf16[256,384]{1,0:T(8,128)(2,1)S(1)}, bf16[256,384]{1,0:T(8,128)(2,1)S(1)}, u32[]{:S(2)}, u32[]{:S(2)}) %collective-permute-start.3) | collective-permute-done | bytes 196640 | tf_op jit(solution)/shard_map/ppermute | solution.py:243
  89.6 1.9 %shard_map.121 = bf16[512,384]{1,0:T(8,128)(2,1)} custom-call(s32[2]{0:T(128)S(1)} %copy-done.10, bf16[512,384]{1,0:T(8,128)(2,1)S(1)} %get-tuple-element.15.inner, bf16[256,384]{1,0:T(8,128)(2,1)S(1)} %collective-permute-done.3.rows, bf16[256,384]{1,0:T(8,128)(2,1)S(1)} %collective-permute-done.4.cols, bf16[128,384]{1,0:T(8,128)(2,1)S(1)} %collective-permute-done.5.corner), custom_call_target="tpu_custom_call" | custom-call | tf_op jit(solution)/shard_map/pallas_call | solution.py:230
  91.6 2.6 %convert_multiply_fusion = f32[1536,384]{1,0:T(8,128)S(1)} fusion(s32[]{:T(128)S(6)} %select_n.43, bf16[768,384]{1,0:T(8,128)(2,1)S(1)} %collective-permute-done.15, bf16[768,384]{1,0:T(8,128)(2,1)S(1)} %fusion.3), kind=kLoop, calls=%fused_computation | loop fusion | flops 4128768 | bytes 3538948 | tf_op jit(solution)/shard_map/div | solution.py:359
  95.1 1.4 %multiply_reduce_fusion = (f32[384]{0:T(512)S(1)}, f32[384,1152]{1,0:T(8,128)}) fusion(bf16[384,1152]{1,0:T(8,128)(2,1)S(1)} %copy-done, f32[384,384]{1,0:T(8,128)S(1)} %get-tuple-element.20, f32[384,384]{1,0:T(8,128)S(1)} %get-tuple-element.21, f32[384,384]{1,0:T(8,128)S(1)} %get-tuple-element.22), kind=kLoop, calls=%fused_computation.5 | loop fusion | flops 2211456 | bytes 4425216 | tf_op jit(solution)/shard_map/reduce_sum | solution.py:362
  (78 shorter events, 13.9 us)
Async XLA Ops:
  0.6 11.5 %copy-start.12 = (f32[384]{0:T(512)S(1)}, f32[384]{0:T(512)}, u32[]{:S(2)}) copy-start(f32[384]{0:T(512)} %param.11) | copy-start | bytes 4612
  0.6 11.5 %copy-start.11 = (f32[6,2883]{1,0:T(8,128)S(1)}, f32[6,2883]{1,0:T(8,128)}, u32[]{:S(2)}) copy-start(f32[6,2883]{1,0:T(8,128)} %param.14) | copy-start | bytes 207580
  2.4 8.0 %collective-permute-start = (bf16[272,384]{1,0:T(8,128)(2,1)S(1)}, bf16[272,384]{1,0:T(8,128)(2,1)S(1)}, u32[]{:S(2)}, u32[]{:S(2)}) collective-permute-start(bf16[272,384]{1,0:T(8,128)(2,1)S(1)} %fusion.7), channel_id=1, source_target_pairs={{4,0},{8,4},{12,8},{0,12},{5,1},{9,5},{13,9},{1,13},{6,2},{10,6},{... | collective-permute-start | bytes 626696 | tf_op jit(solution)/shard_map/ppermute | solution.py:243
  7.5 6.8 %copy-start = (bf16[384,1152]{1,0:T(8,128)(2,1)S(1)}, bf16[384,1152]{1,0:T(8,128)(2,1)}, u32[]{:S(2)}) copy-start(bf16[384,1152]{1,0:T(8,128)(2,1)} %qkv_weight.3) | copy-start | bytes 2654212
  7.6 6.8 %copy-start.2 = (bf16[2,16,16,384]{3,2,1,0:T(8,128)(2,1)S(1)}, bf16[2,16,16,384]{3,2,1,0:T(8,128)(2,1)}, u32[]{:S(2)}) copy-start(bf16[2,16,16,384]{3,2,1,0:T(8,128)(2,1)} %param.15) | copy-start | bytes 1179652
  7.6 6.8 %copy-start.3 = (bf16[384,384]{1,0:T(8,128)(2,1)S(1)}, bf16[384,384]{1,0:T(8,128)(2,1)}, u32[]{:S(2)}) copy-start(bf16[384,384]{1,0:T(8,128)(2,1)} %out_weight.3) | copy-start | bytes 884740
  7.6 11.6 %collective-permute-start.1 = (bf16[288,384]{1,0:T(8,128)(2,1)S(1)}, bf16[288,384]{1,0:T(8,128)(2,1)S(1)}, u32[]{:S(2)}, u32[]{:S(2)}) collective-permute-start(bf16[288,384]{1,0:T(8,128)(2,1)S(1)} %fusion.6), channel_id=1, source_target_pairs={{2,0},{0,2},{3,1},{1,3},{6,4},{4,6},{7,5},{5,7},{10,8},{8,10},{11,... | collective-permute-start | bytes 663560 | tf_op jit(solution)/shard_map/ppermute | solution.py:243
  10.5 9.4 %collective-permute-start.2 = (bf16[144,384]{1,0:T(8,128)(2,1)S(1)}, bf16[144,384]{1,0:T(8,128)(2,1)S(1)}, u32[]{:S(2)}, u32[]{:S(2)}) collective-permute-start(bf16[144,384]{1,0:T(8,128)(2,1)S(1)} %pad_maximum_fusion.1), channel_id=1, source_target_pairs={{2,0},{0,2},{3,1},{1,3},{6,4},{4,6},{7,5},{5,7},{10,8},{8,10},{11,... | collective-permute-start | bytes 331784 | tf_op jit(solution)/shard_map/ppermute | solution.py:243
  13.8 6.7 %copy-start.1 = (bf16[2,16,16,384]{3,2,1,0:T(8,128)(2,1)S(1)}, bf16[2,16,16,384]{3,2,1,0:T(8,128)(2,1)}, u32[]{:S(2)}) copy-start(bf16[2,16,16,384]{3,2,1,0:T(8,128)(2,1)} %param.8) | copy-start | bytes 1179652
  13.9 6.7 %copy-start.10 = (s32[2]{0:T(128)S(1)}, s32[2]{0:T(128)}, u32[]{:S(2)}) copy-start(s32[2]{0:T(128)} %shift.3) | copy-start | bytes 28
  14.4 6.1 %copy-start.5 = (bf16[272,384]{1,0:T(8,128)(2,1)S(1)}, bf16[272,384]{1,0:T(8,128)(2,1)}, u32[]{:S(2)}) copy-start(bf16[272,384]{1,0:T(8,128)(2,1)} %copy-done.4) | copy-start | bytes 626692
  37.1 2.2 %collective-permute-start.6 = (bf16[768,384]{1,0:T(8,128)(2,1)S(1)}, bf16[768,384]{1,0:T(8,128)(2,1)}, u32[]{:S(2)}, u32[]{:S(2)}) collective-permute-start(bf16[768,384]{1,0:T(8,128)(2,1)S(1)} %constant_dynamic-slice_fusion.5), channel_id=1, source_target_pairs={{2,0},{0,2},{3,1},{1,3},{6,4},{4,6},{7,5},{5,7},{10,8},{8,10},{11,... | collective-permute-start | bytes 1769480 | tf_op jit(solution)/shard_map/ppermute | solution.py:243
  40.5 8.5 %collective-permute-start.7 = (bf16[384,384]{1,0:T(8,128)(2,1)S(1)}, bf16[384,384]{1,0:T(8,128)(2,1)S(1)}, u32[]{:S(2)}, u32[]{:S(2)}) collective-permute-start(bf16[384,384]{1,0:T(8,128)(2,1)S(1)} %constant_dynamic-slice_fusion.4), channel_id=1, source_target_pairs={{1,0},{0,1},{3,2},{2,3},{5,4},{4,5},{7,6},{6,7},{9,8},{8,9},{11,10... | collective-permute-start | bytes 884744 | tf_op jit(solution)/shard_map/ppermute | solution.py:243
  49.2 5.5 %collective-permute-start.10 = (bf16[96,384]{1,0:T(8,128)(2,1)S(1)}, bf16[96,384]{1,0:T(8,128)(2,1)S(1)}, u32[]{:S(2)}, u32[]{:S(2)}) collective-permute-start(bf16[96,384]{1,0:T(8,128)(2,1)S(1)} %get-tuple-element.24), channel_id=1, source_target_pairs={{4,0},{8,4},{12,8},{0,12},{5,1},{9,5},{13,9},{1,13},{6,2},{10,6},{... | collective-permute-start | bytes 221192 | tf_op jit(solution)/shard_map/ppermute | solution.py:243
  53.2 7.4 %collective-permute-start.9 = (bf16[96,384]{1,0:T(8,128)(2,1)S(1)}, bf16[96,384]{1,0:T(8,128)(2,1)S(1)}, u32[]{:S(2)}, u32[]{:S(2)}) collective-permute-start(bf16[96,384]{1,0:T(8,128)(2,1)S(1)} %get-tuple-element.25), channel_id=1, source_target_pairs={{8,0},{12,4},{0,8},{4,12},{9,1},{13,5},{1,9},{5,13},{10,2},{14,6},... | collective-permute-start | bytes 221192 | tf_op jit(solution)/shard_map/ppermute | solution.py:243
  53.2 7.4 %collective-permute-start.8 = (bf16[96,384]{1,0:T(8,128)(2,1)S(1)}, bf16[96,384]{1,0:T(8,128)(2,1)S(1)}, u32[]{:S(2)}, u32[]{:S(2)}) collective-permute-start(bf16[96,384]{1,0:T(8,128)(2,1)S(1)} %get-tuple-element.23), channel_id=1, source_target_pairs={{12,0},{0,4},{4,8},{8,12},{13,1},{1,5},{5,9},{9,13},{14,2},{2,6},{... | collective-permute-start | bytes 221192 | tf_op jit(solution)/shard_map/ppermute | solution.py:243
  60.7 3.3 %collective-permute-start.11 = (bf16[96,384]{1,0:T(8,128)(2,1)S(1)}, bf16[96,384]{1,0:T(8,128)(2,1)S(1)}, u32[]{:S(2)}, u32[]{:S(2)}) collective-permute-start(bf16[96,384]{1,0:T(8,128)(2,1)S(1)} %add_convert_fusion.2), channel_id=1, source_target_pairs={{4,0},{8,4},{12,8},{0,12},{5,1},{9,5},{13,9},{1,13},{6,2},{10,6},{... | collective-permute-start | bytes 221192 | tf_op jit(solution)/shard_map/ppermute | solution.py:243
  60.8 5.3 %collective-permute-start.12 = (bf16[96,384]{1,0:T(8,128)(2,1)S(1)}, bf16[96,384]{1,0:T(8,128)(2,1)S(1)}, u32[]{:S(2)}, u32[]{:S(2)}) collective-permute-start(bf16[96,384]{1,0:T(8,128)(2,1)S(1)} %add_convert_fusion.2), channel_id=1, source_target_pairs={{8,0},{12,4},{0,8},{4,12},{9,1},{13,5},{1,9},{5,13},{10,2},{14,6},... | collective-permute-start | bytes 221192 | tf_op jit(solution)/shard_map/ppermute | solution.py:243
  61.8 6.4 %collective-permute-start.13 = (bf16[96,384]{1,0:T(8,128)(2,1)S(1)}, bf16[96,384]{1,0:T(8,128)(2,1)S(1)}, u32[]{:S(2)}, u32[]{:S(2)}) collective-permute-start(bf16[96,384]{1,0:T(8,128)(2,1)S(1)} %add_convert_fusion.2), channel_id=1, source_target_pairs={{12,0},{0,4},{4,8},{8,12},{13,1},{1,5},{5,9},{9,13},{14,2},{2,6},{... | collective-permute-start | bytes 221192 | tf_op jit(solution)/shard_map/ppermute | solution.py:243
  68.4 6.1 %collective-permute-start.14 = (bf16[384,384]{1,0:T(8,128)(2,1)S(1)}, bf16[384,384]{1,0:T(8,128)(2,1)S(1)}, u32[]{:S(2)}, u32[]{:S(2)}) collective-permute-start(bf16[384,384]{1,0:T(8,128)(2,1)S(1)} %constant_dynamic-slice_fusion), channel_id=1, source_target_pairs={{1,0},{0,1},{3,2},{2,3},{5,4},{4,5},{7,6},{6,7},{9,8},{8,9},{11,10... | collective-permute-start | bytes 884744 | tf_op jit(solution)/shard_map/ppermute | solution.py:243
  76.0 15.6 %collective-permute-start.15 = (bf16[768,384]{1,0:T(8,128)(2,1)S(1)}, bf16[768,384]{1,0:T(8,128)(2,1)S(1)}, u32[]{:S(2)}, u32[]{:S(2)}) collective-permute-start(bf16[768,384]{1,0:T(8,128)(2,1)S(1)} %fusion.3), channel_id=1, source_target_pairs={{2,0},{0,2},{3,1},{1,3},{6,4},{4,6},{7,5},{5,7},{10,8},{8,10},{11,... | collective-permute-start | bytes 1769480 | tf_op jit(solution)/shard_map/ppermute | solution.py:243
  79.4 8.4 %collective-permute-start.3 = (bf16[256,384]{1,0:T(8,128)(2,1)S(1)}, bf16[256,384]{1,0:T(8,128)(2,1)S(1)}, u32[]{:S(2)}, u32[]{:S(2)}) collective-permute-start(bf16[256,384]{1,0:T(8,128)(2,1)S(1)} %bitcast.40), channel_id=1, source_target_pairs={{12,0},{0,4},{4,8},{8,12},{13,1},{1,5},{5,9},{9,13},{14,2},{2,6},{... | collective-permute-start | bytes 589832 | tf_op jit(solution)/shard_map/ppermute | solution.py:243
  79.5 9.2 %collective-permute-start.4 = (bf16[256,384]{1,0:T(8,128)(2,1)S(1)}, bf16[256,384]{1,0:T(8,128)(2,1)S(1)}, u32[]{:S(2)}, u32[]{:S(2)}) collective-permute-start(bf16[256,384]{1,0:T(8,128)(2,1)S(1)} %bitcast.39), channel_id=1, source_target_pairs={{2,0},{0,2},{3,1},{1,3},{6,4},{4,6},{7,5},{5,7},{10,8},{8,10},{11,... | collective-permute-start | bytes 589832 | tf_op jit(solution)/shard_map/ppermute | solution.py:243
  87.8 1.8 %collective-permute-start.5 = (bf16[128,384]{1,0:T(8,128)(2,1)S(1)}, bf16[128,384]{1,0:T(8,128)(2,1)S(1)}, u32[]{:S(2)}, u32[]{:S(2)}) collective-permute-start(bf16[128,384]{1,0:T(8,128)(2,1)S(1)} %slice_bitcast_fusion), channel_id=1, source_target_pairs={{2,0},{0,2},{3,1},{1,3},{6,4},{4,6},{7,5},{5,7},{10,8},{8,10},{11,... | collective-permute-start | bytes 294920 | tf_op jit(solution)/shard_map/ppermute | solution.py:243
  (6 other events, 7.9 us)
where the time goes:
time: 97.8 us; the launch traced here: 97.2 us
  waiting for transfers between devices  37.2 us (38%)
  Pallas kernels  21.3 us (22%)
  starting transfers between devices  20.8 us (21%)
  local copies, waits for them, and re-layouts  8.64 us (9%)
  other arithmetic  8.22 us (8%)
    ppermute x16, waiting for transfers between devices, passed_along(): lax.ppermute(block, axis, [((i - distance) % count, i) for i in range(cou...  37.2 us
    pallas_call x3, Pallas kernels, local_call(): pl.pallas_call(kernel, out_shape=[jax.ShapeDtypeStruct(shape, dtype) for...  21.3 us
    ppermute x16, starting transfers between devices, passed_along(): lax.ppermute(block, axis, [((i - distance) % count, i) for i in range(cou...  20.8 us
    unnamed x36, local copies, waits for them, and re-layouts  5.01 us
    div x1, other arithmetic, shards(): grads = grads.astype(f32) / tiles  2.61 us
  transfers between devices with their start and end apart: 16, of which 11 were waited for; matrix products, arithmetic and copies ran while one was open for 3% of the time, Pallas kernels for 7%

commit v1 on v0

v1 whole, which is shorter than its diff:
```python
import functools
import math

import jax
import jax.numpy as jnp
from jax import lax
from jax.experimental import pallas as pl
from jax.experimental.pallas import tpu as pltpu
from jax.sharding import PartitionSpec as P

MODEL_WIDTH = 384
HEADS = 6
HEAD_WIDTH = 64
RIM = 8
SIDE = 16
TOKENS = 512
HALF = 256
EPS = 1e-05
LOG2E = math.log2(math.e)

bf16 = jnp.bfloat16
f32 = jnp.float32


def nn(a, b):
    return lax.dot_general(a, b, (((1,), (0,)), ((), ())), preferred_element_type=f32)


def nt(a, b):
    return lax.dot_general(a, b, (((1,), (1,)), ((), ())), preferred_element_type=f32)


def tn(a, b):
    return lax.dot_general(a, b, (((0,), (0,)), ((), ())), preferred_element_type=f32)


def iota(shape, dim):
    return lax.broadcasted_iota(jnp.int32, shape, dim)


def prepare_kernel(strips, cot, out_weight, qkv_weight, *outs):
    bias_blocks, d_context_t, qkv_weight_t = outs[:3], outs[3], outs[4]
    plain = strips[...] * LOG2E
    high = plain.astype(bf16)
    rest = plain - high.astype(f32)
    middle = rest.astype(bf16)
    low = (rest - middle.astype(f32)).astype(bf16)
    turn = iota((TOKENS, TOKENS), 0) + iota((TOKENS, TOKENS), 1) == TOKENS - 2
    turn = turn.astype(f32).astype(bf16)
    turned = nn(high, turn) + nn(middle, turn) + nn(low, turn)
    lane = iota((SIDE, TOKENS), 1)
    for entry in range(HEADS * 3):
        head, frame = divmod(entry, 3)
        first = 2 * (head * 3 + 2 - frame)
        even = jnp.broadcast_to(turned[first : first + 1, :], (SIDE, TOKENS))
        odd = jnp.broadcast_to(turned[first + 1 : first + 2, :], (SIDE, TOKENS))
        even = pltpu.roll(even, TOKENS - 15, 1, stride=1, stride_axis=0)
        odd = pltpu.roll(odd, TOKENS - 31, 1, stride=1, stride_axis=0)
        rows = jnp.where(lane % 32 < 16, even, odd)
        for row in range(SIDE):
            start = (15 - row) * SIDE
            bias_blocks[head // 2][entry % 6, row * SIDE : (row + 1) * SIDE, :] = rows[
                :, start : start + HALF
            ]
    d_context_t[...] = nt(out_weight[...], cot[...]).astype(bf16)
    qkv_weight_t[...] = qkv_weight[...].T


def source_onehots(row_shift, col_shift, sign):
    token = iota((HALF, 1), 0)
    row = token // SIDE + sign * row_shift
    col = token % SIDE + sign * col_shift
    if sign > 0:
        row_out, col_out = row >= SIDE, col >= SIDE
        near_row, near_col = row - SIDE, col - SIDE
    else:
        row_out, col_out = row < 0, col < 0
        near_row, near_col = row + RIM, col + RIM
    inner = jnp.where(row_out | col_out, -1, row * SIDE + col)
    rows = jnp.where(row_out & ~col_out, near_row * SIDE + col, -1)
    cols = jnp.where(col_out & ~row_out, row * RIM + near_col, -1)
    corner = jnp.where(row_out & col_out, near_row * RIM + near_col, -1)
    return [
        (iota((HALF, count), 1) == place).astype(f32).astype(bf16)
        for place, count in ((inner, HALF), (rows, 128), (cols, 128), (corner, 64))
    ]


def flag_strip(flags, first, count, width):
    total = count * width
    repeat = (iota((width, total), 1) % width == iota((width, total), 0)).astype(f32).astype(bf16)
    spread = nn(flags[first : first + count, :], repeat)
    keep = iota((count, total), 1) // width == iota((count, total), 0)
    strip = jnp.sum(jnp.where(keep, spread, 0.0), 0, keepdims=True)
    return jnp.broadcast_to(strip, (128, total)).astype(bf16)


def layer_norm(rolled):
    centred = rolled - jnp.mean(rolled, -1, keepdims=True)
    inv_std = lax.rsqrt(jnp.mean(centred * centred, -1, keepdims=True) + EPS)
    return centred * inv_std, inv_std


def attention_head(head, qkv_t, kv, penalty, bias_blocks, d_context_t):
    pair, side = divmod(head, 2)
    at = head * HEAD_WIDTH
    scale = LOG2E * HEAD_WIDTH ** (-0.5)
    zeros = jnp.zeros((HEAD_WIDTH, TOKENS), bf16)
    key_pair = kv[:, pair * 128 : pair * 128 + 128]
    value_pair = kv[:, MODEL_WIDTH + pair * 128 : MODEL_WIDTH + pair * 128 + 128]
    q_t = qkv_t[at : at + HEAD_WIDTH, :]
    k_t = qkv_t[MODEL_WIDTH + at : MODEL_WIDTH + at + HEAD_WIDTH, :]
    v_t = qkv_t[2 * MODEL_WIDTH + at : 2 * MODEL_WIDTH + at + HEAD_WIDTH, :]
    d_t = d_context_t[at : at + HEAD_WIDTH, :]
    d_eighth = d_t * 0.125
    q_wide = jnp.concatenate([q_t, zeros] if side == 0 else [zeros, q_t], 0)
    d_wide = jnp.concatenate([d_eighth, zeros] if side == 0 else [zeros, d_eighth], 0)
    context_parts = []
    dq_parts = []
    dk_parts = [0.0, 0.0]
    dv_parts = [0.0, 0.0]
    for b in range(2):
        lanes = slice(b * HALF, (b + 1) * HALF)
        scores = nn(key_pair, q_wide[:, lanes])
        d_probs = nn(value_pair, d_wide[:, lanes])
        halves = [slice(a * HALF, (a + 1) * HALF) for a in range(2)]
        s = [
            scores[halves[a]] * scale
            + bias_blocks[side * 3 + b - a + 1]
            + penalty[halves[a], lanes]
            for a in range(2)
        ]
        top = jnp.maximum(jnp.max(s[0], 0, keepdims=True), jnp.max(s[1], 0, keepdims=True))
        e = [jnp.exp2(s[a] - top) for a in range(2)]
        total = jnp.sum(e[0], 0, keepdims=True) + jnp.sum(e[1], 0, keepdims=True)
        inverse = 1.0 / total
        p = [e[a] * inverse for a in range(2)]
        pb = [p[a].astype(bf16) for a in range(2)]
        context_parts.append(nn(v_t[:, :HALF], pb[0]) + nn(v_t[:, HALF:], pb[1]))
        dp = [d_probs[halves[a]] for a in range(2)]
        delta = jnp.sum(p[0] * dp[0], 0, keepdims=True) + jnp.sum(p[1] * dp[1], 0, keepdims=True)
        ds = [(p[a] * (dp[a] - delta)).astype(bf16) for a in range(2)]
        dq_parts.append(nn(k_t[:, :HALF], ds[0]) + nn(k_t[:, HALF:], ds[1]))
        for a in range(2):
            dk_parts[a] = dk_parts[a] + nt(q_t[:, lanes], ds[a])
            dv_parts[a] = dv_parts[a] + nt(d_t[:, lanes], pb[a])
    return [
        jnp.concatenate(parts, 1).astype(bf16)
        for parts in (context_parts, dq_parts, dk_parts, dv_parts)
    ]


def finish_pair(left, right, normed_t, cot, grads, d_qkv, context_t):
    context, *d_parts = [jnp.concatenate(both, 0) for both in zip(left, right)]
    context_t[...] = context
    for kind in range(3):
        d_qkv[:, kind * 128 : kind * 128 + 128] = d_parts[kind].T
    grads[:128, :] = nn(context, cot[...]).astype(bf16)
    grads[128:, :] = nn(normed_t[...], d_qkv[...]).astype(bf16)


def first_kernel(
    shift,
    inner,
    halo,
    flags,
    gain,
    qkv_weight,
    qkv_weight_t,
    bias_blocks,
    d_context_t,
    cot,
    grads,
    d_qkv,
    context_t,
    rolled_out,
    qkv_t,
    kv,
    normed_t,
    penalty,
):
    onehots = source_onehots(shift[0], shift[1], 1)
    rolled = []
    on_diagonal = iota((HALF, HALF), 0) == iota((HALF, HALF), 1)
    for t in range(2):
        parts = (
            inner[t * 256 : t * 256 + 256, :],
            halo[t * 128 : t * 128 + 128, :],
            halo[256 + t * 128 : 384 + t * 128, :],
            halo[512 + t * 64 : 576 + t * 64, :],
        )
        rolled.append(sum(nn(hot, part) for hot, part in zip(onehots, parts)))
        strips = (
            flag_strip(flags[:32, :16], t * 16, 16, 16),
            flag_strip(flags[32:48, :16], t * 8, 8, 16),
            flag_strip(flags[48:80, :8], t * 16, 16, 8),
            flag_strip(flags[80:96, :8], t * 8, 8, 8),
        )
        marks = sum(nt(hot, strip) for hot, strip in zip(onehots, strips))
        column = jnp.where(marks > 0.5, -1e30, 0.0)
        wide = jnp.concatenate([column, column], 1)
        own = jnp.where(on_diagonal, 0.0, wide)
        penalty[t * HALF : (t + 1) * HALF, t * HALF : (t + 1) * HALF] = own
        penalty[t * HALF : (t + 1) * HALF, (1 - t) * HALF : (2 - t) * HALF] = wide
    rolled = jnp.concatenate(rolled, 0)
    rolled_out[...] = rolled.astype(bf16)
    xhat, _ = layer_norm(rolled)
    normed = (xhat * gain[...]).astype(bf16)
    normed_t[...] = normed.T
    qkv_t[...] = nt(qkv_weight_t[...], normed).astype(bf16)
    kv[...] = nn(normed, qkv_weight[:, MODEL_WIDTH:]).astype(bf16)
    heads = [attention_head(h, qkv_t, kv, penalty, bias_blocks, d_context_t) for h in range(2)]
    finish_pair(*heads, normed_t, cot, grads, d_qkv, context_t)


def left_kernel(pair, qkv_t, kv, penalty, bias_blocks, d_context_t, left):
    parts = attention_head(2 * pair, qkv_t, kv, penalty, bias_blocks, d_context_t)
    left[...] = jnp.concatenate(parts, 0)


def right_kernel(
    pair, qkv_t, kv, penalty, bias_blocks, d_context_t, left, normed_t, cot, *outs
):
    right = attention_head(2 * pair + 1, qkv_t, kv, penalty, bias_blocks, d_context_t)
    parts = [left[k * HEAD_WIDTH : (k + 1) * HEAD_WIDTH, :] for k in range(4)]
    finish_pair(parts, right, normed_t, cot, *outs)


def token_kernel(
    rolled, gain, qkv_weight, out_weight, d0, d1, d2, c0, c1, c2, update, d_rolled
):
    xhat, inv_std = layer_norm(rolled[...].astype(f32))
    d_normed = 0.0
    for pair, d_qkv in enumerate((d0, d1, d2)):
        columns = [
            qkv_weight[:, k * MODEL_WIDTH + pair * 128 : k * MODEL_WIDTH + pair * 128 + 128]
            for k in range(3)
        ]
        d_normed = d_normed + nt(d_qkv[...], jnp.concatenate(columns, 1))
    d_xhat = d_normed * gain[...]
    d_rolled[...] = (
        inv_std
        * (
            d_xhat
            - jnp.mean(d_xhat, -1, keepdims=True)
            - xhat * jnp.mean(d_xhat * xhat, -1, keepdims=True)
        )
    ).astype(bf16)
    context_t = jnp.concatenate([c0[...], c1[...], c2[...]], 0)
    update[...] = tn(context_t, out_weight[...]).astype(bf16)


def finish_kernel(pair, scale, *refs):
    core, mine, other, weight, gain = refs[:5]
    qkv_grad, out_grad, partial, gain_grad = refs[-4:]
    before = refs[-5] if pair else None
    first = core[0] == 0
    own, far = mine[...].astype(f32), other[...].astype(f32)
    upper = jnp.where(first, own, far) * scale
    lower = jnp.where(first, far, own) * scale
    out_grad[...] = upper[:128]
    block = jnp.concatenate([upper[128:], lower], 0)
    qkv_grad[...] = block
    product = block * weight[...].astype(f32)
    kind = pl.program_id(0)

    @pl.when(kind == 0)
    def _():
        partial[...] = (product + before[...]) if pair else product

    @pl.when(kind > 0)
    def _():
        partial[...] += product

    gain_grad[...] = jnp.sum(partial[...].T, 0, keepdims=True) / gain[...]


def unroll_kernel(shift, inner, halo, field_grad):
    onehots = source_onehots(shift[0], shift[1], -1)
    for t in range(2):
        parts = (
            inner[t * 256 : t * 256 + 256, :],
            halo[t * 128 : t * 128 + 128, :],
            halo[256 + t * 128 : 384 + t * 128, :],
            halo[512 + t * 64 : 576 + t * 64, :],
        )
        field_grad[t * 256 : t * 256 + 256, :] = sum(
            nn(hot, part) for hot, part in zip(onehots, parts)
        ).astype(bf16)


def local_call(kernel, shapes, inputs, scalars=0, micros=1, limit=24, after=(), hold=False):
    vmem = pl.BlockSpec(memory_space=pltpu.VMEM)
    smem = pl.BlockSpec(memory_space=pltpu.SMEM)
    anywhere = [pl.BlockSpec(memory_space=pl.ANY)] * len(after)
    count = len(inputs)
    held = list(after) if hold else []

    def body(*refs):
        kernel(*refs[:count], *refs[count + len(after) : len(refs) - len(held)])

    return pl.pallas_call(
        body,
        out_shape=[jax.ShapeDtypeStruct(shape, dtype) for shape, dtype in shapes]
        + [jax.ShapeDtypeStruct(array.shape, array.dtype) for array in held],
        in_specs=[smem] * scalars + [vmem] * (count - scalars) + anywhere,
        out_specs=[vmem] * len(shapes) + anywhere[: len(held)],
        input_output_aliases={count + i: len(shapes) + i for i in range(len(held))},
        compiler_params=pltpu.CompilerParams(vmem_limit_bytes=limit * 2**20),
        cost_estimate=pl.CostEstimate(
            flops=micros * 10**9, bytes_accessed=10**6, transcendentals=0
        ),
    )(*inputs, *after)


def finish_call(pair, scale, core, mine, other, qkv_weight, gain, earlier):
    width = MODEL_WIDTH
    half = pl.BlockSpec((256, 128), lambda k: (0, k))
    whole = pl.BlockSpec((width, 128), lambda k: (0, 0))
    row = pl.BlockSpec((1, width), lambda k: (0, 0))
    columns = pl.BlockSpec((width, 128), lambda k: (0, 3 * k + pair))
    in_specs = [pl.BlockSpec(memory_space=pltpu.SMEM), half, half, columns, row]
    inputs = [core, mine, other, qkv_weight, gain]
    aliases = {}
    if pair:
        in_specs += [pl.BlockSpec(memory_space=pl.ANY)] * 2 + [whole]
        inputs += list(earlier[:3])
        aliases = {5: 0, 6: 1}
    return pl.pallas_call(
        functools.partial(finish_kernel, pair, scale),
        grid=(3,),
        out_shape=[
            jax.ShapeDtypeStruct((width, 3 * width), f32),
            jax.ShapeDtypeStruct((width, width), f32),
            jax.ShapeDtypeStruct((width, 128), f32),
            jax.ShapeDtypeStruct((1, width), f32),
        ],
        in_specs=in_specs,
        out_specs=[columns, pl.BlockSpec((128, 128), lambda k: (pair, k)), whole, row],
        input_output_aliases=aliases,
        compiler_params=pltpu.CompilerParams(vmem_limit_bytes=16 * 2**20),
    )(*inputs)


def passed_along(block, axis, distance):
    count = lax.axis_size(axis)
    return lax.ppermute(block, axis, [((i - distance) % count, i) for i in range(count)])


def swapped(block, axis, bit):
    return lax.ppermute(block, axis, [(i, i ^ bit) for i in range(lax.axis_size(axis))])


def upper_side(axis, bit):
    return (lax.axis_index(axis) & bit) // bit


def halve(block, axis, bit):
    side = upper_side(axis, bit)
    share = block.shape[0] // 2
    far = lax.dynamic_slice_in_dim(block, (1 - side) * share, share, 0)
    own = lax.dynamic_slice_in_dim(block, side * share, share, 0)
    return (own.astype(f32) + swapped(far, axis, bit).astype(f32)).astype(bf16)


def double(block, axis, bit):
    other = swapped(block, axis, bit)
    above = upper_side(axis, bit) == 1
    return jnp.concatenate([jnp.where(above, other, block), jnp.where(above, block, other)], 0)


def axis_bits(axis):
    count = lax.axis_size(axis)
    return [(axis, 1 << k) for k in range(count.bit_length() - 1)]


def shards(
    state_field,
    outlier_flags,
    window_shift,
    layer_norm_gain,
    qkv_weight,
    out_weight,
    position_bias,
    cotangent,
):
    width = MODEL_WIDTH
    wide = lambda tokens: ((tokens, width), bf16)
    rows = passed_along(state_field[:, :RIM].reshape(-1, width), "sy", -1)
    marks = outlier_flags.astype(bf16)
    row_marks = passed_along(marks[:, :RIM].reshape(2 * RIM, SIDE), "sy", -1)
    cols = passed_along(state_field[:, :, :RIM].reshape(-1, width), "sx", -1)
    col_marks = passed_along(marks[:, :, :RIM].reshape(2 * SIDE, RIM), "sx", -1)
    strips = jnp.pad(
        position_bias.reshape(HEADS, 3, 31, 31), ((0, 0), (0, 0), (0, 1), (0, 1))
    )
    strips = strips.reshape(HEADS, 3, 16, 2, 32).transpose(0, 1, 3, 2, 4).reshape(36, TOKENS)
    cot_rows = cotangent.reshape(TOKENS, width)
    *bias_blocks, d_context_t, qkv_weight_t = local_call(
        prepare_kernel,
        [((6, HALF, HALF), f32)] * 3 + [((width, TOKENS), bf16), wide(3 * width)],
        [strips, cot_rows, out_weight, qkv_weight],
        micros=3,
    )
    corner = passed_along(
        rows.reshape(2 * RIM, SIDE, width)[:, :RIM].reshape(-1, width), "sx", -1
    )
    corner_marks = passed_along(row_marks[:, :RIM], "sx", -1)
    halo = jnp.concatenate([rows, cols, corner], 0)
    all_marks = jnp.concatenate(
        [jnp.pad(m, ((0, 0), (0, 128 - m.shape[1])))
         for m in (marks.reshape(2 * SIDE, SIDE), row_marks, col_marks, corner_marks)],
        0,
    )
    gain = layer_norm_gain.reshape(1, width)
    pair_shapes = [wide(TOKENS), wide(TOKENS), ((128, TOKENS), bf16)]
    grads, d_qkv, context_t, rolled, *shared = local_call(
        first_kernel,
        pair_shapes
        + [
            wide(TOKENS),
            ((3 * width, TOKENS), bf16),
            ((TOKENS, 2 * width), bf16),
            ((width, TOKENS), bf16),
            ((TOKENS, TOKENS), f32),
        ],
        [
            window_shift,
            state_field.reshape(TOKENS, width),
            halo,
            all_marks,
            gain,
            qkv_weight,
            qkv_weight_t,
            bias_blocks[0],
            d_context_t,
            cot_rows,
        ],
        scalars=1,
        micros=6,
    )
    bits = axis_bits("sx") + axis_bits("ta") + axis_bits("sy")
    results = [(grads, d_qkv, context_t)]
    qkv_t, kv, normed_t, penalty = shared
    common = lambda pair: [qkv_t, kv, penalty, bias_blocks[pair], d_context_t]
    left = lambda pair, after: local_call(
        functools.partial(left_kernel, pair),
        [((4 * HEAD_WIDTH, TOKENS), bf16)],
        common(pair),
        micros=2,
        after=after,
    )
    right = lambda pair, part, after: local_call(
        functools.partial(right_kernel, pair),
        pair_shapes,
        [*common(pair), *part, normed_t, cot_rows],
        micros=3,
        after=after,
    )
    part = left(1, [])
    first = halve(grads, *bits[0])
    results.append(right(1, part, [first]))
    first = halve(first, *bits[1])
    part = left(2, [first])
    first = halve(first, *bits[2])
    second = halve(results[1][0], *bits[0])
    results.append(right(2, part, [first, second]))
    first = halve(first, *bits[3])
    second = halve(second, *bits[1])
    update, d_rolled, first, second = local_call(
        token_kernel,
        [wide(TOKENS), wide(TOKENS)],
        [rolled, gain, qkv_weight, out_weight]
        + [r[1] for r in results]
        + [r[2] for r in results],
        micros=2,
        after=[first, second],
        hold=True,
    )
    shares = [first, second, results[2][0]]
    grid = d_rolled.reshape(2, SIDE, SIDE, width)
    below = passed_along(grid[:, RIM:].reshape(-1, width), "sy", 1)
    beside = passed_along(grid[:, :, RIM:].reshape(-1, width), "sx", 1)
    across = passed_along(
        below.reshape(2 * RIM, SIDE, width)[:, RIM:].reshape(-1, width), "sx", 1
    )
    (field_grad,) = local_call(
        unroll_kernel,
        [wide(TOKENS)],
        [window_shift, d_rolled, jnp.concatenate([below, beside, across], 0)],
        scalars=1,
    )
    scale = 1.0 / (lax.axis_size("sy") * lax.axis_size("sx") * lax.axis_size("ta"))
    core = lax.axis_index("sx").astype(jnp.int32).reshape(1)
    done = None
    for pair in range(3):
        share = shares[pair]
        for axis, bit in bits[(4, 2, 0)[pair] :]:
            share = halve(share, axis, bit)
        for axis, bit in bits[:0:-1]:
            share = double(share, axis, bit)
        other = swapped(share, *bits[0])
        done = finish_call(pair, scale, core, share, other, qkv_weight, gain, done)
    qkv_grad, out_grad, _, gain_grad = done
    shape = state_field.shape
    return (
        update.reshape(shape),
        field_grad.reshape(shape),
        qkv_grad,
        out_grad,
        gain_grad.reshape(width),
    )


def solution(mesh):
    in_specs = (
        P(("groups", "ta"), "sy", "sx", None),
        P(("groups", "ta"), "sy", "sx"),
        P(),
        P(),
        P(),
        P(),
        P(),
        P(("groups", "ta"), "sy", "sx", None),
    )
    out_specs = (
        P(("groups", "ta"), "sy", "sx", None),
        P(("groups", "ta"), "sy", "sx", None),
        P("groups", None),
        P("groups", None),
        P("groups"),
    )
    return jax.shard_map(shards, mesh=mesh, in_specs=in_specs, out_specs=out_specs, check_vma=False)
```

time: 97.8 us -> 118 us (1.21)
  starting transfers between devices: 20.8 us -> 52.6 us
  waiting for transfers between devices: 37.2 us -> 13.9 us
  local copies, waits for them, and re-layouts: 8.64 us -> 22.5 us
  other arithmetic: 8.22 us -> 3.14 us
  Pallas kernels: 21.3 us -> 24.6 us
    ppermute x0 -> x24, starting transfers between devices: none -> 41.3 us  [swapped(): lax.ppermute(block, axis, [(i, i ^ bit) for i in range(lax.axis_size(axis...]
    ppermute x16 -> x9, waiting for transfers between devices: 37.2 us -> 1.01 us  [passed_along(): lax.ppermute(block, axis, [((i - distance) % count, i) for i in range(cou...]
    unnamed x36 -> x62, local copies, waits for them, and re-layouts: 5.01 us -> 18.2 us
    ppermute x0 -> x24, waiting for transfers between devices: none -> 12.9 us  [swapped(): lax.ppermute(block, axis, [(i, i ^ bit) for i in range(lax.axis_size(axis...]
    ppermute x16 -> x9, starting transfers between devices: 20.8 us -> 11.3 us  [passed_along(): lax.ppermute(block, axis, [((i - distance) % count, i) for i in range(cou...]
    pallas_call x3 -> x11, Pallas kernels: 21.3 us -> 24.6 us  [the longest x8 19.5 us: local_call(): pl.pallas_call(body, out_shape=[jax.ShapeDtypeStruct(shape, dtype) for sh...]
    div x2 -> x0, other arithmetic: 3.19 us -> none  [the longest x1 2.61 us: shards(): grads = grads.astype(f32) / tiles]
    reduce_sum x1 -> x0, other arithmetic: 1.45 us -> none  [shards(): gain_grad = jnp.sum(qkv_grad * qkv_weight.astype(f32), 1) / layer_norm_gain]
  transfers between devices with their start and end apart: 16 -> 33, of which waited for: 11 -> 11; matrix products, arithmetic and copies ran while one was open for 3% -> 3% of each run, Pallas kernels for 7% -> 13%
where the time goes in v1:
time: 118 us
  starting transfers between devices  52.6 us (45%)
  Pallas kernels  24.6 us (21%)
  local copies, waits for them, and re-layouts  22.5 us (19%)
  waiting for transfers between devices  13.9 us (12%)
  other arithmetic  3.14 us (3%)
  between operations  1.23 us (1%)
    ppermute x24, starting transfers between devices, swapped(): lax.ppermute(block, axis, [(i, i ^ bit) for i in range(lax.axis_size(axis...  41.3 us
    pallas_call x8, Pallas kernels, local_call(): pl.pallas_call(body, out_shape=[jax.ShapeDtypeStruct(shape, dtype) for sh...  19.5 us
    unnamed x62, local copies, waits for them, and re-layouts  18.2 us
    ppermute x24, waiting for transfers between devices, swapped(): lax.ppermute(block, axis, [(i, i ^ bit) for i in range(lax.axis_size(axis...  12.9 us
    ppermute x9, starting transfers between devices, passed_along(): lax.ppermute(block, axis, [((i - distance) % count, i) for i in range(cou...  11.3 us
    pallas_call x3, Pallas kernels, finish_call(): pl.pallas_call(functools.partial(finish_kernel, pair, scale), grid=(3,),...  5.14 us
  transfers between devices with their start and end apart: 33, of which 11 were waited for; matrix products, arithmetic and copies ran while one was open for 3% of the time, Pallas kernels for 13%

profile of v1, /device:TPU:1, one launch (start us, length us, event | category | flops | bytes accessed | tf_op | source)
XLA Modules:
  0.0 118.0 jit_solution(10058587431870253733)
XLA Ops:
  1.5 4.2 %collective-permute-start.3 = (bf16[16,16]{1,0:T(8,128)(2,1)S(1)}, bf16[16,16]{1,0:T(8,128)(2,1)S(1)}, u32[]{:S(2)}, u32[]{:S(2)}) collective-permute-start(bf16[16,16]{1,0:T(8,128)(2,1)S(1)} %slice_bitcast_fusion.2), channel_id=1, source_target_pairs={{4,0},{8,4},{12,8},{0,12},{5,1},{9,5},{13,9},{1,13},{6,2},{10,6},{... | collective-permute-start | bytes 1544 | tf_op jit(solution)/shard_map/ppermute | solution.py:347
  10.6 2.8 %shard_map.119 = (f32[6,256,256]{2,1,0:T(8,128)S(1)}, f32[6,256,256]{2,1,0:T(8,128)S(1)}, f32[6,256,256]{2,1,0:T(8,128)S(1)}, bf16[384,512]{1,0:T(8,128)(2,1)S(1)}, bf16[1152,384]{1,0:T(8,128)(2,1)S(1)}) custom-call(f32[36,512]{1,0:T(8,128)S(1)} %reshape.87.refs_0_, bf16[512,384]{1,0:T(8,128)(2,1)S(1)} %bitcast.30, bf16[384,384]{1,0:T(8,128)(2,1)S(1)} %copy-done.3, ...), custom_call_target="tpu_custom_call" | custom-call | flops 3000000000 | bytes 1000000 | tf_op jit(solution)/shard_map/pallas_call | solution.py:302
  23.8 5.8 %shard_map.120 = (bf16[512,384]{1,0:T(8,128)(2,1)S(1)}, bf16[512,384]{1,0:T(8,128)(2,1)S(1)}, bf16[128,512]{1,0:T(8,128)(2,1)S(1)}, bf16[512,384]{1,0:T(8,128)(2...) custom-call(s32[2]{0:T(128)S(1)} %copy-done.4, ...), custom_call_target="tpu_custom_call" | custom-call | flops 6000000000 | bytes 1000000 | tf_op jit(solution)/shard_map/pallas_call | solution.py:302
  43.9 1.9 %shard_map.122 = (bf16[512,384]{1,0:T(8,128)(2,1)S(1)}, bf16[512,384]{1,0:T(8,128)(2,1)S(1)}, bf16[128,512]{1,0:T(8,128)(2,1)S(1)}) custom-call(bf16[1152,512]{1,0:T(8,128)(2,1)S(1)} %get-tuple-element.42.refs_0_, bf16[512,768]{1,0:T(8,128)(2,1)S(1)} %copy-done.14, f32[512,512]{1,0:T(8,128)S(1)} %copy-done.11, f32[6,256,256]{2,1,0:T(8,128)S(1)} %copy-done.8, ...), custom_call_target="tpu_custom_call" | custom-call | flops 3000000000 | bytes 1000000 | tf_op jit(solution)/shard_map/pallas_call | solution.py:302
  50.1 1.7 %shard_map.123.refs_5_ = bf16[256,512]{1,0:T(8,128)(2,1)S(1)} custom-call(bf16[1152,512]{1,0:T(8,128)(2,1)S(1)} %get-tuple-element.42.refs_0_, bf16[512,768]{1,0:T(8,128)(2,1)S(1)} %copy-done.14, f32[512,512]{1,0:T(8,128)S(1)} %copy-done.11, f32[6,256,256]{2,1,0:T(8,128)S(1)} %copy-done.6, bf16[384,512]{1,0:T(8,128)(2,1)S(1)} %copy-done.17, ...), custom_call_target="tpu_custom_call" | custom-call | flops 2000000000 | bytes 1000000 | tf_op jit(solution)/shard_map/pallas_call | solution.py:302
  51.7 1.9 %collective-permute-done.10 = bf16[32,384]{1,0:T(8,128)(2,1)S(1)} collective-permute-done((bf16[32,384]{1,0:T(8,128)(2,1)S(1)}, bf16[32,384]{1,0:T(8,128)(2,1)S(1)}, u32[]{:S(2)}, u32[]{:S(2)}) %collective-permute-start.10) | collective-permute-done | bytes 24608 | tf_op jit(solution)/shard_map/ppermute | solution.py:351
  55.0 1.9 %shard_map.124 = (bf16[512,384]{1,0:T(8,128)(2,1)S(1)}, bf16[512,384]{1,0:T(8,128)(2,1)S(1)}, bf16[128,512]{1,0:T(8,128)(2,1)S(1)}) custom-call(bf16[1152,512]{1,0:T(8,128)(2,1)S(1)} %get-tuple-element.42.refs_0_, bf16[512,768]{1,0:T(8,128)(2,1)S(1)} %copy-done.14, f32[512,512]{1,0:T(8,128)S(1)} %copy-done.11, f32[6,256,256]{2,1,0:T(8,128)S(1)} %copy-done.6, ...), custom_call_target="tpu_custom_call" | custom-call | flops 3000000000 | bytes 1000000 | tf_op jit(solution)/shard_map/pallas_call | solution.py:302
  57.4 2.0 %shard_map.125 = (bf16[512,384]{1,0:T(8,128)(2,1)}, bf16[512,384]{1,0:T(8,128)(2,1)S(1)}, bf16[32,384]{1,0:T(8,128)(2,1)S(1)}, bf16[128,384]{1,0:T(8,128)(2,1)S(1)}) custom-call(bf16[512,384]{1,0:T(8,128)(2,1)S(1)} %copy-done.21, f32[1,384]{1,0:T(1,128)S(1)} %reshape.84.refs_4_.refs_1_, ...), custom_call_target="tpu_custom_call", output_to_operand_aliasing={{2}: (10, {}), {3}: (11, {})} | custom-call | flops 2000000000 | bytes 1000000 | tf_op jit(solution)/shard_map/pallas_call | solution.py:302
  60.7 5.1 %collective-permute-start.15 = (bf16[256,384]{1,0:T(8,128)(2,1)S(1)}, bf16[256,384]{1,0:T(8,128)(2,1)S(1)}, u32[]{:S(2)}, u32[]{:S(2)}) collective-permute-start(bf16[256,384]{1,0:T(8,128)(2,1)S(1)} %constant_dynamic-slice_fusion.5), channel_id=1, source_target_pairs={{0,2},{2,0},{1,3},{3,1},{4,6},{6,4},{5,7},{7,5},{8,10},{10,8},{9,1... | collective-permute-start | bytes 589832 | tf_op jit(solution)/shard_map/ppermute | solution.py:351
  66.2 2.6 %collective-permute-start.24 = (bf16[32,384]{1,0:T(8,128)(2,1)S(1)}, bf16[32,384]{1,0:T(8,128)(2,1)S(1)}, u32[]{:S(2)}, u32[]{:S(2)}) collective-permute-start(bf16[32,384]{1,0:T(8,128)(2,1)S(1)} %constant_dynamic-slice_fusion), channel_id=1, source_target_pairs={{0,8},{4,12},{8,0},{12,4},{1,9},{5,13},{9,1},{13,5},{2,10},{6,14},... | collective-permute-start | bytes 73736 | tf_op jit(solution)/shard_map/ppermute | solution.py:351
  71.7 2.9 %collective-permute-start.25 = (bf16[32,384]{1,0:T(8,128)(2,1)S(1)}, bf16[32,384]{1,0:T(8,128)(2,1)S(1)}, u32[]{:S(2)}, u32[]{:S(2)}) collective-permute-start(bf16[32,384]{1,0:T(8,128)(2,1)S(1)} %add_convert_fusion.9), channel_id=1, source_target_pairs={{0,8},{4,12},{8,0},{12,4},{1,9},{5,13},{9,1},{13,5},{2,10},{6,14},... | collective-permute-start | bytes 73736 | tf_op jit(solution)/shard_map/ppermute | solution.py:351
  74.6 2.0 %collective-permute-start.30 = (bf16[64,384]{1,0:T(8,128)(2,1)S(1)}, bf16[64,384]{1,0:T(8,128)(2,1)S(1)}, u32[]{:S(2)}, u32[]{:S(2)}) collective-permute-start(bf16[64,384]{1,0:T(8,128)(2,1)S(1)} %pad_maximum_fusion.10), channel_id=1, source_target_pairs={{0,4},{4,0},{8,12},{12,8},{1,5},{5,1},{9,13},{13,9},{2,6},{6,2},{1... | collective-permute-start | bytes 147464 | tf_op jit(solution)/shard_map/ppermute | solution.py:351
  76.6 2.1 %collective-permute-start.26 = (bf16[64,384]{1,0:T(8,128)(2,1)S(1)}, bf16[64,384]{1,0:T(8,128)(2,1)S(1)}, u32[]{:S(2)}, u32[]{:S(2)}) collective-permute-start(bf16[64,384]{1,0:T(8,128)(2,1)S(1)} %pad_maximum_fusion.9), channel_id=1, source_target_pairs={{0,4},{4,0},{8,12},{12,8},{1,5},{5,1},{9,13},{13,9},{2,6},{6,2},{1... | collective-permute-start | bytes 147464 | tf_op jit(solution)/shard_map/ppermute | solution.py:351
  82.4 1.8 %collective-permute-start.17 = (bf16[64,384]{1,0:T(8,128)(2,1)S(1)}, bf16[64,384]{1,0:T(8,128)(2,1)S(1)}, u32[]{:S(2)}, u32[]{:S(2)}) collective-permute-start(bf16[64,384]{1,0:T(8,128)(2,1)S(1)} %constant_dynamic-slice_fusion.3), channel_id=1, source_target_pairs={{0,4},{4,0},{8,12},{12,8},{1,5},{5,1},{9,13},{13,9},{2,6},{6,2},{1... | collective-permute-start | bytes 147464 | tf_op jit(solution)/shard_map/ppermute | solution.py:351
  84.2 4.8 %collective-permute-start.14 = (bf16[128,384]{1,0:T(8,128)(2,1)S(1)}, bf16[128,384]{1,0:T(8,128)(2,1)S(1)}, u32[]{:S(2)}, u32[]{:S(2)}) collective-permute-start(bf16[128,384]{1,0:T(8,128)(2,1)S(1)} %slice_bitcast_fusion), channel_id=1, source_target_pairs={{2,0},{0,2},{3,1},{1,3},{6,4},{4,6},{7,5},{5,7},{10,8},{8,10},{11,... | collective-permute-start | bytes 294920 | tf_op jit(solution)/shard_map/ppermute | solution.py:347
  89.8 3.1 %collective-permute-done.18 = bf16[32,384]{1,0:T(8,128)(2,1)S(1)} collective-permute-done((bf16[32,384]{1,0:T(8,128)(2,1)S(1)}, bf16[32,384]{1,0:T(8,128)(2,1)S(1)}, u32[]{:S(2)}, u32[]{:S(2)}) %collective-permute-start.18) | collective-permute-done | bytes 24608 | tf_op jit(solution)/shard_map/ppermute | solution.py:351
  93.5 5.0 %collective-permute-start.32 = (bf16[256,384]{1,0:T(8,128)(2,1)S(1)}, bf16[256,384]{1,0:T(8,128)(2,1)S(1)}, u32[]{:S(2)}, u32[]{:S(2)}) collective-permute-start(bf16[256,384]{1,0:T(8,128)(2,1)S(1)} %pad_maximum_fusion.4.refs_1_), channel_id=1, source_target_pairs={{0,2},{2,0},{1,3},{3,1},{4,6},{6,4},{5,7},{7,5},{8,10},{10,8},{9,1... | collective-permute-start | bytes 589832 | tf_op jit(solution)/shard_map/ppermute | solution.py:351
  98.8 2.7 %collective-permute-done.20 = bf16[64,384]{1,0:T(8,128)(2,1)S(1)} collective-permute-done((bf16[64,384]{1,0:T(8,128)(2,1)S(1)}, bf16[64,384]{1,0:T(8,128)(2,1)S(1)}, u32[]{:S(2)}, u32[]{:S(2)}) %collective-permute-start.20) | collective-permute-done | bytes 49184 | tf_op jit(solution)/shard_map/ppermute | solution.py:351
  102.9 4.2 %collective-permute-start.28 = (bf16[256,384]{1,0:T(8,128)(2,1)S(1)}, bf16[256,384]{1,0:T(8,128)(2,1)S(1)}, u32[]{:S(2)}, u32[]{:S(2)}) collective-permute-start(bf16[256,384]{1,0:T(8,128)(2,1)S(1)} %pad_maximum_fusion.3.refs_1_), channel_id=1, source_target_pairs={{0,2},{2,0},{1,3},{3,1},{4,6},{6,4},{5,7},{7,5},{8,10},{10,8},{9,1... | collective-permute-start | bytes 589832 | tf_op jit(solution)/shard_map/ppermute | solution.py:351
  107.1 3.1 %collective-permute-start.22 = (bf16[256,384]{1,0:T(8,128)(2,1)S(1)}, bf16[256,384]{1,0:T(8,128)(2,1)S(1)}, u32[]{:S(2)}, u32[]{:S(2)}) collective-permute-start(bf16[256,384]{1,0:T(8,128)(2,1)S(1)} %pad_maximum_fusion.2.refs_1_), channel_id=1, source_target_pairs={{0,2},{2,0},{1,3},{3,1},{4,6},{6,4},{5,7},{7,5},{8,10},{10,8},{9,1... | collective-permute-start | bytes 589832 | tf_op jit(solution)/shard_map/ppermute | solution.py:351
  110.3 2.0 %shard_map.126 = bf16[512,384]{1,0:T(8,128)(2,1)} custom-call(s32[2]{0:T(128)S(1)} %copy-done.4, bf16[512,384]{1,0:T(8,128)(2,1)S(1)} %get-tuple-element.56.refs_1_, bf16[640,384]{1,0:T(8,128)(2,1)S(1)} %pad_maximum_fusion.1.refs_2_), custom_call_target="tpu_custom_call" | custom-call | flops 1000000000 | bytes 1000000 | tf_op jit(solution)/shard_map/pallas_call | solution.py:302
  112.2 1.7 %shard_map.127 = (f32[384,1152]{1,0:T(8,128)}, f32[384,384]{1,0:T(8,128)}, f32[384,128]{1,0:T(8,128)S(1)}, f32[1,384]{1,0:T(1,128)}) custom-call(s32[1]{0:T(128)} %bitcast.18.refs_0_, bf16[256,384]{1,0:T(8,128)(2,1)S(1)} %pad_maximum_fusion.4.refs_1_, bf16[256,384]{1,0:T(8,128)(2,1)S(1)} %collective-permute-done.32.refs_2_, bf16[384,1152]{1,0:T(8,128)(2,1)S(1)} %copy-done, ...), custom_call_target="tpu_custom_call" | custom-call | tf_op jit(solution)/shard_map/pallas_call | solution.py:329
  113.9 1.7 %shard_map.128 = (f32[384,1152]{1,0:T(8,128)}, f32[384,384]{1,0:T(8,128)}, f32[384,128]{1,0:T(8,128)S(1)}, f32[1,384]{1,0:T(1,128)}) custom-call(s32[1]{0:T(128)} %bitcast.18.refs_0_, bf16[256,384]{1,0:T(8,128)(2,1)S(1)} %pad_maximum_fusion.3.refs_1_, ...), custom_call_target="tpu_custom_call", output_to_operand_aliasing={{0}: (5, {}), {1}: (6, {})} | custom-call | tf_op jit(solution)/shard_map/pallas_call | solution.py:329
  115.6 1.8 %shard_map.129 = (f32[384,1152]{1,0:T(8,128)}, f32[384,384]{1,0:T(8,128)}, f32[384,128]{1,0:T(8,128)}, f32[1,384]{1,0:T(1,128)S(1)}) custom-call(s32[1]{0:T(128)} %bitcast.18.refs_0_, bf16[256,384]{1,0:T(8,128)(2,1)S(1)} %pad_maximum_fusion.2.refs_1_, ...), custom_call_target="tpu_custom_call", output_to_operand_aliasing={{0}: (5, {}), {1}: (6, {})} | custom-call | tf_op jit(solution)/shard_map/pallas_call | solution.py:329
  (173 shorter events, 48.3 us)
Async XLA Ops:
  1.5 17.0 %collective-permute-start.3 = (bf16[16,16]{1,0:T(8,128)(2,1)S(1)}, bf16[16,16]{1,0:T(8,128)(2,1)S(1)}, u32[]{:S(2)}, u32[]{:S(2)}) collective-permute-start(bf16[16,16]{1,0:T(8,128)(2,1)S(1)} %slice_bitcast_fusion.2), channel_id=1, source_target_pairs={{4,0},{8,4},{12,8},{0,12},{5,1},{9,5},{13,9},{1,13},{6,2},{10,6},{... | collective-permute-start | bytes 1544 | tf_op jit(solution)/shard_map/ppermute | solution.py:347
  5.7 13.5 %collective-permute-start.4 = (bf16[32,8]{1,0:T(8,128)(2,1)S(1)}, bf16[32,8]{1,0:T(8,128)(2,1)S(1)}, u32[]{:S(2)}, u32[]{:S(2)}) collective-permute-start(bf16[32,8]{1,0:T(8,128)(2,1)S(1)} %bitcast.41), channel_id=1, source_target_pairs={{2,0},{0,2},{3,1},{1,3},{6,4},{4,6},{7,5},{5,7},{10,8},{8,10},{11,... | collective-permute-start | bytes 1544 | tf_op jit(solution)/shard_map/ppermute | solution.py:347
  7.6 11.2 %collective-permute-start = (bf16[256,384]{1,0:T(8,128)(2,1)S(1)}, bf16[256,384]{1,0:T(8,128)(2,1)S(1)}, u32[]{:S(2)}, u32[]{:S(2)}) collective-permute-start(bf16[256,384]{1,0:T(8,128)(2,1)S(1)} %bitcast.40), channel_id=1, source_target_pairs={{4,0},{8,4},{12,8},{0,12},{5,1},{9,5},{13,9},{1,13},{6,2},{10,6},{... | collective-permute-start | bytes 589832 | tf_op jit(solution)/shard_map/ppermute | solution.py:347
  8.7 11.0 %collective-permute-start.1 = (bf16[256,384]{1,0:T(8,128)(2,1)S(1)}, bf16[256,384]{1,0:T(8,128)(2,1)S(1)}, u32[]{:S(2)}, u32[]{:S(2)}) collective-permute-start(bf16[256,384]{1,0:T(8,128)(2,1)S(1)} %bitcast.39), channel_id=1, source_target_pairs={{2,0},{0,2},{3,1},{1,3},{6,4},{4,6},{7,5},{5,7},{10,8},{8,10},{11,... | collective-permute-start | bytes 589832 | tf_op jit(solution)/shard_map/ppermute | solution.py:347
  35.0 6.6 %collective-permute-start.6 = (bf16[256,384]{1,0:T(8,128)(2,1)}, bf16[256,384]{1,0:T(8,128)(2,1)}, u32[]{:S(2)}, u32[]{:S(2)}) collective-permute-start(bf16[256,384]{1,0:T(8,128)(2,1)} %constant_dynamic-slice_fusion.11), channel_id=1, source_target_pairs={{0,2},{2,0},{1,3},{3,1},{4,6},{6,4},{5,7},{7,5},{8,10},{10,8},{9,1... | collective-permute-start | bytes 589832 | tf_op jit(solution)/shard_map/ppermute | solution.py:351
  42.6 4.2 %collective-permute-start.7 = (bf16[128,384]{1,0:T(8,128)(2,1)S(1)}, bf16[128,384]{1,0:T(8,128)(2,1)S(1)}, u32[]{:S(2)}, u32[]{:S(2)}) collective-permute-start(bf16[128,384]{1,0:T(8,128)(2,1)S(1)} %constant_dynamic-slice_fusion.10), channel_id=1, source_target_pairs={{0,1},{1,0},{2,3},{3,2},{4,5},{5,4},{6,7},{7,6},{8,9},{9,8},{10,11... | collective-permute-start | bytes 294920 | tf_op jit(solution)/shard_map/ppermute | solution.py:351
  48.3 5.3 %collective-permute-start.9 = (bf16[256,384]{1,0:T(8,128)(2,1)S(1)}, bf16[256,384]{1,0:T(8,128)(2,1)S(1)}, u32[]{:S(2)}, u32[]{:S(2)}) collective-permute-start(bf16[256,384]{1,0:T(8,128)(2,1)S(1)} %constant_dynamic-slice_fusion.8), channel_id=1, source_target_pairs={{0,2},{2,0},{1,3},{3,1},{4,6},{6,4},{5,7},{7,5},{8,10},{10,8},{9,1... | collective-permute-start | bytes 589832 | tf_op jit(solution)/shard_map/ppermute | solution.py:351
  59.4 6.8 %collective-permute-start.23 = (bf16[64,384]{1,0:T(8,128)(2,1)S(1)}, bf16[64,384]{1,0:T(8,128)(2,1)S(1)}, u32[]{:S(2)}, u32[]{:S(2)}) collective-permute-start(bf16[64,384]{1,0:T(8,128)(2,1)S(1)} %constant_dynamic-slice_fusion.1), channel_id=1, source_target_pairs={{0,4},{4,0},{8,12},{12,8},{1,5},{5,1},{9,13},{13,9},{2,6},{6,2},{1... | collective-permute-start | bytes 147464 | tf_op jit(solution)/shard_map/ppermute | solution.py:351
  60.7 18.0 %collective-permute-start.15 = (bf16[256,384]{1,0:T(8,128)(2,1)S(1)}, bf16[256,384]{1,0:T(8,128)(2,1)S(1)}, u32[]{:S(2)}, u32[]{:S(2)}) collective-permute-start(bf16[256,384]{1,0:T(8,128)(2,1)S(1)} %constant_dynamic-slice_fusion.5), channel_id=1, source_target_pairs={{0,2},{2,0},{1,3},{3,1},{4,6},{6,4},{5,7},{7,5},{8,10},{10,8},{9,1... | collective-permute-start | bytes 589832 | tf_op jit(solution)/shard_map/ppermute | solution.py:351
  65.8 4.2 %collective-permute-start.29 = (bf16[32,384]{1,0:T(8,128)(2,1)S(1)}, bf16[32,384]{1,0:T(8,128)(2,1)S(1)}, u32[]{:S(2)}, u32[]{:S(2)}) collective-permute-start(bf16[32,384]{1,0:T(8,128)(2,1)S(1)} %get-tuple-element.59), channel_id=1, source_target_pairs={{0,8},{4,12},{8,0},{12,4},{1,9},{5,13},{9,1},{13,5},{2,10},{6,14},... | collective-permute-start | bytes 73736 | tf_op jit(solution)/shard_map/ppermute | solution.py:351
  65.9 18.3 %collective-permute-start.12 = (bf16[256,384]{1,0:T(8,128)(2,1)S(1)}, bf16[256,384]{1,0:T(8,128)(2,1)S(1)}, u32[]{:S(2)}, u32[]{:S(2)}) collective-permute-start(bf16[256,384]{1,0:T(8,128)(2,1)S(1)} %bitcast.38), channel_id=1, source_target_pairs={{12,0},{0,4},{4,8},{8,12},{13,1},{1,5},{5,9},{9,13},{14,2},{2,6},{... | collective-permute-start | bytes 589832 | tf_op jit(solution)/shard_map/ppermute | solution.py:347
  66.0 44.2 %collective-permute-start.13 = (bf16[256,384]{1,0:T(8,128)(2,1)S(1)}, bf16[256,384]{1,0:T(8,128)(2,1)S(1)}, u32[]{:S(2)}, u32[]{:S(2)}) collective-permute-start(bf16[256,384]{1,0:T(8,128)(2,1)S(1)} %bitcast.37), channel_id=1, source_target_pairs={{2,0},{0,2},{3,1},{1,3},{6,4},{4,6},{7,5},{5,7},{10,8},{8,10},{11,... | collective-permute-start | bytes 589832 | tf_op jit(solution)/shard_map/ppermute | solution.py:347
  66.2 5.5 %collective-permute-start.24 = (bf16[32,384]{1,0:T(8,128)(2,1)S(1)}, bf16[32,384]{1,0:T(8,128)(2,1)S(1)}, u32[]{:S(2)}, u32[]{:S(2)}) collective-permute-start(bf16[32,384]{1,0:T(8,128)(2,1)S(1)} %constant_dynamic-slice_fusion), channel_id=1, source_target_pairs={{0,8},{4,12},{8,0},{12,4},{1,9},{5,13},{9,1},{13,5},{2,10},{6,14},... | collective-permute-start | bytes 73736 | tf_op jit(solution)/shard_map/ppermute | solution.py:351
  71.7 4.9 %collective-permute-start.25 = (bf16[32,384]{1,0:T(8,128)(2,1)S(1)}, bf16[32,384]{1,0:T(8,128)(2,1)S(1)}, u32[]{:S(2)}, u32[]{:S(2)}) collective-permute-start(bf16[32,384]{1,0:T(8,128)(2,1)S(1)} %add_convert_fusion.9), channel_id=1, source_target_pairs={{0,8},{4,12},{8,0},{12,4},{1,9},{5,13},{9,1},{13,5},{2,10},{6,14},... | collective-permute-start | bytes 73736 | tf_op jit(solution)/shard_map/ppermute | solution.py:351
  74.6 5.5 %collective-permute-start.30 = (bf16[64,384]{1,0:T(8,128)(2,1)S(1)}, bf16[64,384]{1,0:T(8,128)(2,1)S(1)}, u32[]{:S(2)}, u32[]{:S(2)}) collective-permute-start(bf16[64,384]{1,0:T(8,128)(2,1)S(1)} %pad_maximum_fusion.10), channel_id=1, source_target_pairs={{0,4},{4,0},{8,12},{12,8},{1,5},{5,1},{9,13},{13,9},{2,6},{6,2},{1... | collective-permute-start | bytes 147464 | tf_op jit(solution)/shard_map/ppermute | solution.py:351
  80.8 9.0 %collective-permute-start.31 = (bf16[128,384]{1,0:T(8,128)(2,1)S(1)}, bf16[128,384]{1,0:T(8,128)(2,1)S(1)}, u32[]{:S(2)}, u32[]{:S(2)}) collective-permute-start(bf16[128,384]{1,0:T(8,128)(2,1)S(1)} %pad_maximum_fusion.7), channel_id=1, source_target_pairs={{0,1},{1,0},{2,3},{3,2},{4,5},{5,4},{6,7},{7,6},{8,9},{9,8},{10,11... | collective-permute-start | bytes 294920 | tf_op jit(solution)/shard_map/ppermute | solution.py:351
  82.1 16.7 %collective-permute-start.27 = (bf16[128,384]{1,0:T(8,128)(2,1)S(1)}, bf16[128,384]{1,0:T(8,128)(2,1)S(1)}, u32[]{:S(2)}, u32[]{:S(2)}) collective-permute-start(bf16[128,384]{1,0:T(8,128)(2,1)S(1)} %pad_maximum_fusion.6), channel_id=1, source_target_pairs={{0,1},{1,0},{2,3},{3,2},{4,5},{5,4},{6,7},{7,6},{8,9},{9,8},{10,11... | collective-permute-start | bytes 294920 | tf_op jit(solution)/shard_map/ppermute | solution.py:351
  82.4 6.6 %collective-permute-start.17 = (bf16[64,384]{1,0:T(8,128)(2,1)S(1)}, bf16[64,384]{1,0:T(8,128)(2,1)S(1)}, u32[]{:S(2)}, u32[]{:S(2)}) collective-permute-start(bf16[64,384]{1,0:T(8,128)(2,1)S(1)} %constant_dynamic-slice_fusion.3), channel_id=1, source_target_pairs={{0,4},{4,0},{8,12},{12,8},{1,5},{5,1},{9,13},{13,9},{2,6},{6,2},{1... | collective-permute-start | bytes 147464 | tf_op jit(solution)/shard_map/ppermute | solution.py:351
  84.2 26.0 %collective-permute-start.14 = (bf16[128,384]{1,0:T(8,128)(2,1)S(1)}, bf16[128,384]{1,0:T(8,128)(2,1)S(1)}, u32[]{:S(2)}, u32[]{:S(2)}) collective-permute-start(bf16[128,384]{1,0:T(8,128)(2,1)S(1)} %slice_bitcast_fusion), channel_id=1, source_target_pairs={{2,0},{0,2},{3,1},{1,3},{6,4},{4,6},{7,5},{5,7},{10,8},{8,10},{11,... | collective-permute-start | bytes 294920 | tf_op jit(solution)/shard_map/ppermute | solution.py:347
  92.9 5.5 %collective-permute-start.19 = (bf16[32,384]{1,0:T(8,128)(2,1)S(1)}, bf16[32,384]{1,0:T(8,128)(2,1)S(1)}, u32[]{:S(2)}, u32[]{:S(2)}) collective-permute-start(bf16[32,384]{1,0:T(8,128)(2,1)S(1)} %add_convert_fusion.10), channel_id=1, source_target_pairs={{0,8},{4,12},{8,0},{12,4},{1,9},{5,13},{9,1},{13,5},{2,10},{6,14},... | collective-permute-start | bytes 73736 | tf_op jit(solution)/shard_map/ppermute | solution.py:351
  93.5 18.7 %collective-permute-start.32 = (bf16[256,384]{1,0:T(8,128)(2,1)S(1)}, bf16[256,384]{1,0:T(8,128)(2,1)S(1)}, u32[]{:S(2)}, u32[]{:S(2)}) collective-permute-start(bf16[256,384]{1,0:T(8,128)(2,1)S(1)} %pad_maximum_fusion.4.refs_1_), channel_id=1, source_target_pairs={{0,2},{2,0},{1,3},{3,1},{4,6},{6,4},{5,7},{7,5},{8,10},{10,8},{9,1... | collective-permute-start | bytes 589832 | tf_op jit(solution)/shard_map/ppermute | solution.py:351
  101.6 5.5 %collective-permute-start.21 = (bf16[128,384]{1,0:T(8,128)(2,1)S(1)}, bf16[128,384]{1,0:T(8,128)(2,1)S(1)}, u32[]{:S(2)}, u32[]{:S(2)}) collective-permute-start(bf16[128,384]{1,0:T(8,128)(2,1)S(1)} %pad_maximum_fusion.5), channel_id=1, source_target_pairs={{0,1},{1,0},{2,3},{3,2},{4,5},{5,4},{6,7},{7,6},{8,9},{9,8},{10,11... | collective-permute-start | bytes 294920 | tf_op jit(solution)/shard_map/ppermute | solution.py:351
  102.9 11.0 %collective-permute-start.28 = (bf16[256,384]{1,0:T(8,128)(2,1)S(1)}, bf16[256,384]{1,0:T(8,128)(2,1)S(1)}, u32[]{:S(2)}, u32[]{:S(2)}) collective-permute-start(bf16[256,384]{1,0:T(8,128)(2,1)S(1)} %pad_maximum_fusion.3.refs_1_), channel_id=1, source_target_pairs={{0,2},{2,0},{1,3},{3,1},{4,6},{6,4},{5,7},{7,5},{8,10},{10,8},{9,1... | collective-permute-start | bytes 589832 | tf_op jit(solution)/shard_map/ppermute | solution.py:351
  107.1 8.5 %collective-permute-start.22 = (bf16[256,384]{1,0:T(8,128)(2,1)S(1)}, bf16[256,384]{1,0:T(8,128)(2,1)S(1)}, u32[]{:S(2)}, u32[]{:S(2)}) collective-permute-start(bf16[256,384]{1,0:T(8,128)(2,1)S(1)} %pad_maximum_fusion.2.refs_1_), channel_id=1, source_target_pairs={{0,2},{2,0},{1,3},{3,1},{4,6},{6,4},{5,7},{7,5},{8,10},{10,8},{9,1... | collective-permute-start | bytes 589832 | tf_op jit(solution)/shard_map/ppermute | solution.py:351
  (40 other events, 132.7 us)

commit v2 on v1

v2 whole, which is shorter than its diff:
```python
import math

import jax
import jax.numpy as jnp
from jax import lax
from jax.experimental import pallas as pl
from jax.experimental.pallas import tpu as pltpu
from jax.sharding import PartitionSpec as P

MODEL_WIDTH = 384
HEADS = 6
HEAD_WIDTH = 64
RIM = 8
SIDE = 16
TOKENS = 512
HALF = 256
EPS = 1e-05
LOG2E = math.log2(math.e)

bf16 = jnp.bfloat16
f32 = jnp.float32


def nn(a, b):
    return lax.dot_general(a, b, (((1,), (0,)), ((), ())), preferred_element_type=f32)


def nt(a, b):
    return lax.dot_general(a, b, (((1,), (1,)), ((), ())), preferred_element_type=f32)


def tn(a, b):
    return lax.dot_general(a, b, (((0,), (0,)), ((), ())), preferred_element_type=f32)


def iota(shape, dim):
    return lax.broadcasted_iota(jnp.int32, shape, dim)


def prepare_kernel(strips, cot, out_weight, qkv_weight, *refs):
    outs, (bias_blocks, d_context_t, qkv_weight_t), sems = refs[:5], refs[5:8], refs[8]
    parts = [bias_blocks.at[k] for k in range(3)] + [d_context_t, qkv_weight_t]
    copies = [pltpu.make_async_copy(part, outs[k], sems.at[k]) for k, part in enumerate(parts)]
    qkv_weight_t[...] = qkv_weight[...].T
    copies[4].start()
    d_context_t[...] = nt(out_weight[...], cot[...]).astype(bf16)
    copies[3].start()
    plain = strips[...] * LOG2E
    high = plain.astype(bf16)
    rest = plain - high.astype(f32)
    middle = rest.astype(bf16)
    low = (rest - middle.astype(f32)).astype(bf16)
    turn = iota((TOKENS, TOKENS), 0) + iota((TOKENS, TOKENS), 1) == TOKENS - 2
    turn = turn.astype(f32).astype(bf16)
    turned = nn(high, turn) + nn(middle, turn) + nn(low, turn)
    lane = iota((SIDE, TOKENS), 1)
    for entry in range(HEADS * 3):
        head, frame = divmod(entry, 3)
        first = 2 * (head * 3 + 2 - frame)
        even = jnp.broadcast_to(turned[first : first + 1, :], (SIDE, TOKENS))
        odd = jnp.broadcast_to(turned[first + 1 : first + 2, :], (SIDE, TOKENS))
        even = pltpu.roll(even, TOKENS - 15, 1, stride=1, stride_axis=0)
        odd = pltpu.roll(odd, TOKENS - 31, 1, stride=1, stride_axis=0)
        rows = jnp.where(lane % 32 < 16, even, odd)
        for row in range(SIDE):
            start = (15 - row) * SIDE
            bias_blocks[head // 2, entry % 6, row * SIDE : (row + 1) * SIDE, :] = rows[
                :, start : start + HALF
            ]
        if entry % 6 == 5:
            copies[head // 2].start()
    for copy in copies:
        copy.wait()


def source_onehots(row_shift, col_shift, sign):
    token = iota((HALF, 1), 0)
    row = token // SIDE + sign * row_shift
    col = token % SIDE + sign * col_shift
    if sign > 0:
        row_out, col_out = row >= SIDE, col >= SIDE
        near_row, near_col = row - SIDE, col - SIDE
    else:
        row_out, col_out = row < 0, col < 0
        near_row, near_col = row + RIM, col + RIM
    inner = jnp.where(row_out | col_out, -1, row * SIDE + col)
    rows = jnp.where(row_out & ~col_out, near_row * SIDE + col, -1)
    cols = jnp.where(col_out & ~row_out, row * RIM + near_col, -1)
    corner = jnp.where(row_out & col_out, near_row * RIM + near_col, -1)
    return [
        (iota((HALF, count), 1) == place).astype(f32).astype(bf16)
        for place, count in ((inner, HALF), (rows, 128), (cols, 128), (corner, 64))
    ]


def flag_strip(flags, first, count, width):
    total = count * width
    repeat = (iota((width, total), 1) % width == iota((width, total), 0)).astype(f32).astype(bf16)
    spread = nn(flags[first : first + count, :], repeat)
    keep = iota((count, total), 1) // width == iota((count, total), 0)
    strip = jnp.sum(jnp.where(keep, spread, 0.0), 0, keepdims=True)
    return jnp.broadcast_to(strip, (128, total)).astype(bf16)


def layer_norm(rolled):
    centred = rolled - jnp.mean(rolled, -1, keepdims=True)
    inv_std = lax.rsqrt(jnp.mean(centred * centred, -1, keepdims=True) + EPS)
    return centred * inv_std, inv_std


def attention_head(head, qkv_t, kv, penalty, bias_blocks, d_context_t):
    pair, side = divmod(head, 2)
    at = head * HEAD_WIDTH
    scale = LOG2E * HEAD_WIDTH ** (-0.5)
    zeros = jnp.zeros((HEAD_WIDTH, TOKENS), bf16)
    key_pair = kv[:, pair * 128 : pair * 128 + 128]
    value_pair = kv[:, MODEL_WIDTH + pair * 128 : MODEL_WIDTH + pair * 128 + 128]
    q_t = qkv_t[at : at + HEAD_WIDTH, :]
    k_t = qkv_t[MODEL_WIDTH + at : MODEL_WIDTH + at + HEAD_WIDTH, :]
    v_t = qkv_t[2 * MODEL_WIDTH + at : 2 * MODEL_WIDTH + at + HEAD_WIDTH, :]
    d_t = d_context_t[at : at + HEAD_WIDTH, :]
    d_eighth = d_t * 0.125
    q_wide = jnp.concatenate([q_t, zeros] if side == 0 else [zeros, q_t], 0)
    d_wide = jnp.concatenate([d_eighth, zeros] if side == 0 else [zeros, d_eighth], 0)
    context_parts = []
    dq_parts = []
    dk_parts = [0.0, 0.0]
    dv_parts = [0.0, 0.0]
    for b in range(2):
        lanes = slice(b * HALF, (b + 1) * HALF)
        scores = nn(key_pair, q_wide[:, lanes])
        d_probs = nn(value_pair, d_wide[:, lanes])
        halves = [slice(a * HALF, (a + 1) * HALF) for a in range(2)]
        s = [
            scores[halves[a]] * scale
            + bias_blocks[side * 3 + b - a + 1]
            + penalty[halves[a], lanes]
            for a in range(2)
        ]
        top = jnp.maximum(jnp.max(s[0], 0, keepdims=True), jnp.max(s[1], 0, keepdims=True))
        e = [jnp.exp2(s[a] - top) for a in range(2)]
        total = jnp.sum(e[0], 0, keepdims=True) + jnp.sum(e[1], 0, keepdims=True)
        inverse = 1.0 / total
        p = [e[a] * inverse for a in range(2)]
        pb = [p[a].astype(bf16) for a in range(2)]
        context_parts.append(nn(v_t[:, :HALF], pb[0]) + nn(v_t[:, HALF:], pb[1]))
        dp = [d_probs[halves[a]] for a in range(2)]
        delta = jnp.sum(p[0] * dp[0], 0, keepdims=True) + jnp.sum(p[1] * dp[1], 0, keepdims=True)
        ds = [(p[a] * (dp[a] - delta)).astype(bf16) for a in range(2)]
        dq_parts.append(nn(k_t[:, :HALF], ds[0]) + nn(k_t[:, HALF:], ds[1]))
        for a in range(2):
            dk_parts[a] = dk_parts[a] + nt(q_t[:, lanes], ds[a])
            dv_parts[a] = dv_parts[a] + nt(d_t[:, lanes], pb[a])
    return [
        jnp.concatenate(parts, 1).astype(bf16)
        for parts in (context_parts, dq_parts, dk_parts, dv_parts)
    ]


def main_kernel(
    shift,
    inner,
    halo,
    flags,
    gain,
    qkv_weight,
    cot,
    weight_t_far,
    d_context_far,
    bias0_far,
    bias1_far,
    bias2_far,
    grads,
    d_rolled,
    kept_far,
    context_far,
    penalty,
    qkv_weight_t,
    d_context_t,
    bias_blocks,
    context_t,
    d_qkv,
    sems,
):
    sources = (weight_t_far, d_context_far, bias0_far, bias1_far, bias2_far)
    places = [qkv_weight_t, d_context_t] + [bias_blocks.at[k] for k in range(3)]
    arrivals = [
        pltpu.make_async_copy(source, place, sems.at[k])
        for k, (source, place) in enumerate(zip(sources, places))
    ]
    for copy in arrivals:
        copy.start()
    onehots = source_onehots(shift[0], shift[1], 1)
    rolled = []
    on_diagonal = iota((HALF, HALF), 0) == iota((HALF, HALF), 1)
    for t in range(2):
        parts = (
            inner[t * 256 : t * 256 + 256, :],
            halo[t * 128 : t * 128 + 128, :],
            halo[256 + t * 128 : 384 + t * 128, :],
            halo[512 + t * 64 : 576 + t * 64, :],
        )
        rolled.append(sum(nn(hot, part) for hot, part in zip(onehots, parts)))
        strips = (
            flag_strip(flags[:32, :16], t * 16, 16, 16),
            flag_strip(flags[32:48, :16], t * 8, 8, 16),
            flag_strip(flags[48:80, :8], t * 16, 16, 8),
            flag_strip(flags[80:96, :8], t * 8, 8, 8),
        )
        marks = sum(nt(hot, strip) for hot, strip in zip(onehots, strips))
        column = jnp.where(marks > 0.5, -1e30, 0.0)
        wide = jnp.concatenate([column, column], 1)
        own = jnp.where(on_diagonal, 0.0, wide)
        penalty[t * HALF : (t + 1) * HALF, t * HALF : (t + 1) * HALF] = own
        penalty[t * HALF : (t + 1) * HALF, (1 - t) * HALF : (2 - t) * HALF] = wide
    xhat, inv_std = layer_norm(jnp.concatenate(rolled, 0))
    normed = (xhat * gain[...]).astype(bf16)
    normed_t = normed.T
    kv = nn(normed, qkv_weight[:, MODEL_WIDTH:]).astype(bf16)
    arrivals[0].wait()
    qkv_t = nt(qkv_weight_t[...], normed).astype(bf16)
    arrivals[1].wait()
    for pair in range(HEADS // 2):
        arrivals[2 + pair].wait()
        heads = [
            attention_head(2 * pair + side, qkv_t, kv, penalty, bias_blocks.at[pair], d_context_t)
            for side in range(2)
        ]
        context, *d_parts = [jnp.concatenate(both, 0) for both in zip(*heads)]
        context_t[pair * 128 : pair * 128 + 128, :] = context
        d_pair = jnp.concatenate([part.T for part in d_parts], 1)
        for kind in range(3):
            first = kind * MODEL_WIDTH + pair * 128
            d_qkv[:, first : first + 128] = d_pair[:, kind * 128 : kind * 128 + 128]
        first = pair * TOKENS
        grads[first : first + 128, :] = nn(context, cot[...]).astype(bf16)
        grads[first + 128 : first + TOKENS, :] = nn(normed_t, d_pair).astype(bf16)
    keep_context = pltpu.make_async_copy(context_t, context_far, sems.at[0])
    keep_context.start()
    d_xhat = nt(d_qkv[...], qkv_weight[...]) * gain[...]
    d_rolled[...] = (
        inv_std
        * (
            d_xhat
            - jnp.mean(d_xhat, -1, keepdims=True)
            - xhat * jnp.mean(d_xhat * xhat, -1, keepdims=True)
        )
    ).astype(bf16)
    keep = pltpu.make_async_copy(d_rolled, kept_far, sems.at[1])
    keep.start()
    keep_context.wait()
    keep.wait()


def place_kernel(
    shift, halo, out_weight, kept_far, context_far, field_grad, update, kept, context_t, sems
):
    copies = [
        pltpu.make_async_copy(kept_far, kept, sems.at[0]),
        pltpu.make_async_copy(context_far, context_t, sems.at[1]),
    ]
    for copy in copies:
        copy.start()
    onehots = source_onehots(shift[0], shift[1], -1)
    for copy in copies:
        copy.wait()
    for t in range(2):
        parts = (
            kept[t * 256 : t * 256 + 256, :],
            halo[t * 128 : t * 128 + 128, :],
            halo[256 + t * 128 : 384 + t * 128, :],
            halo[512 + t * 64 : 576 + t * 64, :],
        )
        field_grad[t * 256 : t * 256 + 256, :] = sum(
            nn(hot, part) for hot, part in zip(onehots, parts)
        ).astype(bf16)
    update[...] = tn(context_t[...], out_weight[...]).astype(bf16)


def finish_kernel(scale, place, *refs):
    mine, other, (weight, gain) = refs[:4], refs[4:8], refs[8:10]
    qkv_far, out_far, gain_grad, qkv_grad, out_grad, sems = refs[10:]
    first_core, bit_one, bit_two = place[0] == 0, place[1] == 1, place[2] == 1
    sides = []
    for shares in (mine, other):
        shares = [share[...].astype(f32) * scale for share in shares]
        shares = [jnp.where(bit_one, shares[k ^ 1], shares[k]) for k in range(4)]
        sides.append([jnp.where(bit_two, shares[k ^ 2], shares[k]) for k in range(4)])
    lower = [jnp.where(first_core, a, b) for a, b in zip(*sides)]
    upper = [jnp.where(first_core, b, a) for a, b in zip(*sides)]
    whole = jnp.concatenate(lower + upper, 0)
    copies = []
    partial = 0.0
    for kind in range(3):
        columns = slice(kind * MODEL_WIDTH, (kind + 1) * MODEL_WIDTH)
        block = jnp.concatenate(
            [
                whole[pair * TOKENS + 128 : (pair + 1) * TOKENS, kind * 128 : kind * 128 + 128]
                for pair in range(3)
            ],
            1,
        )
        qkv_grad[:, columns] = block
        copies.append(
            pltpu.make_async_copy(
                qkv_grad.at[:, columns], qkv_far.at[:, columns], sems.at[kind]
            )
        )
        copies[-1].start()
        product = block * weight[:, columns].astype(f32)
        partial = partial + product[:, :128] + product[:, 128:256] + product[:, 256:]
    for pair in range(3):
        out_grad[pair * 128 : pair * 128 + 128, :] = whole[pair * TOKENS : pair * TOKENS + 128]
    copies.append(pltpu.make_async_copy(out_grad, out_far, sems.at[3]))
    copies[-1].start()
    gain_grad[...] = jnp.sum(partial.T, 0, keepdims=True) / gain[...]
    for copy in copies:
        copy.wait()


def local_call(kernel, shapes, inputs, far_in=0, far_out=0, scratch=(), copies=0, micros=1):
    vmem = pl.BlockSpec(memory_space=pltpu.VMEM)
    smem = pl.BlockSpec(memory_space=pltpu.SMEM)
    far = pl.BlockSpec(memory_space=pltpu.HBM)
    return pl.pallas_call(
        kernel,
        out_shape=[jax.ShapeDtypeStruct(shape, dtype) for shape, dtype in shapes],
        in_specs=[smem if array.dtype == jnp.int32 else vmem for array in inputs[: len(inputs) - far_in]]
        + [far] * far_in,
        out_specs=[vmem] * (len(shapes) - far_out) + [far] * far_out,
        scratch_shapes=[pltpu.VMEM(shape, dtype) for shape, dtype in scratch]
        + [pltpu.SemaphoreType.DMA((copies,))],
        compiler_params=pltpu.CompilerParams(vmem_limit_bytes=32 * 2**20),
        cost_estimate=pl.CostEstimate(
            flops=micros * 10**9, bytes_accessed=10**6, transcendentals=0
        ),
    )(*inputs)


def passed_along(block, axis, distance):
    count = lax.axis_size(axis)
    return lax.ppermute(block, axis, [((i - distance) % count, i) for i in range(count)])


def index_bit(axis, bit):
    return (lax.axis_index(axis) & bit) // bit


def swapped(block, *bits):
    axes = tuple(axis for axis, _ in bits)
    sizes = [lax.axis_size(axis) for axis in axes]
    route = []
    for source in range(math.prod(sizes)):
        rest, places = source, []
        for size in sizes[::-1]:
            rest, place = divmod(rest, size)
            places.append(place)
        target = 0
        for size, place, (_, bit) in zip(sizes, places[::-1], bits):
            target = target * size + (place ^ bit)
        route.append((source, target))
    return lax.ppermute(block, axes, route)


def add_up(*pieces):
    return sum(piece.astype(f32) for piece in pieces).astype(bf16)


def all_sum(block):
    core, one, two = ("sx", 1), ("ta", 1), ("sy", 1)
    rest = [
        (axis, 1 << k)
        for axis in ("ta", "sy")
        for k in range(1, lax.axis_size(axis).bit_length() - 1)
    ]
    half = block.shape[0] // 2
    side = index_bit(*core)
    pick = lambda array, place, size: lax.dynamic_slice_in_dim(array, place * size, size, 0)
    block = add_up(pick(block, side, half), swapped(pick(block, 1 - side, half), core))
    share = half // 4
    mine = 2 * index_bit(*one) + index_bit(*two)
    groups = [[two], [one], [two, one]]
    arrived = [
        swapped(pick(block, mine ^ offset, share), *group)
        for offset, group in zip((1, 2, 3), groups)
    ]
    quarter = add_up(pick(block, mine, share), *arrived)
    for bit in rest:
        quarter = add_up(quarter, swapped(quarter, bit))
    quarters = [quarter] + [swapped(quarter, *group) for group in groups]
    return quarters, [swapped(quarter, core) for quarter in quarters]


def shards(
    state_field,
    outlier_flags,
    window_shift,
    layer_norm_gain,
    qkv_weight,
    out_weight,
    position_bias,
    cotangent,
):
    width = MODEL_WIDTH
    wide = lambda tokens: ((tokens, width), bf16)
    rows = passed_along(state_field[:, :RIM].reshape(-1, width), "sy", -1)
    cols = passed_along(state_field[:, :, :RIM].reshape(-1, width), "sx", -1)
    marks = outlier_flags.astype(bf16)
    row_marks = passed_along(marks[:, :RIM].reshape(2 * RIM, SIDE), "sy", -1)
    col_marks = passed_along(marks[:, :, :RIM].reshape(2 * SIDE, RIM), "sx", -1)
    strips = jnp.pad(
        position_bias.reshape(HEADS, 3, 31, 31), ((0, 0), (0, 0), (0, 1), (0, 1))
    )
    strips = strips.reshape(HEADS, 3, 16, 2, 32).transpose(0, 1, 3, 2, 4).reshape(36, TOKENS)
    cot_rows = cotangent.reshape(TOKENS, width)
    pair_bias = ((6, HALF, HALF), f32)
    *bias_blocks, d_context_t, qkv_weight_t = local_call(
        prepare_kernel,
        [pair_bias] * 3 + [((width, TOKENS), bf16), wide(3 * width)],
        [strips, cot_rows, out_weight, qkv_weight],
        far_out=5,
        scratch=[((3, 6, HALF, HALF), f32), ((width, TOKENS), bf16), wide(3 * width)],
        copies=5,
        micros=3,
    )
    corner = passed_along(
        rows.reshape(2 * RIM, SIDE, width)[:, :RIM].reshape(-1, width), "sx", -1
    )
    corner_marks = passed_along(row_marks[:, :RIM], "sx", -1)
    halo = jnp.concatenate([rows, cols, corner], 0)
    all_marks = jnp.concatenate(
        [
            jnp.pad(m, ((0, 0), (0, 128 - m.shape[1])))
            for m in (marks.reshape(2 * SIDE, SIDE), row_marks, col_marks, corner_marks)
        ],
        0,
    )
    gain = layer_norm_gain.reshape(1, width)
    grads, d_rolled, kept, context_t = local_call(
        main_kernel,
        [wide(3 * TOKENS), wide(TOKENS), wide(TOKENS), ((width, TOKENS), bf16)],
        [
            window_shift,
            state_field.reshape(TOKENS, width),
            halo,
            all_marks,
            gain,
            qkv_weight,
            cot_rows,
            qkv_weight_t,
            d_context_t,
            *bias_blocks,
        ],
        far_in=5,
        far_out=2,
        scratch=[
            ((TOKENS, TOKENS), f32),
            wide(3 * width),
            ((width, TOKENS), bf16),
            ((3, 6, HALF, HALF), f32),
            ((width, TOKENS), bf16),
            ((TOKENS, 3 * width), bf16),
        ],
        copies=5,
        micros=12,
    )
    grid = d_rolled.reshape(2, SIDE, SIDE, width)
    below = passed_along(grid[:, RIM:].reshape(-1, width), "sy", 1)
    beside = passed_along(grid[:, :, RIM:].reshape(-1, width), "sx", 1)
    across = passed_along(
        below.reshape(2 * RIM, SIDE, width)[:, RIM:].reshape(-1, width), "sx", 1
    )
    field_grad, update = local_call(
        place_kernel,
        [wide(TOKENS), wide(TOKENS)],
        [
            window_shift,
            jnp.concatenate([below, beside, across], 0),
            out_weight,
            kept,
            context_t,
        ],
        far_in=2,
        scratch=[wide(TOKENS), ((width, TOKENS), bf16)],
        copies=2,
        micros=2,
    )
    quarters, others = all_sum(grads)
    tiles = lax.axis_size("sy") * lax.axis_size("sx") * lax.axis_size("ta")
    place = jnp.stack([index_bit("sx", 1), index_bit("sy", 1), index_bit("ta", 1)])
    gain_grad, qkv_grad, out_grad = finish_call(
        1.0 / tiles, [place.astype(jnp.int32), *quarters, *others, qkv_weight, gain]
    )
    shape = state_field.shape
    return (
        update.reshape(shape),
        field_grad.reshape(shape),
        qkv_grad,
        out_grad,
        gain_grad.reshape(width),
    )


def finish_call(scale, inputs):
    width = MODEL_WIDTH

    def kernel(*refs):
        gain_grad, qkv_far, out_far, *scratch = refs[len(inputs) :]
        finish_kernel(scale, *refs[: len(inputs)], qkv_far, out_far, gain_grad, *scratch)

    return local_call(
        kernel,
        [((1, width), f32), ((width, 3 * width), f32), ((width, width), f32)],
        inputs,
        far_out=2,
        scratch=[((width, 3 * width), f32), ((width, width), f32)],
        copies=4,
    )


def solution(mesh):
    in_specs = (
        P(("groups", "ta"), "sy", "sx", None),
        P(("groups", "ta"), "sy", "sx"),
        P(),
        P(),
        P(),
        P(),
        P(),
        P(("groups", "ta"), "sy", "sx", None),
    )
    out_specs = (
        P(("groups", "ta"), "sy", "sx", None),
        P(("groups", "ta"), "sy", "sx", None),
        P("groups", None),
        P("groups", None),
        P("groups"),
    )
    return jax.shard_map(shards, mesh=mesh, in_specs=in_specs, out_specs=out_specs, check_vma=False)
```

time: 118 us -> 87.9 us (0.74)
  starting transfers between devices: 52.6 us -> 23.1 us
  local copies, waits for them, and re-layouts: 22.5 us -> 17.2 us
  waiting for transfers between devices: 13.9 us -> 18.3 us
    ppermute x24 -> x12, starting transfers between devices: 41.3 us -> 13 us  [swapped(): return lax.ppermute(block, axes, route)]
    unnamed x62 -> x42, local copies, waits for them, and re-layouts: 18.2 us -> 12.9 us
    ppermute x24 -> x12, waiting for transfers between devices: 12.9 us -> 17.2 us  [swapped(): return lax.ppermute(block, axes, route)]
    ppermute x9, starting transfers between devices: 11.3 us -> 10.1 us  [passed_along(): lax.ppermute(block, axis, [((i - distance) % count, i) for i in range(cou...]
    pallas_call x11 -> x4, Pallas kernels: 24.6 us -> 24.1 us  [local_call(): pl.pallas_call(kernel, out_shape=[jax.ShapeDtypeStruct(shape, dtype) for...]
  transfers between devices with their start and end apart: 33 -> 21, of which waited for: 11 -> 8; matrix products, arithmetic and copies ran while one was open for 3% -> 5% of each run, Pallas kernels for 13% -> 8%
where the time goes in v2:
time: 87.9 us; the launch traced here: 87.5 us
  Pallas kernels  24.1 us (27%)
  starting transfers between devices  23.1 us (26%)
  waiting for transfers between devices  18.3 us (21%)
  local copies, waits for them, and re-layouts  17.2 us (20%)
  other arithmetic  3.77 us (4%)
  between operations  0.97 us (1%)
    pallas_call x4, Pallas kernels, local_call(): pl.pallas_call(kernel, out_shape=[jax.ShapeDtypeStruct(shape, dtype) for...  24.1 us
    ppermute x12, waiting for transfers between devices, swapped(): return lax.ppermute(block, axes, route)  17.2 us
    ppermute x12, starting transfers between devices, swapped(): return lax.ppermute(block, axes, route)  13 us
    unnamed x42, local copies, waits for them, and re-layouts  12.9 us
    ppermute x9, starting transfers between devices, passed_along(): lax.ppermute(block, axis, [((i - distance) % count, i) for i in range(cou...  10.1 us
    convert_element_type x3, other arithmetic, add_up(): return sum((piece.astype(f32) for piece in pieces)).astype(bf16)  2.26 us
  transfers between devices with their start and end apart: 21, of which 8 were waited for; matrix products, arithmetic and copies ran while one was open for 5% of the time, Pallas kernels for 8%

profile of v2, /device:TPU:1, one launch (start us, length us, event | category | flops | bytes accessed | tf_op | source)
XLA Modules:
  0.0 87.5 jit_solution(4601049075695630886)
XLA Ops:
  1.4 4.2 %collective-permute-start.3 = (bf16[16,16]{1,0:T(8,128)(2,1)S(1)}, bf16[16,16]{1,0:T(8,128)(2,1)S(1)}, u32[]{:S(2)}, u32[]{:S(2)}) collective-permute-start(bf16[16,16]{1,0:T(8,128)(2,1)S(1)} %slice_bitcast_fusion.2), channel_id=1, source_target_pairs={{4,0},{8,4},{12,8},{0,12},{5,1},{9,5},{13,9},{1,13},{6,2},{10,6},{... | collective-permute-start | bytes 1544 | tf_op jit(solution)/shard_map/ppermute | solution.py:342
  9.0 1.2 %reshape.83 = f32[6,3,31,31]{3,2,1,0:T(8,128)S(1)} reshape(f32[6,2883]{1,0:T(8,128)} %param.14) | data formatting | bytes 138384 | tf_op jit(solution)/shard_map/reshape | solution.py:412
  10.4 4.2 %shard_map.119 = (f32[6,256,256]{2,1,0:T(8,128)S(1)}, f32[6,256,256]{2,1,0:T(8,128)S(1)}, f32[6,256,256]{2,1,0:T(8,128)S(1)}, bf16[384,512]{1,0:T(8,128)(2,1)S(1)}, bf16[1152,384]{1,0:T(8,128)(2,1)S(1)}) custom-call(f32[36,512]{1,0:T(8,128)S(1)} %reshape.85.strips, bf16[512,384]{1,0:T(8,128)(2,1)S(1)} %bitcast.32, bf16[384,384]{1,0:T(8,128)(2,1)S(1)} %copy-done.3, ...), custom_call_target="tpu_custom_call" | custom-call | flops 3000000000 | bytes 1000000 | tf_op jit(solution)/shard_map/pallas_call | solution.py:325
  15.8 1.2 %copy-done.7 = f32[6,256,256]{2,1,0:T(8,128)} copy-done((f32[6,256,256]{2,1,0:T(8,128)}, f32[6,256,256]{2,1,0:T(8,128)S(1)}, u32[]{:S(2)}) %copy-start.7) | copy-done | bytes 1572888
  21.7 1.4 %copy-done.6 = f32[6,256,256]{2,1,0:T(8,128)S(1)} copy-done((f32[6,256,256]{2,1,0:T(8,128)S(1)}, f32[6,256,256]{2,1,0:T(8,128)}, u32[]{:S(2)}) %copy-start.6) | copy-done | bytes 1572888
  23.1 1.4 %copy-done.8 = f32[6,256,256]{2,1,0:T(8,128)S(1)} copy-done((f32[6,256,256]{2,1,0:T(8,128)S(1)}, f32[6,256,256]{2,1,0:T(8,128)}, u32[]{:S(2)}) %copy-start.8) | copy-done | bytes 1572888
  24.5 1.4 %copy-done.10 = f32[6,256,256]{2,1,0:T(8,128)S(1)} copy-done((f32[6,256,256]{2,1,0:T(8,128)S(1)}, f32[6,256,256]{2,1,0:T(8,128)}, u32[]{:S(2)}) %copy-start.10) | copy-done | bytes 1572888
  25.9 1.2 %copy-done.16 = bf16[1152,384]{1,0:T(8,128)(2,1)S(1)} copy-done((bf16[1152,384]{1,0:T(8,128)(2,1)S(1)}, bf16[1152,384]{1,0:T(8,128)(2,1)}, u32[]{:S(2)}) %copy-start.16) | copy-done | bytes 884760
  27.1 14.7 %shard_map.120 = (bf16[1536,384]{1,0:T(8,128)(2,1)S(1)}, bf16[512,384]{1,0:T(8,128)(2,1)S(1)}, bf16[512,384]{1,0:T(8,128)(2,1)S(1)}, bf16[384,512]{1,0:T(8,128)(2,1)S(1)}) custom-call(s32[2]{0:T(128)S(1)} %copy-done.4, bf16[512,384]{1,0:T(8,128)(2,1)S(1)} %bitcast.29, bf16[640,384]{1,0:T(8,128)(2,1)S(1)} %pad_maximum_fusion.halo, ...), custom_call_target="tpu_custom_call" | custom-call | flops 12000000000 | bytes 1000000 | tf_op jit(solution)/shard_map/pallas_call | solution.py:325
  44.3 2.2 %collective-permute-done.9 = bf16[768,384]{1,0:T(8,128)(2,1)} collective-permute-done((bf16[768,384]{1,0:T(8,128)(2,1)}, bf16[768,384]{1,0:T(8,128)(2,1)}, u32[]{:S(2)}, u32[]{:S(2)}) %collective-permute-start.9) | collective-permute-done | bytes 589856 | tf_op jit(solution)/shard_map/ppermute | solution.py:362
  46.5 1.2 %add_convert_fusion = bf16[768,384]{1,0:T(8,128)(2,1)S(1)} fusion(bf16[768,384]{1,0:T(8,128)(2,1)} %collective-permute-done.9, bf16[1536,384]{1,0:T(8,128)(2,1)S(1)} %get-tuple-element.29, s32[]{:T(128)S(6)} %select_n.26), kind=kLoop, calls=%fused_computation | loop fusion | flops 1179648 | bytes 1769476 | tf_op jit(solution)/shard_map/convert_element_type | solution.py:366
  48.6 1.2 %collective-permute-start.10 = (bf16[192,384]{1,0:T(8,128)(2,1)S(1)}, bf16[192,384]{1,0:T(8,128)(2,1)S(1)}, u32[]{:S(2)}, u32[]{:S(2)}) collective-permute-start(bf16[192,384]{1,0:T(8,128)(2,1)S(1)} %get-tuple-element.33), channel_id=1, source_target_pairs={{0,4},{4,0},{8,12},{12,8},{1,5},{5,1},{9,13},{13,9},{2,6},{6,2},{1... | collective-permute-start | bytes 442376 | tf_op jit(solution)/shard_map/ppermute | solution.py:362
  49.8 1.2 %collective-permute-start.11 = (bf16[192,384]{1,0:T(8,128)(2,1)S(1)}, bf16[192,384]{1,0:T(8,128)(2,1)S(1)}, u32[]{:S(2)}, u32[]{:S(2)}) collective-permute-start(bf16[192,384]{1,0:T(8,128)(2,1)S(1)} %get-tuple-element.35), channel_id=1, source_target_pairs={{0,1},{1,0},{2,3},{3,2},{4,5},{5,4},{6,7},{7,6},{8,9},{9,8},{10,11... | collective-permute-start | bytes 442376 | tf_op jit(solution)/shard_map/ppermute | solution.py:362
  51.3 1.4 %collective-permute-start.6 = (bf16[256,384]{1,0:T(8,128)(2,1)S(1)}, bf16[256,384]{1,0:T(8,128)(2,1)S(1)}, u32[]{:S(2)}, u32[]{:S(2)}) collective-permute-start(bf16[256,384]{1,0:T(8,128)(2,1)S(1)} %bitcast.40), channel_id=1, source_target_pairs={{12,0},{0,4},{4,8},{8,12},{13,1},{1,5},{5,9},{9,13},{14,2},{2,6},{... | collective-permute-start | bytes 589832 | tf_op jit(solution)/shard_map/ppermute | solution.py:342
  52.8 1.4 %collective-permute-start.7 = (bf16[256,384]{1,0:T(8,128)(2,1)S(1)}, bf16[256,384]{1,0:T(8,128)(2,1)S(1)}, u32[]{:S(2)}, u32[]{:S(2)}) collective-permute-start(bf16[256,384]{1,0:T(8,128)(2,1)S(1)} %bitcast.38), channel_id=1, source_target_pairs={{2,0},{0,2},{3,1},{1,3},{6,4},{4,6},{7,5},{5,7},{10,8},{8,10},{11,... | collective-permute-start | bytes 589832 | tf_op jit(solution)/shard_map/ppermute | solution.py:342
  54.6 7.6 %collective-permute-done.12 = bf16[192,384]{1,0:T(8,128)(2,1)S(1)} collective-permute-done((bf16[192,384]{1,0:T(8,128)(2,1)S(1)}, bf16[192,384]{1,0:T(8,128)(2,1)S(1)}, u32[]{:S(2)}, u32[]{:S(2)}) %collective-permute-start.12) | collective-permute-done | bytes 147488 | tf_op jit(solution)/shard_map/ppermute | solution.py:362
  64.4 6.4 %collective-permute-done.13 = bf16[192,384]{1,0:T(8,128)(2,1)S(1)} collective-permute-done((bf16[192,384]{1,0:T(8,128)(2,1)S(1)}, bf16[192,384]{1,0:T(8,128)(2,1)S(1)}, u32[]{:S(2)}, u32[]{:S(2)}) %collective-permute-start.13) | collective-permute-done | bytes 147488 | tf_op jit(solution)/shard_map/ppermute | solution.py:362
  70.9 1.6 %collective-permute-start.15 = (bf16[192,384]{1,0:T(8,128)(2,1)S(1)}, bf16[192,384]{1,0:T(8,128)(2,1)S(1)}, u32[]{:S(2)}, u32[]{:S(2)}) collective-permute-start(bf16[192,384]{1,0:T(8,128)(2,1)S(1)} %add_convert_fusion.1.refs_1_), channel_id=1, source_target_pairs={{0,1},{1,0},{2,3},{3,2},{4,5},{5,4},{6,7},{7,6},{8,9},{9,8},{10,11... | collective-permute-start | bytes 442376 | tf_op jit(solution)/shard_map/ppermute | solution.py:362
  73.7 1.6 %collective-permute-start.17 = (bf16[192,384]{1,0:T(8,128)(2,1)S(1)}, bf16[192,384]{1,0:T(8,128)(2,1)S(1)}, u32[]{:S(2)}, u32[]{:S(2)}) collective-permute-start(bf16[192,384]{1,0:T(8,128)(2,1)S(1)} %add_convert_fusion.1.refs_1_), channel_id=1, source_target_pairs={{0,2},{2,0},{1,3},{3,1},{4,6},{6,4},{5,7},{7,5},{8,10},{10,8},{9,1... | collective-permute-start | bytes 442376 | tf_op jit(solution)/shard_map/ppermute | solution.py:362
  75.4 3.0 %collective-permute-start.18 = (bf16[192,384]{1,0:T(8,128)(2,1)S(1)}, bf16[192,384]{1,0:T(8,128)(2,1)S(1)}, u32[]{:S(2)}, u32[]{:S(2)}) collective-permute-start(bf16[192,384]{1,0:T(8,128)(2,1)S(1)} %collective-permute-done.14.refs_2_), channel_id=1, source_target_pairs={{0,2},{2,0},{1,3},{3,1},{4,6},{6,4},{5,7},{7,5},{8,10},{10,8},{9,1... | collective-permute-start | bytes 442376 | tf_op jit(solution)/shard_map/ppermute | solution.py:362
  78.4 1.3 %collective-permute-start.19 = (bf16[192,384]{1,0:T(8,128)(2,1)S(1)}, bf16[192,384]{1,0:T(8,128)(2,1)S(1)}, u32[]{:S(2)}, u32[]{:S(2)}) collective-permute-start(bf16[192,384]{1,0:T(8,128)(2,1)S(1)} %collective-permute-done.15.refs_3_), channel_id=1, source_target_pairs={{0,2},{2,0},{1,3},{3,1},{4,6},{6,4},{5,7},{7,5},{8,10},{10,8},{9,1... | collective-permute-start | bytes 442376 | tf_op jit(solution)/shard_map/ppermute | solution.py:362
  80.2 1.3 %collective-permute-start.20 = (bf16[192,384]{1,0:T(8,128)(2,1)S(1)}, bf16[192,384]{1,0:T(8,128)(2,1)S(1)}, u32[]{:S(2)}, u32[]{:S(2)}) collective-permute-start(bf16[192,384]{1,0:T(8,128)(2,1)S(1)} %collective-permute-done.16.refs_4_), channel_id=1, source_target_pairs={{0,2},{2,0},{1,3},{3,1},{4,6},{6,4},{5,7},{7,5},{8,10},{10,8},{9,1... | collective-permute-start | bytes 442376 | tf_op jit(solution)/shard_map/ppermute | solution.py:362
  81.5 2.7 %shard_map.121 = (bf16[512,384]{1,0:T(8,128)(2,1)}, bf16[512,384]{1,0:T(8,128)(2,1)}) custom-call(s32[2]{0:T(128)S(1)} %copy-done.4, bf16[640,384]{1,0:T(8,128)(2,1)S(1)} %pad_maximum_fusion.1.halo, bf16[384,384]{1,0:T(8,128)(2,1)S(1)} %copy-done.3, bf16[512,384]{1,0:T(8,128)(2,1)S(1)} %copy-done.12, bf16[384,512]{1,0:T(8,128)(2,1)S(1)} %copy-done.14), custom_call_target="tpu_custom_call" | custom-call | flops 2000000000 | bytes 1000000 | tf_op jit(solution)/shard_map/pallas_call | solution.py:325
  84.3 2.6 %shard_map.122 = (f32[1,384]{1,0:T(1,128)S(1)}, f32[384,1152]{1,0:T(8,128)}, f32[384,384]{1,0:T(8,128)}) custom-call(s32[3]{0:T(128)S(1)} %pad_add_fusion.refs_0_, bf16[192,384]{1,0:T(8,128)(2,1)S(1)} %add_convert_fusion.1.refs_1_, bf16[192,384]{1,0:T(8,128)(2,1)S(1)} %collective-permute-done.14.refs_2_, ...), custom_call_target="tpu_custom_call" | custom-call | flops 1000000000 | bytes 1000000 | tf_op jit(solution)/shard_map/pallas_call | solution.py:325
  (87 shorter events, 18.9 us)
Async XLA Ops:
  1.4 18.4 %collective-permute-start.3 = (bf16[16,16]{1,0:T(8,128)(2,1)S(1)}, bf16[16,16]{1,0:T(8,128)(2,1)S(1)}, u32[]{:S(2)}, u32[]{:S(2)}) collective-permute-start(bf16[16,16]{1,0:T(8,128)(2,1)S(1)} %slice_bitcast_fusion.2), channel_id=1, source_target_pairs={{4,0},{8,4},{12,8},{0,12},{5,1},{9,5},{13,9},{1,13},{6,2},{10,6},{... | collective-permute-start | bytes 1544 | tf_op jit(solution)/shard_map/ppermute | solution.py:342
  5.5 14.9 %collective-permute-start.4 = (bf16[32,8]{1,0:T(8,128)(2,1)S(1)}, bf16[32,8]{1,0:T(8,128)(2,1)S(1)}, u32[]{:S(2)}, u32[]{:S(2)}) collective-permute-start(bf16[32,8]{1,0:T(8,128)(2,1)S(1)} %bitcast.41), channel_id=1, source_target_pairs={{2,0},{0,2},{3,1},{1,3},{6,4},{4,6},{7,5},{5,7},{10,8},{8,10},{11,... | collective-permute-start | bytes 1544 | tf_op jit(solution)/shard_map/ppermute | solution.py:342
  7.4 3.0 %copy-start.1 = (bf16[384,1152]{1,0:T(8,128)(2,1)S(1)}, bf16[384,1152]{1,0:T(8,128)(2,1)}, u32[]{:S(2)}) copy-start(bf16[384,1152]{1,0:T(8,128)(2,1)} %refs_9_.1) | copy-start | bytes 2654212
  7.5 12.7 %collective-permute-start = (bf16[256,384]{1,0:T(8,128)(2,1)S(1)}, bf16[256,384]{1,0:T(8,128)(2,1)S(1)}, u32[]{:S(2)}, u32[]{:S(2)}) collective-permute-start(bf16[256,384]{1,0:T(8,128)(2,1)S(1)} %bitcast.39), channel_id=1, source_target_pairs={{4,0},{8,4},{12,8},{0,12},{5,1},{9,5},{13,9},{1,13},{6,2},{10,6},{... | collective-permute-start | bytes 589832 | tf_op jit(solution)/shard_map/ppermute | solution.py:342
  8.8 12.3 %collective-permute-start.1 = (bf16[256,384]{1,0:T(8,128)(2,1)S(1)}, bf16[256,384]{1,0:T(8,128)(2,1)S(1)}, u32[]{:S(2)}, u32[]{:S(2)}) collective-permute-start(bf16[256,384]{1,0:T(8,128)(2,1)S(1)} %bitcast.37), channel_id=1, source_target_pairs={{2,0},{0,2},{3,1},{1,3},{6,4},{4,6},{7,5},{5,7},{10,8},{8,10},{11,... | collective-permute-start | bytes 589832 | tf_op jit(solution)/shard_map/ppermute | solution.py:342
  19.8 1.2 %collective-permute-start.5 = (bf16[16,8]{1,0:T(8,128)(2,1)S(1)}, bf16[16,8]{1,0:T(8,128)(2,1)S(1)}, u32[]{:S(2)}, u32[]{:S(2)}) collective-permute-start(bf16[16,8]{1,0:T(8,128)(2,1)S(1)} %bitcast.43), channel_id=1, source_target_pairs={{2,0},{0,2},{3,1},{1,3},{6,4},{4,6},{7,5},{5,7},{10,8},{8,10},{11,... | collective-permute-start | bytes 776 | tf_op jit(solution)/shard_map/ppermute | solution.py:342
  20.2 1.4 %collective-permute-start.2 = (bf16[128,384]{1,0:T(8,128)(2,1)S(1)}, bf16[128,384]{1,0:T(8,128)(2,1)S(1)}, u32[]{:S(2)}, u32[]{:S(2)}) collective-permute-start(bf16[128,384]{1,0:T(8,128)(2,1)S(1)} %slice_bitcast_fusion.1), channel_id=1, source_target_pairs={{2,0},{0,2},{3,1},{1,3},{6,4},{4,6},{7,5},{5,7},{10,8},{8,10},{11,... | collective-permute-start | bytes 294920 | tf_op jit(solution)/shard_map/ppermute | solution.py:342
  44.1 2.3 %collective-permute-start.9 = (bf16[768,384]{1,0:T(8,128)(2,1)}, bf16[768,384]{1,0:T(8,128)(2,1)}, u32[]{:S(2)}, u32[]{:S(2)}) collective-permute-start(bf16[768,384]{1,0:T(8,128)(2,1)} %constant_dynamic-slice_fusion.3), channel_id=1, source_target_pairs={{0,2},{2,0},{1,3},{3,1},{4,6},{6,4},{5,7},{7,5},{8,10},{10,8},{9,1... | collective-permute-start | bytes 1769480 | tf_op jit(solution)/shard_map/ppermute | solution.py:362
  48.6 5.6 %collective-permute-start.10 = (bf16[192,384]{1,0:T(8,128)(2,1)S(1)}, bf16[192,384]{1,0:T(8,128)(2,1)S(1)}, u32[]{:S(2)}, u32[]{:S(2)}) collective-permute-start(bf16[192,384]{1,0:T(8,128)(2,1)S(1)} %get-tuple-element.33), channel_id=1, source_target_pairs={{0,4},{4,0},{8,12},{12,8},{1,5},{5,1},{9,13},{13,9},{2,6},{6,2},{1... | collective-permute-start | bytes 442376 | tf_op jit(solution)/shard_map/ppermute | solution.py:362
  49.8 4.8 %collective-permute-start.11 = (bf16[192,384]{1,0:T(8,128)(2,1)S(1)}, bf16[192,384]{1,0:T(8,128)(2,1)S(1)}, u32[]{:S(2)}, u32[]{:S(2)}) collective-permute-start(bf16[192,384]{1,0:T(8,128)(2,1)S(1)} %get-tuple-element.35), channel_id=1, source_target_pairs={{0,1},{1,0},{2,3},{3,2},{4,5},{5,4},{6,7},{7,6},{8,9},{9,8},{10,11... | collective-permute-start | bytes 442376 | tf_op jit(solution)/shard_map/ppermute | solution.py:362
  51.0 11.3 %collective-permute-start.12 = (bf16[192,384]{1,0:T(8,128)(2,1)S(1)}, bf16[192,384]{1,0:T(8,128)(2,1)S(1)}, u32[]{:S(2)}, u32[]{:S(2)}) collective-permute-start(bf16[192,384]{1,0:T(8,128)(2,1)S(1)} %get-tuple-element.34), channel_id=1, source_target_pairs={{0,5},{1,4},{4,1},{5,0},{8,13},{9,12},{12,9},{13,8},{2,7},{3,6},{6... | collective-permute-start | bytes 442376 | tf_op jit(solution)/shard_map/ppermute | solution.py:362
  51.3 12.0 %collective-permute-start.6 = (bf16[256,384]{1,0:T(8,128)(2,1)S(1)}, bf16[256,384]{1,0:T(8,128)(2,1)S(1)}, u32[]{:S(2)}, u32[]{:S(2)}) collective-permute-start(bf16[256,384]{1,0:T(8,128)(2,1)S(1)} %bitcast.40), channel_id=1, source_target_pairs={{12,0},{0,4},{4,8},{8,12},{13,1},{1,5},{5,9},{9,13},{14,2},{2,6},{... | collective-permute-start | bytes 589832 | tf_op jit(solution)/shard_map/ppermute | solution.py:342
  52.8 28.8 %copy-start.12 = (bf16[512,384]{1,0:T(8,128)(2,1)S(1)}, bf16[512,384]{1,0:T(8,128)(2,1)}, u32[]{:S(2)}) copy-start(bf16[512,384]{1,0:T(8,128)(2,1)} %copy-done.11) | copy-start | bytes 1179652
  52.8 28.8 %copy-start.14 = (bf16[384,512]{1,0:T(8,128)(2,1)S(1)}, bf16[384,512]{1,0:T(8,128)(2,1)}, u32[]{:S(2)}) copy-start(bf16[384,512]{1,0:T(8,128)(2,1)} %copy-done.13) | copy-start | bytes 1179652
  52.8 20.9 %collective-permute-start.7 = (bf16[256,384]{1,0:T(8,128)(2,1)S(1)}, bf16[256,384]{1,0:T(8,128)(2,1)S(1)}, u32[]{:S(2)}, u32[]{:S(2)}) collective-permute-start(bf16[256,384]{1,0:T(8,128)(2,1)S(1)} %bitcast.38), channel_id=1, source_target_pairs={{2,0},{0,2},{3,1},{1,3},{6,4},{4,6},{7,5},{5,7},{10,8},{8,10},{11,... | collective-permute-start | bytes 589832 | tf_op jit(solution)/shard_map/ppermute | solution.py:342
  63.3 7.5 %collective-permute-start.13 = (bf16[192,384]{1,0:T(8,128)(2,1)S(1)}, bf16[192,384]{1,0:T(8,128)(2,1)S(1)}, u32[]{:S(2)}, u32[]{:S(2)}) collective-permute-start(bf16[192,384]{1,0:T(8,128)(2,1)S(1)} %add_convert_fusion.2), channel_id=1, source_target_pairs={{0,8},{4,12},{8,0},{12,4},{1,9},{5,13},{9,1},{13,5},{2,10},{6,14},... | collective-permute-start | bytes 442376 | tf_op jit(solution)/shard_map/ppermute | solution.py:362
  63.4 10.3 %collective-permute-start.8 = (bf16[128,384]{1,0:T(8,128)(2,1)S(1)}, bf16[128,384]{1,0:T(8,128)(2,1)S(1)}, u32[]{:S(2)}, u32[]{:S(2)}) collective-permute-start(bf16[128,384]{1,0:T(8,128)(2,1)S(1)} %slice_bitcast_fusion), channel_id=1, source_target_pairs={{2,0},{0,2},{3,1},{1,3},{6,4},{4,6},{7,5},{5,7},{10,8},{8,10},{11,... | collective-permute-start | bytes 294920 | tf_op jit(solution)/shard_map/ppermute | solution.py:342
  70.8 4.6 %collective-permute-start.14 = (bf16[192,384]{1,0:T(8,128)(2,1)S(1)}, bf16[192,384]{1,0:T(8,128)(2,1)S(1)}, u32[]{:S(2)}, u32[]{:S(2)}) collective-permute-start(bf16[192,384]{1,0:T(8,128)(2,1)S(1)} %add_convert_fusion.1.refs_1_), channel_id=1, source_target_pairs={{0,4},{4,0},{8,12},{12,8},{1,5},{5,1},{9,13},{13,9},{2,6},{6,2},{1... | collective-permute-start | bytes 442376 | tf_op jit(solution)/shard_map/ppermute | solution.py:362
  70.9 7.5 %collective-permute-start.15 = (bf16[192,384]{1,0:T(8,128)(2,1)S(1)}, bf16[192,384]{1,0:T(8,128)(2,1)S(1)}, u32[]{:S(2)}, u32[]{:S(2)}) collective-permute-start(bf16[192,384]{1,0:T(8,128)(2,1)S(1)} %add_convert_fusion.1.refs_1_), channel_id=1, source_target_pairs={{0,1},{1,0},{2,3},{3,2},{4,5},{5,4},{6,7},{7,6},{8,9},{9,8},{10,11... | collective-permute-start | bytes 442376 | tf_op jit(solution)/shard_map/ppermute | solution.py:362
  72.5 7.7 %collective-permute-start.16 = (bf16[192,384]{1,0:T(8,128)(2,1)S(1)}, bf16[192,384]{1,0:T(8,128)(2,1)S(1)}, u32[]{:S(2)}, u32[]{:S(2)}) collective-permute-start(bf16[192,384]{1,0:T(8,128)(2,1)S(1)} %add_convert_fusion.1.refs_1_), channel_id=1, source_target_pairs={{0,5},{1,4},{4,1},{5,0},{8,13},{9,12},{12,9},{13,8},{2,7},{3,6},{6... | collective-permute-start | bytes 442376 | tf_op jit(solution)/shard_map/ppermute | solution.py:362
  73.7 10.5 %collective-permute-start.17 = (bf16[192,384]{1,0:T(8,128)(2,1)S(1)}, bf16[192,384]{1,0:T(8,128)(2,1)S(1)}, u32[]{:S(2)}, u32[]{:S(2)}) collective-permute-start(bf16[192,384]{1,0:T(8,128)(2,1)S(1)} %add_convert_fusion.1.refs_1_), channel_id=1, source_target_pairs={{0,2},{2,0},{1,3},{3,1},{4,6},{6,4},{5,7},{7,5},{8,10},{10,8},{9,1... | collective-permute-start | bytes 442376 | tf_op jit(solution)/shard_map/ppermute | solution.py:362
  75.4 8.8 %collective-permute-start.18 = (bf16[192,384]{1,0:T(8,128)(2,1)S(1)}, bf16[192,384]{1,0:T(8,128)(2,1)S(1)}, u32[]{:S(2)}, u32[]{:S(2)}) collective-permute-start(bf16[192,384]{1,0:T(8,128)(2,1)S(1)} %collective-permute-done.14.refs_2_), channel_id=1, source_target_pairs={{0,2},{2,0},{1,3},{3,1},{4,6},{6,4},{5,7},{7,5},{8,10},{10,8},{9,1... | collective-permute-start | bytes 442376 | tf_op jit(solution)/shard_map/ppermute | solution.py:362
  78.4 5.8 %collective-permute-start.19 = (bf16[192,384]{1,0:T(8,128)(2,1)S(1)}, bf16[192,384]{1,0:T(8,128)(2,1)S(1)}, u32[]{:S(2)}, u32[]{:S(2)}) collective-permute-start(bf16[192,384]{1,0:T(8,128)(2,1)S(1)} %collective-permute-done.15.refs_3_), channel_id=1, source_target_pairs={{0,2},{2,0},{1,3},{3,1},{4,6},{6,4},{5,7},{7,5},{8,10},{10,8},{9,1... | collective-permute-start | bytes 442376 | tf_op jit(solution)/shard_map/ppermute | solution.py:362
  80.2 4.1 %collective-permute-start.20 = (bf16[192,384]{1,0:T(8,128)(2,1)S(1)}, bf16[192,384]{1,0:T(8,128)(2,1)S(1)}, u32[]{:S(2)}, u32[]{:S(2)}) collective-permute-start(bf16[192,384]{1,0:T(8,128)(2,1)S(1)} %collective-permute-done.16.refs_4_), channel_id=1, source_target_pairs={{0,2},{2,0},{1,3},{3,1},{4,6},{6,4},{5,7},{7,5},{8,10},{10,8},{9,1... | collective-permute-start | bytes 442376 | tf_op jit(solution)/shard_map/ppermute | solution.py:362
  (18 other events, 27.4 us)

commit v3 on v2

--- a/solution.py
+++ b/solution.py
@@ -1,3 +1,4 @@
+import functools
 import math
 
 import jax
@@ -163,27 +164,35 @@
     halo,
     flags,
     gain,
-    qkv_weight,
-    cot,
+    core,
+    weight_far,
     weight_t_far,
     d_context_far,
     bias0_far,
+    cot_far,
     bias1_far,
     bias2_far,
-    grads,
-    d_rolled,
-    kept_far,
+    keep_far,
+    send_far,
+    d_rolled_far,
     context_far,
     penalty,
+    qkv_weight,
     qkv_weight_t,
     d_context_t,
     bias_blocks,
+    cot,
     context_t,
     d_qkv,
+    grads,
+    d_rolled,
     sems,
 ):
-    sources = (weight_t_far, d_context_far, bias0_far, bias1_far, bias2_far)
-    places = [qkv_weight_t, d_context_t] + [bias_blocks.at[k] for k in range(3)]
+    sources = (
+        weight_far, weight_t_far, d_context_far, bias0_far, cot_far, bias1_far, bias2_far
+    )
+    places = [qkv_weight, qkv_weight_t, d_context_t, bias_blocks.at[0], cot]
+    places += [bias_blocks.at[1], bias_blocks.at[2]]
     arrivals = [
         pltpu.make_async_copy(source, place, sems.at[k])
         for k, (source, place) in enumerate(zip(sources, places))
@@ -216,12 +225,13 @@
     xhat, inv_std = layer_norm(jnp.concatenate(rolled, 0))
     normed = (xhat * gain[...]).astype(bf16)
     normed_t = normed.T
+    arrivals[0].wait()
     kv = nn(normed, qkv_weight[:, MODEL_WIDTH:]).astype(bf16)
-    arrivals[0].wait()
+    arrivals[1].wait()
     qkv_t = nt(qkv_weight_t[...], normed).astype(bf16)
-    arrivals[1].wait()
+    arrivals[2].wait()
     for pair in range(HEADS // 2):
-        arrivals[2 + pair].wait()
+        arrivals[(3, 5, 6)[pair]].wait()
         heads = [
             attention_head(2 * pair + side, qkv_t, kv, penalty, bias_blocks.at[pair], d_context_t)
             for side in range(2)
@@ -233,8 +243,12 @@
             first = kind * MODEL_WIDTH + pair * 128
             d_qkv[:, first : first + 128] = d_pair[:, kind * 128 : kind * 128 + 128]
         first = pair * TOKENS
+        if pair == 0:
+            arrivals[4].wait()
         grads[first : first + 128, :] = nn(context, cot[...]).astype(bf16)
         grads[first + 128 : first + TOKENS, :] = nn(normed_t, d_pair).astype(bf16)
+        for block in (2 * pair, 2 * pair + 1):
+            to_half(grads, block, core[0], keep_far, send_far, sems)
     keep_context = pltpu.make_async_copy(context_t, context_far, sems.at[0])
     keep_context.start()
     d_xhat = nt(d_qkv[...], qkv_weight[...]) * gain[...]
@@ -246,14 +260,40 @@
             - xhat * jnp.mean(d_xhat * xhat, -1, keepdims=True)
         )
     ).astype(bf16)
-    keep = pltpu.make_async_copy(d_rolled, kept_far, sems.at[1])
+    keep = pltpu.make_async_copy(d_rolled, d_rolled_far, sems.at[1])
     keep.start()
+    for block in range(6):
+        source, target = half_block(grads, block, keep_far)
+        pltpu.make_async_copy(source, target, sems.at[7 + block]).wait()
     keep_context.wait()
     keep.wait()
 
 
+def half_block(grads, block, half):
+    place = block % 3 * HALF
+    return grads.at[pl.ds(block * HALF, HALF), :], half.at[pl.ds(place, HALF), :]
+
+
+def to_half(grads, block, core, keep_far, send_far, sems):
+    for half, side in ((keep_far, block // 3), (send_far, 1 - block // 3)):
+
+        @pl.when(core == side)
+        def _():
+            source, target = half_block(grads, block, half)
+            pltpu.make_async_copy(source, target, sems.at[7 + block]).start()
+
+
 def place_kernel(
-    shift, halo, out_weight, kept_far, context_far, field_grad, update, kept, context_t, sems
+    shift,
+    halo,
+    out_weight,
+    kept_far,
+    context_far,
+    field_grad,
+    update,
+    kept,
+    context_t,
+    sems,
 ):
     copies = [
         pltpu.make_async_copy(kept_far, kept, sems.at[0]),
@@ -279,16 +319,11 @@
 
 def finish_kernel(scale, place, *refs):
     mine, other, (weight, gain) = refs[:4], refs[4:8], refs[8:10]
-    qkv_far, out_far, gain_grad, qkv_grad, out_grad, sems = refs[10:]
-    first_core, bit_one, bit_two = place[0] == 0, place[1] == 1, place[2] == 1
-    sides = []
-    for shares in (mine, other):
-        shares = [share[...].astype(f32) * scale for share in shares]
-        shares = [jnp.where(bit_one, shares[k ^ 1], shares[k]) for k in range(4)]
-        sides.append([jnp.where(bit_two, shares[k ^ 2], shares[k]) for k in range(4)])
-    lower = [jnp.where(first_core, a, b) for a, b in zip(*sides)]
-    upper = [jnp.where(first_core, b, a) for a, b in zip(*sides)]
-    whole = jnp.concatenate(lower + upper, 0)
+    gain_grad, qkv_far, out_far, shares, qkv_grad, out_grad, sems = refs[10:]
+    for side, group in ((place[0], mine), (1 - place[0], other)):
+        for offset in range(4):
+            shares[side * 4 + (offset ^ place[1])] = group[offset][...]
+    whole = shares[...].reshape(3 * TOKENS, MODEL_WIDTH).astype(f32) * scale
     copies = []
     partial = 0.0
     for kind in range(3):
@@ -313,24 +348,26 @@
         out_grad[pair * 128 : pair * 128 + 128, :] = whole[pair * TOKENS : pair * TOKENS + 128]
     copies.append(pltpu.make_async_copy(out_grad, out_far, sems.at[3]))
     copies[-1].start()
-    gain_grad[...] = jnp.sum(partial.T, 0, keepdims=True) / gain[...]
+    gain_grad[...] = (jnp.sum(partial.T, 0, keepdims=True) / gain[...]).reshape(MODEL_WIDTH)
     for copy in copies:
         copy.wait()
 
 
-def local_call(kernel, shapes, inputs, far_in=0, far_out=0, scratch=(), copies=0, micros=1):
+def local_call(
+    kernel, shapes, inputs, far_in=0, far_out=0, scratch=(), copies=0, micros=1, limit=24
+):
     vmem = pl.BlockSpec(memory_space=pltpu.VMEM)
     smem = pl.BlockSpec(memory_space=pltpu.SMEM)
-    far = pl.BlockSpec(memory_space=pltpu.HBM)
+    far = pl.BlockSpec(memory_space=pl.ANY)
+    near = inputs[: len(inputs) - far_in]
     return pl.pallas_call(
         kernel,
         out_shape=[jax.ShapeDtypeStruct(shape, dtype) for shape, dtype in shapes],
-        in_specs=[smem if array.dtype == jnp.int32 else vmem for array in inputs[: len(inputs) - far_in]]
-        + [far] * far_in,
+        in_specs=[smem if array.dtype == jnp.int32 else vmem for array in near] + [far] * far_in,
         out_specs=[vmem] * (len(shapes) - far_out) + [far] * far_out,
         scratch_shapes=[pltpu.VMEM(shape, dtype) for shape, dtype in scratch]
         + [pltpu.SemaphoreType.DMA((copies,))],
-        compiler_params=pltpu.CompilerParams(vmem_limit_bytes=32 * 2**20),
+        compiler_params=pltpu.CompilerParams(vmem_limit_bytes=limit * 2**20),
         cost_estimate=pl.CostEstimate(
             flops=micros * 10**9, bytes_accessed=10**6, transcendentals=0
         ),
@@ -340,6 +377,10 @@
 def passed_along(block, axis, distance):
     count = lax.axis_size(axis)
     return lax.ppermute(block, axis, [((i - distance) % count, i) for i in range(count)])
+
+
+CORE = ("sx", 1)
+GROUPS = ([("sy", 1)], [("ta", 1)], [("sy", 1), ("ta", 1)])
 
 
 def index_bit(axis, bit):
@@ -366,29 +407,28 @@
     return sum(piece.astype(f32) for piece in pieces).astype(bf16)
 
 
-def all_sum(block):
-    core, one, two = ("sx", 1), ("ta", 1), ("sy", 1)
+def sum_quarter(keep, send):
+    block = add_up(keep, swapped(send, CORE))
+    share = block.shape[0] // 4
+    mine = quarter_index()
+    pick = lambda place: lax.dynamic_slice_in_dim(block, place * share, share, 0)
+    arrived = [swapped(pick(mine ^ k), *GROUPS[k - 1]) for k in (1, 2, 3)]
+    return add_up(pick(mine), *arrived)
+
+
+def sum_rest(quarter):
     rest = [
         (axis, 1 << k)
         for axis in ("ta", "sy")
         for k in range(1, lax.axis_size(axis).bit_length() - 1)
     ]
-    half = block.shape[0] // 2
-    side = index_bit(*core)
-    pick = lambda array, place, size: lax.dynamic_slice_in_dim(array, place * size, size, 0)
-    block = add_up(pick(block, side, half), swapped(pick(block, 1 - side, half), core))
-    share = half // 4
-    mine = 2 * index_bit(*one) + index_bit(*two)
-    groups = [[two], [one], [two, one]]
-    arrived = [
-        swapped(pick(block, mine ^ offset, share), *group)
-        for offset, group in zip((1, 2, 3), groups)
-    ]
-    quarter = add_up(pick(block, mine, share), *arrived)
     for bit in rest:
         quarter = add_up(quarter, swapped(quarter, bit))
-    quarters = [quarter] + [swapped(quarter, *group) for group in groups]
-    return quarters, [swapped(quarter, core) for quarter in quarters]
+    return quarter
+
+
+def quarter_index():
+    return 2 * index_bit("ta", 1) + index_bit("sy", 1)
 
 
 def shards(
@@ -403,10 +443,11 @@
 ):
     width = MODEL_WIDTH
     wide = lambda tokens: ((tokens, width), bf16)
-    rows = passed_along(state_field[:, :RIM].reshape(-1, width), "sy", -1)
+    first_rows = state_field[:, :RIM].reshape(-1, width)
+    rows = passed_along(first_rows, "sy", -1)
+    marks = outlier_flags.astype(bf16) + first_rows[0, 0] * 0
+    row_marks = passed_along(marks[:, :RIM].reshape(2 * RIM, SIDE), "sy", -1)
     cols = passed_along(state_field[:, :, :RIM].reshape(-1, width), "sx", -1)
-    marks = outlier_flags.astype(bf16)
-    row_marks = passed_along(marks[:, :RIM].reshape(2 * RIM, SIDE), "sy", -1)
     col_marks = passed_along(marks[:, :, :RIM].reshape(2 * SIDE, RIM), "sx", -1)
     strips = jnp.pad(
         position_bias.reshape(HEADS, 3, 31, 31), ((0, 0), (0, 0), (0, 1), (0, 1))
@@ -422,6 +463,7 @@
         scratch=[((3, 6, HALF, HALF), f32), ((width, TOKENS), bf16), wide(3 * width)],
         copies=5,
         micros=3,
+        limit=60,
     )
     corner = passed_along(
         rows.reshape(2 * RIM, SIDE, width)[:, :RIM].reshape(-1, width), "sx", -1
@@ -436,33 +478,42 @@
         0,
     )
     gain = layer_norm_gain.reshape(1, width)
-    grads, d_rolled, kept, context_t = local_call(
+    core = index_bit(*CORE).astype(jnp.int32).reshape(1)
+    keep, send, d_rolled, context_t = local_call(
         main_kernel,
-        [wide(3 * TOKENS), wide(TOKENS), wide(TOKENS), ((width, TOKENS), bf16)],
+        [wide(2 * width)] * 2 + [wide(TOKENS), ((width, TOKENS), bf16)],
         [
             window_shift,
             state_field.reshape(TOKENS, width),
             halo,
             all_marks,
             gain,
+            core,
             qkv_weight,
-            cot_rows,
             qkv_weight_t,
             d_context_t,
-            *bias_blocks,
+            bias_blocks[0],
+            cot_rows,
+            bias_blocks[1],
+            bias_blocks[2],
         ],
-        far_in=5,
-        far_out=2,
+        far_in=7,
+        far_out=4,
         scratch=[
             ((TOKENS, TOKENS), f32),
+            ((width, 3 * width), bf16),
             wide(3 * width),
             ((width, TOKENS), bf16),
             ((3, 6, HALF, HALF), f32),
+            wide(TOKENS),
             ((width, TOKENS), bf16),
             ((TOKENS, 3 * width), bf16),
+            wide(3 * TOKENS),
+            wide(TOKENS),
         ],
-        copies=5,
+        copies=13,
         micros=12,
+        limit=60,
     )
     grid = d_rolled.reshape(2, SIDE, SIDE, width)
     below = passed_along(grid[:, RIM:].reshape(-1, width), "sy", 1)
@@ -470,6 +521,7 @@
     across = passed_along(
         below.reshape(2 * RIM, SIDE, width)[:, RIM:].reshape(-1, width), "sx", 1
     )
+    quarter = sum_quarter(keep, send)
     field_grad, update = local_call(
         place_kernel,
         [wide(TOKENS), wide(TOKENS)],
@@ -477,7 +529,7 @@
             window_shift,
             jnp.concatenate([below, beside, across], 0),
             out_weight,
-            kept,
+            d_rolled,
             context_t,
         ],
         far_in=2,
@@ -485,11 +537,13 @@
         copies=2,
         micros=2,
     )
-    quarters, others = all_sum(grads)
+    quarter = sum_rest(quarter)
+    quarters = [quarter] + [swapped(quarter, *group) for group in GROUPS]
+    others = [swapped(piece, CORE) for piece in quarters]
     tiles = lax.axis_size("sy") * lax.axis_size("sx") * lax.axis_size("ta")
-    place = jnp.stack([index_bit("sx", 1), index_bit("sy", 1), index_bit("ta", 1)])
+    place = jnp.stack([index_bit(*CORE), quarter_index()]).astype(jnp.int32)
     gain_grad, qkv_grad, out_grad = finish_call(
-        1.0 / tiles, [place.astype(jnp.int32), *quarters, *others, qkv_weight, gain]
+        1.0 / tiles, [place, *quarters, *others, qkv_weight, gain]
     )
     shape = state_field.shape
     return (
@@ -497,23 +551,22 @@
         field_grad.reshape(shape),
         qkv_grad,
         out_grad,
-        gain_grad.reshape(width),
+        gain_grad,
     )
 
 
 def finish_call(scale, inputs):
     width = MODEL_WIDTH
-
-    def kernel(*refs):
-        gain_grad, qkv_far, out_far, *scratch = refs[len(inputs) :]
-        finish_kernel(scale, *refs[: len(inputs)], qkv_far, out_far, gain_grad, *scratch)
-
     return local_call(
-        kernel,
-        [((1, width), f32), ((width, 3 * width), f32), ((width, width), f32)],
+        functools.partial(finish_kernel, scale),
+        [((width,), f32), ((width, 3 * width), f32), ((width, width), f32)],
         inputs,
         far_out=2,
-        scratch=[((width, 3 * width), f32), ((width, width), f32)],
+        scratch=[
+            ((8, width // 2, width), bf16),
+            ((width, 3 * width), f32),
+            ((width, width), f32),
+        ],
         copies=4,
     )
 

time: 87.9 us -> 77.3 us (0.88)
  local copies, waits for them, and re-layouts: 17.2 us -> 5.14 us
  Pallas kernels: 24.1 us -> 26.3 us
  waiting for transfers between devices: 18.3 us -> 16.9 us
    unnamed x42 -> x14, local copies, waits for them, and re-layouts: 12.9 us -> 0.03 us
    pallas_call x4, Pallas kernels: 24.1 us -> 26.3 us  [local_call(): pl.pallas_call(kernel, out_shape=[jax.ShapeDtypeStruct(shape, dtype) for...]
    ppermute x12, waiting for transfers between devices: 17.2 us -> 16.2 us  [swapped(): return lax.ppermute(block, axes, route)]
    convert_element_type x3, other arithmetic: 2.26 us -> 1.33 us  [add_up(): return sum((piece.astype(f32) for piece in pieces)).astype(bf16)]
  transfers between devices with their start and end apart: 21 -> 21, of which waited for: 8 -> 5; matrix products, arithmetic and copies ran while one was open for 5% -> 7% of each run, Pallas kernels for 8% -> 11%
where the time goes in v3:
time: 77.3 us; the launch traced here: 76.5 us
  Pallas kernels  26.3 us (34%)
  starting transfers between devices  22.8 us (29%)
  waiting for transfers between devices  16.9 us (22%)
  local copies, waits for them, and re-layouts  5.14 us (7%)
  other arithmetic  3.64 us (5%)
  between operations  1.73 us (2%)
    pallas_call x4, Pallas kernels, local_call(): pl.pallas_call(kernel, out_shape=[jax.ShapeDtypeStruct(shape, dtype) for...  26.3 us
    ppermute x12, waiting for transfers between devices, swapped(): return lax.ppermute(block, axes, route)  16.2 us
    ppermute x12, starting transfers between devices, swapped(): return lax.ppermute(block, axes, route)  12.6 us
    ppermute x9, starting transfers between devices, passed_along(): lax.ppermute(block, axis, [((i - distance) % count, i) for i in range(cou...  10.3 us
  transfers between devices with their start and end apart: 21, of which 5 were waited for; matrix products, arithmetic and copies ran while one was open for 7% of the time, Pallas kernels for 11%

profile of v3, /device:TPU:1, one launch (start us, length us, event | category | flops | bytes accessed | tf_op | source)
XLA Modules:
  0.0 76.5 jit_solution(6627616319074581154)
XLA Ops:
  0.6 1.0 %slice.30 = bf16[2,8,16,384]{3,2,1,0:T(8,128)(2,1)S(1)} slice(bf16[2,16,16,384]{3,2,1,0:T(8,128)(2,1)} %param.8), slice={[0:2], [0:8], [0:16], [0:384]} | slice | bytes 393216 | tf_op jit(solution)/shard_map/slice | solution.py:446
  1.6 4.2 %collective-permute-start = (bf16[256,384]{1,0:T(8,128)(2,1)S(1)}, bf16[256,384]{1,0:T(8,128)(2,1)S(1)}, u32[]{:S(2)}, u32[]{:S(2)}) collective-permute-start(bf16[256,384]{1,0:T(8,128)(2,1)S(1)} %bitcast.36), channel_id=1, source_target_pairs={{4,0},{8,4},{12,8},{0,12},{5,1},{9,5},{13,9},{1,13},{6,2},{10,6},{... | collective-permute-start | bytes 589832 | tf_op jit(solution)/shard_map/ppermute | solution.py:379
  7.9 1.2 %collective-permute-start.4 = (bf16[32,8]{1,0:T(8,128)(2,1)S(1)}, bf16[32,8]{1,0:T(8,128)(2,1)S(1)}, u32[]{:S(2)}, u32[]{:S(2)}) collective-permute-start(bf16[32,8]{1,0:T(8,128)(2,1)S(1)} %bitcast.40), channel_id=1, source_target_pairs={{2,0},{0,2},{3,1},{1,3},{6,4},{4,6},{7,5},{5,7},{10,8},{8,10},{11,... | collective-permute-start | bytes 1544 | tf_op jit(solution)/shard_map/ppermute | solution.py:379
  9.1 0.9 %slice.31 = bf16[2,16,8,384]{3,2,1,0:T(8,128)(2,1)S(1)} slice(bf16[2,16,16,384]{3,2,1,0:T(8,128)(2,1)} %param.8), slice={[0:2], [0:16], [0:8], [0:384]} | slice | bytes 393216 | tf_op jit(solution)/shard_map/slice | solution.py:450
  10.1 1.2 %reshape.85 = f32[6,3,31,31]{3,2,1,0:T(8,128)S(1)} reshape(f32[6,2883]{1,0:T(8,128)} %param.14) | data formatting | bytes 138384 | tf_op jit(solution)/shard_map/reshape | solution.py:453
  11.4 0.8 %reshape.87.strips = f32[36,512]{1,0:T(8,128)} reshape(f32[6,3,2,16,32]{4,3,2,1,0:T(8,128)S(1)} %copy.13) | data formatting | bytes 147456 | tf_op jit(solution)/shard_map/reshape | solution.py:455
  12.2 5.4 %shard_map.119 = (f32[6,256,256]{2,1,0:T(8,128)}, f32[6,256,256]{2,1,0:T(8,128)}, f32[6,256,256]{2,1,0:T(8,128)}, bf16[384,512]{1,0:T(8,128)(2,1)}, bf16[1152,384]{1,0:T(8,128)(2,1)}) custom-call(f32[36,512]{1,0:T(8,128)} %reshape.87.strips, bf16[512,384]{1,0:T(8,128)(2,1)} %bitcast.43, bf16[384,384]{1,0:T(8,128)(2,1)} %out_weight.3, bf16[384,1152]{1,0:T(8,128)(2,1)} %refs_8_.1), custom_call_target="tpu_custom_call" | custom-call | flops 3000000000 | bytes 1000000 | tf_op jit(solution)/shard_map/pallas_call | solution.py:363
  20.1 0.8 %pad_maximum_fusion.halo = bf16[640,384]{1,0:T(8,128)(2,1)} fusion(bf16[128,384]{1,0:T(8,128)(2,1)S(1)} %collective-permute-done.2, bf16[256,384]{1,0:T(8,128)(2,1)S(1)} %collective-permute-done.1, bf16[256,384]{1,0:T(8,128)(2,1)S(1)} %collective-permute-done), kind=kLoop, calls=%fused_computation.1 | loop fusion | flops 1474560 | bytes 983040 | tf_op jit(solution)/shard_map/concatenate | solution.py:472
  21.0 15.2 %shard_map.120 = (bf16[768,384]{1,0:T(8,128)(2,1)}, bf16[768,384]{1,0:T(8,128)(2,1)}, bf16[512,384]{1,0:T(8,128)(2,1)}, bf16[384,512]{1,0:T(8,128)(2,1)}) custom-call(s32[2]{0:T(128)} %shift.3, bf16[512,384]{1,0:T(8,128)(2,1)} %bitcast.34, bf16[640,384]{1,0:T(8,128)(2,1)} %pad_maximum_fusion.halo, bf16[96,128]{1,0:T(8,128)(2,1)} %fusion.7.flags, ...), custom_call_target="tpu_custom_call" | custom-call | flops 12000000000 | bytes 1000000 | tf_op jit(solution)/shard_map/pallas_call | solution.py:363
  36.6 1.9 %collective-permute-done.9 = bf16[768,384]{1,0:T(8,128)(2,1)S(1)} collective-permute-done((bf16[768,384]{1,0:T(8,128)(2,1)}, bf16[768,384]{1,0:T(8,128)(2,1)S(1)}, u32[]{:S(2)}, u32[]{:S(2)}) %collective-permute-start.9) | collective-permute-done | bytes 589856 | tf_op jit(solution)/shard_map/ppermute | solution.py:403
  38.5 1.2 %add_convert_fusion = bf16[768,384]{1,0:T(8,128)(2,1)S(1)} fusion(bf16[768,384]{1,0:T(8,128)(2,1)S(1)} %collective-permute-done.9, bf16[768,384]{1,0:T(8,128)(2,1)} %get-tuple-element.28), kind=kLoop, calls=%fused_computation | loop fusion | flops 1179648 | bytes 1769472 | tf_op jit(solution)/shard_map/convert_element_type | solution.py:407
  39.7 1.4 %collective-permute-start.10 = (bf16[192,384]{1,0:T(8,128)(2,1)S(1)}, bf16[192,384]{1,0:T(8,128)(2,1)S(1)}, u32[]{:S(2)}, u32[]{:S(2)}) collective-permute-start(bf16[192,384]{1,0:T(8,128)(2,1)S(1)} %get-tuple-element.33), channel_id=1, source_target_pairs={{0,4},{4,0},{8,12},{12,8},{1,5},{5,1},{9,13},{13,9},{2,6},{6,2},{1... | collective-permute-start | bytes 442376 | tf_op jit(solution)/shard_map/ppermute | solution.py:403
  41.1 1.2 %collective-permute-start.11 = (bf16[192,384]{1,0:T(8,128)(2,1)S(1)}, bf16[192,384]{1,0:T(8,128)(2,1)S(1)}, u32[]{:S(2)}, u32[]{:S(2)}) collective-permute-start(bf16[192,384]{1,0:T(8,128)(2,1)S(1)} %get-tuple-element.35), channel_id=1, source_target_pairs={{0,1},{1,0},{2,3},{3,2},{4,5},{5,4},{6,7},{7,6},{8,9},{9,8},{10,11... | collective-permute-start | bytes 442376 | tf_op jit(solution)/shard_map/ppermute | solution.py:403
  42.5 1.3 %collective-permute-start.6 = (bf16[256,384]{1,0:T(8,128)(2,1)S(1)}, bf16[256,384]{1,0:T(8,128)(2,1)S(1)}, u32[]{:S(2)}, u32[]{:S(2)}) collective-permute-start(bf16[256,384]{1,0:T(8,128)(2,1)S(1)} %bitcast.39), channel_id=1, source_target_pairs={{12,0},{0,4},{4,8},{8,12},{13,1},{1,5},{5,9},{9,13},{14,2},{2,6},{... | collective-permute-start | bytes 589832 | tf_op jit(solution)/shard_map/ppermute | solution.py:379
  43.9 1.5 %collective-permute-start.7 = (bf16[256,384]{1,0:T(8,128)(2,1)S(1)}, bf16[256,384]{1,0:T(8,128)(2,1)S(1)}, u32[]{:S(2)}, u32[]{:S(2)}) collective-permute-start(bf16[256,384]{1,0:T(8,128)(2,1)S(1)} %bitcast.35), channel_id=1, source_target_pairs={{2,0},{0,2},{3,1},{1,3},{6,4},{4,6},{7,5},{5,7},{10,8},{8,10},{11,... | collective-permute-start | bytes 589832 | tf_op jit(solution)/shard_map/ppermute | solution.py:379
  45.9 7.4 %collective-permute-done.12 = bf16[192,384]{1,0:T(8,128)(2,1)S(1)} collective-permute-done((bf16[192,384]{1,0:T(8,128)(2,1)S(1)}, bf16[192,384]{1,0:T(8,128)(2,1)S(1)}, u32[]{:S(2)}, u32[]{:S(2)}) %collective-permute-start.12) | collective-permute-done | bytes 147488 | tf_op jit(solution)/shard_map/ppermute | solution.py:403
  53.4 1.2 %collective-permute-start.8 = (bf16[128,384]{1,0:T(8,128)(2,1)S(1)}, bf16[128,384]{1,0:T(8,128)(2,1)S(1)}, u32[]{:S(2)}, u32[]{:S(2)}) collective-permute-start(bf16[128,384]{1,0:T(8,128)(2,1)S(1)} %slice_bitcast_fusion), channel_id=1, source_target_pairs={{2,0},{0,2},{3,1},{1,3},{6,4},{4,6},{7,5},{5,7},{10,8},{8,10},{11,... | collective-permute-start | bytes 294920 | tf_op jit(solution)/shard_map/ppermute | solution.py:379
  54.6 6.3 %collective-permute-done.13 = bf16[192,384]{1,0:T(8,128)(2,1)S(1)} collective-permute-done((bf16[192,384]{1,0:T(8,128)(2,1)S(1)}, bf16[192,384]{1,0:T(8,128)(2,1)S(1)}, u32[]{:S(2)}, u32[]{:S(2)}) %collective-permute-start.13) | collective-permute-done | bytes 147488 | tf_op jit(solution)/shard_map/ppermute | solution.py:403
  61.4 2.3 %collective-permute-start.16 = (bf16[192,384]{1,0:T(8,128)(2,1)S(1)}, bf16[192,384]{1,0:T(8,128)(2,1)S(1)}, u32[]{:S(2)}, u32[]{:S(2)}) collective-permute-start(bf16[192,384]{1,0:T(8,128)(2,1)S(1)} %add_convert_fusion.1.refs_0_), channel_id=1, source_target_pairs={{0,5},{1,4},{4,1},{5,0},{8,13},{9,12},{12,9},{13,8},{2,7},{3,6},{6... | collective-permute-start | bytes 442376 | tf_op jit(solution)/shard_map/ppermute | solution.py:403
  63.9 1.7 %collective-permute-start.17 = (bf16[192,384]{1,0:T(8,128)(2,1)S(1)}, bf16[192,384]{1,0:T(8,128)(2,1)S(1)}, u32[]{:S(2)}, u32[]{:S(2)}) collective-permute-start(bf16[192,384]{1,0:T(8,128)(2,1)S(1)} %add_convert_fusion.1.refs_0_), channel_id=1, source_target_pairs={{0,2},{2,0},{1,3},{3,1},{4,6},{6,4},{5,7},{7,5},{8,10},{10,8},{9,1... | collective-permute-start | bytes 442376 | tf_op jit(solution)/shard_map/ppermute | solution.py:403
  65.6 3.0 %collective-permute-start.18 = (bf16[192,384]{1,0:T(8,128)(2,1)S(1)}, bf16[192,384]{1,0:T(8,128)(2,1)S(1)}, u32[]{:S(2)}, u32[]{:S(2)}) collective-permute-start(bf16[192,384]{1,0:T(8,128)(2,1)S(1)} %collective-permute-done.14.refs_1_), channel_id=1, source_target_pairs={{0,2},{2,0},{1,3},{3,1},{4,6},{6,4},{5,7},{7,5},{8,10},{10,8},{9,1... | collective-permute-start | bytes 442376 | tf_op jit(solution)/shard_map/ppermute | solution.py:403
  68.7 1.9 %collective-permute-start.19 = (bf16[192,384]{1,0:T(8,128)(2,1)S(1)}, bf16[192,384]{1,0:T(8,128)(2,1)S(1)}, u32[]{:S(2)}, u32[]{:S(2)}) collective-permute-start(bf16[192,384]{1,0:T(8,128)(2,1)S(1)} %collective-permute-done.15.refs_2_), channel_id=1, source_target_pairs={{0,2},{2,0},{1,3},{3,1},{4,6},{6,4},{5,7},{7,5},{8,10},{10,8},{9,1... | collective-permute-start | bytes 442376 | tf_op jit(solution)/shard_map/ppermute | solution.py:403
  70.6 2.7 %shard_map.121 = (bf16[512,384]{1,0:T(8,128)(2,1)}, bf16[512,384]{1,0:T(8,128)(2,1)}) custom-call(s32[2]{0:T(128)S(1)} %copy-done.4, bf16[640,384]{1,0:T(8,128)(2,1)S(1)} %pad_maximum_fusion.1.halo, bf16[384,384]{1,0:T(8,128)(2,1)S(1)} %copy-done.3, bf16[512,384]{1,0:T(8,128)(2,1)S(1)} %copy-done, bf16[384,512]{1,0:T(8,128)(2,1)S(1)} %copy-done.5), custom_call_target="tpu_custom_call" | custom-call | flops 2000000000 | bytes 1000000 | tf_op jit(solution)/shard_map/pallas_call | solution.py:363
  73.4 2.9 %shard_map.122 = (f32[384]{0:T(512)}, f32[384,1152]{1,0:T(8,128)}, f32[384,384]{1,0:T(8,128)}) custom-call(s32[2]{0:T(128)S(1)} %pad_add_fusion.place, bf16[192,384]{1,0:T(8,128)(2,1)S(1)} %add_convert_fusion.1.refs_0_, bf16[192,384]{1,0:T(8,128)(2,1)S(1)} %collective-permute-done.14.refs_1_, bf16[192,384]{1,0:T(8,128)(2,1)S(1)} %collective-permute-done.15.refs_2_, ...), custom_call_target="tpu_custom_call" | custom-call | flops 1000000000 | bytes 1000000 | tf_op jit(solution)/shard_map/pallas_call | solution.py:363
  (58 shorter events, 6.1 us)
Async XLA Ops:
  1.6 17.1 %collective-permute-start = (bf16[256,384]{1,0:T(8,128)(2,1)S(1)}, bf16[256,384]{1,0:T(8,128)(2,1)S(1)}, u32[]{:S(2)}, u32[]{:S(2)}) collective-permute-start(bf16[256,384]{1,0:T(8,128)(2,1)S(1)} %bitcast.36), channel_id=1, source_target_pairs={{4,0},{8,4},{12,8},{0,12},{5,1},{9,5},{13,9},{1,13},{6,2},{10,6},{... | collective-permute-start | bytes 589832 | tf_op jit(solution)/shard_map/ppermute | solution.py:379
  7.7 10.5 %collective-permute-start.3 = (bf16[16,16]{1,0:T(8,128)(2,1)S(1)}, bf16[16,16]{1,0:T(8,128)(2,1)S(1)}, u32[]{:S(2)}, u32[]{:S(2)}) collective-permute-start(bf16[16,16]{1,0:T(8,128)(2,1)S(1)} %slice_bitcast_fusion.2), channel_id=1, source_target_pairs={{4,0},{8,4},{12,8},{0,12},{5,1},{9,5},{13,9},{1,13},{6,2},{10,6},{... | collective-permute-start | bytes 1544 | tf_op jit(solution)/shard_map/ppermute | solution.py:379
  7.9 10.9 %collective-permute-start.4 = (bf16[32,8]{1,0:T(8,128)(2,1)S(1)}, bf16[32,8]{1,0:T(8,128)(2,1)S(1)}, u32[]{:S(2)}, u32[]{:S(2)}) collective-permute-start(bf16[32,8]{1,0:T(8,128)(2,1)S(1)} %bitcast.40), channel_id=1, source_target_pairs={{2,0},{0,2},{3,1},{1,3},{6,4},{4,6},{7,5},{5,7},{10,8},{8,10},{11,... | collective-permute-start | bytes 1544 | tf_op jit(solution)/shard_map/ppermute | solution.py:379
  10.0 10.1 %collective-permute-start.1 = (bf16[256,384]{1,0:T(8,128)(2,1)S(1)}, bf16[256,384]{1,0:T(8,128)(2,1)S(1)}, u32[]{:S(2)}, u32[]{:S(2)}) collective-permute-start(bf16[256,384]{1,0:T(8,128)(2,1)S(1)} %bitcast.38), channel_id=1, source_target_pairs={{2,0},{0,2},{3,1},{1,3},{6,4},{4,6},{7,5},{5,7},{10,8},{8,10},{11,... | collective-permute-start | bytes 589832 | tf_op jit(solution)/shard_map/ppermute | solution.py:379
  18.2 1.3 %collective-permute-start.5 = (bf16[16,8]{1,0:T(8,128)(2,1)S(1)}, bf16[16,8]{1,0:T(8,128)(2,1)S(1)}, u32[]{:S(2)}, u32[]{:S(2)}) collective-permute-start(bf16[16,8]{1,0:T(8,128)(2,1)S(1)} %bitcast.42), channel_id=1, source_target_pairs={{2,0},{0,2},{3,1},{1,3},{6,4},{4,6},{7,5},{5,7},{10,8},{8,10},{11,... | collective-permute-start | bytes 776 | tf_op jit(solution)/shard_map/ppermute | solution.py:379
  18.7 1.4 %collective-permute-start.2 = (bf16[128,384]{1,0:T(8,128)(2,1)S(1)}, bf16[128,384]{1,0:T(8,128)(2,1)S(1)}, u32[]{:S(2)}, u32[]{:S(2)}) collective-permute-start(bf16[128,384]{1,0:T(8,128)(2,1)S(1)} %slice_bitcast_fusion.1), channel_id=1, source_target_pairs={{2,0},{0,2},{3,1},{1,3},{6,4},{4,6},{7,5},{5,7},{10,8},{8,10},{11,... | collective-permute-start | bytes 294920 | tf_op jit(solution)/shard_map/ppermute | solution.py:379
  36.2 2.3 %collective-permute-start.9 = (bf16[768,384]{1,0:T(8,128)(2,1)}, bf16[768,384]{1,0:T(8,128)(2,1)S(1)}, u32[]{:S(2)}, u32[]{:S(2)}) collective-permute-start(bf16[768,384]{1,0:T(8,128)(2,1)} %get-tuple-element.29), channel_id=1, source_target_pairs={{0,2},{2,0},{1,3},{3,1},{4,6},{6,4},{5,7},{7,5},{8,10},{10,8},{9,1... | collective-permute-start | bytes 1769480 | tf_op jit(solution)/shard_map/ppermute | solution.py:403
  39.7 5.6 %collective-permute-start.10 = (bf16[192,384]{1,0:T(8,128)(2,1)S(1)}, bf16[192,384]{1,0:T(8,128)(2,1)S(1)}, u32[]{:S(2)}, u32[]{:S(2)}) collective-permute-start(bf16[192,384]{1,0:T(8,128)(2,1)S(1)} %get-tuple-element.33), channel_id=1, source_target_pairs={{0,4},{4,0},{8,12},{12,8},{1,5},{5,1},{9,13},{13,9},{2,6},{6,2},{1... | collective-permute-start | bytes 442376 | tf_op jit(solution)/shard_map/ppermute | solution.py:403
  41.1 4.8 %collective-permute-start.11 = (bf16[192,384]{1,0:T(8,128)(2,1)S(1)}, bf16[192,384]{1,0:T(8,128)(2,1)S(1)}, u32[]{:S(2)}, u32[]{:S(2)}) collective-permute-start(bf16[192,384]{1,0:T(8,128)(2,1)S(1)} %get-tuple-element.35), channel_id=1, source_target_pairs={{0,1},{1,0},{2,3},{3,2},{4,5},{5,4},{6,7},{7,6},{8,9},{9,8},{10,11... | collective-permute-start | bytes 442376 | tf_op jit(solution)/shard_map/ppermute | solution.py:403
  42.3 10.9 %collective-permute-start.12 = (bf16[192,384]{1,0:T(8,128)(2,1)S(1)}, bf16[192,384]{1,0:T(8,128)(2,1)S(1)}, u32[]{:S(2)}, u32[]{:S(2)}) collective-permute-start(bf16[192,384]{1,0:T(8,128)(2,1)S(1)} %get-tuple-element.34), channel_id=1, source_target_pairs={{0,5},{1,4},{4,1},{5,0},{8,13},{9,12},{12,9},{13,8},{2,7},{3,6},{6... | collective-permute-start | bytes 442376 | tf_op jit(solution)/shard_map/ppermute | solution.py:403
  42.5 28.1 %copy-start.3 = (bf16[384,384]{1,0:T(8,128)(2,1)S(1)}, bf16[384,384]{1,0:T(8,128)(2,1)}, u32[]{:S(2)}) copy-start(bf16[384,384]{1,0:T(8,128)(2,1)} %out_weight.3) | copy-start | bytes 884740
  42.5 28.1 %copy-start.4 = (s32[2]{0:T(128)S(1)}, s32[2]{0:T(128)}, u32[]{:S(2)}) copy-start(s32[2]{0:T(128)} %shift.3) | copy-start | bytes 28
  42.5 28.1 %copy-start.5 = (bf16[384,512]{1,0:T(8,128)(2,1)S(1)}, bf16[384,512]{1,0:T(8,128)(2,1)}, u32[]{:S(2)}) copy-start(bf16[384,512]{1,0:T(8,128)(2,1)} %get-tuple-element.25.context_far) | copy-start | bytes 1179652
  42.5 10.9 %collective-permute-start.6 = (bf16[256,384]{1,0:T(8,128)(2,1)S(1)}, bf16[256,384]{1,0:T(8,128)(2,1)S(1)}, u32[]{:S(2)}, u32[]{:S(2)}) collective-permute-start(bf16[256,384]{1,0:T(8,128)(2,1)S(1)} %bitcast.39), channel_id=1, source_target_pairs={{12,0},{0,4},{4,8},{8,12},{13,1},{1,5},{5,9},{9,13},{14,2},{2,6},{... | collective-permute-start | bytes 589832 | tf_op jit(solution)/shard_map/ppermute | solution.py:379
  43.9 19.9 %collective-permute-start.7 = (bf16[256,384]{1,0:T(8,128)(2,1)S(1)}, bf16[256,384]{1,0:T(8,128)(2,1)S(1)}, u32[]{:S(2)}, u32[]{:S(2)}) collective-permute-start(bf16[256,384]{1,0:T(8,128)(2,1)S(1)} %bitcast.35), channel_id=1, source_target_pairs={{2,0},{0,2},{3,1},{1,3},{6,4},{4,6},{7,5},{5,7},{10,8},{8,10},{11,... | collective-permute-start | bytes 589832 | tf_op jit(solution)/shard_map/ppermute | solution.py:379
  53.3 7.7 %collective-permute-start.13 = (bf16[192,384]{1,0:T(8,128)(2,1)S(1)}, bf16[192,384]{1,0:T(8,128)(2,1)S(1)}, u32[]{:S(2)}, u32[]{:S(2)}) collective-permute-start(bf16[192,384]{1,0:T(8,128)(2,1)S(1)} %add_convert_fusion.2), channel_id=1, source_target_pairs={{0,8},{4,12},{8,0},{12,4},{1,9},{5,13},{9,1},{13,5},{2,10},{6,14},... | collective-permute-start | bytes 442376 | tf_op jit(solution)/shard_map/ppermute | solution.py:403
  53.4 10.4 %collective-permute-start.8 = (bf16[128,384]{1,0:T(8,128)(2,1)S(1)}, bf16[128,384]{1,0:T(8,128)(2,1)S(1)}, u32[]{:S(2)}, u32[]{:S(2)}) collective-permute-start(bf16[128,384]{1,0:T(8,128)(2,1)S(1)} %slice_bitcast_fusion), channel_id=1, source_target_pairs={{2,0},{0,2},{3,1},{1,3},{6,4},{4,6},{7,5},{5,7},{10,8},{8,10},{11,... | collective-permute-start | bytes 294920 | tf_op jit(solution)/shard_map/ppermute | solution.py:379
  61.0 4.6 %collective-permute-start.14 = (bf16[192,384]{1,0:T(8,128)(2,1)S(1)}, bf16[192,384]{1,0:T(8,128)(2,1)S(1)}, u32[]{:S(2)}, u32[]{:S(2)}) collective-permute-start(bf16[192,384]{1,0:T(8,128)(2,1)S(1)} %add_convert_fusion.1.refs_0_), channel_id=1, source_target_pairs={{0,4},{4,0},{8,12},{12,8},{1,5},{5,1},{9,13},{13,9},{2,6},{6,2},{1... | collective-permute-start | bytes 442376 | tf_op jit(solution)/shard_map/ppermute | solution.py:403
  61.1 7.6 %collective-permute-start.15 = (bf16[192,384]{1,0:T(8,128)(2,1)S(1)}, bf16[192,384]{1,0:T(8,128)(2,1)S(1)}, u32[]{:S(2)}, u32[]{:S(2)}) collective-permute-start(bf16[192,384]{1,0:T(8,128)(2,1)S(1)} %add_convert_fusion.1.refs_0_), channel_id=1, source_target_pairs={{0,1},{1,0},{2,3},{3,2},{4,5},{5,4},{6,7},{7,6},{8,9},{9,8},{10,11... | collective-permute-start | bytes 442376 | tf_op jit(solution)/shard_map/ppermute | solution.py:403
  61.4 9.1 %collective-permute-start.16 = (bf16[192,384]{1,0:T(8,128)(2,1)S(1)}, bf16[192,384]{1,0:T(8,128)(2,1)S(1)}, u32[]{:S(2)}, u32[]{:S(2)}) collective-permute-start(bf16[192,384]{1,0:T(8,128)(2,1)S(1)} %add_convert_fusion.1.refs_0_), channel_id=1, source_target_pairs={{0,5},{1,4},{4,1},{5,0},{8,13},{9,12},{12,9},{13,8},{2,7},{3,6},{6... | collective-permute-start | bytes 442376 | tf_op jit(solution)/shard_map/ppermute | solution.py:403
  63.9 9.5 %collective-permute-start.17 = (bf16[192,384]{1,0:T(8,128)(2,1)S(1)}, bf16[192,384]{1,0:T(8,128)(2,1)S(1)}, u32[]{:S(2)}, u32[]{:S(2)}) collective-permute-start(bf16[192,384]{1,0:T(8,128)(2,1)S(1)} %add_convert_fusion.1.refs_0_), channel_id=1, source_target_pairs={{0,2},{2,0},{1,3},{3,1},{4,6},{6,4},{5,7},{7,5},{8,10},{10,8},{9,1... | collective-permute-start | bytes 442376 | tf_op jit(solution)/shard_map/ppermute | solution.py:403
  65.6 7.7 %collective-permute-start.18 = (bf16[192,384]{1,0:T(8,128)(2,1)S(1)}, bf16[192,384]{1,0:T(8,128)(2,1)S(1)}, u32[]{:S(2)}, u32[]{:S(2)}) collective-permute-start(bf16[192,384]{1,0:T(8,128)(2,1)S(1)} %collective-permute-done.14.refs_1_), channel_id=1, source_target_pairs={{0,2},{2,0},{1,3},{3,1},{4,6},{6,4},{5,7},{7,5},{8,10},{10,8},{9,1... | collective-permute-start | bytes 442376 | tf_op jit(solution)/shard_map/ppermute | solution.py:403
  68.7 4.7 %collective-permute-start.19 = (bf16[192,384]{1,0:T(8,128)(2,1)S(1)}, bf16[192,384]{1,0:T(8,128)(2,1)S(1)}, u32[]{:S(2)}, u32[]{:S(2)}) collective-permute-start(bf16[192,384]{1,0:T(8,128)(2,1)S(1)} %collective-permute-done.15.refs_2_), channel_id=1, source_target_pairs={{0,2},{2,0},{1,3},{3,1},{4,6},{6,4},{5,7},{7,5},{8,10},{10,8},{9,1... | collective-permute-start | bytes 442376 | tf_op jit(solution)/shard_map/ppermute | solution.py:403
  70.6 2.8 %collective-permute-start.20 = (bf16[192,384]{1,0:T(8,128)(2,1)S(1)}, bf16[192,384]{1,0:T(8,128)(2,1)S(1)}, u32[]{:S(2)}, u32[]{:S(2)}) collective-permute-start(bf16[192,384]{1,0:T(8,128)(2,1)S(1)} %collective-permute-done.16.refs_3_), channel_id=1, source_target_pairs={{0,2},{2,0},{1,3},{3,1},{4,6},{6,4},{5,7},{7,5},{8,10},{10,8},{9,1... | collective-permute-start | bytes 442376 | tf_op jit(solution)/shard_map/ppermute | solution.py:403
  (4 other events, 17.3 us)

commit v4 on v3

--- a/solution.py
+++ b/solution.py
@@ -38,9 +38,22 @@
     return lax.broadcasted_iota(jnp.int32, shape, dim)
 
 
-def prepare_kernel(strips, cot, out_weight, qkv_weight, *refs):
-    outs, (bias_blocks, d_context_t, qkv_weight_t), sems = refs[:5], refs[5:8], refs[8]
-    parts = [bias_blocks.at[k] for k in range(3)] + [d_context_t, qkv_weight_t]
+def prepare_kernel(
+    shift,
+    strips,
+    cot,
+    out_weight,
+    qkv_weight,
+    inner_flags,
+    row_flags,
+    col_flags,
+    corner_flags,
+    nothing,
+    *refs,
+):
+    outs, (bias_blocks, d_context_t, qkv_weight_t, penalty), sems = refs[:6], refs[6:10], refs[10]
+    nothing[...] = jnp.zeros_like(nothing)
+    parts = [bias_blocks.at[k] for k in range(3)] + [d_context_t, qkv_weight_t, penalty]
     copies = [pltpu.make_async_copy(part, outs[k], sems.at[k]) for k, part in enumerate(parts)]
     qkv_weight_t[...] = qkv_weight[...].T
     copies[4].start()
@@ -70,6 +83,22 @@
             ]
         if entry % 6 == 5:
             copies[head // 2].start()
+    onehots = source_onehots(shift[0], shift[1], 1)
+    on_diagonal = iota((HALF, HALF), 0) == iota((HALF, HALF), 1)
+    for t in range(2):
+        parts = (
+            flag_strip(inner_flags[t], SIDE),
+            flag_strip(row_flags[t], RIM),
+            flag_strip(col_flags[t], SIDE),
+            flag_strip(corner_flags[t], RIM, RIM),
+        )
+        marks = sum(nt(hot, strip) for hot, strip in zip(onehots, parts))
+        column = jnp.where(marks > 0.5, -1e30, 0.0)
+        wide = jnp.concatenate([column, column], 1)
+        own = jnp.where(on_diagonal, 0.0, wide)
+        penalty[t * HALF : (t + 1) * HALF, t * HALF : (t + 1) * HALF] = own
+        penalty[t * HALF : (t + 1) * HALF, (1 - t) * HALF : (2 - t) * HALF] = wide
+    copies[5].start()
     for copy in copies:
         copy.wait()
 
@@ -80,25 +109,25 @@
     col = token % SIDE + sign * col_shift
     if sign > 0:
         row_out, col_out = row >= SIDE, col >= SIDE
-        near_row, near_col = row - SIDE, col - SIDE
+        near_row, near_col, span = row - SIDE, col - SIDE, SIDE
     else:
         row_out, col_out = row < 0, col < 0
-        near_row, near_col = row + RIM, col + RIM
+        near_row, near_col, span = row + RIM, col + RIM, RIM
     inner = jnp.where(row_out | col_out, -1, row * SIDE + col)
     rows = jnp.where(row_out & ~col_out, near_row * SIDE + col, -1)
-    cols = jnp.where(col_out & ~row_out, row * RIM + near_col, -1)
+    cols = jnp.where(col_out & ~row_out, row * span + near_col, -1)
     corner = jnp.where(row_out & col_out, near_row * RIM + near_col, -1)
     return [
         (iota((HALF, count), 1) == place).astype(f32).astype(bf16)
-        for place, count in ((inner, HALF), (rows, 128), (cols, 128), (corner, 64))
+        for place, count in ((inner, HALF), (rows, 128), (cols, SIDE * span), (corner, 64))
     ]
 
 
-def flag_strip(flags, first, count, width):
-    total = count * width
-    repeat = (iota((width, total), 1) % width == iota((width, total), 0)).astype(f32).astype(bf16)
-    spread = nn(flags[first : first + count, :], repeat)
-    keep = iota((count, total), 1) // width == iota((count, total), 0)
+def flag_strip(flags, count, span=SIDE):
+    total = count * span
+    repeat = (iota((SIDE, total), 1) % span == iota((SIDE, total), 0)).astype(f32).astype(bf16)
+    spread = nn(flags[:count, :].astype(f32).astype(bf16), repeat)
+    keep = iota((count, total), 1) // span == iota((count, total), 0)
     strip = jnp.sum(jnp.where(keep, spread, 0.0), 0, keepdims=True)
     return jnp.broadcast_to(strip, (128, total)).astype(bf16)
 
@@ -160,11 +189,12 @@
 
 def main_kernel(
     shift,
-    inner,
-    halo,
-    flags,
+    core,
     gain,
-    core,
+    inner_far,
+    rows_far,
+    cols_far,
+    corner_far,
     weight_far,
     weight_t_far,
     d_context_far,
@@ -172,11 +202,18 @@
     cot_far,
     bias1_far,
     bias2_far,
+    penalty_far,
     keep_far,
     send_far,
     d_rolled_far,
     context_far,
+    lower_far,
+    right_far,
     penalty,
+    inner,
+    rows,
+    cols,
+    corner,
     qkv_weight,
     qkv_weight_t,
     d_context_t,
@@ -186,13 +223,14 @@
     d_qkv,
     grads,
     d_rolled,
+    right,
     sems,
 ):
-    sources = (
-        weight_far, weight_t_far, d_context_far, bias0_far, cot_far, bias1_far, bias2_far
-    )
-    places = [qkv_weight, qkv_weight_t, d_context_t, bias_blocks.at[0], cot]
-    places += [bias_blocks.at[1], bias_blocks.at[2]]
+    sources = (inner_far, rows_far, cols_far, corner_far, weight_far, weight_t_far)
+    sources += (d_context_far, bias0_far, cot_far, bias1_far, bias2_far, penalty_far)
+    places = [inner, rows, cols, corner, qkv_weight, qkv_weight_t]
+    places += [d_context_t, bias_blocks.at[0], cot, bias_blocks.at[1], bias_blocks.at[2]]
+    places.append(penalty)
     arrivals = [
         pltpu.make_async_copy(source, place, sems.at[k])
         for k, (source, place) in enumerate(zip(sources, places))
@@ -200,38 +238,29 @@
     for copy in arrivals:
         copy.start()
     onehots = source_onehots(shift[0], shift[1], 1)
+    for copy in arrivals[:4]:
+        copy.wait()
     rolled = []
-    on_diagonal = iota((HALF, HALF), 0) == iota((HALF, HALF), 1)
     for t in range(2):
         parts = (
             inner[t * 256 : t * 256 + 256, :],
-            halo[t * 128 : t * 128 + 128, :],
-            halo[256 + t * 128 : 384 + t * 128, :],
-            halo[512 + t * 64 : 576 + t * 64, :],
+            rows[t * 128 : t * 128 + 128, :],
+            cols[t * 256 : t * 256 + 256, :],
+            corner[t * 64 : t * 64 + 64, :],
         )
         rolled.append(sum(nn(hot, part) for hot, part in zip(onehots, parts)))
-        strips = (
-            flag_strip(flags[:32, :16], t * 16, 16, 16),
-            flag_strip(flags[32:48, :16], t * 8, 8, 16),
-            flag_strip(flags[48:80, :8], t * 16, 16, 8),
-            flag_strip(flags[80:96, :8], t * 8, 8, 8),
-        )
-        marks = sum(nt(hot, strip) for hot, strip in zip(onehots, strips))
-        column = jnp.where(marks > 0.5, -1e30, 0.0)
-        wide = jnp.concatenate([column, column], 1)
-        own = jnp.where(on_diagonal, 0.0, wide)
-        penalty[t * HALF : (t + 1) * HALF, t * HALF : (t + 1) * HALF] = own
-        penalty[t * HALF : (t + 1) * HALF, (1 - t) * HALF : (2 - t) * HALF] = wide
     xhat, inv_std = layer_norm(jnp.concatenate(rolled, 0))
-    normed = (xhat * gain[...]).astype(bf16)
+    gain_row = gain[...].reshape(1, MODEL_WIDTH)
+    normed = (xhat * gain_row).astype(bf16)
     normed_t = normed.T
-    arrivals[0].wait()
+    arrivals[4].wait()
     kv = nn(normed, qkv_weight[:, MODEL_WIDTH:]).astype(bf16)
-    arrivals[1].wait()
+    arrivals[5].wait()
     qkv_t = nt(qkv_weight_t[...], normed).astype(bf16)
-    arrivals[2].wait()
+    arrivals[6].wait()
+    arrivals[11].wait()
     for pair in range(HEADS // 2):
-        arrivals[(3, 5, 6)[pair]].wait()
+        arrivals[(7, 9, 10)[pair]].wait()
         heads = [
             attention_head(2 * pair + side, qkv_t, kv, penalty, bias_blocks.at[pair], d_context_t)
             for side in range(2)
@@ -244,29 +273,38 @@
             d_qkv[:, first : first + 128] = d_pair[:, kind * 128 : kind * 128 + 128]
         first = pair * TOKENS
         if pair == 0:
-            arrivals[4].wait()
+            arrivals[8].wait()
         grads[first : first + 128, :] = nn(context, cot[...]).astype(bf16)
         grads[first + 128 : first + TOKENS, :] = nn(normed_t, d_pair).astype(bf16)
         for block in (2 * pair, 2 * pair + 1):
             to_half(grads, block, core[0], keep_far, send_far, sems)
     keep_context = pltpu.make_async_copy(context_t, context_far, sems.at[0])
     keep_context.start()
-    d_xhat = nt(d_qkv[...], qkv_weight[...]) * gain[...]
-    d_rolled[...] = (
-        inv_std
-        * (
-            d_xhat
-            - jnp.mean(d_xhat, -1, keepdims=True)
-            - xhat * jnp.mean(d_xhat * xhat, -1, keepdims=True)
-        )
-    ).astype(bf16)
-    keep = pltpu.make_async_copy(d_rolled, d_rolled_far, sems.at[1])
-    keep.start()
+    d_xhat = nt(d_qkv[...], qkv_weight[...]) * gain_row
+    d_tokens = inv_std * (
+        d_xhat
+        - jnp.mean(d_xhat, -1, keepdims=True)
+        - xhat * jnp.mean(d_xhat * xhat, -1, keepdims=True)
+    )
+    d_rolled[...] = d_tokens.astype(bf16)
+    last_columns = d_tokens.reshape(2 * SIDE, SIDE, MODEL_WIDTH)[:, RIM:, :]
+    right[...] = last_columns.reshape(HALF, MODEL_WIDTH).astype(bf16)
+    copies = [
+        pltpu.make_async_copy(d_rolled, d_rolled_far, sems.at[1]),
+        pltpu.make_async_copy(right, right_far, sems.at[2]),
+    ]
+    for t in range(2):
+        source = d_rolled.at[pl.ds(t * HALF + 128, 128), :]
+        target = lower_far.at[pl.ds(t * 128, 128), :]
+        copies.append(pltpu.make_async_copy(source, target, sems.at[3 + t]))
+    for copy in copies:
+        copy.start()
     for block in range(6):
         source, target = half_block(grads, block, keep_far)
-        pltpu.make_async_copy(source, target, sems.at[7 + block]).wait()
+        pltpu.make_async_copy(source, target, sems.at[12 + block]).wait()
     keep_context.wait()
-    keep.wait()
+    for copy in copies:
+        copy.wait()
 
 
 def half_block(grads, block, half):
@@ -280,7 +318,7 @@
         @pl.when(core == side)
         def _():
             source, target = half_block(grads, block, half)
-            pltpu.make_async_copy(source, target, sems.at[7 + block]).start()
+            pltpu.make_async_copy(source, target, sems.at[12 + block]).start()
 
 
 def place_kernel(
@@ -291,10 +329,12 @@
     context_far,
     field_grad,
     update,
+    nothing,
     kept,
     context_t,
     sems,
 ):
+    nothing[...] = jnp.zeros_like(nothing)
     copies = [
         pltpu.make_async_copy(kept_far, kept, sems.at[0]),
         pltpu.make_async_copy(context_far, context_t, sems.at[1]),
@@ -348,7 +388,8 @@
         out_grad[pair * 128 : pair * 128 + 128, :] = whole[pair * TOKENS : pair * TOKENS + 128]
     copies.append(pltpu.make_async_copy(out_grad, out_far, sems.at[3]))
     copies[-1].start()
-    gain_grad[...] = (jnp.sum(partial.T, 0, keepdims=True) / gain[...]).reshape(MODEL_WIDTH)
+    gain_row = gain[...].reshape(1, MODEL_WIDTH)
+    gain_grad[...] = (jnp.sum(partial.T, 0, keepdims=True) / gain_row).reshape(MODEL_WIDTH)
     for copy in copies:
         copy.wait()
 
@@ -363,7 +404,8 @@
     return pl.pallas_call(
         kernel,
         out_shape=[jax.ShapeDtypeStruct(shape, dtype) for shape, dtype in shapes],
-        in_specs=[smem if array.dtype == jnp.int32 else vmem for array in near] + [far] * far_in,
+        in_specs=[smem if array.dtype == jnp.int32 and array.ndim == 1 else vmem for array in near]
+        + [far] * far_in,
         out_specs=[vmem] * (len(shapes) - far_out) + [far] * far_out,
         scratch_shapes=[pltpu.VMEM(shape, dtype) for shape, dtype in scratch]
         + [pltpu.SemaphoreType.DMA((copies,))],
@@ -377,6 +419,16 @@
 def passed_along(block, axis, distance):
     count = lax.axis_size(axis)
     return lax.ppermute(block, axis, [((i - distance) % count, i) for i in range(count)])
+
+
+def passed_across(block, axis, other, distance):
+    count, width = lax.axis_size(axis), lax.axis_size(other)
+    route = [
+        (((i - distance) % count) * width + (j - distance) % width, i * width + j)
+        for i in range(count)
+        for j in range(width)
+    ]
+    return lax.ppermute(block, (axis, other), route)
 
 
 CORE = ("sx", 1)
@@ -407,8 +459,7 @@
     return sum(piece.astype(f32) for piece in pieces).astype(bf16)
 
 
-def sum_quarter(keep, send):
-    block = add_up(keep, swapped(send, CORE))
+def sum_quarter(block):
     share = block.shape[0] // 4
     mine = quarter_index()
     pick = lambda place: lax.dynamic_slice_in_dim(block, place * share, share, 0)
@@ -416,14 +467,14 @@
     return add_up(pick(mine), *arrived)
 
 
-def sum_rest(quarter):
+def sum_rest(quarter, zero):
     rest = [
         (axis, 1 << k)
         for axis in ("ta", "sy")
         for k in range(1, lax.axis_size(axis).bit_length() - 1)
     ]
     for bit in rest:
-        quarter = add_up(quarter, swapped(quarter, bit))
+        quarter = add_up(quarter, swapped(quarter, bit), zero)
     return quarter
 
 
@@ -443,52 +494,57 @@
 ):
     width = MODEL_WIDTH
     wide = lambda tokens: ((tokens, width), bf16)
-    first_rows = state_field[:, :RIM].reshape(-1, width)
-    rows = passed_along(first_rows, "sy", -1)
-    marks = outlier_flags.astype(bf16) + first_rows[0, 0] * 0
-    row_marks = passed_along(marks[:, :RIM].reshape(2 * RIM, SIDE), "sy", -1)
-    cols = passed_along(state_field[:, :, :RIM].reshape(-1, width), "sx", -1)
-    col_marks = passed_along(marks[:, :, :RIM].reshape(2 * SIDE, RIM), "sx", -1)
+    rows = passed_along(state_field[:, :RIM].reshape(-1, width), "sy", -1)
+    row_flags = passed_along(outlier_flags, "sy", -1)
+    cols = passed_along(state_field, "sx", -1)
+    col_flags = passed_along(outlier_flags, "sx", -1)
+    corner_flags = passed_across(outlier_flags, "sy", "sx", -1)
     strips = jnp.pad(
         position_bias.reshape(HEADS, 3, 31, 31), ((0, 0), (0, 0), (0, 1), (0, 1))
     )
     strips = strips.reshape(HEADS, 3, 16, 2, 32).transpose(0, 1, 3, 2, 4).reshape(36, TOKENS)
     cot_rows = cotangent.reshape(TOKENS, width)
     pair_bias = ((6, HALF, HALF), f32)
-    *bias_blocks, d_context_t, qkv_weight_t = local_call(
+    nothing, *bias_blocks, d_context_t, qkv_weight_t, penalty = local_call(
         prepare_kernel,
-        [pair_bias] * 3 + [((width, TOKENS), bf16), wide(3 * width)],
-        [strips, cot_rows, out_weight, qkv_weight],
-        far_out=5,
-        scratch=[((3, 6, HALF, HALF), f32), ((width, TOKENS), bf16), wide(3 * width)],
-        copies=5,
-        micros=3,
-        limit=60,
-    )
-    corner = passed_along(
-        rows.reshape(2 * RIM, SIDE, width)[:, :RIM].reshape(-1, width), "sx", -1
-    )
-    corner_marks = passed_along(row_marks[:, :RIM], "sx", -1)
-    halo = jnp.concatenate([rows, cols, corner], 0)
-    all_marks = jnp.concatenate(
-        [
-            jnp.pad(m, ((0, 0), (0, 128 - m.shape[1])))
-            for m in (marks.reshape(2 * SIDE, SIDE), row_marks, col_marks, corner_marks)
-        ],
-        0,
-    )
-    gain = layer_norm_gain.reshape(1, width)
-    core = index_bit(*CORE).astype(jnp.int32).reshape(1)
-    keep, send, d_rolled, context_t = local_call(
-        main_kernel,
-        [wide(2 * width)] * 2 + [wide(TOKENS), ((width, TOKENS), bf16)],
+        [((16, 128), bf16)] + [pair_bias] * 3 + [((width, TOKENS), bf16), wide(3 * width), ((TOKENS, TOKENS), f32)],
         [
             window_shift,
+            strips,
+            cot_rows,
+            out_weight,
+            qkv_weight,
+            outlier_flags,
+            row_flags,
+            col_flags,
+            corner_flags,
+        ],
+        far_out=6,
+        scratch=[
+            ((3, 6, HALF, HALF), f32),
+            ((width, TOKENS), bf16),
+            wide(3 * width),
+            ((TOKENS, TOKENS), f32),
+        ],
+        copies=6,
+        micros=3,
+        limit=62,
+    )
+    corner_message = rows.reshape(2 * RIM, SIDE, width)[:, :RIM] + nothing[0, 0]
+    corner = passed_along(corner_message.reshape(-1, width), "sx", -1)
+    core = index_bit(*CORE).astype(jnp.int32).reshape(1)
+    keep, send, d_rolled, context_t, lower, right = local_call(
+        main_kernel,
+        [wide(2 * width)] * 2
+        + [wide(TOKENS), ((width, TOKENS), bf16), wide(HALF), wide(HALF)],
+        [
+            window_shift,
+            core,
+            layer_norm_gain,
             state_field.reshape(TOKENS, width),
-            halo,
-            all_marks,
-            gain,
-            core,
+            rows,
+            cols.reshape(TOKENS, width),
+            corner,
             qkv_weight,
             qkv_weight_t,
             d_context_t,
@@ -496,11 +552,16 @@
             cot_rows,
             bias_blocks[1],
             bias_blocks[2],
+            penalty,
         ],
-        far_in=7,
-        far_out=4,
+        far_in=12,
+        far_out=6,
         scratch=[
             ((TOKENS, TOKENS), f32),
+            wide(TOKENS),
+            wide(HALF),
+            wide(TOKENS),
+            wide(128),
             ((width, 3 * width), bf16),
             wide(3 * width),
             ((width, TOKENS), bf16),
@@ -510,21 +571,21 @@
             ((TOKENS, 3 * width), bf16),
             wide(3 * TOKENS),
             wide(TOKENS),
+            wide(HALF),
         ],
-        copies=13,
+        copies=18,
         micros=12,
-        limit=60,
-    )
-    grid = d_rolled.reshape(2, SIDE, SIDE, width)
-    below = passed_along(grid[:, RIM:].reshape(-1, width), "sy", 1)
-    beside = passed_along(grid[:, :, RIM:].reshape(-1, width), "sx", 1)
-    across = passed_along(
-        below.reshape(2 * RIM, SIDE, width)[:, RIM:].reshape(-1, width), "sx", 1
-    )
-    quarter = sum_quarter(keep, send)
-    field_grad, update = local_call(
+        limit=62,
+    )
+    below = passed_along(lower, "sy", 1)
+    beside = passed_along(right, "sx", 1)
+    block = add_up(keep, swapped(send, CORE))
+    across = below.reshape(2 * RIM, SIDE, width)[:, RIM:] + block[0, 0] * 0
+    across = passed_along(across.reshape(-1, width), "sx", 1)
+    quarter = sum_quarter(block)
+    field_grad, update, nothing = local_call(
         place_kernel,
-        [wide(TOKENS), wide(TOKENS)],
+        [wide(TOKENS), wide(TOKENS), ((16, 128), bf16)],
         [
             window_shift,
             jnp.concatenate([below, beside, across], 0),
@@ -537,13 +598,13 @@
         copies=2,
         micros=2,
     )
-    quarter = sum_rest(quarter)
+    quarter = sum_rest(quarter, nothing[0, 0])
     quarters = [quarter] + [swapped(quarter, *group) for group in GROUPS]
     others = [swapped(piece, CORE) for piece in quarters]
     tiles = lax.axis_size("sy") * lax.axis_size("sx") * lax.axis_size("ta")
     place = jnp.stack([index_bit(*CORE), quarter_index()]).astype(jnp.int32)
     gain_grad, qkv_grad, out_grad = finish_call(
-        1.0 / tiles, [place, *quarters, *others, qkv_weight, gain]
+        1.0 / tiles, [place, *quarters, *others, qkv_weight, layer_norm_gain]
     )
     shape = state_field.shape
     return (

time: 77.3 us -> 80.1 us (1.036)
  waiting for transfers between devices: 16.9 us -> 19.2 us
  Pallas kernels: 26.3 us -> 27.9 us
  other arithmetic: 3.64 us -> 2.14 us
  local copies, waits for them, and re-layouts: 5.14 us -> 6.6 us
  starting transfers between devices: 22.8 us -> 21.4 us
    ppermute x9 -> x8, waiting for transfers between devices: 0.74 us -> 5.09 us  [passed_along(): lax.ppermute(block, axis, [((i - distance) % count, i) for i in range(cou...]
    ppermute x12, waiting for transfers between devices: 16.2 us -> 14.1 us  [swapped(): return lax.ppermute(block, axes, route)]
    pallas_call x4, Pallas kernels: 26.3 us -> 27.9 us  [local_call(): pl.pallas_call(kernel, out_shape=[jax.ShapeDtypeStruct(shape, dtype) for...]
    concatenate x2 -> x0, other arithmetic: 1.46 us -> none  [the longest x1 0.85 us: shards(): halo = jnp.concatenate([rows, cols, corner], 0)]
    unnamed x14 -> x24, local copies, waits for them, and re-layouts: 0.03 us -> 1.4 us
    ppermute x9 -> x8, starting transfers between devices: 10.3 us -> 9.03 us  [passed_along(): lax.ppermute(block, axis, [((i - distance) % count, i) for i in range(cou...]
    slice x5 -> x4, local copies, waits for them, and re-layouts: 2.45 us -> 3.15 us  [the longest x1 1.18 us: shards(): corner_message = rows.reshape(2 * RIM, SIDE, width)[:, :RIM] + nothing[0, 0]]
  transfers between devices with their start and end apart: 21 -> 21, of which waited for: 5 -> 10; matrix products, arithmetic and copies ran while one was open for 7% -> 9% of each run, Pallas kernels for 11% -> 11%
where the time goes in v4:
time: 80.1 us; the launch traced here: 79.6 us
  Pallas kernels  27.9 us (35%)
  starting transfers between devices  21.4 us (27%)
  waiting for transfers between devices  19.2 us (24%)
  local copies, waits for them, and re-layouts  6.6 us (8%)
  between operations  2.32 us (3%)
  other arithmetic  2.14 us (3%)
    pallas_call x4, Pallas kernels, local_call(): pl.pallas_call(kernel, out_shape=[jax.ShapeDtypeStruct(shape, dtype) for...  27.9 us
    ppermute x12, waiting for transfers between devices, swapped(): return lax.ppermute(block, axes, route)  14.1 us
    ppermute x12, starting transfers between devices, swapped(): return lax.ppermute(block, axes, route)  12.3 us
    ppermute x8, starting transfers between devices, passed_along(): lax.ppermute(block, axis, [((i - distance) % count, i) for i in range(cou...  9.03 us
    ppermute x8, waiting for transfers between devices, passed_along(): lax.ppermute(block, axis, [((i - distance) % count, i) for i in range(cou...  5.09 us
  transfers between devices with their start and end apart: 21, of which 10 were waited for; matrix products, arithmetic and copies ran while one was open for 9% of the time, Pallas kernels for 11%

profile of v4, /device:TPU:1, one launch (start us, length us, event | category | flops | bytes accessed | tf_op | source)
XLA Modules:
  0.0 79.6 jit_solution(14528863390841960969)
XLA Ops:
  0.6 4.2 %collective-permute-start.2 = (s32[2,16,16]{2,1,0:T(8,128)}, s32[2,16,16]{2,1,0:T(8,128)S(1)}, u32[]{:S(2)}, u32[]{:S(2)}) collective-permute-start(s32[2,16,16]{2,1,0:T(8,128)} %inner_flags.1), channel_id=1, source_target_pairs={{4,0},{8,4},{12,8},{0,12},{5,1},{9,5},{13,9},{1,13},{6,2},{10,6},{... | collective-permute-start | bytes 6152 | tf_op jit(solution)/shard_map/ppermute | solution.py:421
  4.8 1.0 %collective-permute-start.3 = (s32[2,16,16]{2,1,0:T(8,128)}, s32[2,16,16]{2,1,0:T(8,128)S(1)}, u32[]{:S(2)}, u32[]{:S(2)}) collective-permute-start(s32[2,16,16]{2,1,0:T(8,128)} %inner_flags.1), channel_id=1, source_target_pairs={{2,0},{0,2},{3,1},{1,3},{6,4},{4,6},{7,5},{5,7},{10,8},{8,10},{11,... | collective-permute-start | bytes 6152 | tf_op jit(solution)/shard_map/ppermute | solution.py:421
  6.4 0.9 %slice.18 = bf16[2,8,16,384]{3,2,1,0:T(8,128)(2,1)S(1)} slice(bf16[2,16,16,384]{3,2,1,0:T(8,128)(2,1)} %param.8), slice={[0:2], [0:8], [0:16], [0:384]} | slice | bytes 393216 | tf_op jit(solution)/shard_map/slice | solution.py:497
  7.5 1.2 %reshape.61 = f32[6,3,31,31]{3,2,1,0:T(8,128)S(1)} reshape(f32[6,2883]{1,0:T(8,128)} %param.14) | data formatting | bytes 138384 | tf_op jit(solution)/shard_map/reshape | solution.py:503
  10.2 6.4 %shard_map.119 = (bf16[16,128]{1,0:T(8,128)(2,1)}, f32[6,256,256]{2,1,0:T(8,128)}, f32[6,256,256]{2,1,0:T(8,128)}, f32[6,256,256]{2,1,0:T(8,128)}, bf16[384,512]...) custom-call(s32[2]{0:T(128)} %shift.5, f32[36,512]{1,0:T(8,128)} %reshape.63.strips, ...), custom_call_target="tpu_custom_call" | custom-call | flops 3000000000 | bytes 1000000 | tf_op jit(solution)/shard_map/pallas_call | solution.py:404
  16.6 1.2 %slice.20 = bf16[1,1]{1,0:T(2,128)(2,1)} slice(bf16[16,128]{1,0:T(8,128)(2,1)} %get-tuple-element.24), slice={[0:1], [0:1]} | slice | bytes 4 | tf_op jit(solution)/shard_map/slice | solution.py:533
  18.8 1.0 %collective-permute-done.5.corner_far = bf16[128,384]{1,0:T(8,128)(2,1)S(1)} collective-permute-done((bf16[128,384]{1,0:T(8,128)(2,1)S(1)}, bf16[128,384]{1,0:T(8,128)(2,1)S(1)}, u32[]{:S(2)}, u32[]{:S(2)}) %collective-permute-start.5) | collective-permute-done | bytes 98336 | tf_op jit(solution)/shard_map/ppermute | solution.py:421
  20.6 15.9 %shard_map.120 = (bf16[768,384]{1,0:T(8,128)(2,1)}, bf16[768,384]{1,0:T(8,128)(2,1)}, bf16[512,384]{1,0:T(8,128)(2,1)}, bf16[384,512]{1,0:T(8,128)(2,1)}, bf16[2...) custom-call(s32[2]{0:T(128)} %shift.5, s32[1]{0:T(128)} %bitcast.core, f32[384]{0:T(512)} %refs_9_.1, ...), custom_call_target="tpu_custom_call" | custom-call | flops 12000000000 | bytes 1000000 | tf_op jit(solution)/shard_map/pallas_call | solution.py:404
  36.9 1.3 %collective-permute-start.6 = (bf16[256,384]{1,0:T(8,128)(2,1)}, bf16[256,384]{1,0:T(8,128)(2,1)S(1)}, u32[]{:S(2)}, u32[]{:S(2)}) collective-permute-start(bf16[256,384]{1,0:T(8,128)(2,1)} %get-tuple-element.31), channel_id=1, source_target_pairs={{12,0},{0,4},{4,8},{8,12},{13,1},{1,5},{5,9},{9,13},{14,2},{2,6},{... | collective-permute-start | bytes 589832 | tf_op jit(solution)/shard_map/ppermute | solution.py:421
  38.8 1.2 %add_convert_fusion = bf16[768,384]{1,0:T(8,128)(2,1)S(1)} fusion(bf16[768,384]{1,0:T(8,128)(2,1)S(1)} %collective-permute-done.8, bf16[768,384]{1,0:T(8,128)(2,1)} %get-tuple-element.33), kind=kLoop, calls=%fused_computation | loop fusion | flops 1179648 | bytes 1769472 | tf_op jit(solution)/shard_map/convert_element_type | solution.py:459
  41.2 4.1 %collective-permute-done.6 = bf16[256,384]{1,0:T(8,128)(2,1)S(1)} collective-permute-done((bf16[256,384]{1,0:T(8,128)(2,1)}, bf16[256,384]{1,0:T(8,128)(2,1)S(1)}, u32[]{:S(2)}, u32[]{:S(2)}) %collective-permute-start.6) | collective-permute-done | bytes 196640 | tf_op jit(solution)/shard_map/ppermute | solution.py:421
  45.3 1.0 %collective-permute-start.9 = (bf16[128,384]{1,0:T(8,128)(2,1)S(1)}, bf16[128,384]{1,0:T(8,128)(2,1)S(1)}, u32[]{:S(2)}, u32[]{:S(2)}) collective-permute-start(bf16[128,384]{1,0:T(8,128)(2,1)S(1)} %fusion), channel_id=1, source_target_pairs={{2,0},{0,2},{3,1},{1,3},{6,4},{4,6},{7,5},{5,7},{10,8},{8,10},{11,... | collective-permute-start | bytes 294920 | tf_op jit(solution)/shard_map/ppermute | solution.py:421
  46.5 1.3 %collective-permute-start.11 = (bf16[192,384]{1,0:T(8,128)(2,1)S(1)}, bf16[192,384]{1,0:T(8,128)(2,1)S(1)}, u32[]{:S(2)}, u32[]{:S(2)}) collective-permute-start(bf16[192,384]{1,0:T(8,128)(2,1)S(1)} %get-tuple-element.45), channel_id=1, source_target_pairs={{0,1},{1,0},{2,3},{3,2},{4,5},{5,4},{6,7},{7,6},{8,9},{9,8},{10,11... | collective-permute-start | bytes 442376 | tf_op jit(solution)/shard_map/ppermute | solution.py:455
  47.8 1.4 %collective-permute-start.12 = (bf16[192,384]{1,0:T(8,128)(2,1)S(1)}, bf16[192,384]{1,0:T(8,128)(2,1)S(1)}, u32[]{:S(2)}, u32[]{:S(2)}) collective-permute-start(bf16[192,384]{1,0:T(8,128)(2,1)S(1)} %get-tuple-element.44), channel_id=1, source_target_pairs={{0,5},{1,4},{4,1},{5,0},{8,13},{9,12},{12,9},{13,8},{2,7},{3,6},{6... | collective-permute-start | bytes 442376 | tf_op jit(solution)/shard_map/ppermute | solution.py:455
  49.2 2.7 %collective-permute-done.10 = bf16[192,384]{1,0:T(8,128)(2,1)S(1)} collective-permute-done((bf16[192,384]{1,0:T(8,128)(2,1)S(1)}, bf16[192,384]{1,0:T(8,128)(2,1)S(1)}, u32[]{:S(2)}, u32[]{:S(2)}) %collective-permute-start.10) | collective-permute-done | bytes 147488 | tf_op jit(solution)/shard_map/ppermute | solution.py:455
  52.0 4.0 %collective-permute-done.12 = bf16[192,384]{1,0:T(8,128)(2,1)S(1)} collective-permute-done((bf16[192,384]{1,0:T(8,128)(2,1)S(1)}, bf16[192,384]{1,0:T(8,128)(2,1)S(1)}, u32[]{:S(2)}, u32[]{:S(2)}) %collective-permute-start.12) | collective-permute-done | bytes 147488 | tf_op jit(solution)/shard_map/ppermute | solution.py:455
  56.7 2.7 %shard_map.121 = (bf16[512,384]{1,0:T(8,128)(2,1)}, bf16[512,384]{1,0:T(8,128)(2,1)}, bf16[16,128]{1,0:T(8,128)(2,1)S(1)}) custom-call(s32[2]{0:T(128)S(1)} %copy-done.3, bf16[640,384]{1,0:T(8,128)(2,1)S(1)} %pad_maximum_fusion.halo, bf16[384,384]{1,0:T(8,128)(2,1)S(1)} %copy-done.1, bf16[512,384]{1,0:T(8,128)(2,1)S(1)} %copy-done.4, ...), custom_call_target="tpu_custom_call" | custom-call | flops 2000000000 | bytes 1000000 | tf_op jit(solution)/shard_map/pallas_call | solution.py:404
  60.6 5.0 %collective-permute-done.13 = bf16[192,384]{1,0:T(8,128)(2,1)S(1)} collective-permute-done((bf16[192,384]{1,0:T(8,128)(2,1)S(1)}, bf16[192,384]{1,0:T(8,128)(2,1)S(1)}, u32[]{:S(2)}, u32[]{:S(2)}) %collective-permute-start.13) | collective-permute-done | bytes 147488 | tf_op jit(solution)/shard_map/ppermute | solution.py:455
  65.8 2.6 %collective-permute-start.16 = (bf16[192,384]{1,0:T(8,128)(2,1)S(1)}, bf16[192,384]{1,0:T(8,128)(2,1)S(1)}, u32[]{:S(2)}, u32[]{:S(2)}) collective-permute-start(bf16[192,384]{1,0:T(8,128)(2,1)S(1)} %add_convert_fusion.1.refs_0_), channel_id=1, source_target_pairs={{0,5},{1,4},{4,1},{5,0},{8,13},{9,12},{12,9},{13,8},{2,7},{3,6},{6... | collective-permute-start | bytes 442376 | tf_op jit(solution)/shard_map/ppermute | solution.py:455
  68.3 1.3 %collective-permute-start.17 = (bf16[192,384]{1,0:T(8,128)(2,1)S(1)}, bf16[192,384]{1,0:T(8,128)(2,1)S(1)}, u32[]{:S(2)}, u32[]{:S(2)}) collective-permute-start(bf16[192,384]{1,0:T(8,128)(2,1)S(1)} %add_convert_fusion.1.refs_0_), channel_id=1, source_target_pairs={{0,2},{2,0},{1,3},{3,1},{4,6},{6,4},{5,7},{7,5},{8,10},{10,8},{9,1... | collective-permute-start | bytes 442376 | tf_op jit(solution)/shard_map/ppermute | solution.py:455
  70.6 2.3 %collective-permute-start.18 = (bf16[192,384]{1,0:T(8,128)(2,1)S(1)}, bf16[192,384]{1,0:T(8,128)(2,1)S(1)}, u32[]{:S(2)}, u32[]{:S(2)}) collective-permute-start(bf16[192,384]{1,0:T(8,128)(2,1)S(1)} %collective-permute-done.14.refs_1_), channel_id=1, source_target_pairs={{0,2},{2,0},{1,3},{3,1},{4,6},{6,4},{5,7},{7,5},{8,10},{10,8},{9,1... | collective-permute-start | bytes 442376 | tf_op jit(solution)/shard_map/ppermute | solution.py:455
  72.9 2.3 %collective-permute-start.19 = (bf16[192,384]{1,0:T(8,128)(2,1)S(1)}, bf16[192,384]{1,0:T(8,128)(2,1)S(1)}, u32[]{:S(2)}, u32[]{:S(2)}) collective-permute-start(bf16[192,384]{1,0:T(8,128)(2,1)S(1)} %collective-permute-done.15.refs_2_), channel_id=1, source_target_pairs={{0,2},{2,0},{1,3},{3,1},{4,6},{6,4},{5,7},{7,5},{8,10},{10,8},{9,1... | collective-permute-start | bytes 442376 | tf_op jit(solution)/shard_map/ppermute | solution.py:455
  75.3 0.9 %collective-permute-done.19.refs_6_ = bf16[192,384]{1,0:T(8,128)(2,1)S(1)} collective-permute-done((bf16[192,384]{1,0:T(8,128)(2,1)S(1)}, bf16[192,384]{1,0:T(8,128)(2,1)S(1)}, u32[]{:S(2)}, u32[]{:S(2)}) %collective-permute-start.19) | collective-permute-done | bytes 147488 | tf_op jit(solution)/shard_map/ppermute | solution.py:455
  76.6 2.9 %shard_map.122 = (f32[384]{0:T(512)}, f32[384,1152]{1,0:T(8,128)}, f32[384,384]{1,0:T(8,128)}) custom-call(s32[2]{0:T(128)S(1)} %pad_add_fusion.place, bf16[192,384]{1,0:T(8,128)(2,1)S(1)} %add_convert_fusion.1.refs_0_, bf16[192,384]{1,0:T(8,128)(2,1)S(1)} %collective-permute-done.14.refs_1_, bf16[192,384]{1,0:T(8,128)(2,1)S(1)} %collective-permute-done.15.refs_2_, ...), custom_call_target="tpu_custom_call" | custom-call | flops 1000000000 | bytes 1000000 | tf_op jit(solution)/shard_map/pallas_call | solution.py:404
  (62 shorter events, 8.5 us)
Async XLA Ops:
  0.6 8.9 %collective-permute-start.2 = (s32[2,16,16]{2,1,0:T(8,128)}, s32[2,16,16]{2,1,0:T(8,128)S(1)}, u32[]{:S(2)}, u32[]{:S(2)}) collective-permute-start(s32[2,16,16]{2,1,0:T(8,128)} %inner_flags.1), channel_id=1, source_target_pairs={{4,0},{8,4},{12,8},{0,12},{5,1},{9,5},{13,9},{1,13},{6,2},{10,6},{... | collective-permute-start | bytes 6152 | tf_op jit(solution)/shard_map/ppermute | solution.py:421
  4.8 4.7 %collective-permute-start.3 = (s32[2,16,16]{2,1,0:T(8,128)}, s32[2,16,16]{2,1,0:T(8,128)S(1)}, u32[]{:S(2)}, u32[]{:S(2)}) collective-permute-start(s32[2,16,16]{2,1,0:T(8,128)} %inner_flags.1), channel_id=1, source_target_pairs={{2,0},{0,2},{3,1},{1,3},{6,4},{4,6},{7,5},{5,7},{10,8},{8,10},{11,... | collective-permute-start | bytes 6152 | tf_op jit(solution)/shard_map/ppermute | solution.py:421
  5.8 3.8 %collective-permute-start.4 = (s32[2,16,16]{2,1,0:T(8,128)}, s32[2,16,16]{2,1,0:T(8,128)S(1)}, u32[]{:S(2)}, u32[]{:S(2)}) collective-permute-start(s32[2,16,16]{2,1,0:T(8,128)} %inner_flags.1), channel_id=1, source_target_pairs={{6,0},{4,2},{10,4},{8,6},{14,8},{12,10},{2,12},{0,14},{7,1},{5,3},... | collective-permute-start | bytes 6152 | tf_op jit(solution)/shard_map/ppermute | solution.py:431
  5.8 14.0 %collective-permute-start.1 = (bf16[2,16,16,384]{3,2,1,0:T(8,128)(2,1)}, bf16[2,16,16,384]{3,2,1,0:T(8,128)(2,1)S(1)}, u32[]{:S(2)}, u32[]{:S(2)}) collective-permute-start(bf16[2,16,16,384]{3,2,1,0:T(8,128)(2,1)} %param.8), channel_id=1, source_target_pairs={{2,0},{0,2},{3,1},{1,3},{6,4},{4,6},{7,5},{5,7},{10,8},{8,10},{11,... | collective-permute-start | bytes 1179656 | tf_op jit(solution)/shard_map/ppermute | solution.py:421
  7.3 10.5 %collective-permute-start = (bf16[256,384]{1,0:T(8,128)(2,1)S(1)}, bf16[256,384]{1,0:T(8,128)(2,1)S(1)}, u32[]{:S(2)}, u32[]{:S(2)}) collective-permute-start(bf16[256,384]{1,0:T(8,128)(2,1)S(1)} %bitcast.25), channel_id=1, source_target_pairs={{4,0},{8,4},{12,8},{0,12},{5,1},{9,5},{13,9},{1,13},{6,2},{10,6},{... | collective-permute-start | bytes 589832 | tf_op jit(solution)/shard_map/ppermute | solution.py:421
  18.5 1.4 %collective-permute-start.5 = (bf16[128,384]{1,0:T(8,128)(2,1)S(1)}, bf16[128,384]{1,0:T(8,128)(2,1)S(1)}, u32[]{:S(2)}, u32[]{:S(2)}) collective-permute-start(bf16[128,384]{1,0:T(8,128)(2,1)S(1)} %fusion.1), channel_id=1, source_target_pairs={{2,0},{0,2},{3,1},{1,3},{6,4},{4,6},{7,5},{5,7},{10,8},{8,10},{11,... | collective-permute-start | bytes 294920 | tf_op jit(solution)/shard_map/ppermute | solution.py:421
  36.5 2.3 %collective-permute-start.8 = (bf16[768,384]{1,0:T(8,128)(2,1)}, bf16[768,384]{1,0:T(8,128)(2,1)S(1)}, u32[]{:S(2)}, u32[]{:S(2)}) collective-permute-start(bf16[768,384]{1,0:T(8,128)(2,1)} %get-tuple-element.34), channel_id=1, source_target_pairs={{0,2},{2,0},{1,3},{3,1},{4,6},{6,4},{5,7},{7,5},{8,10},{10,8},{9,1... | collective-permute-start | bytes 1769480 | tf_op jit(solution)/shard_map/ppermute | solution.py:455
  36.9 8.4 %collective-permute-start.6 = (bf16[256,384]{1,0:T(8,128)(2,1)}, bf16[256,384]{1,0:T(8,128)(2,1)S(1)}, u32[]{:S(2)}, u32[]{:S(2)}) collective-permute-start(bf16[256,384]{1,0:T(8,128)(2,1)} %get-tuple-element.31), channel_id=1, source_target_pairs={{12,0},{0,4},{4,8},{8,12},{13,1},{1,5},{5,9},{9,13},{14,2},{2,6},{... | collective-permute-start | bytes 589832 | tf_op jit(solution)/shard_map/ppermute | solution.py:421
  38.2 10.9 %collective-permute-start.7 = (bf16[256,384]{1,0:T(8,128)(2,1)}, bf16[256,384]{1,0:T(8,128)(2,1)S(1)}, u32[]{:S(2)}, u32[]{:S(2)}) collective-permute-start(bf16[256,384]{1,0:T(8,128)(2,1)} %get-tuple-element.32), channel_id=1, source_target_pairs={{2,0},{0,2},{3,1},{1,3},{6,4},{4,6},{7,5},{5,7},{10,8},{8,10},{11,... | collective-permute-start | bytes 589832 | tf_op jit(solution)/shard_map/ppermute | solution.py:421
  40.0 16.6 %copy-start.1 = (bf16[384,384]{1,0:T(8,128)(2,1)S(1)}, bf16[384,384]{1,0:T(8,128)(2,1)}, u32[]{:S(2)}) copy-start(bf16[384,384]{1,0:T(8,128)(2,1)} %out_weight.3) | copy-start | bytes 884740
  45.3 3.8 %collective-permute-start.9 = (bf16[128,384]{1,0:T(8,128)(2,1)S(1)}, bf16[128,384]{1,0:T(8,128)(2,1)S(1)}, u32[]{:S(2)}, u32[]{:S(2)}) collective-permute-start(bf16[128,384]{1,0:T(8,128)(2,1)S(1)} %fusion), channel_id=1, source_target_pairs={{2,0},{0,2},{3,1},{1,3},{6,4},{4,6},{7,5},{5,7},{10,8},{8,10},{11,... | collective-permute-start | bytes 294920 | tf_op jit(solution)/shard_map/ppermute | solution.py:421
  46.4 5.5 %collective-permute-start.10 = (bf16[192,384]{1,0:T(8,128)(2,1)S(1)}, bf16[192,384]{1,0:T(8,128)(2,1)S(1)}, u32[]{:S(2)}, u32[]{:S(2)}) collective-permute-start(bf16[192,384]{1,0:T(8,128)(2,1)S(1)} %get-tuple-element.43), channel_id=1, source_target_pairs={{0,4},{4,0},{8,12},{12,8},{1,5},{5,1},{9,13},{13,9},{2,6},{6,2},{1... | collective-permute-start | bytes 442376 | tf_op jit(solution)/shard_map/ppermute | solution.py:455
  46.5 5.5 %collective-permute-start.11 = (bf16[192,384]{1,0:T(8,128)(2,1)S(1)}, bf16[192,384]{1,0:T(8,128)(2,1)S(1)}, u32[]{:S(2)}, u32[]{:S(2)}) collective-permute-start(bf16[192,384]{1,0:T(8,128)(2,1)S(1)} %get-tuple-element.45), channel_id=1, source_target_pairs={{0,1},{1,0},{2,3},{3,2},{4,5},{5,4},{6,7},{7,6},{8,9},{9,8},{10,11... | collective-permute-start | bytes 442376 | tf_op jit(solution)/shard_map/ppermute | solution.py:455
  47.8 8.2 %collective-permute-start.12 = (bf16[192,384]{1,0:T(8,128)(2,1)S(1)}, bf16[192,384]{1,0:T(8,128)(2,1)S(1)}, u32[]{:S(2)}, u32[]{:S(2)}) collective-permute-start(bf16[192,384]{1,0:T(8,128)(2,1)S(1)} %get-tuple-element.44), channel_id=1, source_target_pairs={{0,5},{1,4},{4,1},{5,0},{8,13},{9,12},{12,9},{13,8},{2,7},{3,6},{6... | collective-permute-start | bytes 442376 | tf_op jit(solution)/shard_map/ppermute | solution.py:455
  56.1 9.5 %collective-permute-start.13 = (bf16[192,384]{1,0:T(8,128)(2,1)S(1)}, bf16[192,384]{1,0:T(8,128)(2,1)S(1)}, u32[]{:S(2)}, u32[]{:S(2)}) collective-permute-start(bf16[192,384]{1,0:T(8,128)(2,1)S(1)} %add_convert_fusion.2), channel_id=1, source_target_pairs={{0,8},{4,12},{8,0},{12,4},{1,9},{5,13},{9,1},{13,5},{2,10},{6,14},... | collective-permute-start | bytes 442376 | tf_op jit(solution)/shard_map/ppermute | solution.py:455
  56.7 19.9 %copy-start = (bf16[384,1152]{1,0:T(8,128)(2,1)S(1)}, bf16[384,1152]{1,0:T(8,128)(2,1)}, u32[]{:S(2)}) copy-start(bf16[384,1152]{1,0:T(8,128)(2,1)} %refs_8_.1) | copy-start | bytes 2654212
  56.7 19.9 %copy-start.2 = (f32[384]{0:T(512)S(1)}, f32[384]{0:T(512)}, u32[]{:S(2)}) copy-start(f32[384]{0:T(512)} %refs_9_.1) | copy-start | bytes 4612
  65.6 5.0 %collective-permute-start.14 = (bf16[192,384]{1,0:T(8,128)(2,1)S(1)}, bf16[192,384]{1,0:T(8,128)(2,1)S(1)}, u32[]{:S(2)}, u32[]{:S(2)}) collective-permute-start(bf16[192,384]{1,0:T(8,128)(2,1)S(1)} %add_convert_fusion.1.refs_0_), channel_id=1, source_target_pairs={{0,4},{4,0},{8,12},{12,8},{1,5},{5,1},{9,13},{13,9},{2,6},{6,2},{1... | collective-permute-start | bytes 442376 | tf_op jit(solution)/shard_map/ppermute | solution.py:455
  65.7 7.2 %collective-permute-start.15 = (bf16[192,384]{1,0:T(8,128)(2,1)S(1)}, bf16[192,384]{1,0:T(8,128)(2,1)S(1)}, u32[]{:S(2)}, u32[]{:S(2)}) collective-permute-start(bf16[192,384]{1,0:T(8,128)(2,1)S(1)} %add_convert_fusion.1.refs_0_), channel_id=1, source_target_pairs={{0,1},{1,0},{2,3},{3,2},{4,5},{5,4},{6,7},{7,6},{8,9},{9,8},{10,11... | collective-permute-start | bytes 442376 | tf_op jit(solution)/shard_map/ppermute | solution.py:455
  65.8 9.4 %collective-permute-start.16 = (bf16[192,384]{1,0:T(8,128)(2,1)S(1)}, bf16[192,384]{1,0:T(8,128)(2,1)S(1)}, u32[]{:S(2)}, u32[]{:S(2)}) collective-permute-start(bf16[192,384]{1,0:T(8,128)(2,1)S(1)} %add_convert_fusion.1.refs_0_), channel_id=1, source_target_pairs={{0,5},{1,4},{4,1},{5,0},{8,13},{9,12},{12,9},{13,8},{2,7},{3,6},{6... | collective-permute-start | bytes 442376 | tf_op jit(solution)/shard_map/ppermute | solution.py:455
  68.3 6.9 %collective-permute-start.17 = (bf16[192,384]{1,0:T(8,128)(2,1)S(1)}, bf16[192,384]{1,0:T(8,128)(2,1)S(1)}, u32[]{:S(2)}, u32[]{:S(2)}) collective-permute-start(bf16[192,384]{1,0:T(8,128)(2,1)S(1)} %add_convert_fusion.1.refs_0_), channel_id=1, source_target_pairs={{0,2},{2,0},{1,3},{3,1},{4,6},{6,4},{5,7},{7,5},{8,10},{10,8},{9,1... | collective-permute-start | bytes 442376 | tf_op jit(solution)/shard_map/ppermute | solution.py:455
  70.6 4.7 %collective-permute-start.18 = (bf16[192,384]{1,0:T(8,128)(2,1)S(1)}, bf16[192,384]{1,0:T(8,128)(2,1)S(1)}, u32[]{:S(2)}, u32[]{:S(2)}) collective-permute-start(bf16[192,384]{1,0:T(8,128)(2,1)S(1)} %collective-permute-done.14.refs_1_), channel_id=1, source_target_pairs={{0,2},{2,0},{1,3},{3,1},{4,6},{6,4},{5,7},{7,5},{8,10},{10,8},{9,1... | collective-permute-start | bytes 442376 | tf_op jit(solution)/shard_map/ppermute | solution.py:455
  72.9 3.3 %collective-permute-start.19 = (bf16[192,384]{1,0:T(8,128)(2,1)S(1)}, bf16[192,384]{1,0:T(8,128)(2,1)S(1)}, u32[]{:S(2)}, u32[]{:S(2)}) collective-permute-start(bf16[192,384]{1,0:T(8,128)(2,1)S(1)} %collective-permute-done.15.refs_2_), channel_id=1, source_target_pairs={{0,2},{2,0},{1,3},{3,1},{4,6},{6,4},{5,7},{7,5},{8,10},{10,8},{9,1... | collective-permute-start | bytes 442376 | tf_op jit(solution)/shard_map/ppermute | solution.py:455
  75.2 1.4 %collective-permute-start.20 = (bf16[192,384]{1,0:T(8,128)(2,1)S(1)}, bf16[192,384]{1,0:T(8,128)(2,1)S(1)}, u32[]{:S(2)}, u32[]{:S(2)}) collective-permute-start(bf16[192,384]{1,0:T(8,128)(2,1)S(1)} %collective-permute-done.16.refs_3_), channel_id=1, source_target_pairs={{0,2},{2,0},{1,3},{3,1},{4,6},{6,4},{5,7},{7,5},{8,10},{10,8},{9,1... | collective-permute-start | bytes 442376 | tf_op jit(solution)/shard_map/ppermute | solution.py:455
  (9 other events, 55.1 us)

commit v5 on v4

--- a/solution.py
+++ b/solution.py
@@ -12,6 +12,7 @@
 HEADS = 6
 HEAD_WIDTH = 64
 RIM = 8
+RELS = 2883
 SIDE = 16
 TOKENS = 512
 HALF = 256
@@ -38,43 +39,43 @@
     return lax.broadcasted_iota(jnp.int32, shape, dim)
 
 
-def prepare_kernel(
-    shift,
-    strips,
-    cot,
-    out_weight,
-    qkv_weight,
-    inner_flags,
-    row_flags,
-    col_flags,
-    corner_flags,
-    nothing,
-    *refs,
-):
-    outs, (bias_blocks, d_context_t, qkv_weight_t, penalty), sems = refs[:6], refs[6:10], refs[10]
-    nothing[...] = jnp.zeros_like(nothing)
-    parts = [bias_blocks.at[k] for k in range(3)] + [d_context_t, qkv_weight_t, penalty]
+def prepare_kernel(position_bias, cot_far, out_far, weight_far, blank, *refs):
+    blank[...] = jnp.zeros_like(blank)
+    outs, (table, cot, out_weight, qkv_weight), refs = refs[:5], refs[5:9], refs[9:]
+    bias_blocks, d_context_t, qkv_weight_t, sems = refs
+    arrivals = [
+        pltpu.make_async_copy(source, place, sems.at[5 + k])
+        for k, (source, place) in enumerate(
+            ((weight_far, qkv_weight), (out_far, out_weight), (cot_far, cot))
+        )
+    ]
+    for copy in arrivals:
+        copy.start()
+    parts = [bias_blocks.at[k] for k in range(3)] + [d_context_t, qkv_weight_t]
     copies = [pltpu.make_async_copy(part, outs[k], sems.at[k]) for k, part in enumerate(parts)]
-    qkv_weight_t[...] = qkv_weight[...].T
-    copies[4].start()
-    d_context_t[...] = nt(out_weight[...], cot[...]).astype(bf16)
-    copies[3].start()
-    plain = strips[...] * LOG2E
+    table[...] = jnp.zeros_like(table)
+    table[:HEADS, :RELS] = position_bias[...] * LOG2E
+    plain = table[...]
+    frames = [plain[:, :1024]] + [
+        pltpu.roll(plain, plain.shape[1] - frame * 961, 1)[:, :1024] for frame in (1, 2)
+    ]
+    plain = jnp.concatenate(frames, 0)
     high = plain.astype(bf16)
     rest = plain - high.astype(f32)
     middle = rest.astype(bf16)
     low = (rest - middle.astype(f32)).astype(bf16)
-    turn = iota((TOKENS, TOKENS), 0) + iota((TOKENS, TOKENS), 1) == TOKENS - 2
-    turn = turn.astype(f32).astype(bf16)
-    turned = nn(high, turn) + nn(middle, turn) + nn(low, turn)
+    slot = iota((1, 1024), 1)
+    source = 960 - 62 * (slot // 32 % 16) - 31 * (slot // 512) - slot % 32
+    pick = (iota((1024, 1024), 0) == source).astype(f32).astype(bf16)
+    turned = nn(high, pick) + nn(middle, pick) + nn(low, pick)
     lane = iota((SIDE, TOKENS), 1)
     for entry in range(HEADS * 3):
         head, frame = divmod(entry, 3)
-        first = 2 * (head * 3 + 2 - frame)
-        even = jnp.broadcast_to(turned[first : first + 1, :], (SIDE, TOKENS))
-        odd = jnp.broadcast_to(turned[first + 1 : first + 2, :], (SIDE, TOKENS))
+        first = (2 - frame) * 8 + head
+        even = jnp.broadcast_to(turned[first : first + 1, :TOKENS], (SIDE, TOKENS))
+        odd = jnp.broadcast_to(turned[first : first + 1, TOKENS:], (SIDE, TOKENS))
         even = pltpu.roll(even, TOKENS - 15, 1, stride=1, stride_axis=0)
-        odd = pltpu.roll(odd, TOKENS - 31, 1, stride=1, stride_axis=0)
+        odd = pltpu.roll(odd, 1, 1, stride=1, stride_axis=0)
         rows = jnp.where(lane % 32 < 16, even, odd)
         for row in range(SIDE):
             start = (15 - row) * SIDE
@@ -83,22 +84,15 @@
             ]
         if entry % 6 == 5:
             copies[head // 2].start()
-    onehots = source_onehots(shift[0], shift[1], 1)
-    on_diagonal = iota((HALF, HALF), 0) == iota((HALF, HALF), 1)
-    for t in range(2):
-        parts = (
-            flag_strip(inner_flags[t], SIDE),
-            flag_strip(row_flags[t], RIM),
-            flag_strip(col_flags[t], SIDE),
-            flag_strip(corner_flags[t], RIM, RIM),
-        )
-        marks = sum(nt(hot, strip) for hot, strip in zip(onehots, parts))
-        column = jnp.where(marks > 0.5, -1e30, 0.0)
-        wide = jnp.concatenate([column, column], 1)
-        own = jnp.where(on_diagonal, 0.0, wide)
-        penalty[t * HALF : (t + 1) * HALF, t * HALF : (t + 1) * HALF] = own
-        penalty[t * HALF : (t + 1) * HALF, (1 - t) * HALF : (2 - t) * HALF] = wide
-    copies[5].start()
+        if entry == 5:
+            arrivals[0].wait()
+            qkv_weight_t[...] = qkv_weight[...].T
+            copies[4].start()
+        if entry == 11:
+            arrivals[1].wait()
+            arrivals[2].wait()
+            d_context_t[...] = nt(out_weight[...], cot[...]).astype(bf16)
+            copies[3].start()
     for copy in copies:
         copy.wait()
 
@@ -190,6 +184,10 @@
 def main_kernel(
     shift,
     core,
+    inner_flags,
+    row_flags,
+    col_flags,
+    corner_flags,
     gain,
     inner_far,
     rows_far,
@@ -202,7 +200,6 @@
     cot_far,
     bias1_far,
     bias2_far,
-    penalty_far,
     keep_far,
     send_far,
     d_rolled_far,
@@ -227,10 +224,9 @@
     sems,
 ):
     sources = (inner_far, rows_far, cols_far, corner_far, weight_far, weight_t_far)
-    sources += (d_context_far, bias0_far, cot_far, bias1_far, bias2_far, penalty_far)
+    sources += (d_context_far, bias0_far, cot_far, bias1_far, bias2_far)
     places = [inner, rows, cols, corner, qkv_weight, qkv_weight_t]
     places += [d_context_t, bias_blocks.at[0], cot, bias_blocks.at[1], bias_blocks.at[2]]
-    places.append(penalty)
     arrivals = [
         pltpu.make_async_copy(source, place, sems.at[k])
         for k, (source, place) in enumerate(zip(sources, places))
@@ -238,6 +234,20 @@
     for copy in arrivals:
         copy.start()
     onehots = source_onehots(shift[0], shift[1], 1)
+    on_diagonal = iota((HALF, HALF), 0) == iota((HALF, HALF), 1)
+    for t in range(2):
+        strips = (
+            flag_strip(inner_flags[t], SIDE),
+            flag_strip(row_flags[t], RIM),
+            flag_strip(col_flags[t], SIDE),
+            flag_strip(corner_flags[t], RIM, RIM),
+        )
+        marks = sum(nt(hot, strip) for hot, strip in zip(onehots, strips))
+        column = jnp.where(marks > 0.5, -1e30, 0.0)
+        wide = jnp.concatenate([column, column], 1)
+        own = jnp.where(on_diagonal, 0.0, wide)
+        penalty[t * HALF : (t + 1) * HALF, t * HALF : (t + 1) * HALF] = own
+        penalty[t * HALF : (t + 1) * HALF, (1 - t) * HALF : (2 - t) * HALF] = wide
     for copy in arrivals[:4]:
         copy.wait()
     rolled = []
@@ -258,7 +268,6 @@
     arrivals[5].wait()
     qkv_t = nt(qkv_weight_t[...], normed).astype(bf16)
     arrivals[6].wait()
-    arrivals[11].wait()
     for pair in range(HEADS // 2):
         arrivals[(7, 9, 10)[pair]].wait()
         heads = [
@@ -301,7 +310,7 @@
         copy.start()
     for block in range(6):
         source, target = half_block(grads, block, keep_far)
-        pltpu.make_async_copy(source, target, sems.at[12 + block]).wait()
+        pltpu.make_async_copy(source, target, sems.at[11 + block]).wait()
     keep_context.wait()
     for copy in copies:
         copy.wait()
@@ -318,7 +327,7 @@
         @pl.when(core == side)
         def _():
             source, target = half_block(grads, block, half)
-            pltpu.make_async_copy(source, target, sems.at[12 + block]).start()
+            pltpu.make_async_copy(source, target, sems.at[11 + block]).start()
 
 
 def place_kernel(
@@ -329,12 +338,10 @@
     context_far,
     field_grad,
     update,
-    nothing,
     kept,
     context_t,
     sems,
 ):
-    nothing[...] = jnp.zeros_like(nothing)
     copies = [
         pltpu.make_async_copy(kept_far, kept, sems.at[0]),
         pltpu.make_async_copy(context_far, context_t, sems.at[1]),
@@ -459,7 +466,8 @@
     return sum(piece.astype(f32) for piece in pieces).astype(bf16)
 
 
-def sum_quarter(block):
+def sum_quarter(keep, send):
+    block = add_up(keep, swapped(send, CORE))
     share = block.shape[0] // 4
     mine = quarter_index()
     pick = lambda place: lax.dynamic_slice_in_dim(block, place * share, share, 0)
@@ -467,14 +475,14 @@
     return add_up(pick(mine), *arrived)
 
 
-def sum_rest(quarter, zero):
+def sum_rest(quarter):
     rest = [
         (axis, 1 << k)
         for axis in ("ta", "sy")
         for k in range(1, lax.axis_size(axis).bit_length() - 1)
     ]
     for bit in rest:
-        quarter = add_up(quarter, swapped(quarter, bit), zero)
+        quarter = add_up(quarter, swapped(quarter, bit))
     return quarter
 
 
@@ -499,39 +507,29 @@
     cols = passed_along(state_field, "sx", -1)
     col_flags = passed_along(outlier_flags, "sx", -1)
     corner_flags = passed_across(outlier_flags, "sy", "sx", -1)
-    strips = jnp.pad(
-        position_bias.reshape(HEADS, 3, 31, 31), ((0, 0), (0, 0), (0, 1), (0, 1))
-    )
-    strips = strips.reshape(HEADS, 3, 16, 2, 32).transpose(0, 1, 3, 2, 4).reshape(36, TOKENS)
     cot_rows = cotangent.reshape(TOKENS, width)
     pair_bias = ((6, HALF, HALF), f32)
-    nothing, *bias_blocks, d_context_t, qkv_weight_t, penalty = local_call(
+    blank, *bias_blocks, d_context_t, qkv_weight_t = local_call(
         prepare_kernel,
-        [((16, 128), bf16)] + [pair_bias] * 3 + [((width, TOKENS), bf16), wide(3 * width), ((TOKENS, TOKENS), f32)],
-        [
-            window_shift,
-            strips,
-            cot_rows,
-            out_weight,
-            qkv_weight,
-            outlier_flags,
-            row_flags,
-            col_flags,
-            corner_flags,
-        ],
-        far_out=6,
+        [wide(128)] + [pair_bias] * 3 + [((width, TOKENS), bf16), wide(3 * width)],
+        [position_bias, cot_rows, out_weight, qkv_weight],
+        far_in=3,
+        far_out=5,
         scratch=[
+            ((8, 3072), f32),
+            wide(TOKENS),
+            wide(width),
+            ((width, 3 * width), bf16),
             ((3, 6, HALF, HALF), f32),
             ((width, TOKENS), bf16),
             wide(3 * width),
-            ((TOKENS, TOKENS), f32),
         ],
-        copies=6,
+        copies=8,
         micros=3,
         limit=62,
     )
-    corner_message = rows.reshape(2 * RIM, SIDE, width)[:, :RIM] + nothing[0, 0]
-    corner = passed_along(corner_message.reshape(-1, width), "sx", -1)
+    corner_message = rows.reshape(2 * RIM, SIDE, width)[:, :RIM].reshape(-1, width) + blank
+    corner = passed_along(corner_message, "sx", -1)
     core = index_bit(*CORE).astype(jnp.int32).reshape(1)
     keep, send, d_rolled, context_t, lower, right = local_call(
         main_kernel,
@@ -540,6 +538,10 @@
         [
             window_shift,
             core,
+            outlier_flags,
+            row_flags,
+            col_flags,
+            corner_flags,
             layer_norm_gain,
             state_field.reshape(TOKENS, width),
             rows,
@@ -552,9 +554,8 @@
             cot_rows,
             bias_blocks[1],
             bias_blocks[2],
-            penalty,
         ],
-        far_in=12,
+        far_in=11,
         far_out=6,
         scratch=[
             ((TOKENS, TOKENS), f32),
@@ -573,19 +574,19 @@
             wide(TOKENS),
             wide(HALF),
         ],
-        copies=18,
+        copies=17,
         micros=12,
         limit=62,
     )
     below = passed_along(lower, "sy", 1)
     beside = passed_along(right, "sx", 1)
-    block = add_up(keep, swapped(send, CORE))
-    across = below.reshape(2 * RIM, SIDE, width)[:, RIM:] + block[0, 0] * 0
-    across = passed_along(across.reshape(-1, width), "sx", 1)
-    quarter = sum_quarter(block)
-    field_grad, update, nothing = local_call(
+    across = passed_along(
+        below.reshape(2 * RIM, SIDE, width)[:, RIM:].reshape(-1, width), "sx", 1
+    )
+    quarter = sum_quarter(keep, send)
+    field_grad, update = local_call(
         place_kernel,
-        [wide(TOKENS), wide(TOKENS), ((16, 128), bf16)],
+        [wide(TOKENS), wide(TOKENS)],
         [
             window_shift,
             jnp.concatenate([below, beside, across], 0),
@@ -598,7 +599,7 @@
         copies=2,
         micros=2,
     )
-    quarter = sum_rest(quarter, nothing[0, 0])
+    quarter = sum_rest(quarter)
     quarters = [quarter] + [swapped(quarter, *group) for group in GROUPS]
     others = [swapped(piece, CORE) for piece in quarters]
     tiles = lax.axis_size("sy") * lax.axis_size("sx") * lax.axis_size("ta")

time: 80.1 us -> 77 us (0.961)
  local copies, waits for them, and re-layouts: 6.6 us -> 1.81 us
  waiting for transfers between devices: 19.2 us -> 20.8 us
  between operations: 2.32 us -> 1.07 us
  starting transfers between devices: 21.4 us -> 22.5 us
    ppermute x8, starting transfers between devices: 9.03 us -> 11.4 us  [passed_along(): lax.ppermute(block, axis, [((i - distance) % count, i) for i in range(cou...]
    ppermute x1, waiting for transfers between devices: 0.01 us -> 2.32 us  [passed_across(): return lax.ppermute(block, (axis, other), route)]
    slice x3 -> x0, local copies, waits for them, and re-layouts: 2.2 us -> none  [the longest x1 1.18 us: shards(): corner_message = rows.reshape(2 * RIM, SIDE, width)[:, :RIM] + nothing[0, 0]]
    reshape x2 -> x1, local copies, waits for them, and re-layouts: 1.96 us -> 0.01 us  [shards(): below.reshape(2 * RIM, SIDE, width)[:, RIM:].reshape(-1, width)]
    ppermute x8, waiting for transfers between devices: 5.09 us -> 3.66 us  [passed_along(): lax.ppermute(block, axis, [((i - distance) % count, i) for i in range(cou...]
    ppermute x12, starting transfers between devices: 12.3 us -> 11.1 us  [swapped(): return lax.ppermute(block, axes, route)]
    add x0 -> x1, other arithmetic: none -> 0.98 us  [shards(): rows.reshape(2 * RIM, SIDE, width)[:, :RIM].reshape(-1, width) + blank]
  transfers between devices with their start and end apart: 21 -> 21, of which waited for: 10 -> 10; matrix products, arithmetic and copies ran while one was open for 9% -> 3% of each run, Pallas kernels for 11% -> 12%
where the time goes in v5:
time: 77 us; the launch traced here: 76.7 us
  Pallas kernels  28 us (36%)
  starting transfers between devices  22.5 us (29%)
  waiting for transfers between devices  20.8 us (27%)
  other arithmetic  2.44 us (3%)
  local copies, waits for them, and re-layouts  1.81 us (2%)
  between operations  1.07 us (1%)
    pallas_call x4, Pallas kernels, local_call(): pl.pallas_call(kernel, out_shape=[jax.ShapeDtypeStruct(shape, dtype) for...  28 us
    ppermute x12, waiting for transfers between devices, swapped(): return lax.ppermute(block, axes, route)  14.8 us
    ppermute x8, starting transfers between devices, passed_along(): lax.ppermute(block, axis, [((i - distance) % count, i) for i in range(cou...  11.4 us
    ppermute x12, starting transfers between devices, swapped(): return lax.ppermute(block, axes, route)  11.1 us
    ppermute x8, waiting for transfers between devices, passed_along(): lax.ppermute(block, axis, [((i - distance) % count, i) for i in range(cou...  3.66 us
    ppermute x1, waiting for transfers between devices, passed_across(): return lax.ppermute(block, (axis, other), route)  2.32 us
  transfers between devices with their start and end apart: 21, of which 10 were waited for; matrix products, arithmetic and copies ran while one was open for 3% of the time, Pallas kernels for 12%

profile of v5, /device:TPU:1, one launch (start us, length us, event | category | flops | bytes accessed | tf_op | source)
XLA Modules:
  0.0 76.7 jit_solution(4764168143322343115)
XLA Ops:
  1.7 4.8 %collective-permute-start.3 = (bf16[256,384]{1,0:T(8,128)(2,1)S(1)}, bf16[256,384]{1,0:T(8,128)(2,1)S(1)}, u32[]{:S(2)}, u32[]{:S(2)}) collective-permute-start(bf16[256,384]{1,0:T(8,128)(2,1)S(1)} %bitcast.17), channel_id=1, source_target_pairs={{4,0},{8,4},{12,8},{0,12},{5,1},{9,5},{13,9},{1,13},{6,2},{10,6},{... | collective-permute-start | bytes 589832 | tf_op jit(solution)/shard_map/ppermute | solution.py:428
  6.5 6.7 %shard_map.119 = (bf16[128,384]{1,0:T(8,128)(2,1)}, f32[6,256,256]{2,1,0:T(8,128)}, f32[6,256,256]{2,1,0:T(8,128)}, f32[6,256,256]{2,1,0:T(8,128)}, bf16[384,512]{1,0:T(8,128)(2,1)}, /*index=5*/bf16[1152,384]{1,0:T(8,128)(2,1)}) custom-call(f32[6,2883]{1,0:T(8,128)} %position_bias.1, bf16[512,384]{1,0:T(8,128)(2,1)} %bitcast.20, ...), custom_call_target="tpu_custom_call" | custom-call | flops 3000000000 | bytes 1000000 | tf_op jit(solution)/shard_map/pallas_call | solution.py:411
  13.2 1.0 %fusion = bf16[128,384]{1,0:T(8,128)(2,1)S(1)} fusion(bf16[128,384]{1,0:T(8,128)(2,1)} %get-tuple-element.22, bf16[16,16,384]{2,1,0:T(8,128)(2,1)S(1)} %bitcast.19), kind=kLoop, calls=%fused_computation.6 | loop fusion | flops 49152 | bytes 294912 | tf_op jit(solution)/shard_map/add | solution.py:531
  14.6 2.1 %collective-permute-start = (s32[2,16,16]{2,1,0:T(8,128)S(1)}, s32[2,16,16]{2,1,0:T(8,128)S(1)}, u32[]{:S(2)}, u32[]{:S(2)}) collective-permute-start(s32[2,16,16]{2,1,0:T(8,128)S(1)} %copy-done.11), channel_id=1, source_target_pairs={{4,0},{8,4},{12,8},{0,12},{5,1},{9,5},{13,9},{1,13},{6,2},{10,6},{... | collective-permute-start | bytes 6152 | tf_op jit(solution)/shard_map/ppermute | solution.py:428
  17.9 2.3 %collective-permute-done.2.corner_flags = s32[2,16,16]{2,1,0:T(8,128)S(1)} collective-permute-done((s32[2,16,16]{2,1,0:T(8,128)S(1)}, s32[2,16,16]{2,1,0:T(8,128)S(1)}, u32[]{:S(2)}, u32[]{:S(2)}) %collective-permute-start.2) | collective-permute-done | bytes 2080 | tf_op jit(solution)/shard_map/ppermute | solution.py:438
  21.0 15.8 %shard_map.120 = (bf16[768,384]{1,0:T(8,128)(2,1)}, bf16[768,384]{1,0:T(8,128)(2,1)}, bf16[512,384]{1,0:T(8,128)(2,1)}, bf16[384,512]{1,0:T(8,128)(2,1)}, bf16[2...) custom-call(s32[2]{0:T(128)} %shift.3, s32[1]{0:T(128)} %bitcast.core, s32[2,16,16]{2,1,0:T(8,128)} %inner_flags.1, ...), custom_call_target="tpu_custom_call" | custom-call | flops 12000000000 | bytes 1000000 | tf_op jit(solution)/shard_map/pallas_call | solution.py:411
  37.0 2.0 %collective-permute-done.9 = bf16[768,384]{1,0:T(8,128)(2,1)S(1)} collective-permute-done((bf16[768,384]{1,0:T(8,128)(2,1)}, bf16[768,384]{1,0:T(8,128)(2,1)S(1)}, u32[]{:S(2)}, u32[]{:S(2)}) %collective-permute-start.9) | collective-permute-done | bytes 589856 | tf_op jit(solution)/shard_map/ppermute | solution.py:462
  39.1 1.2 %add_convert_fusion = bf16[768,384]{1,0:T(8,128)(2,1)S(1)} fusion(bf16[768,384]{1,0:T(8,128)(2,1)S(1)} %collective-permute-done.9, bf16[768,384]{1,0:T(8,128)(2,1)} %get-tuple-element.34), kind=kLoop, calls=%fused_computation | loop fusion | flops 1179648 | bytes 1769472 | tf_op jit(solution)/shard_map/convert_element_type | solution.py:466
  40.5 1.3 %collective-permute-start.11 = (bf16[192,384]{1,0:T(8,128)(2,1)S(1)}, bf16[192,384]{1,0:T(8,128)(2,1)S(1)}, u32[]{:S(2)}, u32[]{:S(2)}) collective-permute-start(bf16[192,384]{1,0:T(8,128)(2,1)S(1)} %get-tuple-element.41), channel_id=1, source_target_pairs={{0,1},{1,0},{2,3},{3,2},{4,5},{5,4},{6,7},{7,6},{8,9},{9,8},{10,11... | collective-permute-start | bytes 442376 | tf_op jit(solution)/shard_map/ppermute | solution.py:462
  41.7 1.4 %collective-permute-start.12 = (bf16[192,384]{1,0:T(8,128)(2,1)S(1)}, bf16[192,384]{1,0:T(8,128)(2,1)S(1)}, u32[]{:S(2)}, u32[]{:S(2)}) collective-permute-start(bf16[192,384]{1,0:T(8,128)(2,1)S(1)} %get-tuple-element.40), channel_id=1, source_target_pairs={{0,5},{1,4},{4,1},{5,0},{8,13},{9,12},{12,9},{13,8},{2,7},{3,6},{6... | collective-permute-start | bytes 442376 | tf_op jit(solution)/shard_map/ppermute | solution.py:462
  43.2 1.2 %collective-permute-start.7 = (bf16[256,384]{1,0:T(8,128)(2,1)S(1)}, bf16[256,384]{1,0:T(8,128)(2,1)S(1)}, u32[]{:S(2)}, u32[]{:S(2)}) collective-permute-start(bf16[256,384]{1,0:T(8,128)(2,1)S(1)} %copy-done.8), channel_id=1, source_target_pairs={{2,0},{0,2},{3,1},{1,3},{6,4},{4,6},{7,5},{5,7},{10,8},{8,10},{11,... | collective-permute-start | bytes 589832 | tf_op jit(solution)/shard_map/ppermute | solution.py:428
  44.4 1.3 %collective-permute-done.10 = bf16[192,384]{1,0:T(8,128)(2,1)S(1)} collective-permute-done((bf16[192,384]{1,0:T(8,128)(2,1)S(1)}, bf16[192,384]{1,0:T(8,128)(2,1)S(1)}, u32[]{:S(2)}, u32[]{:S(2)}) %collective-permute-start.10) | collective-permute-done | bytes 147488 | tf_op jit(solution)/shard_map/ppermute | solution.py:462
  45.7 4.1 %collective-permute-done.12 = bf16[192,384]{1,0:T(8,128)(2,1)S(1)} collective-permute-done((bf16[192,384]{1,0:T(8,128)(2,1)S(1)}, bf16[192,384]{1,0:T(8,128)(2,1)S(1)}, u32[]{:S(2)}, u32[]{:S(2)}) %collective-permute-start.12) | collective-permute-done | bytes 147488 | tf_op jit(solution)/shard_map/ppermute | solution.py:462
  50.3 2.9 %collective-permute-done.6 = bf16[256,384]{1,0:T(8,128)(2,1)S(1)} collective-permute-done((bf16[256,384]{1,0:T(8,128)(2,1)S(1)}, bf16[256,384]{1,0:T(8,128)(2,1)S(1)}, u32[]{:S(2)}, u32[]{:S(2)}) %collective-permute-start.6) | collective-permute-done | bytes 196640 | tf_op jit(solution)/shard_map/ppermute | solution.py:428
  53.2 2.3 %collective-permute-start.8 = (bf16[128,384]{1,0:T(8,128)(2,1)S(1)}, bf16[128,384]{1,0:T(8,128)(2,1)S(1)}, u32[]{:S(2)}, u32[]{:S(2)}) collective-permute-start(bf16[128,384]{1,0:T(8,128)(2,1)S(1)} %slice_bitcast_fusion), channel_id=1, source_target_pairs={{2,0},{0,2},{3,1},{1,3},{6,4},{4,6},{7,5},{5,7},{10,8},{8,10},{11,... | collective-permute-start | bytes 294920 | tf_op jit(solution)/shard_map/ppermute | solution.py:428
  55.5 4.8 %collective-permute-done.13 = bf16[192,384]{1,0:T(8,128)(2,1)S(1)} collective-permute-done((bf16[192,384]{1,0:T(8,128)(2,1)S(1)}, bf16[192,384]{1,0:T(8,128)(2,1)S(1)}, u32[]{:S(2)}, u32[]{:S(2)}) %collective-permute-start.13) | collective-permute-done | bytes 147488 | tf_op jit(solution)/shard_map/ppermute | solution.py:462
  60.4 1.3 %collective-permute-start.15 = (bf16[192,384]{1,0:T(8,128)(2,1)S(1)}, bf16[192,384]{1,0:T(8,128)(2,1)S(1)}, u32[]{:S(2)}, u32[]{:S(2)}) collective-permute-start(bf16[192,384]{1,0:T(8,128)(2,1)S(1)} %add_convert_fusion.1.refs_0_), channel_id=1, source_target_pairs={{0,1},{1,0},{2,3},{3,2},{4,5},{5,4},{6,7},{7,6},{8,9},{9,8},{10,11... | collective-permute-start | bytes 442376 | tf_op jit(solution)/shard_map/ppermute | solution.py:462
  61.7 1.4 %collective-permute-start.16 = (bf16[192,384]{1,0:T(8,128)(2,1)S(1)}, bf16[192,384]{1,0:T(8,128)(2,1)S(1)}, u32[]{:S(2)}, u32[]{:S(2)}) collective-permute-start(bf16[192,384]{1,0:T(8,128)(2,1)S(1)} %add_convert_fusion.1.refs_0_), channel_id=1, source_target_pairs={{0,5},{1,4},{4,1},{5,0},{8,13},{9,12},{12,9},{13,8},{2,7},{3,6},{6... | collective-permute-start | bytes 442376 | tf_op jit(solution)/shard_map/ppermute | solution.py:462
  63.2 1.4 %collective-permute-start.17 = (bf16[192,384]{1,0:T(8,128)(2,1)S(1)}, bf16[192,384]{1,0:T(8,128)(2,1)S(1)}, u32[]{:S(2)}, u32[]{:S(2)}) collective-permute-start(bf16[192,384]{1,0:T(8,128)(2,1)S(1)} %add_convert_fusion.1.refs_0_), channel_id=1, source_target_pairs={{0,2},{2,0},{1,3},{3,1},{4,6},{6,4},{5,7},{7,5},{8,10},{10,8},{9,1... | collective-permute-start | bytes 442376 | tf_op jit(solution)/shard_map/ppermute | solution.py:462
  65.3 2.3 %collective-permute-start.18 = (bf16[192,384]{1,0:T(8,128)(2,1)S(1)}, bf16[192,384]{1,0:T(8,128)(2,1)S(1)}, u32[]{:S(2)}, u32[]{:S(2)}) collective-permute-start(bf16[192,384]{1,0:T(8,128)(2,1)S(1)} %collective-permute-done.14.refs_1_), channel_id=1, source_target_pairs={{0,2},{2,0},{1,3},{3,1},{4,6},{6,4},{5,7},{7,5},{8,10},{10,8},{9,1... | collective-permute-start | bytes 442376 | tf_op jit(solution)/shard_map/ppermute | solution.py:462
  67.6 1.8 %collective-permute-done.16.refs_3_ = bf16[192,384]{1,0:T(8,128)(2,1)S(1)} collective-permute-done((bf16[192,384]{1,0:T(8,128)(2,1)S(1)}, bf16[192,384]{1,0:T(8,128)(2,1)S(1)}, u32[]{:S(2)}, u32[]{:S(2)}) %collective-permute-start.16) | collective-permute-done | bytes 147488 | tf_op jit(solution)/shard_map/ppermute | solution.py:462
  69.4 1.3 %collective-permute-start.20 = (bf16[192,384]{1,0:T(8,128)(2,1)S(1)}, bf16[192,384]{1,0:T(8,128)(2,1)S(1)}, u32[]{:S(2)}, u32[]{:S(2)}) collective-permute-start(bf16[192,384]{1,0:T(8,128)(2,1)S(1)} %collective-permute-done.16.refs_3_), channel_id=1, source_target_pairs={{0,2},{2,0},{1,3},{3,1},{4,6},{6,4},{5,7},{7,5},{8,10},{10,8},{9,1... | collective-permute-start | bytes 442376 | tf_op jit(solution)/shard_map/ppermute | solution.py:462
  70.8 2.7 %shard_map.121 = (bf16[512,384]{1,0:T(8,128)(2,1)}, bf16[512,384]{1,0:T(8,128)(2,1)}) custom-call(s32[2]{0:T(128)S(1)} %copy-done.3, bf16[640,384]{1,0:T(8,128)(2,1)S(1)} %pad_maximum_fusion.halo, bf16[384,384]{1,0:T(8,128)(2,1)S(1)} %copy-done.1, bf16[512,384]{1,0:T(8,128)(2,1)S(1)} %copy-done.4, bf16[384,512]{1,0:T(8,128)(2,1)S(1)} %copy-done.5), custom_call_target="tpu_custom_call" | custom-call | flops 2000000000 | bytes 1000000 | tf_op jit(solution)/shard_map/pallas_call | solution.py:411
  73.6 2.9 %shard_map.122 = (f32[384]{0:T(512)}, f32[384,1152]{1,0:T(8,128)}, f32[384,384]{1,0:T(8,128)}) custom-call(s32[2]{0:T(128)S(1)} %pad_add_fusion.place, bf16[192,384]{1,0:T(8,128)(2,1)S(1)} %add_convert_fusion.1.refs_0_, bf16[192,384]{1,0:T(8,128)(2,1)S(1)} %collective-permute-done.14.refs_1_, bf16[192,384]{1,0:T(8,128)(2,1)S(1)} %collective-permute-done.15.refs_2_, ...), custom_call_target="tpu_custom_call" | custom-call | flops 1000000000 | bytes 1000000 | tf_op jit(solution)/shard_map/pallas_call | solution.py:411
  (61 shorter events, 5.4 us)
Async XLA Ops:
  0.6 19.6 %collective-permute-start.4 = (bf16[2,16,16,384]{3,2,1,0:T(8,128)(2,1)}, bf16[2,16,16,384]{3,2,1,0:T(8,128)(2,1)S(1)}, u32[]{:S(2)}, u32[]{:S(2)}) collective-permute-start(bf16[2,16,16,384]{3,2,1,0:T(8,128)(2,1)} %param.8), channel_id=1, source_target_pairs={{2,0},{0,2},{3,1},{1,3},{6,4},{4,6},{7,5},{5,7},{10,8},{8,10},{11,... | collective-permute-start | bytes 1179656 | tf_op jit(solution)/shard_map/ppermute | solution.py:428
  1.7 11.5 %collective-permute-start.3 = (bf16[256,384]{1,0:T(8,128)(2,1)S(1)}, bf16[256,384]{1,0:T(8,128)(2,1)S(1)}, u32[]{:S(2)}, u32[]{:S(2)}) collective-permute-start(bf16[256,384]{1,0:T(8,128)(2,1)S(1)} %bitcast.17), channel_id=1, source_target_pairs={{4,0},{8,4},{12,8},{0,12},{5,1},{9,5},{13,9},{1,13},{6,2},{10,6},{... | collective-permute-start | bytes 589832 | tf_op jit(solution)/shard_map/ppermute | solution.py:428
  14.2 6.0 %collective-permute-start.5 = (bf16[128,384]{1,0:T(8,128)(2,1)S(1)}, bf16[128,384]{1,0:T(8,128)(2,1)S(1)}, u32[]{:S(2)}, u32[]{:S(2)}) collective-permute-start(bf16[128,384]{1,0:T(8,128)(2,1)S(1)} %fusion), channel_id=1, source_target_pairs={{2,0},{0,2},{3,1},{1,3},{6,4},{4,6},{7,5},{5,7},{10,8},{8,10},{11,... | collective-permute-start | bytes 294920 | tf_op jit(solution)/shard_map/ppermute | solution.py:428
  14.6 3.0 %collective-permute-start = (s32[2,16,16]{2,1,0:T(8,128)S(1)}, s32[2,16,16]{2,1,0:T(8,128)S(1)}, u32[]{:S(2)}, u32[]{:S(2)}) collective-permute-start(s32[2,16,16]{2,1,0:T(8,128)S(1)} %copy-done.11), channel_id=1, source_target_pairs={{4,0},{8,4},{12,8},{0,12},{5,1},{9,5},{13,9},{1,13},{6,2},{10,6},{... | collective-permute-start | bytes 6152 | tf_op jit(solution)/shard_map/ppermute | solution.py:428
  16.7 1.2 %collective-permute-start.1 = (s32[2,16,16]{2,1,0:T(8,128)S(1)}, s32[2,16,16]{2,1,0:T(8,128)S(1)}, u32[]{:S(2)}, u32[]{:S(2)}) collective-permute-start(s32[2,16,16]{2,1,0:T(8,128)S(1)} %copy-done.11), channel_id=1, source_target_pairs={{2,0},{0,2},{3,1},{1,3},{6,4},{4,6},{7,5},{5,7},{10,8},{8,10},{11,... | collective-permute-start | bytes 6152 | tf_op jit(solution)/shard_map/ppermute | solution.py:428
  17.0 3.2 %collective-permute-start.2 = (s32[2,16,16]{2,1,0:T(8,128)S(1)}, s32[2,16,16]{2,1,0:T(8,128)S(1)}, u32[]{:S(2)}, u32[]{:S(2)}) collective-permute-start(s32[2,16,16]{2,1,0:T(8,128)S(1)} %copy-done.11), channel_id=1, source_target_pairs={{6,0},{4,2},{10,4},{8,6},{14,8},{12,10},{2,12},{0,14},{7,1},{5,3},... | collective-permute-start | bytes 6152 | tf_op jit(solution)/shard_map/ppermute | solution.py:438
  36.8 2.3 %collective-permute-start.9 = (bf16[768,384]{1,0:T(8,128)(2,1)}, bf16[768,384]{1,0:T(8,128)(2,1)S(1)}, u32[]{:S(2)}, u32[]{:S(2)}) collective-permute-start(bf16[768,384]{1,0:T(8,128)(2,1)} %get-tuple-element.35), channel_id=1, source_target_pairs={{0,2},{2,0},{1,3},{3,1},{4,6},{6,4},{5,7},{7,5},{8,10},{10,8},{9,1... | collective-permute-start | bytes 1769480 | tf_op jit(solution)/shard_map/ppermute | solution.py:462
  40.3 30.5 %copy-start.1 = (bf16[384,384]{1,0:T(8,128)(2,1)S(1)}, bf16[384,384]{1,0:T(8,128)(2,1)}, u32[]{:S(2)}) copy-start(bf16[384,384]{1,0:T(8,128)(2,1)} %out_weight.1) | copy-start | bytes 884740
  40.3 30.5 %copy-start.3 = (s32[2]{0:T(128)S(1)}, s32[2]{0:T(128)}, u32[]{:S(2)}) copy-start(s32[2]{0:T(128)} %shift.3) | copy-start | bytes 28
  40.3 30.5 %copy-start.4 = (bf16[512,384]{1,0:T(8,128)(2,1)S(1)}, bf16[512,384]{1,0:T(8,128)(2,1)}, u32[]{:S(2)}) copy-start(bf16[512,384]{1,0:T(8,128)(2,1)} %get-tuple-element.30.kept_far) | copy-start | bytes 1179652
  40.4 5.3 %collective-permute-start.10 = (bf16[192,384]{1,0:T(8,128)(2,1)S(1)}, bf16[192,384]{1,0:T(8,128)(2,1)S(1)}, u32[]{:S(2)}, u32[]{:S(2)}) collective-permute-start(bf16[192,384]{1,0:T(8,128)(2,1)S(1)} %get-tuple-element.39), channel_id=1, source_target_pairs={{0,4},{4,0},{8,12},{12,8},{1,5},{5,1},{9,13},{13,9},{2,6},{6,2},{1... | collective-permute-start | bytes 442376 | tf_op jit(solution)/shard_map/ppermute | solution.py:462
  40.5 5.3 %collective-permute-start.11 = (bf16[192,384]{1,0:T(8,128)(2,1)S(1)}, bf16[192,384]{1,0:T(8,128)(2,1)S(1)}, u32[]{:S(2)}, u32[]{:S(2)}) collective-permute-start(bf16[192,384]{1,0:T(8,128)(2,1)S(1)} %get-tuple-element.41), channel_id=1, source_target_pairs={{0,1},{1,0},{2,3},{3,2},{4,5},{5,4},{6,7},{7,6},{8,9},{9,8},{10,11... | collective-permute-start | bytes 442376 | tf_op jit(solution)/shard_map/ppermute | solution.py:462
  41.7 8.1 %collective-permute-start.12 = (bf16[192,384]{1,0:T(8,128)(2,1)S(1)}, bf16[192,384]{1,0:T(8,128)(2,1)S(1)}, u32[]{:S(2)}, u32[]{:S(2)}) collective-permute-start(bf16[192,384]{1,0:T(8,128)(2,1)S(1)} %get-tuple-element.40), channel_id=1, source_target_pairs={{0,5},{1,4},{4,1},{5,0},{8,13},{9,12},{12,9},{13,8},{2,7},{3,6},{6... | collective-permute-start | bytes 442376 | tf_op jit(solution)/shard_map/ppermute | solution.py:462
  43.1 10.0 %collective-permute-start.6 = (bf16[256,384]{1,0:T(8,128)(2,1)S(1)}, bf16[256,384]{1,0:T(8,128)(2,1)S(1)}, u32[]{:S(2)}, u32[]{:S(2)}) collective-permute-start(bf16[256,384]{1,0:T(8,128)(2,1)S(1)} %copy-done.9), channel_id=1, source_target_pairs={{12,0},{0,4},{4,8},{8,12},{13,1},{1,5},{5,9},{9,13},{14,2},{2,6},{... | collective-permute-start | bytes 589832 | tf_op jit(solution)/shard_map/ppermute | solution.py:428
  43.2 20.0 %collective-permute-start.7 = (bf16[256,384]{1,0:T(8,128)(2,1)S(1)}, bf16[256,384]{1,0:T(8,128)(2,1)S(1)}, u32[]{:S(2)}, u32[]{:S(2)}) collective-permute-start(bf16[256,384]{1,0:T(8,128)(2,1)S(1)} %copy-done.8), channel_id=1, source_target_pairs={{2,0},{0,2},{3,1},{1,3},{6,4},{4,6},{7,5},{5,7},{10,8},{8,10},{11,... | collective-permute-start | bytes 589832 | tf_op jit(solution)/shard_map/ppermute | solution.py:428
  49.9 10.4 %collective-permute-start.13 = (bf16[192,384]{1,0:T(8,128)(2,1)S(1)}, bf16[192,384]{1,0:T(8,128)(2,1)S(1)}, u32[]{:S(2)}, u32[]{:S(2)}) collective-permute-start(bf16[192,384]{1,0:T(8,128)(2,1)S(1)} %add_convert_fusion.2), channel_id=1, source_target_pairs={{0,8},{4,12},{8,0},{12,4},{1,9},{5,13},{9,1},{13,5},{2,10},{6,14},... | collective-permute-start | bytes 442376 | tf_op jit(solution)/shard_map/ppermute | solution.py:462
  53.2 10.0 %collective-permute-start.8 = (bf16[128,384]{1,0:T(8,128)(2,1)S(1)}, bf16[128,384]{1,0:T(8,128)(2,1)S(1)}, u32[]{:S(2)}, u32[]{:S(2)}) collective-permute-start(bf16[128,384]{1,0:T(8,128)(2,1)S(1)} %slice_bitcast_fusion), channel_id=1, source_target_pairs={{2,0},{0,2},{3,1},{1,3},{6,4},{4,6},{7,5},{5,7},{10,8},{8,10},{11,... | collective-permute-start | bytes 294920 | tf_op jit(solution)/shard_map/ppermute | solution.py:428
  60.4 5.0 %collective-permute-start.14 = (bf16[192,384]{1,0:T(8,128)(2,1)S(1)}, bf16[192,384]{1,0:T(8,128)(2,1)S(1)}, u32[]{:S(2)}, u32[]{:S(2)}) collective-permute-start(bf16[192,384]{1,0:T(8,128)(2,1)S(1)} %add_convert_fusion.1.refs_0_), channel_id=1, source_target_pairs={{0,4},{4,0},{8,12},{12,8},{1,5},{5,1},{9,13},{13,9},{2,6},{6,2},{1... | collective-permute-start | bytes 442376 | tf_op jit(solution)/shard_map/ppermute | solution.py:462
  60.4 7.2 %collective-permute-start.15 = (bf16[192,384]{1,0:T(8,128)(2,1)S(1)}, bf16[192,384]{1,0:T(8,128)(2,1)S(1)}, u32[]{:S(2)}, u32[]{:S(2)}) collective-permute-start(bf16[192,384]{1,0:T(8,128)(2,1)S(1)} %add_convert_fusion.1.refs_0_), channel_id=1, source_target_pairs={{0,1},{1,0},{2,3},{3,2},{4,5},{5,4},{6,7},{7,6},{8,9},{9,8},{10,11... | collective-permute-start | bytes 442376 | tf_op jit(solution)/shard_map/ppermute | solution.py:462
  61.7 7.7 %collective-permute-start.16 = (bf16[192,384]{1,0:T(8,128)(2,1)S(1)}, bf16[192,384]{1,0:T(8,128)(2,1)S(1)}, u32[]{:S(2)}, u32[]{:S(2)}) collective-permute-start(bf16[192,384]{1,0:T(8,128)(2,1)S(1)} %add_convert_fusion.1.refs_0_), channel_id=1, source_target_pairs={{0,5},{1,4},{4,1},{5,0},{8,13},{9,12},{12,9},{13,8},{2,7},{3,6},{6... | collective-permute-start | bytes 442376 | tf_op jit(solution)/shard_map/ppermute | solution.py:462
  63.2 10.3 %collective-permute-start.17 = (bf16[192,384]{1,0:T(8,128)(2,1)S(1)}, bf16[192,384]{1,0:T(8,128)(2,1)S(1)}, u32[]{:S(2)}, u32[]{:S(2)}) collective-permute-start(bf16[192,384]{1,0:T(8,128)(2,1)S(1)} %add_convert_fusion.1.refs_0_), channel_id=1, source_target_pairs={{0,2},{2,0},{1,3},{3,1},{4,6},{6,4},{5,7},{7,5},{8,10},{10,8},{9,1... | collective-permute-start | bytes 442376 | tf_op jit(solution)/shard_map/ppermute | solution.py:462
  65.3 8.2 %collective-permute-start.18 = (bf16[192,384]{1,0:T(8,128)(2,1)S(1)}, bf16[192,384]{1,0:T(8,128)(2,1)S(1)}, u32[]{:S(2)}, u32[]{:S(2)}) collective-permute-start(bf16[192,384]{1,0:T(8,128)(2,1)S(1)} %collective-permute-done.14.refs_1_), channel_id=1, source_target_pairs={{0,2},{2,0},{1,3},{3,1},{4,6},{6,4},{5,7},{7,5},{8,10},{10,8},{9,1... | collective-permute-start | bytes 442376 | tf_op jit(solution)/shard_map/ppermute | solution.py:462
  67.6 5.9 %collective-permute-start.19 = (bf16[192,384]{1,0:T(8,128)(2,1)S(1)}, bf16[192,384]{1,0:T(8,128)(2,1)S(1)}, u32[]{:S(2)}, u32[]{:S(2)}) collective-permute-start(bf16[192,384]{1,0:T(8,128)(2,1)S(1)} %collective-permute-done.15.refs_2_), channel_id=1, source_target_pairs={{0,2},{2,0},{1,3},{3,1},{4,6},{6,4},{5,7},{7,5},{8,10},{10,8},{9,1... | collective-permute-start | bytes 442376 | tf_op jit(solution)/shard_map/ppermute | solution.py:462
  69.4 4.1 %collective-permute-start.20 = (bf16[192,384]{1,0:T(8,128)(2,1)S(1)}, bf16[192,384]{1,0:T(8,128)(2,1)S(1)}, u32[]{:S(2)}, u32[]{:S(2)}) collective-permute-start(bf16[192,384]{1,0:T(8,128)(2,1)S(1)} %collective-permute-done.16.refs_3_), channel_id=1, source_target_pairs={{0,2},{2,0},{1,3},{3,1},{4,6},{6,4},{5,7},{7,5},{8,10},{10,8},{9,1... | collective-permute-start | bytes 442376 | tf_op jit(solution)/shard_map/ppermute | solution.py:462
  (12 other events, 70.9 us)

commit v6 on v5

--- a/solution.py
+++ b/solution.py
@@ -59,21 +59,23 @@
     frames = [plain[:, :1024]] + [
         pltpu.roll(plain, plain.shape[1] - frame * 961, 1)[:, :1024] for frame in (1, 2)
     ]
-    plain = jnp.concatenate(frames, 0)
+    frames = jnp.concatenate(frames, 0)
+    plain = jnp.concatenate([frames, pltpu.roll(frames, 31, 1)], 0)
     high = plain.astype(bf16)
     rest = plain - high.astype(f32)
     middle = rest.astype(bf16)
     low = (rest - middle.astype(f32)).astype(bf16)
-    slot = iota((1, 1024), 1)
-    source = 960 - 62 * (slot // 32 % 16) - 31 * (slot // 512) - slot % 32
-    pick = (iota((1024, 1024), 0) == source).astype(f32).astype(bf16)
-    turned = nn(high, pick) + nn(middle, pick) + nn(low, pick)
+    slot = iota((1, TOKENS), 1)
+    source = 960 - 62 * (slot // 32) - slot % 32
+    pick = (iota((1024, TOKENS), 0) == source).astype(f32).astype(bf16)
+    turned = nn(jnp.concatenate([high, middle, low], 0), pick)
+    turned = turned[:48] + turned[48:96] + turned[96:]
     lane = iota((SIDE, TOKENS), 1)
     for entry in range(HEADS * 3):
         head, frame = divmod(entry, 3)
         first = (2 - frame) * 8 + head
-        even = jnp.broadcast_to(turned[first : first + 1, :TOKENS], (SIDE, TOKENS))
-        odd = jnp.broadcast_to(turned[first : first + 1, TOKENS:], (SIDE, TOKENS))
+        even = jnp.broadcast_to(turned[first : first + 1, :], (SIDE, TOKENS))
+        odd = jnp.broadcast_to(turned[24 + first : 25 + first, :], (SIDE, TOKENS))
         even = pltpu.roll(even, TOKENS - 15, 1, stride=1, stride_axis=0)
         odd = pltpu.roll(odd, 1, 1, stride=1, stride_axis=0)
         rows = jnp.where(lane % 32 < 16, even, odd)
@@ -120,7 +122,7 @@
 def flag_strip(flags, count, span=SIDE):
     total = count * span
     repeat = (iota((SIDE, total), 1) % span == iota((SIDE, total), 0)).astype(f32).astype(bf16)
-    spread = nn(flags[:count, :].astype(f32).astype(bf16), repeat)
+    spread = nn(flags[:count, :].astype(bf16), repeat)
     keep = iota((count, total), 1) // span == iota((count, total), 0)
     strip = jnp.sum(jnp.where(keep, spread, 0.0), 0, keepdims=True)
     return jnp.broadcast_to(strip, (128, total)).astype(bf16)
@@ -185,9 +187,7 @@
     shift,
     core,
     inner_flags,
-    row_flags,
     col_flags,
-    corner_flags,
     gain,
     inner_far,
     rows_far,
@@ -235,12 +235,14 @@
         copy.start()
     onehots = source_onehots(shift[0], shift[1], 1)
     on_diagonal = iota((HALF, HALF), 0) == iota((HALF, HALF), 1)
+    for copy in arrivals[:4]:
+        copy.wait()
     for t in range(2):
         strips = (
-            flag_strip(inner_flags[t], SIDE),
-            flag_strip(row_flags[t], RIM),
-            flag_strip(col_flags[t], SIDE),
-            flag_strip(corner_flags[t], RIM, RIM),
+            flag_strip(inner_flags[t].astype(f32), SIDE),
+            flag_strip(rows[256:272, :SIDE][t * RIM : (t + 1) * RIM], RIM),
+            flag_strip(col_flags[t].astype(f32), SIDE),
+            flag_strip(corner[128:144, :SIDE][t * RIM : (t + 1) * RIM], RIM, RIM),
         )
         marks = sum(nt(hot, strip) for hot, strip in zip(onehots, strips))
         column = jnp.where(marks > 0.5, -1e30, 0.0)
@@ -248,8 +250,6 @@
         own = jnp.where(on_diagonal, 0.0, wide)
         penalty[t * HALF : (t + 1) * HALF, t * HALF : (t + 1) * HALF] = own
         penalty[t * HALF : (t + 1) * HALF, (1 - t) * HALF : (2 - t) * HALF] = wide
-    for copy in arrivals[:4]:
-        copy.wait()
     rolled = []
     for t in range(2):
         parts = (
@@ -428,16 +428,6 @@
     return lax.ppermute(block, axis, [((i - distance) % count, i) for i in range(count)])
 
 
-def passed_across(block, axis, other, distance):
-    count, width = lax.axis_size(axis), lax.axis_size(other)
-    route = [
-        (((i - distance) % count) * width + (j - distance) % width, i * width + j)
-        for i in range(count)
-        for j in range(width)
-    ]
-    return lax.ppermute(block, (axis, other), route)
-
-
 CORE = ("sx", 1)
 GROUPS = ([("sy", 1)], [("ta", 1)], [("sy", 1), ("ta", 1)])
 
@@ -502,16 +492,22 @@
 ):
     width = MODEL_WIDTH
     wide = lambda tokens: ((tokens, width), bf16)
-    rows = passed_along(state_field[:, :RIM].reshape(-1, width), "sy", -1)
-    row_flags = passed_along(outlier_flags, "sy", -1)
+    row_flags = outlier_flags[:, :RIM].reshape(2 * RIM, SIDE).astype(bf16)
+    row_message = jnp.concatenate(
+        [
+            state_field[:, :RIM].reshape(-1, width),
+            jnp.pad(row_flags, ((0, 0), (0, width - SIDE))),
+        ],
+        0,
+    )
+    rows = passed_along(row_message, "sy", -1)
     cols = passed_along(state_field, "sx", -1)
     col_flags = passed_along(outlier_flags, "sx", -1)
-    corner_flags = passed_across(outlier_flags, "sy", "sx", -1)
     cot_rows = cotangent.reshape(TOKENS, width)
     pair_bias = ((6, HALF, HALF), f32)
     blank, *bias_blocks, d_context_t, qkv_weight_t = local_call(
         prepare_kernel,
-        [wide(128)] + [pair_bias] * 3 + [((width, TOKENS), bf16), wide(3 * width)],
+        [wide(144)] + [pair_bias] * 3 + [((width, TOKENS), bf16), wide(3 * width)],
         [position_bias, cot_rows, out_weight, qkv_weight],
         far_in=3,
         far_out=5,
@@ -528,8 +524,14 @@
         micros=3,
         limit=62,
     )
-    corner_message = rows.reshape(2 * RIM, SIDE, width)[:, :RIM].reshape(-1, width) + blank
-    corner = passed_along(corner_message, "sx", -1)
+    corner_message = jnp.concatenate(
+        [
+            rows[: 2 * RIM * SIDE].reshape(2 * RIM, SIDE, width)[:, :RIM].reshape(-1, width),
+            rows[2 * RIM * SIDE :],
+        ],
+        0,
+    )
+    corner = passed_along(corner_message + blank, "sx", -1)
     core = index_bit(*CORE).astype(jnp.int32).reshape(1)
     keep, send, d_rolled, context_t, lower, right = local_call(
         main_kernel,
@@ -539,9 +541,7 @@
             window_shift,
             core,
             outlier_flags,
-            row_flags,
             col_flags,
-            corner_flags,
             layer_norm_gain,
             state_field.reshape(TOKENS, width),
             rows,
@@ -560,9 +560,9 @@
         scratch=[
             ((TOKENS, TOKENS), f32),
             wide(TOKENS),
-            wide(HALF),
+            wide(HALF + 16),
             wide(TOKENS),
-            wide(128),
+            wide(144),
             ((width, 3 * width), bf16),
             wide(3 * width),
             ((width, TOKENS), bf16),

time: 77 us -> 74.6 us (0.969)
  starting transfers between devices: 22.5 us -> 20.6 us
  waiting for transfers between devices: 20.8 us -> 19.5 us
    ppermute x8 -> x7, starting transfers between devices: 11.4 us -> 7.84 us  [passed_along(): lax.ppermute(block, axis, [((i - distance) % count, i) for i in range(cou...]
    ppermute x1 -> x0, waiting for transfers between devices: 2.32 us -> none  [passed_across(): return lax.ppermute(block, (axis, other), route)]
    ppermute x12, starting transfers between devices: 11.1 us -> 12.7 us  [swapped(): return lax.ppermute(block, axes, route)]
    ppermute x12, waiting for transfers between devices: 14.8 us -> 15.8 us  [swapped(): return lax.ppermute(block, axes, route)]
    ppermute x8 -> x7, waiting for transfers between devices: 3.66 us -> 3.65 us  [passed_along(): lax.ppermute(block, axis, [((i - distance) % count, i) for i in range(cou...]
  transfers between devices with their start and end apart: 21 -> 19, of which waited for: 10 -> 9; matrix products, arithmetic and copies ran while one was open for 3% -> 4% of each run, Pallas kernels for 12% -> 12%
where the time goes in v6:
time: 74.6 us; the launch traced here: 74.2 us
  Pallas kernels  28.1 us (38%)
  starting transfers between devices  20.6 us (28%)
  waiting for transfers between devices  19.5 us (26%)
  other arithmetic  3.14 us (4%)
  local copies, waits for them, and re-layouts  1.86 us (2%)
  between operations  1.05 us (1%)
    pallas_call x4, Pallas kernels, local_call(): pl.pallas_call(kernel, out_shape=[jax.ShapeDtypeStruct(shape, dtype) for...  28.1 us
    ppermute x12, waiting for transfers between devices, swapped(): return lax.ppermute(block, axes, route)  15.8 us
    ppermute x12, starting transfers between devices, swapped(): return lax.ppermute(block, axes, route)  12.7 us
    ppermute x7, starting transfers between devices, passed_along(): lax.ppermute(block, axis, [((i - distance) % count, i) for i in range(cou...  7.84 us
    ppermute x7, waiting for transfers between devices, passed_along(): lax.ppermute(block, axis, [((i - distance) % count, i) for i in range(cou...  3.65 us
  transfers between devices with their start and end apart: 19, of which 9 were waited for; matrix products, arithmetic and copies ran while one was open for 4% of the time, Pallas kernels for 12%

profile of v6, /device:TPU:1, one launch (start us, length us, event | category | flops | bytes accessed | tf_op | source)
XLA Modules:
  0.0 74.2 jit_solution(13713555770367468456)
XLA Ops:
  0.8 0.9 %slice.19 = bf16[2,8,16,384]{3,2,1,0:T(8,128)(2,1)S(1)} slice(bf16[2,16,16,384]{3,2,1,0:T(8,128)(2,1)} %param.8), slice={[0:2], [0:8], [0:16], [0:384]} | slice | bytes 393216 | tf_op jit(solution)/shard_map/slice | solution.py:498
  2.4 4.8 %collective-permute-start.1 = (bf16[272,384]{1,0:T(8,128)(2,1)S(1)}, bf16[272,384]{1,0:T(8,128)(2,1)S(1)}, u32[]{:S(2)}, u32[]{:S(2)}) collective-permute-start(bf16[272,384]{1,0:T(8,128)(2,1)S(1)} %fusion.1), channel_id=1, source_target_pairs={{4,0},{8,4},{12,8},{0,12},{5,1},{9,5},{13,9},{1,13},{6,2},{10,6},{... | collective-permute-start | bytes 626696 | tf_op jit(solution)/shard_map/ppermute | solution.py:428
  7.3 6.0 %shard_map.119 = (bf16[144,384]{1,0:T(8,128)(2,1)}, f32[6,256,256]{2,1,0:T(8,128)}, f32[6,256,256]{2,1,0:T(8,128)}, f32[6,256,256]{2,1,0:T(8,128)}, bf16[384,512]{1,0:T(8,128)(2,1)}, /*index=5*/bf16[1152,384]{1,0:T(8,128)(2,1)}) custom-call(f32[6,2883]{1,0:T(8,128)} %position_bias.1, bf16[512,384]{1,0:T(8,128)(2,1)} %bitcast.20, ...), custom_call_target="tpu_custom_call" | custom-call | flops 3000000000 | bytes 1000000 | tf_op jit(solution)/shard_map/pallas_call | solution.py:411
  13.4 1.0 %maximum_add_fusion = bf16[144,384]{1,0:T(8,128)(2,1)S(1)} fusion(bf16[144,384]{1,0:T(8,128)(2,1)} %get-tuple-element.22, bf16[16,384]{1,0:T(8,128)(2,1)S(1)} %slice.28, bf16[128,384]{1,0:T(8,128)(2,1)S(1)} %slice_bitcast_fusion.1), kind=kLoop, calls=%fused_computation.7 | loop fusion | flops 331776 | bytes 331776 | tf_op jit(solution)/shard_map/add | solution.py:534
  14.9 1.0 %collective-permute-done.col_flags = s32[2,16,16]{2,1,0:T(8,128)S(1)} collective-permute-done((s32[2,16,16]{2,1,0:T(8,128)S(1)}, s32[2,16,16]{2,1,0:T(8,128)S(1)}, u32[]{:S(2)}, u32[]{:S(2)}) %collective-permute-start) | collective-permute-done | bytes 2080 | tf_op jit(solution)/shard_map/ppermute | solution.py:428
  16.7 16.5 %shard_map.120 = (bf16[768,384]{1,0:T(8,128)(2,1)}, bf16[768,384]{1,0:T(8,128)(2,1)}, bf16[512,384]{1,0:T(8,128)(2,1)}, bf16[384,512]{1,0:T(8,128)(2,1)}, bf16[2...) custom-call(s32[2]{0:T(128)} %shift.3, s32[1]{0:T(128)} %bitcast.core, s32[2,16,16]{2,1,0:T(8,128)} %inner_flags.1, ...), custom_call_target="tpu_custom_call" | custom-call | flops 12000000000 | bytes 1000000 | tf_op jit(solution)/shard_map/pallas_call | solution.py:411
  33.5 2.0 %collective-permute-done.7 = bf16[768,384]{1,0:T(8,128)(2,1)S(1)} collective-permute-done((bf16[768,384]{1,0:T(8,128)(2,1)}, bf16[768,384]{1,0:T(8,128)(2,1)S(1)}, u32[]{:S(2)}, u32[]{:S(2)}) %collective-permute-start.7) | collective-permute-done | bytes 589856 | tf_op jit(solution)/shard_map/ppermute | solution.py:452
  35.4 1.2 %add_convert_fusion = bf16[768,384]{1,0:T(8,128)(2,1)S(1)} fusion(bf16[768,384]{1,0:T(8,128)(2,1)S(1)} %collective-permute-done.7, bf16[768,384]{1,0:T(8,128)(2,1)} %get-tuple-element.34), kind=kLoop, calls=%fused_computation | loop fusion | flops 1179648 | bytes 1769472 | tf_op jit(solution)/shard_map/convert_element_type | solution.py:456
  37.0 2.2 %collective-permute-start.8 = (bf16[192,384]{1,0:T(8,128)(2,1)S(1)}, bf16[192,384]{1,0:T(8,128)(2,1)S(1)}, u32[]{:S(2)}, u32[]{:S(2)}) collective-permute-start(bf16[192,384]{1,0:T(8,128)(2,1)S(1)} %get-tuple-element.39), channel_id=1, source_target_pairs={{0,4},{4,0},{8,12},{12,8},{1,5},{5,1},{9,13},{13,9},{2,6},{6,2},{1... | collective-permute-start | bytes 442376 | tf_op jit(solution)/shard_map/ppermute | solution.py:452
  39.6 1.1 %collective-permute-start.5 = (bf16[256,384]{1,0:T(8,128)(2,1)S(1)}, bf16[256,384]{1,0:T(8,128)(2,1)S(1)}, u32[]{:S(2)}, u32[]{:S(2)}) collective-permute-start(bf16[256,384]{1,0:T(8,128)(2,1)S(1)} %copy-done.9), channel_id=1, source_target_pairs={{2,0},{0,2},{3,1},{1,3},{6,4},{4,6},{7,5},{5,7},{10,8},{8,10},{11,... | collective-permute-start | bytes 589832 | tf_op jit(solution)/shard_map/ppermute | solution.py:428
  40.7 2.3 %collective-permute-done.10 = bf16[192,384]{1,0:T(8,128)(2,1)S(1)} collective-permute-done((bf16[192,384]{1,0:T(8,128)(2,1)S(1)}, bf16[192,384]{1,0:T(8,128)(2,1)S(1)}, u32[]{:S(2)}, u32[]{:S(2)}) %collective-permute-start.10) | collective-permute-done | bytes 147488 | tf_op jit(solution)/shard_map/ppermute | solution.py:452
  42.9 3.2 %collective-permute-done.8 = bf16[192,384]{1,0:T(8,128)(2,1)S(1)} collective-permute-done((bf16[192,384]{1,0:T(8,128)(2,1)S(1)}, bf16[192,384]{1,0:T(8,128)(2,1)S(1)}, u32[]{:S(2)}, u32[]{:S(2)}) %collective-permute-start.8) | collective-permute-done | bytes 147488 | tf_op jit(solution)/shard_map/ppermute | solution.py:452
  46.7 2.0 %collective-permute-start.11 = (bf16[192,384]{1,0:T(8,128)(2,1)S(1)}, bf16[192,384]{1,0:T(8,128)(2,1)S(1)}, u32[]{:S(2)}, u32[]{:S(2)}) collective-permute-start(bf16[192,384]{1,0:T(8,128)(2,1)S(1)} %add_convert_fusion.2), channel_id=1, source_target_pairs={{0,8},{4,12},{8,0},{12,4},{1,9},{5,13},{9,1},{13,5},{2,10},{6,14},... | collective-permute-start | bytes 442376 | tf_op jit(solution)/shard_map/ppermute | solution.py:452
  48.7 2.7 %collective-permute-done.4 = bf16[256,384]{1,0:T(8,128)(2,1)S(1)} collective-permute-done((bf16[256,384]{1,0:T(8,128)(2,1)S(1)}, bf16[256,384]{1,0:T(8,128)(2,1)S(1)}, u32[]{:S(2)}, u32[]{:S(2)}) %collective-permute-start.4) | collective-permute-done | bytes 196640 | tf_op jit(solution)/shard_map/ppermute | solution.py:428
  51.4 1.1 %collective-permute-start.6 = (bf16[128,384]{1,0:T(8,128)(2,1)S(1)}, bf16[128,384]{1,0:T(8,128)(2,1)S(1)}, u32[]{:S(2)}, u32[]{:S(2)}) collective-permute-start(bf16[128,384]{1,0:T(8,128)(2,1)S(1)} %slice_bitcast_fusion), channel_id=1, source_target_pairs={{2,0},{0,2},{3,1},{1,3},{6,4},{4,6},{7,5},{5,7},{10,8},{8,10},{11,... | collective-permute-start | bytes 294920 | tf_op jit(solution)/shard_map/ppermute | solution.py:428
  52.5 5.4 %collective-permute-done.11 = bf16[192,384]{1,0:T(8,128)(2,1)S(1)} collective-permute-done((bf16[192,384]{1,0:T(8,128)(2,1)S(1)}, bf16[192,384]{1,0:T(8,128)(2,1)S(1)}, u32[]{:S(2)}, u32[]{:S(2)}) %collective-permute-start.11) | collective-permute-done | bytes 147488 | tf_op jit(solution)/shard_map/ppermute | solution.py:452
  58.0 1.3 %collective-permute-start.13 = (bf16[192,384]{1,0:T(8,128)(2,1)S(1)}, bf16[192,384]{1,0:T(8,128)(2,1)S(1)}, u32[]{:S(2)}, u32[]{:S(2)}) collective-permute-start(bf16[192,384]{1,0:T(8,128)(2,1)S(1)} %add_convert_fusion.1.refs_0_), channel_id=1, source_target_pairs={{0,1},{1,0},{2,3},{3,2},{4,5},{5,4},{6,7},{7,6},{8,9},{9,8},{10,11... | collective-permute-start | bytes 442376 | tf_op jit(solution)/shard_map/ppermute | solution.py:452
  59.3 1.4 %collective-permute-start.14 = (bf16[192,384]{1,0:T(8,128)(2,1)S(1)}, bf16[192,384]{1,0:T(8,128)(2,1)S(1)}, u32[]{:S(2)}, u32[]{:S(2)}) collective-permute-start(bf16[192,384]{1,0:T(8,128)(2,1)S(1)} %add_convert_fusion.1.refs_0_), channel_id=1, source_target_pairs={{0,5},{1,4},{4,1},{5,0},{8,13},{9,12},{12,9},{13,8},{2,7},{3,6},{6... | collective-permute-start | bytes 442376 | tf_op jit(solution)/shard_map/ppermute | solution.py:452
  60.8 1.4 %collective-permute-start.15 = (bf16[192,384]{1,0:T(8,128)(2,1)S(1)}, bf16[192,384]{1,0:T(8,128)(2,1)S(1)}, u32[]{:S(2)}, u32[]{:S(2)}) collective-permute-start(bf16[192,384]{1,0:T(8,128)(2,1)S(1)} %add_convert_fusion.1.refs_0_), channel_id=1, source_target_pairs={{0,2},{2,0},{1,3},{3,1},{4,6},{6,4},{5,7},{7,5},{8,10},{10,8},{9,1... | collective-permute-start | bytes 442376 | tf_op jit(solution)/shard_map/ppermute | solution.py:452
  62.9 2.3 %collective-permute-start.16 = (bf16[192,384]{1,0:T(8,128)(2,1)S(1)}, bf16[192,384]{1,0:T(8,128)(2,1)S(1)}, u32[]{:S(2)}, u32[]{:S(2)}) collective-permute-start(bf16[192,384]{1,0:T(8,128)(2,1)S(1)} %collective-permute-done.12.refs_1_), channel_id=1, source_target_pairs={{0,2},{2,0},{1,3},{3,1},{4,6},{6,4},{5,7},{7,5},{8,10},{10,8},{9,1... | collective-permute-start | bytes 442376 | tf_op jit(solution)/shard_map/ppermute | solution.py:452
  65.2 1.8 %collective-permute-done.14.refs_3_ = bf16[192,384]{1,0:T(8,128)(2,1)S(1)} collective-permute-done((bf16[192,384]{1,0:T(8,128)(2,1)S(1)}, bf16[192,384]{1,0:T(8,128)(2,1)S(1)}, u32[]{:S(2)}, u32[]{:S(2)}) %collective-permute-start.14) | collective-permute-done | bytes 147488 | tf_op jit(solution)/shard_map/ppermute | solution.py:452
  67.0 1.3 %collective-permute-start.18 = (bf16[192,384]{1,0:T(8,128)(2,1)S(1)}, bf16[192,384]{1,0:T(8,128)(2,1)S(1)}, u32[]{:S(2)}, u32[]{:S(2)}) collective-permute-start(bf16[192,384]{1,0:T(8,128)(2,1)S(1)} %collective-permute-done.14.refs_3_), channel_id=1, source_target_pairs={{0,2},{2,0},{1,3},{3,1},{4,6},{6,4},{5,7},{7,5},{8,10},{10,8},{9,1... | collective-permute-start | bytes 442376 | tf_op jit(solution)/shard_map/ppermute | solution.py:452
  68.4 2.7 %shard_map.121 = (bf16[512,384]{1,0:T(8,128)(2,1)}, bf16[512,384]{1,0:T(8,128)(2,1)}) custom-call(s32[2]{0:T(128)S(1)} %copy-done.3, bf16[640,384]{1,0:T(8,128)(2,1)S(1)} %pad_maximum_fusion.halo, bf16[384,384]{1,0:T(8,128)(2,1)S(1)} %copy-done.1, bf16[512,384]{1,0:T(8,128)(2,1)S(1)} %copy-done.4, bf16[384,512]{1,0:T(8,128)(2,1)S(1)} %copy-done.5), custom_call_target="tpu_custom_call" | custom-call | flops 2000000000 | bytes 1000000 | tf_op jit(solution)/shard_map/pallas_call | solution.py:411
  71.1 2.9 %shard_map.122 = (f32[384]{0:T(512)}, f32[384,1152]{1,0:T(8,128)}, f32[384,384]{1,0:T(8,128)}) custom-call(s32[2]{0:T(128)S(1)} %pad_add_fusion.place, bf16[192,384]{1,0:T(8,128)(2,1)S(1)} %add_convert_fusion.1.refs_0_, bf16[192,384]{1,0:T(8,128)(2,1)S(1)} %collective-permute-done.12.refs_1_, bf16[192,384]{1,0:T(8,128)(2,1)S(1)} %collective-permute-done.13.refs_2_, ...), custom_call_target="tpu_custom_call" | custom-call | flops 1000000000 | bytes 1000000 | tf_op jit(solution)/shard_map/pallas_call | solution.py:411
  (58 shorter events, 4.8 us)
Async XLA Ops:
  0.6 15.3 %collective-permute-start.2 = (bf16[2,16,16,384]{3,2,1,0:T(8,128)(2,1)}, bf16[2,16,16,384]{3,2,1,0:T(8,128)(2,1)S(1)}, u32[]{:S(2)}, u32[]{:S(2)}) collective-permute-start(bf16[2,16,16,384]{3,2,1,0:T(8,128)(2,1)} %param.8), channel_id=1, source_target_pairs={{2,0},{0,2},{3,1},{1,3},{6,4},{4,6},{7,5},{5,7},{10,8},{8,10},{11,... | collective-permute-start | bytes 1179656 | tf_op jit(solution)/shard_map/ppermute | solution.py:428
  2.4 10.8 %collective-permute-start.1 = (bf16[272,384]{1,0:T(8,128)(2,1)S(1)}, bf16[272,384]{1,0:T(8,128)(2,1)S(1)}, u32[]{:S(2)}, u32[]{:S(2)}) collective-permute-start(bf16[272,384]{1,0:T(8,128)(2,1)S(1)} %fusion.1), channel_id=1, source_target_pairs={{4,0},{8,4},{12,8},{0,12},{5,1},{9,5},{13,9},{1,13},{6,2},{10,6},{... | collective-permute-start | bytes 626696 | tf_op jit(solution)/shard_map/ppermute | solution.py:428
  7.3 7.4 %copy-start.7 = (s32[2,16,16]{2,1,0:T(8,128)S(1)}, s32[2,16,16]{2,1,0:T(8,128)}, u32[]{:S(2)}) copy-start(s32[2,16,16]{2,1,0:T(8,128)} %inner_flags.1) | copy-start | bytes 6148
  14.3 1.6 %collective-permute-start.3 = (bf16[144,384]{1,0:T(8,128)(2,1)S(1)}, bf16[144,384]{1,0:T(8,128)(2,1)S(1)}, u32[]{:S(2)}, u32[]{:S(2)}) collective-permute-start(bf16[144,384]{1,0:T(8,128)(2,1)S(1)} %maximum_add_fusion), channel_id=1, source_target_pairs={{2,0},{0,2},{3,1},{1,3},{6,4},{4,6},{7,5},{5,7},{10,8},{8,10},{11,... | collective-permute-start | bytes 331784 | tf_op jit(solution)/shard_map/ppermute | solution.py:428
  14.7 1.2 %collective-permute-start = (s32[2,16,16]{2,1,0:T(8,128)S(1)}, s32[2,16,16]{2,1,0:T(8,128)S(1)}, u32[]{:S(2)}, u32[]{:S(2)}) collective-permute-start(s32[2,16,16]{2,1,0:T(8,128)S(1)} %copy-done.7), channel_id=1, source_target_pairs={{2,0},{0,2},{3,1},{1,3},{6,4},{4,6},{7,5},{5,7},{10,8},{8,10},{11,... | collective-permute-start | bytes 6152 | tf_op jit(solution)/shard_map/ppermute | solution.py:428
  33.2 2.3 %collective-permute-start.7 = (bf16[768,384]{1,0:T(8,128)(2,1)}, bf16[768,384]{1,0:T(8,128)(2,1)S(1)}, u32[]{:S(2)}, u32[]{:S(2)}) collective-permute-start(bf16[768,384]{1,0:T(8,128)(2,1)} %get-tuple-element.35), channel_id=1, source_target_pairs={{0,2},{2,0},{1,3},{3,1},{4,6},{6,4},{5,7},{7,5},{8,10},{10,8},{9,1... | collective-permute-start | bytes 1769480 | tf_op jit(solution)/shard_map/ppermute | solution.py:452
  36.6 31.7 %copy-start.1 = (bf16[384,384]{1,0:T(8,128)(2,1)S(1)}, bf16[384,384]{1,0:T(8,128)(2,1)}, u32[]{:S(2)}) copy-start(bf16[384,384]{1,0:T(8,128)(2,1)} %out_weight.1) | copy-start | bytes 884740
  36.7 31.7 %copy-start.3 = (s32[2]{0:T(128)S(1)}, s32[2]{0:T(128)}, u32[]{:S(2)}) copy-start(s32[2]{0:T(128)} %shift.3) | copy-start | bytes 28
  36.7 31.7 %copy-start.4 = (bf16[512,384]{1,0:T(8,128)(2,1)S(1)}, bf16[512,384]{1,0:T(8,128)(2,1)}, u32[]{:S(2)}) copy-start(bf16[512,384]{1,0:T(8,128)(2,1)} %get-tuple-element.30.kept_far) | copy-start | bytes 1179652
  36.7 31.7 %copy-start.5 = (bf16[384,512]{1,0:T(8,128)(2,1)S(1)}, bf16[384,512]{1,0:T(8,128)(2,1)}, u32[]{:S(2)}) copy-start(bf16[384,512]{1,0:T(8,128)(2,1)} %get-tuple-element.31.context_far) | copy-start | bytes 1179652
  36.8 6.2 %collective-permute-start.10 = (bf16[192,384]{1,0:T(8,128)(2,1)S(1)}, bf16[192,384]{1,0:T(8,128)(2,1)S(1)}, u32[]{:S(2)}, u32[]{:S(2)}) collective-permute-start(bf16[192,384]{1,0:T(8,128)(2,1)S(1)} %get-tuple-element.40), channel_id=1, source_target_pairs={{0,5},{1,4},{4,1},{5,0},{8,13},{9,12},{12,9},{13,8},{2,7},{3,6},{6... | collective-permute-start | bytes 442376 | tf_op jit(solution)/shard_map/ppermute | solution.py:452
  37.0 9.2 %collective-permute-start.8 = (bf16[192,384]{1,0:T(8,128)(2,1)S(1)}, bf16[192,384]{1,0:T(8,128)(2,1)S(1)}, u32[]{:S(2)}, u32[]{:S(2)}) collective-permute-start(bf16[192,384]{1,0:T(8,128)(2,1)S(1)} %get-tuple-element.39), channel_id=1, source_target_pairs={{0,4},{4,0},{8,12},{12,8},{1,5},{5,1},{9,13},{13,9},{2,6},{6,2},{1... | collective-permute-start | bytes 442376 | tf_op jit(solution)/shard_map/ppermute | solution.py:452
  39.2 7.4 %collective-permute-start.9 = (bf16[192,384]{1,0:T(8,128)(2,1)S(1)}, bf16[192,384]{1,0:T(8,128)(2,1)S(1)}, u32[]{:S(2)}, u32[]{:S(2)}) collective-permute-start(bf16[192,384]{1,0:T(8,128)(2,1)S(1)} %get-tuple-element.41), channel_id=1, source_target_pairs={{0,1},{1,0},{2,3},{3,2},{4,5},{5,4},{6,7},{7,6},{8,9},{9,8},{10,11... | collective-permute-start | bytes 442376 | tf_op jit(solution)/shard_map/ppermute | solution.py:452
  39.5 11.9 %collective-permute-start.4 = (bf16[256,384]{1,0:T(8,128)(2,1)S(1)}, bf16[256,384]{1,0:T(8,128)(2,1)S(1)}, u32[]{:S(2)}, u32[]{:S(2)}) collective-permute-start(bf16[256,384]{1,0:T(8,128)(2,1)S(1)} %copy-done.10), channel_id=1, source_target_pairs={{12,0},{0,4},{4,8},{8,12},{13,1},{1,5},{5,9},{9,13},{14,2},{2,6},{... | collective-permute-start | bytes 589832 | tf_op jit(solution)/shard_map/ppermute | solution.py:428
  39.6 21.1 %collective-permute-start.5 = (bf16[256,384]{1,0:T(8,128)(2,1)S(1)}, bf16[256,384]{1,0:T(8,128)(2,1)S(1)}, u32[]{:S(2)}, u32[]{:S(2)}) collective-permute-start(bf16[256,384]{1,0:T(8,128)(2,1)S(1)} %copy-done.9), channel_id=1, source_target_pairs={{2,0},{0,2},{3,1},{1,3},{6,4},{4,6},{7,5},{5,7},{10,8},{8,10},{11,... | collective-permute-start | bytes 589832 | tf_op jit(solution)/shard_map/ppermute | solution.py:428
  46.7 11.2 %collective-permute-start.11 = (bf16[192,384]{1,0:T(8,128)(2,1)S(1)}, bf16[192,384]{1,0:T(8,128)(2,1)S(1)}, u32[]{:S(2)}, u32[]{:S(2)}) collective-permute-start(bf16[192,384]{1,0:T(8,128)(2,1)S(1)} %add_convert_fusion.2), channel_id=1, source_target_pairs={{0,8},{4,12},{8,0},{12,4},{1,9},{5,13},{9,1},{13,5},{2,10},{6,14},... | collective-permute-start | bytes 442376 | tf_op jit(solution)/shard_map/ppermute | solution.py:452
  51.4 9.3 %collective-permute-start.6 = (bf16[128,384]{1,0:T(8,128)(2,1)S(1)}, bf16[128,384]{1,0:T(8,128)(2,1)S(1)}, u32[]{:S(2)}, u32[]{:S(2)}) collective-permute-start(bf16[128,384]{1,0:T(8,128)(2,1)S(1)} %slice_bitcast_fusion), channel_id=1, source_target_pairs={{2,0},{0,2},{3,1},{1,3},{6,4},{4,6},{7,5},{5,7},{10,8},{8,10},{11,... | collective-permute-start | bytes 294920 | tf_op jit(solution)/shard_map/ppermute | solution.py:428
  57.9 5.0 %collective-permute-start.12 = (bf16[192,384]{1,0:T(8,128)(2,1)S(1)}, bf16[192,384]{1,0:T(8,128)(2,1)S(1)}, u32[]{:S(2)}, u32[]{:S(2)}) collective-permute-start(bf16[192,384]{1,0:T(8,128)(2,1)S(1)} %add_convert_fusion.1.refs_0_), channel_id=1, source_target_pairs={{0,4},{4,0},{8,12},{12,8},{1,5},{5,1},{9,13},{13,9},{2,6},{6,2},{1... | collective-permute-start | bytes 442376 | tf_op jit(solution)/shard_map/ppermute | solution.py:452
  58.0 7.2 %collective-permute-start.13 = (bf16[192,384]{1,0:T(8,128)(2,1)S(1)}, bf16[192,384]{1,0:T(8,128)(2,1)S(1)}, u32[]{:S(2)}, u32[]{:S(2)}) collective-permute-start(bf16[192,384]{1,0:T(8,128)(2,1)S(1)} %add_convert_fusion.1.refs_0_), channel_id=1, source_target_pairs={{0,1},{1,0},{2,3},{3,2},{4,5},{5,4},{6,7},{7,6},{8,9},{9,8},{10,11... | collective-permute-start | bytes 442376 | tf_op jit(solution)/shard_map/ppermute | solution.py:452
  59.3 7.7 %collective-permute-start.14 = (bf16[192,384]{1,0:T(8,128)(2,1)S(1)}, bf16[192,384]{1,0:T(8,128)(2,1)S(1)}, u32[]{:S(2)}, u32[]{:S(2)}) collective-permute-start(bf16[192,384]{1,0:T(8,128)(2,1)S(1)} %add_convert_fusion.1.refs_0_), channel_id=1, source_target_pairs={{0,5},{1,4},{4,1},{5,0},{8,13},{9,12},{12,9},{13,8},{2,7},{3,6},{6... | collective-permute-start | bytes 442376 | tf_op jit(solution)/shard_map/ppermute | solution.py:452
  60.8 10.3 %collective-permute-start.15 = (bf16[192,384]{1,0:T(8,128)(2,1)S(1)}, bf16[192,384]{1,0:T(8,128)(2,1)S(1)}, u32[]{:S(2)}, u32[]{:S(2)}) collective-permute-start(bf16[192,384]{1,0:T(8,128)(2,1)S(1)} %add_convert_fusion.1.refs_0_), channel_id=1, source_target_pairs={{0,2},{2,0},{1,3},{3,1},{4,6},{6,4},{5,7},{7,5},{8,10},{10,8},{9,1... | collective-permute-start | bytes 442376 | tf_op jit(solution)/shard_map/ppermute | solution.py:452
  62.9 8.2 %collective-permute-start.16 = (bf16[192,384]{1,0:T(8,128)(2,1)S(1)}, bf16[192,384]{1,0:T(8,128)(2,1)S(1)}, u32[]{:S(2)}, u32[]{:S(2)}) collective-permute-start(bf16[192,384]{1,0:T(8,128)(2,1)S(1)} %collective-permute-done.12.refs_1_), channel_id=1, source_target_pairs={{0,2},{2,0},{1,3},{3,1},{4,6},{6,4},{5,7},{7,5},{8,10},{10,8},{9,1... | collective-permute-start | bytes 442376 | tf_op jit(solution)/shard_map/ppermute | solution.py:452
  65.2 5.9 %collective-permute-start.17 = (bf16[192,384]{1,0:T(8,128)(2,1)S(1)}, bf16[192,384]{1,0:T(8,128)(2,1)S(1)}, u32[]{:S(2)}, u32[]{:S(2)}) collective-permute-start(bf16[192,384]{1,0:T(8,128)(2,1)S(1)} %collective-permute-done.13.refs_2_), channel_id=1, source_target_pairs={{0,2},{2,0},{1,3},{3,1},{4,6},{6,4},{5,7},{7,5},{8,10},{10,8},{9,1... | collective-permute-start | bytes 442376 | tf_op jit(solution)/shard_map/ppermute | solution.py:452
  67.0 4.1 %collective-permute-start.18 = (bf16[192,384]{1,0:T(8,128)(2,1)S(1)}, bf16[192,384]{1,0:T(8,128)(2,1)S(1)}, u32[]{:S(2)}, u32[]{:S(2)}) collective-permute-start(bf16[192,384]{1,0:T(8,128)(2,1)S(1)} %collective-permute-done.14.refs_3_), channel_id=1, source_target_pairs={{0,2},{2,0},{1,3},{3,1},{4,6},{6,4},{5,7},{7,5},{8,10},{10,8},{9,1... | collective-permute-start | bytes 442376 | tf_op jit(solution)/shard_map/ppermute | solution.py:452
  (8 other events, 23.0 us)

commit v7 on v6

--- a/solution.py
+++ b/solution.py
@@ -458,11 +458,17 @@
 
 def sum_quarter(keep, send):
     block = add_up(keep, swapped(send, CORE))
-    share = block.shape[0] // 4
-    mine = quarter_index()
-    pick = lambda place: lax.dynamic_slice_in_dim(block, place * share, share, 0)
-    arrived = [swapped(pick(mine ^ k), *GROUPS[k - 1]) for k in (1, 2, 3)]
-    return add_up(pick(mine), *arrived)
+    rows, columns = lax.axis_size("sy"), lax.axis_size("ta")
+    squares = [
+        [(i + di) * columns + j + dj for dj in range(2) for di in range(2)]
+        for i in range(0, rows, 2)
+        for j in range(0, columns, 2)
+    ]
+    shares = block.reshape(4, block.shape[0] // 4, block.shape[1])
+    arrived = lax.all_to_all(
+        shares, ("sy", "ta"), split_axis=0, concat_axis=0, axis_index_groups=squares
+    )
+    return add_up(*arrived)
 
 
 def sum_rest(quarter):

time: 74.6 us -> 79.3 us (1.063)
  starting transfers between devices: 20.6 us -> 24.4 us
  other arithmetic: 3.14 us -> 4.01 us
    ppermute x12 -> x9, waiting for transfers between devices: 15.8 us -> 8.4 us  [swapped(): return lax.ppermute(block, axes, route)]
    all_to_all x0 -> x1, waiting for transfers between devices: none -> 6.26 us  [sum_quarter(): lax.all_to_all(shares, ('sy', 'ta'), split_axis=0, concat_axis=0, axis_in...]
    all_to_all x0 -> x1, starting transfers between devices: none -> 3.48 us  [sum_quarter(): lax.all_to_all(shares, ('sy', 'ta'), split_axis=0, concat_axis=0, axis_in...]
    ppermute x7, starting transfers between devices: 7.84 us -> 10.2 us  [passed_along(): lax.ppermute(block, axis, [((i - distance) % count, i) for i in range(cou...]
    ppermute x12 -> x9, starting transfers between devices: 12.7 us -> 10.7 us  [swapped(): return lax.ppermute(block, axes, route)]
    ppermute x7, waiting for transfers between devices: 3.65 us -> 4.81 us  [passed_along(): lax.ppermute(block, axis, [((i - distance) % count, i) for i in range(cou...]
    convert_element_type x3 -> x2, other arithmetic: 1.33 us -> 2.12 us  [add_up(): return sum((piece.astype(f32) for piece in pieces)).astype(bf16)]
  transfers between devices with their start and end apart: 19 -> 17, of which waited for: 9 -> 6; matrix products, arithmetic and copies ran while one was open for 4% -> 4% of each run, Pallas kernels for 12% -> 11%
where the time goes in v7:
time: 79.3 us; the launch traced here: 78.8 us
  Pallas kernels  28.1 us (35%)
  starting transfers between devices  24.4 us (31%)
  waiting for transfers between devices  19.5 us (25%)
  other arithmetic  4.01 us (5%)
  local copies, waits for them, and re-layouts  1.8 us (2%)
  between operations  1.06 us (1%)
    pallas_call x4, Pallas kernels, local_call(): pl.pallas_call(kernel, out_shape=[jax.ShapeDtypeStruct(shape, dtype) for...  28.1 us
    ppermute x9, starting transfers between devices, swapped(): return lax.ppermute(block, axes, route)  10.7 us
    ppermute x7, starting transfers between devices, passed_along(): lax.ppermute(block, axis, [((i - distance) % count, i) for i in range(cou...  10.2 us
    ppermute x9, waiting for transfers between devices, swapped(): return lax.ppermute(block, axes, route)  8.4 us
    all_to_all x1, waiting for transfers between devices, sum_quarter(): lax.all_to_all(shares, ('sy', 'ta'), split_axis=0, concat_axis=0, axis_in...  6.26 us
    ppermute x7, waiting for transfers between devices, passed_along(): lax.ppermute(block, axis, [((i - distance) % count, i) for i in range(cou...  4.81 us
    all_to_all x1, starting transfers between devices, sum_quarter(): lax.all_to_all(shares, ('sy', 'ta'), split_axis=0, concat_axis=0, axis_in...  3.48 us
    convert_element_type x2, other arithmetic, add_up(): return sum((piece.astype(f32) for piece in pieces)).astype(bf16)  2.12 us
  transfers between devices with their start and end apart: 17, of which 6 were waited for; matrix products, arithmetic and copies ran while one was open for 4% of the time, Pallas kernels for 11%

profile of v7, /device:TPU:1, one launch (start us, length us, event | category | flops | bytes accessed | tf_op | source)
XLA Modules:
  0.0 78.8 jit_solution(891964027186482671)
XLA Ops:
  0.8 0.9 %slice.19 = bf16[2,8,16,384]{3,2,1,0:T(8,128)(2,1)S(1)} slice(bf16[2,16,16,384]{3,2,1,0:T(8,128)(2,1)} %param.8), slice={[0:2], [0:8], [0:16], [0:384]} | slice | bytes 393216 | tf_op jit(solution)/shard_map/slice | solution.py:504
  2.4 4.8 %collective-permute-start.1 = (bf16[272,384]{1,0:T(8,128)(2,1)S(1)}, bf16[272,384]{1,0:T(8,128)(2,1)S(1)}, u32[]{:S(2)}, u32[]{:S(2)}) collective-permute-start(bf16[272,384]{1,0:T(8,128)(2,1)S(1)} %fusion.1), channel_id=1, source_target_pairs={{4,0},{8,4},{12,8},{0,12},{5,1},{9,5},{13,9},{1,13},{6,2},{10,6},{... | collective-permute-start | bytes 626696 | tf_op jit(solution)/shard_map/ppermute | solution.py:428
  7.3 6.0 %shard_map.119 = (bf16[144,384]{1,0:T(8,128)(2,1)}, f32[6,256,256]{2,1,0:T(8,128)}, f32[6,256,256]{2,1,0:T(8,128)}, f32[6,256,256]{2,1,0:T(8,128)}, bf16[384,512]{1,0:T(8,128)(2,1)}, /*index=5*/bf16[1152,384]{1,0:T(8,128)(2,1)}) custom-call(f32[6,2883]{1,0:T(8,128)} %position_bias.1, bf16[512,384]{1,0:T(8,128)(2,1)} %bitcast.25, ...), custom_call_target="tpu_custom_call" | custom-call | flops 3000000000 | bytes 1000000 | tf_op jit(solution)/shard_map/pallas_call | solution.py:411
  13.4 1.0 %maximum_add_fusion = bf16[144,384]{1,0:T(8,128)(2,1)S(1)} fusion(bf16[144,384]{1,0:T(8,128)(2,1)} %get-tuple-element.22, bf16[16,384]{1,0:T(8,128)(2,1)S(1)} %slice.28, bf16[128,384]{1,0:T(8,128)(2,1)S(1)} %slice_bitcast_fusion.1), kind=kLoop, calls=%fused_computation.8 | loop fusion | flops 331776 | bytes 331776 | tf_op jit(solution)/shard_map/add | solution.py:540
  14.9 1.0 %collective-permute-done.col_flags = s32[2,16,16]{2,1,0:T(8,128)S(1)} collective-permute-done((s32[2,16,16]{2,1,0:T(8,128)S(1)}, s32[2,16,16]{2,1,0:T(8,128)S(1)}, u32[]{:S(2)}, u32[]{:S(2)}) %collective-permute-start) | collective-permute-done | bytes 2080 | tf_op jit(solution)/shard_map/ppermute | solution.py:428
  16.7 16.5 %shard_map.120 = (bf16[768,384]{1,0:T(8,128)(2,1)}, bf16[768,384]{1,0:T(8,128)(2,1)}, bf16[512,384]{1,0:T(8,128)(2,1)}, bf16[384,512]{1,0:T(8,128)(2,1)}, bf16[2...) custom-call(s32[2]{0:T(128)} %shift.3, s32[1]{0:T(128)} %bitcast.core, s32[2,16,16]{2,1,0:T(8,128)} %inner_flags.1, ...), custom_call_target="tpu_custom_call" | custom-call | flops 12000000000 | bytes 1000000 | tf_op jit(solution)/shard_map/pallas_call | solution.py:411
  33.5 2.0 %collective-permute-done.7 = bf16[768,384]{1,0:T(8,128)(2,1)S(1)} collective-permute-done((bf16[768,384]{1,0:T(8,128)(2,1)}, bf16[768,384]{1,0:T(8,128)(2,1)S(1)}, u32[]{:S(2)}, u32[]{:S(2)}) %collective-permute-start.7) | collective-permute-done | bytes 589856 | tf_op jit(solution)/shard_map/ppermute | solution.py:452
  35.4 2.0 %add_convert_fusion = bf16[768,384]{1,0:T(8,128)(2,1)} fusion(bf16[768,384]{1,0:T(8,128)(2,1)S(1)} %collective-permute-done.7, bf16[768,384]{1,0:T(8,128)(2,1)} %get-tuple-element.34), kind=kLoop, calls=%fused_computation | loop fusion | flops 1179648 | bytes 1769472 | tf_op jit(solution)/shard_map/convert_element_type | solution.py:456
  37.5 3.5 %all-to-all-start = ((bf16[4,192,384]{2,1,0:T(8,128)(2,1)}), bf16[4,192,384]{2,1,0:T(8,128)(2,1)S(1)}, u32[]{:S(2)}, u32[]{:S(2)}) async-start(bf16[4,192,384]{2,1,0:T(8,128)(2,1)} %bitcast.13), calls=%async_computation | async-start | bytes 1179648 | tf_op jit(solution)/shard_map/all_to_all | solution.py:468
  41.0 1.4 %collective-permute-start.4 = (bf16[256,384]{1,0:T(8,128)(2,1)S(1)}, bf16[256,384]{1,0:T(8,128)(2,1)S(1)}, u32[]{:S(2)}, u32[]{:S(2)}) collective-permute-start(bf16[256,384]{1,0:T(8,128)(2,1)S(1)} %copy-done.10), channel_id=1, source_target_pairs={{12,0},{0,4},{4,8},{8,12},{13,1},{1,5},{5,9},{9,13},{14,2},{2,6},{... | collective-permute-start | bytes 589832 | tf_op jit(solution)/shard_map/ppermute | solution.py:428
  43.3 6.3 %all-to-all-done = bf16[4,192,384]{2,1,0:T(8,128)(2,1)S(1)} async-done(((bf16[4,192,384]{2,1,0:T(8,128)(2,1)}), bf16[4,192,384]{2,1,0:T(8,128)(2,1)S(1)}, u32[]{:S(2)}, u32[]{:S(2)}) %all-to-all-start) | async-done | bytes 589856 | tf_op jit(solution)/shard_map/all_to_all | solution.py:468
  49.6 1.8 %collective-permute-start.8 = (bf16[192,384]{1,0:T(8,128)(2,1)S(1)}, bf16[192,384]{1,0:T(8,128)(2,1)S(1)}, u32[]{:S(2)}, u32[]{:S(2)}) collective-permute-start(bf16[192,384]{1,0:T(8,128)(2,1)S(1)} %fusion.2), channel_id=1, source_target_pairs={{0,8},{4,12},{8,0},{12,4},{1,9},{5,13},{9,1},{13,5},{2,10},{6,14},... | collective-permute-start | bytes 442376 | tf_op jit(solution)/shard_map/ppermute | solution.py:452
  51.4 3.8 %collective-permute-done.4 = bf16[256,384]{1,0:T(8,128)(2,1)S(1)} collective-permute-done((bf16[256,384]{1,0:T(8,128)(2,1)S(1)}, bf16[256,384]{1,0:T(8,128)(2,1)S(1)}, u32[]{:S(2)}, u32[]{:S(2)}) %collective-permute-start.4) | collective-permute-done | bytes 196640 | tf_op jit(solution)/shard_map/ppermute | solution.py:428
  55.3 2.4 %collective-permute-start.6 = (bf16[128,384]{1,0:T(8,128)(2,1)S(1)}, bf16[128,384]{1,0:T(8,128)(2,1)S(1)}, u32[]{:S(2)}, u32[]{:S(2)}) collective-permute-start(bf16[128,384]{1,0:T(8,128)(2,1)S(1)} %slice_bitcast_fusion), channel_id=1, source_target_pairs={{2,0},{0,2},{3,1},{1,3},{6,4},{4,6},{7,5},{5,7},{10,8},{8,10},{11,... | collective-permute-start | bytes 294920 | tf_op jit(solution)/shard_map/ppermute | solution.py:428
  57.7 4.7 %collective-permute-done.8 = bf16[192,384]{1,0:T(8,128)(2,1)S(1)} collective-permute-done((bf16[192,384]{1,0:T(8,128)(2,1)S(1)}, bf16[192,384]{1,0:T(8,128)(2,1)S(1)}, u32[]{:S(2)}, u32[]{:S(2)}) %collective-permute-start.8) | collective-permute-done | bytes 147488 | tf_op jit(solution)/shard_map/ppermute | solution.py:452
  62.6 1.2 %collective-permute-start.10 = (bf16[192,384]{1,0:T(8,128)(2,1)S(1)}, bf16[192,384]{1,0:T(8,128)(2,1)S(1)}, u32[]{:S(2)}, u32[]{:S(2)}) collective-permute-start(bf16[192,384]{1,0:T(8,128)(2,1)S(1)} %add_convert_fusion.1.refs_0_), channel_id=1, source_target_pairs={{0,1},{1,0},{2,3},{3,2},{4,5},{5,4},{6,7},{7,6},{8,9},{9,8},{10,11... | collective-permute-start | bytes 442376 | tf_op jit(solution)/shard_map/ppermute | solution.py:452
  63.8 1.4 %collective-permute-start.9 = (bf16[192,384]{1,0:T(8,128)(2,1)S(1)}, bf16[192,384]{1,0:T(8,128)(2,1)S(1)}, u32[]{:S(2)}, u32[]{:S(2)}) collective-permute-start(bf16[192,384]{1,0:T(8,128)(2,1)S(1)} %add_convert_fusion.1.refs_0_), channel_id=1, source_target_pairs={{0,4},{4,0},{8,12},{12,8},{1,5},{5,1},{9,13},{13,9},{2,6},{6,2},{1... | collective-permute-start | bytes 442376 | tf_op jit(solution)/shard_map/ppermute | solution.py:452
  65.4 1.4 %collective-permute-start.12 = (bf16[192,384]{1,0:T(8,128)(2,1)S(1)}, bf16[192,384]{1,0:T(8,128)(2,1)S(1)}, u32[]{:S(2)}, u32[]{:S(2)}) collective-permute-start(bf16[192,384]{1,0:T(8,128)(2,1)S(1)} %add_convert_fusion.1.refs_0_), channel_id=1, source_target_pairs={{0,2},{2,0},{1,3},{3,1},{4,6},{6,4},{5,7},{7,5},{8,10},{10,8},{9,1... | collective-permute-start | bytes 442376 | tf_op jit(solution)/shard_map/ppermute | solution.py:452
  66.8 1.7 %collective-permute-done.11.refs_3_ = bf16[192,384]{1,0:T(8,128)(2,1)S(1)} collective-permute-done((bf16[192,384]{1,0:T(8,128)(2,1)S(1)}, bf16[192,384]{1,0:T(8,128)(2,1)S(1)}, u32[]{:S(2)}, u32[]{:S(2)}) %collective-permute-start.11) | collective-permute-done | bytes 147488 | tf_op jit(solution)/shard_map/ppermute | solution.py:452
  68.4 2.3 %collective-permute-start.15 = (bf16[192,384]{1,0:T(8,128)(2,1)S(1)}, bf16[192,384]{1,0:T(8,128)(2,1)S(1)}, u32[]{:S(2)}, u32[]{:S(2)}) collective-permute-start(bf16[192,384]{1,0:T(8,128)(2,1)S(1)} %collective-permute-done.11.refs_3_), channel_id=1, source_target_pairs={{0,2},{2,0},{1,3},{3,1},{4,6},{6,4},{5,7},{7,5},{8,10},{10,8},{9,1... | collective-permute-start | bytes 442376 | tf_op jit(solution)/shard_map/ppermute | solution.py:452
  70.8 1.3 %collective-permute-start.14 = (bf16[192,384]{1,0:T(8,128)(2,1)S(1)}, bf16[192,384]{1,0:T(8,128)(2,1)S(1)}, u32[]{:S(2)}, u32[]{:S(2)}) collective-permute-start(bf16[192,384]{1,0:T(8,128)(2,1)S(1)} %collective-permute-done.10.refs_2_), channel_id=1, source_target_pairs={{0,2},{2,0},{1,3},{3,1},{4,6},{6,4},{5,7},{7,5},{8,10},{10,8},{9,1... | collective-permute-start | bytes 442376 | tf_op jit(solution)/shard_map/ppermute | solution.py:452
  72.1 0.9 %collective-permute-start.13 = (bf16[192,384]{1,0:T(8,128)(2,1)S(1)}, bf16[192,384]{1,0:T(8,128)(2,1)S(1)}, u32[]{:S(2)}, u32[]{:S(2)}) collective-permute-start(bf16[192,384]{1,0:T(8,128)(2,1)S(1)} %collective-permute-done.9.refs_1_), channel_id=1, source_target_pairs={{0,2},{2,0},{1,3},{3,1},{4,6},{6,4},{5,7},{7,5},{8,10},{10,8},{9,1... | collective-permute-start | bytes 442376 | tf_op jit(solution)/shard_map/ppermute | solution.py:452
  73.0 2.7 %shard_map.121 = (bf16[512,384]{1,0:T(8,128)(2,1)}, bf16[512,384]{1,0:T(8,128)(2,1)}) custom-call(s32[2]{0:T(128)S(1)} %copy-done.3, bf16[640,384]{1,0:T(8,128)(2,1)S(1)} %pad_maximum_fusion.halo, bf16[384,384]{1,0:T(8,128)(2,1)S(1)} %copy-done.1, bf16[512,384]{1,0:T(8,128)(2,1)S(1)} %copy-done.4, bf16[384,512]{1,0:T(8,128)(2,1)S(1)} %copy-done.5), custom_call_target="tpu_custom_call" | custom-call | flops 2000000000 | bytes 1000000 | tf_op jit(solution)/shard_map/pallas_call | solution.py:411
  75.8 2.9 %shard_map.122 = (f32[384]{0:T(512)}, f32[384,1152]{1,0:T(8,128)}, f32[384,384]{1,0:T(8,128)}) custom-call(s32[2]{0:T(128)S(1)} %pad_add_fusion.place, bf16[192,384]{1,0:T(8,128)(2,1)S(1)} %add_convert_fusion.1.refs_0_, bf16[192,384]{1,0:T(8,128)(2,1)S(1)} %collective-permute-done.9.refs_1_, bf16[192,384]{1,0:T(8,128)(2,1)S(1)} %collective-permute-done.10.refs_2_, ...), custom_call_target="tpu_custom_call" | custom-call | flops 1000000000 | bytes 1000000 | tf_op jit(solution)/shard_map/pallas_call | solution.py:411
  (53 shorter events, 3.8 us)
Async XLA Ops:
  0.6 15.3 %collective-permute-start.2 = (bf16[2,16,16,384]{3,2,1,0:T(8,128)(2,1)}, bf16[2,16,16,384]{3,2,1,0:T(8,128)(2,1)S(1)}, u32[]{:S(2)}, u32[]{:S(2)}) collective-permute-start(bf16[2,16,16,384]{3,2,1,0:T(8,128)(2,1)} %param.8), channel_id=1, source_target_pairs={{2,0},{0,2},{3,1},{1,3},{6,4},{4,6},{7,5},{5,7},{10,8},{8,10},{11,... | collective-permute-start | bytes 1179656 | tf_op jit(solution)/shard_map/ppermute | solution.py:428
  2.4 10.9 %collective-permute-start.1 = (bf16[272,384]{1,0:T(8,128)(2,1)S(1)}, bf16[272,384]{1,0:T(8,128)(2,1)S(1)}, u32[]{:S(2)}, u32[]{:S(2)}) collective-permute-start(bf16[272,384]{1,0:T(8,128)(2,1)S(1)} %fusion.1), channel_id=1, source_target_pairs={{4,0},{8,4},{12,8},{0,12},{5,1},{9,5},{13,9},{1,13},{6,2},{10,6},{... | collective-permute-start | bytes 626696 | tf_op jit(solution)/shard_map/ppermute | solution.py:428
  7.3 7.4 %copy-start.7 = (s32[2,16,16]{2,1,0:T(8,128)S(1)}, s32[2,16,16]{2,1,0:T(8,128)}, u32[]{:S(2)}) copy-start(s32[2,16,16]{2,1,0:T(8,128)} %inner_flags.1) | copy-start | bytes 6148
  14.3 1.6 %collective-permute-start.3 = (bf16[144,384]{1,0:T(8,128)(2,1)S(1)}, bf16[144,384]{1,0:T(8,128)(2,1)S(1)}, u32[]{:S(2)}, u32[]{:S(2)}) collective-permute-start(bf16[144,384]{1,0:T(8,128)(2,1)S(1)} %maximum_add_fusion), channel_id=1, source_target_pairs={{2,0},{0,2},{3,1},{1,3},{6,4},{4,6},{7,5},{5,7},{10,8},{8,10},{11,... | collective-permute-start | bytes 331784 | tf_op jit(solution)/shard_map/ppermute | solution.py:428
  14.7 1.2 %collective-permute-start = (s32[2,16,16]{2,1,0:T(8,128)S(1)}, s32[2,16,16]{2,1,0:T(8,128)S(1)}, u32[]{:S(2)}, u32[]{:S(2)}) collective-permute-start(s32[2,16,16]{2,1,0:T(8,128)S(1)} %copy-done.7), channel_id=1, source_target_pairs={{2,0},{0,2},{3,1},{1,3},{6,4},{4,6},{7,5},{5,7},{10,8},{8,10},{11,... | collective-permute-start | bytes 6152 | tf_op jit(solution)/shard_map/ppermute | solution.py:428
  33.1 7.9 %copy-start.10 = (bf16[256,384]{1,0:T(8,128)(2,1)S(1)}, bf16[256,384]{1,0:T(8,128)(2,1)}, u32[]{:S(2)}) copy-start(bf16[256,384]{1,0:T(8,128)(2,1)} %get-tuple-element.28) | copy-start | bytes 589828
  33.1 9.3 %copy-start.9 = (bf16[256,384]{1,0:T(8,128)(2,1)S(1)}, bf16[256,384]{1,0:T(8,128)(2,1)}, u32[]{:S(2)}) copy-start(bf16[256,384]{1,0:T(8,128)(2,1)} %get-tuple-element.29) | copy-start | bytes 589828
  33.2 2.3 %collective-permute-start.7 = (bf16[768,384]{1,0:T(8,128)(2,1)}, bf16[768,384]{1,0:T(8,128)(2,1)S(1)}, u32[]{:S(2)}, u32[]{:S(2)}) collective-permute-start(bf16[768,384]{1,0:T(8,128)(2,1)} %get-tuple-element.35), channel_id=1, source_target_pairs={{0,2},{2,0},{1,3},{3,1},{4,6},{6,4},{5,7},{7,5},{8,10},{10,8},{9,1... | collective-permute-start | bytes 1769480 | tf_op jit(solution)/shard_map/ppermute | solution.py:452
  37.5 12.1 %all-to-all-start = ((bf16[4,192,384]{2,1,0:T(8,128)(2,1)}), bf16[4,192,384]{2,1,0:T(8,128)(2,1)S(1)}, u32[]{:S(2)}, u32[]{:S(2)}) async-start(bf16[4,192,384]{2,1,0:T(8,128)(2,1)} %bitcast.13), calls=%async_computation | async-start | bytes 1179648 | tf_op jit(solution)/shard_map/all_to_all | solution.py:468
  40.9 32.0 %copy-start.1 = (bf16[384,384]{1,0:T(8,128)(2,1)S(1)}, bf16[384,384]{1,0:T(8,128)(2,1)}, u32[]{:S(2)}) copy-start(bf16[384,384]{1,0:T(8,128)(2,1)} %out_weight.1) | copy-start | bytes 884740
  41.0 32.0 %copy-start.3 = (s32[2]{0:T(128)S(1)}, s32[2]{0:T(128)}, u32[]{:S(2)}) copy-start(s32[2]{0:T(128)} %shift.3) | copy-start | bytes 28
  41.0 32.0 %copy-start.4 = (bf16[512,384]{1,0:T(8,128)(2,1)S(1)}, bf16[512,384]{1,0:T(8,128)(2,1)}, u32[]{:S(2)}) copy-start(bf16[512,384]{1,0:T(8,128)(2,1)} %get-tuple-element.30.kept_far) | copy-start | bytes 1179652
  41.0 32.0 %copy-start.5 = (bf16[384,512]{1,0:T(8,128)(2,1)S(1)}, bf16[384,512]{1,0:T(8,128)(2,1)}, u32[]{:S(2)}) copy-start(bf16[384,512]{1,0:T(8,128)(2,1)} %get-tuple-element.31.context_far) | copy-start | bytes 1179652
  41.0 14.3 %collective-permute-start.4 = (bf16[256,384]{1,0:T(8,128)(2,1)S(1)}, bf16[256,384]{1,0:T(8,128)(2,1)S(1)}, u32[]{:S(2)}, u32[]{:S(2)}) collective-permute-start(bf16[256,384]{1,0:T(8,128)(2,1)S(1)} %copy-done.10), channel_id=1, source_target_pairs={{12,0},{0,4},{4,8},{8,12},{13,1},{1,5},{5,9},{9,13},{14,2},{2,6},{... | collective-permute-start | bytes 589832 | tf_op jit(solution)/shard_map/ppermute | solution.py:428
  42.5 22.8 %collective-permute-start.5 = (bf16[256,384]{1,0:T(8,128)(2,1)S(1)}, bf16[256,384]{1,0:T(8,128)(2,1)S(1)}, u32[]{:S(2)}, u32[]{:S(2)}) collective-permute-start(bf16[256,384]{1,0:T(8,128)(2,1)S(1)} %copy-done.9), channel_id=1, source_target_pairs={{2,0},{0,2},{3,1},{1,3},{6,4},{4,6},{7,5},{5,7},{10,8},{8,10},{11,... | collective-permute-start | bytes 589832 | tf_op jit(solution)/shard_map/ppermute | solution.py:428
  49.6 12.8 %collective-permute-start.8 = (bf16[192,384]{1,0:T(8,128)(2,1)S(1)}, bf16[192,384]{1,0:T(8,128)(2,1)S(1)}, u32[]{:S(2)}, u32[]{:S(2)}) collective-permute-start(bf16[192,384]{1,0:T(8,128)(2,1)S(1)} %fusion.2), channel_id=1, source_target_pairs={{0,8},{4,12},{8,0},{12,4},{1,9},{5,13},{9,1},{13,5},{2,10},{6,14},... | collective-permute-start | bytes 442376 | tf_op jit(solution)/shard_map/ppermute | solution.py:452
  55.3 10.0 %collective-permute-start.6 = (bf16[128,384]{1,0:T(8,128)(2,1)S(1)}, bf16[128,384]{1,0:T(8,128)(2,1)S(1)}, u32[]{:S(2)}, u32[]{:S(2)}) collective-permute-start(bf16[128,384]{1,0:T(8,128)(2,1)S(1)} %slice_bitcast_fusion), channel_id=1, source_target_pairs={{2,0},{0,2},{3,1},{1,3},{6,4},{4,6},{7,5},{5,7},{10,8},{8,10},{11,... | collective-permute-start | bytes 294920 | tf_op jit(solution)/shard_map/ppermute | solution.py:428
  62.5 5.9 %collective-permute-start.11 = (bf16[192,384]{1,0:T(8,128)(2,1)S(1)}, bf16[192,384]{1,0:T(8,128)(2,1)S(1)}, u32[]{:S(2)}, u32[]{:S(2)}) collective-permute-start(bf16[192,384]{1,0:T(8,128)(2,1)S(1)} %add_convert_fusion.1.refs_0_), channel_id=1, source_target_pairs={{0,5},{1,4},{4,1},{5,0},{8,13},{9,12},{12,9},{13,8},{2,7},{3,6},{6... | collective-permute-start | bytes 442376 | tf_op jit(solution)/shard_map/ppermute | solution.py:452
  62.6 8.2 %collective-permute-start.10 = (bf16[192,384]{1,0:T(8,128)(2,1)S(1)}, bf16[192,384]{1,0:T(8,128)(2,1)S(1)}, u32[]{:S(2)}, u32[]{:S(2)}) collective-permute-start(bf16[192,384]{1,0:T(8,128)(2,1)S(1)} %add_convert_fusion.1.refs_0_), channel_id=1, source_target_pairs={{0,1},{1,0},{2,3},{3,2},{4,5},{5,4},{6,7},{7,6},{8,9},{9,8},{10,11... | collective-permute-start | bytes 442376 | tf_op jit(solution)/shard_map/ppermute | solution.py:452
  63.8 8.2 %collective-permute-start.9 = (bf16[192,384]{1,0:T(8,128)(2,1)S(1)}, bf16[192,384]{1,0:T(8,128)(2,1)S(1)}, u32[]{:S(2)}, u32[]{:S(2)}) collective-permute-start(bf16[192,384]{1,0:T(8,128)(2,1)S(1)} %add_convert_fusion.1.refs_0_), channel_id=1, source_target_pairs={{0,4},{4,0},{8,12},{12,8},{1,5},{5,1},{9,13},{13,9},{2,6},{6,2},{1... | collective-permute-start | bytes 442376 | tf_op jit(solution)/shard_map/ppermute | solution.py:452
  65.4 10.3 %collective-permute-start.12 = (bf16[192,384]{1,0:T(8,128)(2,1)S(1)}, bf16[192,384]{1,0:T(8,128)(2,1)S(1)}, u32[]{:S(2)}, u32[]{:S(2)}) collective-permute-start(bf16[192,384]{1,0:T(8,128)(2,1)S(1)} %add_convert_fusion.1.refs_0_), channel_id=1, source_target_pairs={{0,2},{2,0},{1,3},{3,1},{4,6},{6,4},{5,7},{7,5},{8,10},{10,8},{9,1... | collective-permute-start | bytes 442376 | tf_op jit(solution)/shard_map/ppermute | solution.py:452
  68.4 7.3 %collective-permute-start.15 = (bf16[192,384]{1,0:T(8,128)(2,1)S(1)}, bf16[192,384]{1,0:T(8,128)(2,1)S(1)}, u32[]{:S(2)}, u32[]{:S(2)}) collective-permute-start(bf16[192,384]{1,0:T(8,128)(2,1)S(1)} %collective-permute-done.11.refs_3_), channel_id=1, source_target_pairs={{0,2},{2,0},{1,3},{3,1},{4,6},{6,4},{5,7},{7,5},{8,10},{10,8},{9,1... | collective-permute-start | bytes 442376 | tf_op jit(solution)/shard_map/ppermute | solution.py:452
  70.8 5.0 %collective-permute-start.14 = (bf16[192,384]{1,0:T(8,128)(2,1)S(1)}, bf16[192,384]{1,0:T(8,128)(2,1)S(1)}, u32[]{:S(2)}, u32[]{:S(2)}) collective-permute-start(bf16[192,384]{1,0:T(8,128)(2,1)S(1)} %collective-permute-done.10.refs_2_), channel_id=1, source_target_pairs={{0,2},{2,0},{1,3},{3,1},{4,6},{6,4},{5,7},{7,5},{8,10},{10,8},{9,1... | collective-permute-start | bytes 442376 | tf_op jit(solution)/shard_map/ppermute | solution.py:452
  72.1 3.7 %collective-permute-start.13 = (bf16[192,384]{1,0:T(8,128)(2,1)S(1)}, bf16[192,384]{1,0:T(8,128)(2,1)S(1)}, u32[]{:S(2)}, u32[]{:S(2)}) collective-permute-start(bf16[192,384]{1,0:T(8,128)(2,1)S(1)} %collective-permute-done.9.refs_1_), channel_id=1, source_target_pairs={{0,2},{2,0},{1,3},{3,1},{4,6},{6,4},{5,7},{7,5},{8,10},{10,8},{9,1... | collective-permute-start | bytes 442376 | tf_op jit(solution)/shard_map/ppermute | solution.py:452
  (6 other events, 10.2 us)

commit v8 on v6

--- a/solution.py
+++ b/solution.py
@@ -200,10 +200,11 @@
     cot_far,
     bias1_far,
     bias2_far,
+    out_weight_far,
     keep_far,
     send_far,
     d_rolled_far,
-    context_far,
+    update_far,
     lower_far,
     right_far,
     penalty,
@@ -221,12 +222,16 @@
     grads,
     d_rolled,
     right,
+    out_weight,
+    update,
     sems,
 ):
     sources = (inner_far, rows_far, cols_far, corner_far, weight_far, weight_t_far)
     sources += (d_context_far, bias0_far, cot_far, bias1_far, bias2_far)
+    sources += (out_weight_far,)
     places = [inner, rows, cols, corner, qkv_weight, qkv_weight_t]
     places += [d_context_t, bias_blocks.at[0], cot, bias_blocks.at[1], bias_blocks.at[2]]
+    places.append(out_weight)
     arrivals = [
         pltpu.make_async_copy(source, place, sems.at[k])
         for k, (source, place) in enumerate(zip(sources, places))
@@ -234,22 +239,8 @@
     for copy in arrivals:
         copy.start()
     onehots = source_onehots(shift[0], shift[1], 1)
-    on_diagonal = iota((HALF, HALF), 0) == iota((HALF, HALF), 1)
     for copy in arrivals[:4]:
         copy.wait()
-    for t in range(2):
-        strips = (
-            flag_strip(inner_flags[t].astype(f32), SIDE),
-            flag_strip(rows[256:272, :SIDE][t * RIM : (t + 1) * RIM], RIM),
-            flag_strip(col_flags[t].astype(f32), SIDE),
-            flag_strip(corner[128:144, :SIDE][t * RIM : (t + 1) * RIM], RIM, RIM),
-        )
-        marks = sum(nt(hot, strip) for hot, strip in zip(onehots, strips))
-        column = jnp.where(marks > 0.5, -1e30, 0.0)
-        wide = jnp.concatenate([column, column], 1)
-        own = jnp.where(on_diagonal, 0.0, wide)
-        penalty[t * HALF : (t + 1) * HALF, t * HALF : (t + 1) * HALF] = own
-        penalty[t * HALF : (t + 1) * HALF, (1 - t) * HALF : (2 - t) * HALF] = wide
     rolled = []
     for t in range(2):
         parts = (
@@ -264,12 +255,26 @@
     normed = (xhat * gain_row).astype(bf16)
     normed_t = normed.T
     arrivals[4].wait()
+    arrivals[5].wait()
     kv = nn(normed, qkv_weight[:, MODEL_WIDTH:]).astype(bf16)
-    arrivals[5].wait()
     qkv_t = nt(qkv_weight_t[...], normed).astype(bf16)
-    arrivals[6].wait()
+    on_diagonal = iota((HALF, HALF), 0) == iota((HALF, HALF), 1)
+    for t in range(2):
+        strips = (
+            flag_strip(inner_flags[t].astype(f32), SIDE),
+            flag_strip(rows[256:272, :SIDE][t * RIM : (t + 1) * RIM], RIM),
+            flag_strip(col_flags[t].astype(f32), SIDE),
+            flag_strip(corner[128:144, :SIDE][t * RIM : (t + 1) * RIM], RIM, RIM),
+        )
+        marks = sum(nt(hot, strip) for hot, strip in zip(onehots, strips))
+        column = jnp.where(marks > 0.5, -1e30, 0.0)
+        wide = jnp.concatenate([column, column], 1)
+        own = jnp.where(on_diagonal, 0.0, wide)
+        penalty[t * HALF : (t + 1) * HALF, t * HALF : (t + 1) * HALF] = own
+        penalty[t * HALF : (t + 1) * HALF, (1 - t) * HALF : (2 - t) * HALF] = wide
+    for copy in arrivals[6:]:
+        copy.wait()
     for pair in range(HEADS // 2):
-        arrivals[(7, 9, 10)[pair]].wait()
         heads = [
             attention_head(2 * pair + side, qkv_t, kv, penalty, bias_blocks.at[pair], d_context_t)
             for side in range(2)
@@ -281,14 +286,10 @@
             first = kind * MODEL_WIDTH + pair * 128
             d_qkv[:, first : first + 128] = d_pair[:, kind * 128 : kind * 128 + 128]
         first = pair * TOKENS
-        if pair == 0:
-            arrivals[8].wait()
         grads[first : first + 128, :] = nn(context, cot[...]).astype(bf16)
         grads[first + 128 : first + TOKENS, :] = nn(normed_t, d_pair).astype(bf16)
-        for block in (2 * pair, 2 * pair + 1):
-            to_half(grads, block, core[0], keep_far, send_far, sems)
-    keep_context = pltpu.make_async_copy(context_t, context_far, sems.at[0])
-    keep_context.start()
+    for block in range(6):
+        to_half(grads, block, core[0], keep_far, send_far, sems)
     d_xhat = nt(d_qkv[...], qkv_weight[...]) * gain_row
     d_tokens = inv_std * (
         d_xhat
@@ -297,10 +298,12 @@
     )
     d_rolled[...] = d_tokens.astype(bf16)
     last_columns = d_tokens.reshape(2 * SIDE, SIDE, MODEL_WIDTH)[:, RIM:, :]
+    update[...] = tn(context_t[...], out_weight[...]).astype(bf16)
     right[...] = last_columns.reshape(HALF, MODEL_WIDTH).astype(bf16)
     copies = [
         pltpu.make_async_copy(d_rolled, d_rolled_far, sems.at[1]),
         pltpu.make_async_copy(right, right_far, sems.at[2]),
+        pltpu.make_async_copy(update, update_far, sems.at[0]),
     ]
     for t in range(2):
         source = d_rolled.at[pl.ds(t * HALF + 128, 128), :]
@@ -310,8 +313,7 @@
         copy.start()
     for block in range(6):
         source, target = half_block(grads, block, keep_far)
-        pltpu.make_async_copy(source, target, sems.at[11 + block]).wait()
-    keep_context.wait()
+        pltpu.make_async_copy(source, target, sems.at[12 + block]).wait()
     for copy in copies:
         copy.wait()
 
@@ -327,30 +329,14 @@
         @pl.when(core == side)
         def _():
             source, target = half_block(grads, block, half)
-            pltpu.make_async_copy(source, target, sems.at[11 + block]).start()
-
-
-def place_kernel(
-    shift,
-    halo,
-    out_weight,
-    kept_far,
-    context_far,
-    field_grad,
-    update,
-    kept,
-    context_t,
-    sems,
-):
-    copies = [
-        pltpu.make_async_copy(kept_far, kept, sems.at[0]),
-        pltpu.make_async_copy(context_far, context_t, sems.at[1]),
-    ]
-    for copy in copies:
-        copy.start()
+            pltpu.make_async_copy(source, target, sems.at[12 + block]).start()
+
+
+def place_kernel(shift, halo, kept_far, field_grad, kept, sems):
+    copy = pltpu.make_async_copy(kept_far, kept, sems.at[0])
+    copy.start()
     onehots = source_onehots(shift[0], shift[1], -1)
-    for copy in copies:
-        copy.wait()
+    copy.wait()
     for t in range(2):
         parts = (
             kept[t * 256 : t * 256 + 256, :],
@@ -361,7 +347,6 @@
         field_grad[t * 256 : t * 256 + 256, :] = sum(
             nn(hot, part) for hot, part in zip(onehots, parts)
         ).astype(bf16)
-    update[...] = tn(context_t[...], out_weight[...]).astype(bf16)
 
 
 def finish_kernel(scale, place, *refs):
@@ -507,7 +492,7 @@
     pair_bias = ((6, HALF, HALF), f32)
     blank, *bias_blocks, d_context_t, qkv_weight_t = local_call(
         prepare_kernel,
-        [wide(144)] + [pair_bias] * 3 + [((width, TOKENS), bf16), wide(3 * width)],
+        [wide(16)] + [pair_bias] * 3 + [((width, TOKENS), bf16), wide(3 * width)],
         [position_bias, cot_rows, out_weight, qkv_weight],
         far_in=3,
         far_out=5,
@@ -527,16 +512,16 @@
     corner_message = jnp.concatenate(
         [
             rows[: 2 * RIM * SIDE].reshape(2 * RIM, SIDE, width)[:, :RIM].reshape(-1, width),
-            rows[2 * RIM * SIDE :],
+            rows[2 * RIM * SIDE :] + blank,
         ],
         0,
     )
-    corner = passed_along(corner_message + blank, "sx", -1)
+    corner = passed_along(corner_message, "sx", -1)
     core = index_bit(*CORE).astype(jnp.int32).reshape(1)
-    keep, send, d_rolled, context_t, lower, right = local_call(
+    keep, send, d_rolled, update, lower, right = local_call(
         main_kernel,
         [wide(2 * width)] * 2
-        + [wide(TOKENS), ((width, TOKENS), bf16), wide(HALF), wide(HALF)],
+        + [wide(TOKENS), wide(TOKENS), wide(HALF), wide(HALF)],
         [
             window_shift,
             core,
@@ -554,8 +539,9 @@
             cot_rows,
             bias_blocks[1],
             bias_blocks[2],
+            out_weight,
         ],
-        far_in=11,
+        far_in=12,
         far_out=6,
         scratch=[
             ((TOKENS, TOKENS), f32),
@@ -573,8 +559,10 @@
             wide(3 * TOKENS),
             wide(TOKENS),
             wide(HALF),
+            wide(width),
+            wide(TOKENS),
         ],
-        copies=17,
+        copies=18,
         micros=12,
         limit=62,
     )
@@ -584,19 +572,13 @@
         below.reshape(2 * RIM, SIDE, width)[:, RIM:].reshape(-1, width), "sx", 1
     )
     quarter = sum_quarter(keep, send)
-    field_grad, update = local_call(
+    (field_grad,) = local_call(
         place_kernel,
-        [wide(TOKENS), wide(TOKENS)],
-        [
-            window_shift,
-            jnp.concatenate([below, beside, across], 0),
-            out_weight,
-            d_rolled,
-            context_t,
-        ],
-        far_in=2,
-        scratch=[wide(TOKENS), ((width, TOKENS), bf16)],
-        copies=2,
+        [wide(TOKENS)],
+        [window_shift, jnp.concatenate([below, beside, across], 0), d_rolled],
+        far_in=1,
+        scratch=[wide(TOKENS)],
+        copies=1,
         micros=2,
     )
     quarter = sum_rest(quarter)

time: 74.6 us -> 73.3 us (0.983)
  Pallas kernels: 28.1 us -> 27 us
    pallas_call x4, Pallas kernels: 28.1 us -> 27 us  [local_call(): pl.pallas_call(kernel, out_shape=[jax.ShapeDtypeStruct(shape, dtype) for...]
  transfers between devices with their start and end apart: 19 -> 19, of which waited for: 9 -> 9; matrix products, arithmetic and copies ran while one was open for 4% -> 4% of each run, Pallas kernels for 12% -> 11%
where the time goes in v8:
time: 73.3 us; the launch traced here: 72.9 us
  Pallas kernels  27 us (37%)
  starting transfers between devices  20.6 us (28%)
  waiting for transfers between devices  19.5 us (27%)
  other arithmetic  2.94 us (4%)
  local copies, waits for them, and re-layouts  1.84 us (3%)
  between operations  1.02 us (1%)
    pallas_call x4, Pallas kernels, local_call(): pl.pallas_call(kernel, out_shape=[jax.ShapeDtypeStruct(shape, dtype) for...  27 us
    ppermute x12, waiting for transfers between devices, swapped(): return lax.ppermute(block, axes, route)  15.9 us
    ppermute x12, starting transfers between devices, swapped(): return lax.ppermute(block, axes, route)  12.7 us
    ppermute x7, starting transfers between devices, passed_along(): lax.ppermute(block, axis, [((i - distance) % count, i) for i in range(cou...  7.91 us
    ppermute x7, waiting for transfers between devices, passed_along(): lax.ppermute(block, axis, [((i - distance) % count, i) for i in range(cou...  3.59 us
  transfers between devices with their start and end apart: 19, of which 9 were waited for; matrix products, arithmetic and copies ran while one was open for 4% of the time, Pallas kernels for 11%

profile of v8, /device:TPU:1, one launch (start us, length us, event | category | flops | bytes accessed | tf_op | source)
XLA Modules:
  0.0 72.9 jit_solution(509994410562315726)
XLA Ops:
  0.8 0.9 %slice.19 = bf16[2,8,16,384]{3,2,1,0:T(8,128)(2,1)S(1)} slice(bf16[2,16,16,384]{3,2,1,0:T(8,128)(2,1)} %param.8), slice={[0:2], [0:8], [0:16], [0:384]} | slice | bytes 393216 | tf_op jit(solution)/shard_map/slice | solution.py:483
  2.4 4.8 %collective-permute-start.1 = (bf16[272,384]{1,0:T(8,128)(2,1)S(1)}, bf16[272,384]{1,0:T(8,128)(2,1)S(1)}, u32[]{:S(2)}, u32[]{:S(2)}) collective-permute-start(bf16[272,384]{1,0:T(8,128)(2,1)S(1)} %fusion.1), channel_id=1, source_target_pairs={{4,0},{8,4},{12,8},{0,12},{5,1},{9,5},{13,9},{1,13},{6,2},{10,6},{... | collective-permute-start | bytes 626696 | tf_op jit(solution)/shard_map/ppermute | solution.py:413
  7.3 6.0 %shard_map.119 = (bf16[16,384]{1,0:T(8,128)(2,1)}, f32[6,256,256]{2,1,0:T(8,128)}, f32[6,256,256]{2,1,0:T(8,128)}, f32[6,256,256]{2,1,0:T(8,128)}, bf16[384,512]{1,0:T(8,128)(2,1)}, /*index=5*/bf16[1152,384]{1,0:T(8,128)(2,1)}) custom-call(f32[6,2883]{1,0:T(8,128)} %position_bias.1, bf16[512,384]{1,0:T(8,128)(2,1)} %bitcast.20, ...), custom_call_target="tpu_custom_call" | custom-call | flops 3000000000 | bytes 1000000 | tf_op jit(solution)/shard_map/pallas_call | solution.py:396
  13.3 0.7 %slice_add_fusion = bf16[16,384]{1,0:T(8,128)(2,1)S(1)} fusion(bf16[16,384]{1,0:T(8,128)(2,1)} %get-tuple-element.20, bf16[272,384]{1,0:T(8,128)(2,1)S(1)} %collective-permute-done.1.rows_far), kind=kLoop, calls=%fused_computation.10 | loop fusion | flops 6144 | bytes 36864 | tf_op jit(solution)/shard_map/add | solution.py:515
  14.6 1.0 %collective-permute-done.col_flags = s32[2,16,16]{2,1,0:T(8,128)S(1)} collective-permute-done((s32[2,16,16]{2,1,0:T(8,128)S(1)}, s32[2,16,16]{2,1,0:T(8,128)S(1)}, u32[]{:S(2)}, u32[]{:S(2)}) %collective-permute-start) | collective-permute-done | bytes 2080 | tf_op jit(solution)/shard_map/ppermute | solution.py:413
  16.4 15.8 %shard_map.120 = (bf16[768,384]{1,0:T(8,128)(2,1)}, bf16[768,384]{1,0:T(8,128)(2,1)}, bf16[512,384]{1,0:T(8,128)(2,1)}, bf16[512,384]{1,0:T(8,128)(2,1)}, bf16[2...) custom-call(s32[2]{0:T(128)} %shift.3, s32[1]{0:T(128)} %bitcast.core, s32[2,16,16]{2,1,0:T(8,128)} %inner_flags.1, ...), custom_call_target="tpu_custom_call" | custom-call | flops 12000000000 | bytes 1000000 | tf_op jit(solution)/shard_map/pallas_call | solution.py:396
  32.5 2.0 %collective-permute-done.7 = bf16[768,384]{1,0:T(8,128)(2,1)S(1)} collective-permute-done((bf16[768,384]{1,0:T(8,128)(2,1)}, bf16[768,384]{1,0:T(8,128)(2,1)S(1)}, u32[]{:S(2)}, u32[]{:S(2)}) %collective-permute-start.7) | collective-permute-done | bytes 589856 | tf_op jit(solution)/shard_map/ppermute | solution.py:437
  34.5 1.2 %add_convert_fusion = bf16[768,384]{1,0:T(8,128)(2,1)S(1)} fusion(bf16[768,384]{1,0:T(8,128)(2,1)S(1)} %collective-permute-done.7, bf16[768,384]{1,0:T(8,128)(2,1)} %get-tuple-element.30), kind=kLoop, calls=%fused_computation | loop fusion | flops 1179648 | bytes 1769472 | tf_op jit(solution)/shard_map/convert_element_type | solution.py:441
  36.1 2.2 %collective-permute-start.8 = (bf16[192,384]{1,0:T(8,128)(2,1)S(1)}, bf16[192,384]{1,0:T(8,128)(2,1)S(1)}, u32[]{:S(2)}, u32[]{:S(2)}) collective-permute-start(bf16[192,384]{1,0:T(8,128)(2,1)S(1)} %get-tuple-element.35), channel_id=1, source_target_pairs={{0,4},{4,0},{8,12},{12,8},{1,5},{5,1},{9,13},{13,9},{2,6},{6,2},{1... | collective-permute-start | bytes 442376 | tf_op jit(solution)/shard_map/ppermute | solution.py:437
  38.6 1.0 %collective-permute-start.5 = (bf16[256,384]{1,0:T(8,128)(2,1)S(1)}, bf16[256,384]{1,0:T(8,128)(2,1)S(1)}, u32[]{:S(2)}, u32[]{:S(2)}) collective-permute-start(bf16[256,384]{1,0:T(8,128)(2,1)S(1)} %copy-done.7), channel_id=1, source_target_pairs={{2,0},{0,2},{3,1},{1,3},{6,4},{4,6},{7,5},{5,7},{10,8},{8,10},{11,... | collective-permute-start | bytes 589832 | tf_op jit(solution)/shard_map/ppermute | solution.py:413
  39.7 2.3 %collective-permute-done.10 = bf16[192,384]{1,0:T(8,128)(2,1)S(1)} collective-permute-done((bf16[192,384]{1,0:T(8,128)(2,1)S(1)}, bf16[192,384]{1,0:T(8,128)(2,1)S(1)}, u32[]{:S(2)}, u32[]{:S(2)}) %collective-permute-start.10) | collective-permute-done | bytes 147488 | tf_op jit(solution)/shard_map/ppermute | solution.py:437
  42.0 3.2 %collective-permute-done.8 = bf16[192,384]{1,0:T(8,128)(2,1)S(1)} collective-permute-done((bf16[192,384]{1,0:T(8,128)(2,1)S(1)}, bf16[192,384]{1,0:T(8,128)(2,1)S(1)}, u32[]{:S(2)}, u32[]{:S(2)}) %collective-permute-start.8) | collective-permute-done | bytes 147488 | tf_op jit(solution)/shard_map/ppermute | solution.py:437
  45.8 2.0 %collective-permute-start.11 = (bf16[192,384]{1,0:T(8,128)(2,1)S(1)}, bf16[192,384]{1,0:T(8,128)(2,1)S(1)}, u32[]{:S(2)}, u32[]{:S(2)}) collective-permute-start(bf16[192,384]{1,0:T(8,128)(2,1)S(1)} %add_convert_fusion.2), channel_id=1, source_target_pairs={{0,8},{4,12},{8,0},{12,4},{1,9},{5,13},{9,1},{13,5},{2,10},{6,14},... | collective-permute-start | bytes 442376 | tf_op jit(solution)/shard_map/ppermute | solution.py:437
  47.8 2.6 %collective-permute-done.4 = bf16[256,384]{1,0:T(8,128)(2,1)S(1)} collective-permute-done((bf16[256,384]{1,0:T(8,128)(2,1)S(1)}, bf16[256,384]{1,0:T(8,128)(2,1)S(1)}, u32[]{:S(2)}, u32[]{:S(2)}) %collective-permute-start.4) | collective-permute-done | bytes 196640 | tf_op jit(solution)/shard_map/ppermute | solution.py:413
  50.4 1.2 %collective-permute-start.6 = (bf16[128,384]{1,0:T(8,128)(2,1)S(1)}, bf16[128,384]{1,0:T(8,128)(2,1)S(1)}, u32[]{:S(2)}, u32[]{:S(2)}) collective-permute-start(bf16[128,384]{1,0:T(8,128)(2,1)S(1)} %slice_bitcast_fusion), channel_id=1, source_target_pairs={{2,0},{0,2},{3,1},{1,3},{6,4},{4,6},{7,5},{5,7},{10,8},{8,10},{11,... | collective-permute-start | bytes 294920 | tf_op jit(solution)/shard_map/ppermute | solution.py:413
  51.7 5.3 %collective-permute-done.11 = bf16[192,384]{1,0:T(8,128)(2,1)S(1)} collective-permute-done((bf16[192,384]{1,0:T(8,128)(2,1)S(1)}, bf16[192,384]{1,0:T(8,128)(2,1)S(1)}, u32[]{:S(2)}, u32[]{:S(2)}) %collective-permute-start.11) | collective-permute-done | bytes 147488 | tf_op jit(solution)/shard_map/ppermute | solution.py:437
  57.1 1.3 %collective-permute-start.13 = (bf16[192,384]{1,0:T(8,128)(2,1)S(1)}, bf16[192,384]{1,0:T(8,128)(2,1)S(1)}, u32[]{:S(2)}, u32[]{:S(2)}) collective-permute-start(bf16[192,384]{1,0:T(8,128)(2,1)S(1)} %add_convert_fusion.1.refs_0_), channel_id=1, source_target_pairs={{0,1},{1,0},{2,3},{3,2},{4,5},{5,4},{6,7},{7,6},{8,9},{9,8},{10,11... | collective-permute-start | bytes 442376 | tf_op jit(solution)/shard_map/ppermute | solution.py:437
  58.4 1.4 %collective-permute-start.14 = (bf16[192,384]{1,0:T(8,128)(2,1)S(1)}, bf16[192,384]{1,0:T(8,128)(2,1)S(1)}, u32[]{:S(2)}, u32[]{:S(2)}) collective-permute-start(bf16[192,384]{1,0:T(8,128)(2,1)S(1)} %add_convert_fusion.1.refs_0_), channel_id=1, source_target_pairs={{0,5},{1,4},{4,1},{5,0},{8,13},{9,12},{12,9},{13,8},{2,7},{3,6},{6... | collective-permute-start | bytes 442376 | tf_op jit(solution)/shard_map/ppermute | solution.py:437
  59.9 1.4 %collective-permute-start.15 = (bf16[192,384]{1,0:T(8,128)(2,1)S(1)}, bf16[192,384]{1,0:T(8,128)(2,1)S(1)}, u32[]{:S(2)}, u32[]{:S(2)}) collective-permute-start(bf16[192,384]{1,0:T(8,128)(2,1)S(1)} %add_convert_fusion.1.refs_0_), channel_id=1, source_target_pairs={{0,2},{2,0},{1,3},{3,1},{4,6},{6,4},{5,7},{7,5},{8,10},{10,8},{9,1... | collective-permute-start | bytes 442376 | tf_op jit(solution)/shard_map/ppermute | solution.py:437
  62.0 2.3 %collective-permute-start.16 = (bf16[192,384]{1,0:T(8,128)(2,1)S(1)}, bf16[192,384]{1,0:T(8,128)(2,1)S(1)}, u32[]{:S(2)}, u32[]{:S(2)}) collective-permute-start(bf16[192,384]{1,0:T(8,128)(2,1)S(1)} %collective-permute-done.12.refs_1_), channel_id=1, source_target_pairs={{0,2},{2,0},{1,3},{3,1},{4,6},{6,4},{5,7},{7,5},{8,10},{10,8},{9,1... | collective-permute-start | bytes 442376 | tf_op jit(solution)/shard_map/ppermute | solution.py:437
  64.3 1.8 %collective-permute-done.14.refs_3_ = bf16[192,384]{1,0:T(8,128)(2,1)S(1)} collective-permute-done((bf16[192,384]{1,0:T(8,128)(2,1)S(1)}, bf16[192,384]{1,0:T(8,128)(2,1)S(1)}, u32[]{:S(2)}, u32[]{:S(2)}) %collective-permute-start.14) | collective-permute-done | bytes 147488 | tf_op jit(solution)/shard_map/ppermute | solution.py:437
  66.1 1.3 %collective-permute-start.18 = (bf16[192,384]{1,0:T(8,128)(2,1)S(1)}, bf16[192,384]{1,0:T(8,128)(2,1)S(1)}, u32[]{:S(2)}, u32[]{:S(2)}) collective-permute-start(bf16[192,384]{1,0:T(8,128)(2,1)S(1)} %collective-permute-done.14.refs_3_), channel_id=1, source_target_pairs={{0,2},{2,0},{1,3},{3,1},{4,6},{6,4},{5,7},{7,5},{8,10},{10,8},{9,1... | collective-permute-start | bytes 442376 | tf_op jit(solution)/shard_map/ppermute | solution.py:437
  67.5 2.3 %shard_map.121 = bf16[512,384]{1,0:T(8,128)(2,1)} custom-call(s32[2]{0:T(128)S(1)} %copy-done.2, bf16[640,384]{1,0:T(8,128)(2,1)S(1)} %pad_maximum_fusion.halo, bf16[512,384]{1,0:T(8,128)(2,1)S(1)} %copy-done.3), custom_call_target="tpu_custom_call" | custom-call | flops 2000000000 | bytes 1000000 | tf_op jit(solution)/shard_map/pallas_call | solution.py:396
  69.8 2.9 %shard_map.122 = (f32[384]{0:T(512)}, f32[384,1152]{1,0:T(8,128)}, f32[384,384]{1,0:T(8,128)}) custom-call(s32[2]{0:T(128)S(1)} %pad_add_fusion.place, bf16[192,384]{1,0:T(8,128)(2,1)S(1)} %add_convert_fusion.1.refs_0_, bf16[192,384]{1,0:T(8,128)(2,1)S(1)} %collective-permute-done.12.refs_1_, bf16[192,384]{1,0:T(8,128)(2,1)S(1)} %collective-permute-done.13.refs_2_, ...), custom_call_target="tpu_custom_call" | custom-call | flops 1000000000 | bytes 1000000 | tf_op jit(solution)/shard_map/pallas_call | solution.py:396
  (54 shorter events, 4.7 us)
Async XLA Ops:
  0.6 15.0 %collective-permute-start.2 = (bf16[2,16,16,384]{3,2,1,0:T(8,128)(2,1)}, bf16[2,16,16,384]{3,2,1,0:T(8,128)(2,1)S(1)}, u32[]{:S(2)}, u32[]{:S(2)}) collective-permute-start(bf16[2,16,16,384]{3,2,1,0:T(8,128)(2,1)} %param.8), channel_id=1, source_target_pairs={{2,0},{0,2},{3,1},{1,3},{6,4},{4,6},{7,5},{5,7},{10,8},{8,10},{11,... | collective-permute-start | bytes 1179656 | tf_op jit(solution)/shard_map/ppermute | solution.py:413
  2.4 10.8 %collective-permute-start.1 = (bf16[272,384]{1,0:T(8,128)(2,1)S(1)}, bf16[272,384]{1,0:T(8,128)(2,1)S(1)}, u32[]{:S(2)}, u32[]{:S(2)}) collective-permute-start(bf16[272,384]{1,0:T(8,128)(2,1)S(1)} %fusion.1), channel_id=1, source_target_pairs={{4,0},{8,4},{12,8},{0,12},{5,1},{9,5},{13,9},{1,13},{6,2},{10,6},{... | collective-permute-start | bytes 626696 | tf_op jit(solution)/shard_map/ppermute | solution.py:413
  7.3 7.2 %copy-start.5 = (s32[2,16,16]{2,1,0:T(8,128)S(1)}, s32[2,16,16]{2,1,0:T(8,128)}, u32[]{:S(2)}) copy-start(s32[2,16,16]{2,1,0:T(8,128)} %inner_flags.1) | copy-start | bytes 6148
  14.1 1.6 %collective-permute-start.3 = (bf16[144,384]{1,0:T(8,128)(2,1)S(1)}, bf16[144,384]{1,0:T(8,128)(2,1)S(1)}, u32[]{:S(2)}, u32[]{:S(2)}) collective-permute-start(bf16[144,384]{1,0:T(8,128)(2,1)S(1)} %pad_maximum_fusion.1), channel_id=1, source_target_pairs={{2,0},{0,2},{3,1},{1,3},{6,4},{4,6},{7,5},{5,7},{10,8},{8,10},{11,... | collective-permute-start | bytes 331784 | tf_op jit(solution)/shard_map/ppermute | solution.py:413
  14.4 1.2 %collective-permute-start = (s32[2,16,16]{2,1,0:T(8,128)S(1)}, s32[2,16,16]{2,1,0:T(8,128)S(1)}, u32[]{:S(2)}, u32[]{:S(2)}) collective-permute-start(s32[2,16,16]{2,1,0:T(8,128)S(1)} %copy-done.5), channel_id=1, source_target_pairs={{2,0},{0,2},{3,1},{1,3},{6,4},{4,6},{7,5},{5,7},{10,8},{8,10},{11,... | collective-permute-start | bytes 6152 | tf_op jit(solution)/shard_map/ppermute | solution.py:413
  32.2 6.3 %copy-start.8 = (bf16[256,384]{1,0:T(8,128)(2,1)S(1)}, bf16[256,384]{1,0:T(8,128)(2,1)}, u32[]{:S(2)}) copy-start(bf16[256,384]{1,0:T(8,128)(2,1)} %get-tuple-element.27) | copy-start | bytes 589828
  32.2 6.4 %copy-start.7 = (bf16[256,384]{1,0:T(8,128)(2,1)S(1)}, bf16[256,384]{1,0:T(8,128)(2,1)}, u32[]{:S(2)}) copy-start(bf16[256,384]{1,0:T(8,128)(2,1)} %get-tuple-element.28) | copy-start | bytes 589828
  32.2 2.3 %collective-permute-start.7 = (bf16[768,384]{1,0:T(8,128)(2,1)}, bf16[768,384]{1,0:T(8,128)(2,1)S(1)}, u32[]{:S(2)}, u32[]{:S(2)}) collective-permute-start(bf16[768,384]{1,0:T(8,128)(2,1)} %get-tuple-element.31), channel_id=1, source_target_pairs={{0,2},{2,0},{1,3},{3,1},{4,6},{6,4},{5,7},{7,5},{8,10},{10,8},{9,1... | collective-permute-start | bytes 1769480 | tf_op jit(solution)/shard_map/ppermute | solution.py:437
  35.7 31.7 %copy-start.2 = (s32[2]{0:T(128)S(1)}, s32[2]{0:T(128)}, u32[]{:S(2)}) copy-start(s32[2]{0:T(128)} %shift.3) | copy-start | bytes 28
  35.7 31.7 %copy-start.3 = (bf16[512,384]{1,0:T(8,128)(2,1)S(1)}, bf16[512,384]{1,0:T(8,128)(2,1)}, u32[]{:S(2)}) copy-start(bf16[512,384]{1,0:T(8,128)(2,1)} %get-tuple-element.29.kept_far) | copy-start | bytes 1179652
  35.8 6.2 %collective-permute-start.10 = (bf16[192,384]{1,0:T(8,128)(2,1)S(1)}, bf16[192,384]{1,0:T(8,128)(2,1)S(1)}, u32[]{:S(2)}, u32[]{:S(2)}) collective-permute-start(bf16[192,384]{1,0:T(8,128)(2,1)S(1)} %get-tuple-element.36), channel_id=1, source_target_pairs={{0,5},{1,4},{4,1},{5,0},{8,13},{9,12},{12,9},{13,8},{2,7},{3,6},{6... | collective-permute-start | bytes 442376 | tf_op jit(solution)/shard_map/ppermute | solution.py:437
  36.1 9.2 %collective-permute-start.8 = (bf16[192,384]{1,0:T(8,128)(2,1)S(1)}, bf16[192,384]{1,0:T(8,128)(2,1)S(1)}, u32[]{:S(2)}, u32[]{:S(2)}) collective-permute-start(bf16[192,384]{1,0:T(8,128)(2,1)S(1)} %get-tuple-element.35), channel_id=1, source_target_pairs={{0,4},{4,0},{8,12},{12,8},{1,5},{5,1},{9,13},{13,9},{2,6},{6,2},{1... | collective-permute-start | bytes 442376 | tf_op jit(solution)/shard_map/ppermute | solution.py:437
  38.3 7.4 %collective-permute-start.9 = (bf16[192,384]{1,0:T(8,128)(2,1)S(1)}, bf16[192,384]{1,0:T(8,128)(2,1)S(1)}, u32[]{:S(2)}, u32[]{:S(2)}) collective-permute-start(bf16[192,384]{1,0:T(8,128)(2,1)S(1)} %get-tuple-element.37), channel_id=1, source_target_pairs={{0,1},{1,0},{2,3},{3,2},{4,5},{5,4},{6,7},{7,6},{8,9},{9,8},{10,11... | collective-permute-start | bytes 442376 | tf_op jit(solution)/shard_map/ppermute | solution.py:437
  38.5 11.9 %collective-permute-start.4 = (bf16[256,384]{1,0:T(8,128)(2,1)S(1)}, bf16[256,384]{1,0:T(8,128)(2,1)S(1)}, u32[]{:S(2)}, u32[]{:S(2)}) collective-permute-start(bf16[256,384]{1,0:T(8,128)(2,1)S(1)} %copy-done.8), channel_id=1, source_target_pairs={{12,0},{0,4},{4,8},{8,12},{13,1},{1,5},{5,9},{9,13},{14,2},{2,6},{... | collective-permute-start | bytes 589832 | tf_op jit(solution)/shard_map/ppermute | solution.py:413
  38.6 21.2 %collective-permute-start.5 = (bf16[256,384]{1,0:T(8,128)(2,1)S(1)}, bf16[256,384]{1,0:T(8,128)(2,1)S(1)}, u32[]{:S(2)}, u32[]{:S(2)}) collective-permute-start(bf16[256,384]{1,0:T(8,128)(2,1)S(1)} %copy-done.7), channel_id=1, source_target_pairs={{2,0},{0,2},{3,1},{1,3},{6,4},{4,6},{7,5},{5,7},{10,8},{8,10},{11,... | collective-permute-start | bytes 589832 | tf_op jit(solution)/shard_map/ppermute | solution.py:413
  45.8 11.2 %collective-permute-start.11 = (bf16[192,384]{1,0:T(8,128)(2,1)S(1)}, bf16[192,384]{1,0:T(8,128)(2,1)S(1)}, u32[]{:S(2)}, u32[]{:S(2)}) collective-permute-start(bf16[192,384]{1,0:T(8,128)(2,1)S(1)} %add_convert_fusion.2), channel_id=1, source_target_pairs={{0,8},{4,12},{8,0},{12,4},{1,9},{5,13},{9,1},{13,5},{2,10},{6,14},... | collective-permute-start | bytes 442376 | tf_op jit(solution)/shard_map/ppermute | solution.py:437
  50.4 9.4 %collective-permute-start.6 = (bf16[128,384]{1,0:T(8,128)(2,1)S(1)}, bf16[128,384]{1,0:T(8,128)(2,1)S(1)}, u32[]{:S(2)}, u32[]{:S(2)}) collective-permute-start(bf16[128,384]{1,0:T(8,128)(2,1)S(1)} %slice_bitcast_fusion), channel_id=1, source_target_pairs={{2,0},{0,2},{3,1},{1,3},{6,4},{4,6},{7,5},{5,7},{10,8},{8,10},{11,... | collective-permute-start | bytes 294920 | tf_op jit(solution)/shard_map/ppermute | solution.py:413
  57.0 5.0 %collective-permute-start.12 = (bf16[192,384]{1,0:T(8,128)(2,1)S(1)}, bf16[192,384]{1,0:T(8,128)(2,1)S(1)}, u32[]{:S(2)}, u32[]{:S(2)}) collective-permute-start(bf16[192,384]{1,0:T(8,128)(2,1)S(1)} %add_convert_fusion.1.refs_0_), channel_id=1, source_target_pairs={{0,4},{4,0},{8,12},{12,8},{1,5},{5,1},{9,13},{13,9},{2,6},{6,2},{1... | collective-permute-start | bytes 442376 | tf_op jit(solution)/shard_map/ppermute | solution.py:437
  57.1 7.2 %collective-permute-start.13 = (bf16[192,384]{1,0:T(8,128)(2,1)S(1)}, bf16[192,384]{1,0:T(8,128)(2,1)S(1)}, u32[]{:S(2)}, u32[]{:S(2)}) collective-permute-start(bf16[192,384]{1,0:T(8,128)(2,1)S(1)} %add_convert_fusion.1.refs_0_), channel_id=1, source_target_pairs={{0,1},{1,0},{2,3},{3,2},{4,5},{5,4},{6,7},{7,6},{8,9},{9,8},{10,11... | collective-permute-start | bytes 442376 | tf_op jit(solution)/shard_map/ppermute | solution.py:437
  58.4 7.7 %collective-permute-start.14 = (bf16[192,384]{1,0:T(8,128)(2,1)S(1)}, bf16[192,384]{1,0:T(8,128)(2,1)S(1)}, u32[]{:S(2)}, u32[]{:S(2)}) collective-permute-start(bf16[192,384]{1,0:T(8,128)(2,1)S(1)} %add_convert_fusion.1.refs_0_), channel_id=1, source_target_pairs={{0,5},{1,4},{4,1},{5,0},{8,13},{9,12},{12,9},{13,8},{2,7},{3,6},{6... | collective-permute-start | bytes 442376 | tf_op jit(solution)/shard_map/ppermute | solution.py:437
  59.9 9.9 %collective-permute-start.15 = (bf16[192,384]{1,0:T(8,128)(2,1)S(1)}, bf16[192,384]{1,0:T(8,128)(2,1)S(1)}, u32[]{:S(2)}, u32[]{:S(2)}) collective-permute-start(bf16[192,384]{1,0:T(8,128)(2,1)S(1)} %add_convert_fusion.1.refs_0_), channel_id=1, source_target_pairs={{0,2},{2,0},{1,3},{3,1},{4,6},{6,4},{5,7},{7,5},{8,10},{10,8},{9,1... | collective-permute-start | bytes 442376 | tf_op jit(solution)/shard_map/ppermute | solution.py:437
  62.0 7.8 %collective-permute-start.16 = (bf16[192,384]{1,0:T(8,128)(2,1)S(1)}, bf16[192,384]{1,0:T(8,128)(2,1)S(1)}, u32[]{:S(2)}, u32[]{:S(2)}) collective-permute-start(bf16[192,384]{1,0:T(8,128)(2,1)S(1)} %collective-permute-done.12.refs_1_), channel_id=1, source_target_pairs={{0,2},{2,0},{1,3},{3,1},{4,6},{6,4},{5,7},{7,5},{8,10},{10,8},{9,1... | collective-permute-start | bytes 442376 | tf_op jit(solution)/shard_map/ppermute | solution.py:437
  64.3 5.5 %collective-permute-start.17 = (bf16[192,384]{1,0:T(8,128)(2,1)S(1)}, bf16[192,384]{1,0:T(8,128)(2,1)S(1)}, u32[]{:S(2)}, u32[]{:S(2)}) collective-permute-start(bf16[192,384]{1,0:T(8,128)(2,1)S(1)} %collective-permute-done.13.refs_2_), channel_id=1, source_target_pairs={{0,2},{2,0},{1,3},{3,1},{4,6},{6,4},{5,7},{7,5},{8,10},{10,8},{9,1... | collective-permute-start | bytes 442376 | tf_op jit(solution)/shard_map/ppermute | solution.py:437
  66.1 3.7 %collective-permute-start.18 = (bf16[192,384]{1,0:T(8,128)(2,1)S(1)}, bf16[192,384]{1,0:T(8,128)(2,1)S(1)}, u32[]{:S(2)}, u32[]{:S(2)}) collective-permute-start(bf16[192,384]{1,0:T(8,128)(2,1)S(1)} %collective-permute-done.14.refs_3_), channel_id=1, source_target_pairs={{0,2},{2,0},{1,3},{3,1},{4,6},{6,4},{5,7},{7,5},{8,10},{10,8},{9,1... | collective-permute-start | bytes 442376 | tf_op jit(solution)/shard_map/ppermute | solution.py:437
  (6 other events, 9.1 us)

commit v9 on v8

--- a/solution.py
+++ b/solution.py
@@ -374,12 +374,14 @@
             )
         )
         copies[-1].start()
-        product = block * weight[:, columns].astype(f32)
-        partial = partial + product[:, :128] + product[:, 128:256] + product[:, 256:]
     for pair in range(3):
         out_grad[pair * 128 : pair * 128 + 128, :] = whole[pair * TOKENS : pair * TOKENS + 128]
     copies.append(pltpu.make_async_copy(out_grad, out_far, sems.at[3]))
     copies[-1].start()
+    for kind in range(3):
+        columns = slice(kind * MODEL_WIDTH, (kind + 1) * MODEL_WIDTH)
+        product = qkv_grad[:, columns] * weight[:, columns].astype(f32)
+        partial = partial + product[:, :128] + product[:, 128:256] + product[:, 256:]
     gain_row = gain[...].reshape(1, MODEL_WIDTH)
     gain_grad[...] = (jnp.sum(partial.T, 0, keepdims=True) / gain_row).reshape(MODEL_WIDTH)
     for copy in copies:
@@ -441,13 +443,16 @@
     return sum(piece.astype(f32) for piece in pieces).astype(bf16)
 
 
-def sum_quarter(keep, send):
-    block = add_up(keep, swapped(send, CORE))
+def sum_quarter(keep, send, below):
+    kept = lax.optimization_barrier(keep.astype(f32))
+    block = add_up(kept, swapped(send, CORE))
     share = block.shape[0] // 4
     mine = quarter_index()
-    pick = lambda place: lax.dynamic_slice_in_dim(block, place * share, share, 0)
-    arrived = [swapped(pick(mine ^ k), *GROUPS[k - 1]) for k in (1, 2, 3)]
-    return add_up(pick(mine), *arrived)
+    pick = lambda array, place: lax.dynamic_slice_in_dim(array, place * share, share, 0)
+    late = pick(lax.optimization_barrier(block), mine ^ 3) + below[:share] * 0
+    pieces = [pick(block, mine ^ 1), pick(block, mine ^ 2), late]
+    arrived = [swapped(piece, *group) for piece, group in zip(pieces, GROUPS)]
+    return add_up(pick(block, mine), *arrived)
 
 
 def sum_rest(quarter):
@@ -571,7 +576,7 @@
     across = passed_along(
         below.reshape(2 * RIM, SIDE, width)[:, RIM:].reshape(-1, width), "sx", 1
     )
-    quarter = sum_quarter(keep, send)
+    quarter = sum_quarter(keep, send, below)
     (field_grad,) = local_call(
         place_kernel,
         [wide(TOKENS)],

time: 73.3 us -> 71.9 us (0.981)
  waiting for transfers between devices: 19.5 us -> 15.9 us
  starting transfers between devices: 20.6 us -> 22.4 us
    ppermute x12, waiting for transfers between devices: 15.9 us -> 9.27 us  [swapped(): return lax.ppermute(block, axes, route)]
    ppermute x7, waiting for transfers between devices: 3.59 us -> 6.61 us  [passed_along(): lax.ppermute(block, axis, [((i - distance) % count, i) for i in range(cou...]
    ppermute x7, starting transfers between devices: 7.91 us -> 9.1 us  [passed_along(): lax.ppermute(block, axis, [((i - distance) % count, i) for i in range(cou...]
    convert_element_type x0 -> x1, other arithmetic: none -> 1.14 us  [sum_quarter(): kept = lax.optimization_barrier(keep.astype(f32))]
    convert_element_type x3, other arithmetic: 1.34 us -> 0.27 us  [add_up(): return sum((piece.astype(f32) for piece in pieces)).astype(bf16)]
  transfers between devices with their start and end apart: 19 -> 19, of which waited for: 9 -> 6; matrix products, arithmetic and copies ran while one was open for 4% -> 6% of each run, Pallas kernels for 11% -> 12%
where the time goes in v9:
time: 71.9 us; the launch traced here: 71.1 us
  Pallas kernels  26.8 us (37%)
  starting transfers between devices  22.4 us (31%)
  waiting for transfers between devices  15.9 us (22%)
  other arithmetic  3.06 us (4%)
  local copies, waits for them, and re-layouts  1.83 us (3%)
  between operations  1.08 us (2%)
    pallas_call x4, Pallas kernels, local_call(): pl.pallas_call(kernel, out_shape=[jax.ShapeDtypeStruct(shape, dtype) for...  26.8 us
    ppermute x12, starting transfers between devices, swapped(): return lax.ppermute(block, axes, route)  13.3 us
    ppermute x12, waiting for transfers between devices, swapped(): return lax.ppermute(block, axes, route)  9.27 us
    ppermute x7, starting transfers between devices, passed_along(): lax.ppermute(block, axis, [((i - distance) % count, i) for i in range(cou...  9.1 us
    ppermute x7, waiting for transfers between devices, passed_along(): lax.ppermute(block, axis, [((i - distance) % count, i) for i in range(cou...  6.61 us
  transfers between devices with their start and end apart: 19, of which 6 were waited for; matrix products, arithmetic and copies ran while one was open for 6% of the time, Pallas kernels for 12%

profile of v9, /device:TPU:1, one launch (start us, length us, event | category | flops | bytes accessed | tf_op | source)
XLA Modules:
  0.0 71.1 jit_solution(1696448794590887380)
XLA Ops:
  0.8 0.9 %slice.22 = bf16[2,8,16,384]{3,2,1,0:T(8,128)(2,1)S(1)} slice(bf16[2,16,16,384]{3,2,1,0:T(8,128)(2,1)} %param.8), slice={[0:2], [0:8], [0:16], [0:384]} | slice | bytes 393216 | tf_op jit(solution)/shard_map/slice | solution.py:488
  1.7 0.7 fusion.3
  2.4 4.8 %collective-permute-start.1 = (bf16[272,384]{1,0:T(8,128)(2,1)S(1)}, bf16[272,384]{1,0:T(8,128)(2,1)S(1)}, u32[]{:S(2)}, u32[]{:S(2)}) collective-permute-start(bf16[272,384]{1,0:T(8,128)(2,1)S(1)} %fusion.1), channel_id=1, source_target_pairs={{4,0},{8,4},{12,8},{0,12},{5,1},{9,5},{13,9},{1,13},{6,2},{10,6},{... | collective-permute-start | bytes 626696 | tf_op jit(solution)/shard_map/ppermute | solution.py:415
  7.3 6.0 %shard_map.119 = (bf16[16,384]{1,0:T(8,128)(2,1)}, f32[6,256,256]{2,1,0:T(8,128)}, f32[6,256,256]{2,1,0:T(8,128)}, f32[6,256,256]{2,1,0:T(8,128)}, bf16[384,512]{1,0:T(8,128)(2,1)}, /*index=5*/bf16[1152,384]{1,0:T(8,128)(2,1)}) custom-call(f32[6,2883]{1,0:T(8,128)} %position_bias.1, bf16[512,384]{1,0:T(8,128)(2,1)} %bitcast.20, ...), custom_call_target="tpu_custom_call" | custom-call | flops 3000000000 | bytes 1000000 | tf_op jit(solution)/shard_map/pallas_call | solution.py:398
  13.3 0.7 %slice_add_fusion = bf16[16,384]{1,0:T(8,128)(2,1)S(1)} fusion(bf16[16,384]{1,0:T(8,128)(2,1)} %get-tuple-element.20, bf16[272,384]{1,0:T(8,128)(2,1)S(1)} %collective-permute-done.1.rows_far), kind=kLoop, calls=%fused_computation.12 | loop fusion | flops 6144 | bytes 36864 | tf_op jit(solution)/shard_map/add | solution.py:520
  14.6 1.0 %collective-permute-done.col_flags = s32[2,16,16]{2,1,0:T(8,128)S(1)} collective-permute-done((s32[2,16,16]{2,1,0:T(8,128)S(1)}, s32[2,16,16]{2,1,0:T(8,128)S(1)}, u32[]{:S(2)}, u32[]{:S(2)}) %collective-permute-start) | collective-permute-done | bytes 2080 | tf_op jit(solution)/shard_map/ppermute | solution.py:415
  15.6 0.6 copy-done.10
  16.4 15.8 %shard_map.120 = (bf16[768,384]{1,0:T(8,128)(2,1)}, bf16[768,384]{1,0:T(8,128)(2,1)}, bf16[512,384]{1,0:T(8,128)(2,1)}, bf16[512,384]{1,0:T(8,128)(2,1)}, bf16[2...) custom-call(s32[2]{0:T(128)} %shift.3, s32[1]{0:T(128)} %bitcast.core, s32[2,16,16]{2,1,0:T(8,128)} %inner_flags.1, ...), custom_call_target="tpu_custom_call" | custom-call | flops 12000000000 | bytes 1000000 | tf_op jit(solution)/shard_map/pallas_call | solution.py:398
  32.5 1.1 %convert_element_type.40 = f32[768,384]{1,0:T(8,128)S(1)} convert(bf16[768,384]{1,0:T(8,128)(2,1)} %get-tuple-element.30) | non-fusion elementwise | flops 294912 | bytes 1769472 | tf_op jit(solution)/shard_map/convert_element_type | solution.py:447
  33.7 0.8 %collective-permute-done.7 = bf16[768,384]{1,0:T(8,128)(2,1)S(1)} collective-permute-done((bf16[768,384]{1,0:T(8,128)(2,1)}, bf16[768,384]{1,0:T(8,128)(2,1)S(1)}, u32[]{:S(2)}, u32[]{:S(2)}) %collective-permute-start.7) | collective-permute-done | bytes 589856 | tf_op jit(solution)/shard_map/ppermute | solution.py:439
  34.8 1.3 %collective-permute-start.9 = (bf16[192,384]{1,0:T(8,128)(2,1)S(1)}, bf16[192,384]{1,0:T(8,128)(2,1)S(1)}, u32[]{:S(2)}, u32[]{:S(2)}) collective-permute-start(bf16[192,384]{1,0:T(8,128)(2,1)S(1)} %get-tuple-element.36), channel_id=1, source_target_pairs={{0,1},{1,0},{2,3},{3,2},{4,5},{5,4},{6,7},{7,6},{8,9},{9,8},{10,11... | collective-permute-start | bytes 442376 | tf_op jit(solution)/shard_map/ppermute | solution.py:439
  36.1 5.6 %collective-permute-done.4 = bf16[256,384]{1,0:T(8,128)(2,1)S(1)} collective-permute-done((bf16[256,384]{1,0:T(8,128)(2,1)S(1)}, bf16[256,384]{1,0:T(8,128)(2,1)S(1)}, u32[]{:S(2)}, u32[]{:S(2)}) %collective-permute-start.4) | collective-permute-done | bytes 196640 | tf_op jit(solution)/shard_map/ppermute | solution.py:415
  41.9 1.9 %collective-permute-start.5 = (bf16[256,384]{1,0:T(8,128)(2,1)S(1)}, bf16[256,384]{1,0:T(8,128)(2,1)S(1)}, u32[]{:S(2)}, u32[]{:S(2)}) collective-permute-start(bf16[256,384]{1,0:T(8,128)(2,1)S(1)} %copy-done.7), channel_id=1, source_target_pairs={{2,0},{0,2},{3,1},{1,3},{6,4},{4,6},{7,5},{5,7},{10,8},{8,10},{11,... | collective-permute-start | bytes 589832 | tf_op jit(solution)/shard_map/ppermute | solution.py:415
  43.8 0.5 collective-permute-done.8
  44.2 2.8 %collective-permute-done.10 = bf16[192,384]{1,0:T(8,128)(2,1)S(1)} collective-permute-done((bf16[192,384]{1,0:T(8,128)(2,1)S(1)}, bf16[192,384]{1,0:T(8,128)(2,1)S(1)}, u32[]{:S(2)}, u32[]{:S(2)}) %collective-permute-start.10) | collective-permute-done | bytes 147488 | tf_op jit(solution)/shard_map/ppermute | solution.py:439
  47.2 2.1 %collective-permute-start.11 = (bf16[192,384]{1,0:T(8,128)(2,1)S(1)}, bf16[192,384]{1,0:T(8,128)(2,1)S(1)}, u32[]{:S(2)}, u32[]{:S(2)}) collective-permute-start(bf16[192,384]{1,0:T(8,128)(2,1)S(1)} %add_convert_fusion.2), channel_id=1, source_target_pairs={{0,8},{4,12},{8,0},{12,4},{1,9},{5,13},{9,1},{13,5},{2,10},{6,14},... | collective-permute-start | bytes 442376 | tf_op jit(solution)/shard_map/ppermute | solution.py:439
  49.2 1.6 %collective-permute-start.6 = (bf16[128,384]{1,0:T(8,128)(2,1)S(1)}, bf16[128,384]{1,0:T(8,128)(2,1)S(1)}, u32[]{:S(2)}, u32[]{:S(2)}) collective-permute-start(bf16[128,384]{1,0:T(8,128)(2,1)S(1)} %slice_bitcast_fusion), channel_id=1, source_target_pairs={{2,0},{0,2},{3,1},{1,3},{6,4},{4,6},{7,5},{5,7},{10,8},{8,10},{11,... | collective-permute-start | bytes 294920 | tf_op jit(solution)/shard_map/ppermute | solution.py:415
  50.9 5.2 %collective-permute-done.11 = bf16[192,384]{1,0:T(8,128)(2,1)S(1)} collective-permute-done((bf16[192,384]{1,0:T(8,128)(2,1)S(1)}, bf16[192,384]{1,0:T(8,128)(2,1)S(1)}, u32[]{:S(2)}, u32[]{:S(2)}) %collective-permute-start.11) | collective-permute-done | bytes 147488 | tf_op jit(solution)/shard_map/ppermute | solution.py:439
  56.3 2.4 %collective-permute-start.14 = (bf16[192,384]{1,0:T(8,128)(2,1)S(1)}, bf16[192,384]{1,0:T(8,128)(2,1)S(1)}, u32[]{:S(2)}, u32[]{:S(2)}) collective-permute-start(bf16[192,384]{1,0:T(8,128)(2,1)S(1)} %add_convert_fusion.1.refs_0_), channel_id=1, source_target_pairs={{0,5},{1,4},{4,1},{5,0},{8,13},{9,12},{12,9},{13,8},{2,7},{3,6},{6... | collective-permute-start | bytes 442376 | tf_op jit(solution)/shard_map/ppermute | solution.py:439
  58.9 2.4 %collective-permute-start.15 = (bf16[192,384]{1,0:T(8,128)(2,1)S(1)}, bf16[192,384]{1,0:T(8,128)(2,1)S(1)}, u32[]{:S(2)}, u32[]{:S(2)}) collective-permute-start(bf16[192,384]{1,0:T(8,128)(2,1)S(1)} %add_convert_fusion.1.refs_0_), channel_id=1, source_target_pairs={{0,2},{2,0},{1,3},{3,1},{4,6},{6,4},{5,7},{7,5},{8,10},{10,8},{9,1... | collective-permute-start | bytes 442376 | tf_op jit(solution)/shard_map/ppermute | solution.py:439
  61.4 2.6 %collective-permute-start.16 = (bf16[192,384]{1,0:T(8,128)(2,1)S(1)}, bf16[192,384]{1,0:T(8,128)(2,1)S(1)}, u32[]{:S(2)}, u32[]{:S(2)}) collective-permute-start(bf16[192,384]{1,0:T(8,128)(2,1)S(1)} %collective-permute-done.12.refs_1_), channel_id=1, source_target_pairs={{0,2},{2,0},{1,3},{3,1},{4,6},{6,4},{5,7},{7,5},{8,10},{10,8},{9,1... | collective-permute-start | bytes 442376 | tf_op jit(solution)/shard_map/ppermute | solution.py:439
  64.0 1.8 %collective-permute-start.17 = (bf16[192,384]{1,0:T(8,128)(2,1)S(1)}, bf16[192,384]{1,0:T(8,128)(2,1)S(1)}, u32[]{:S(2)}, u32[]{:S(2)}) collective-permute-start(bf16[192,384]{1,0:T(8,128)(2,1)S(1)} %collective-permute-done.13.refs_2_), channel_id=1, source_target_pairs={{0,2},{2,0},{1,3},{3,1},{4,6},{6,4},{5,7},{7,5},{8,10},{10,8},{9,1... | collective-permute-start | bytes 442376 | tf_op jit(solution)/shard_map/ppermute | solution.py:439
  65.8 2.3 %shard_map.121 = bf16[512,384]{1,0:T(8,128)(2,1)} custom-call(s32[2]{0:T(128)S(1)} %copy-done.2, bf16[640,384]{1,0:T(8,128)(2,1)S(1)} %pad_maximum_fusion.halo, bf16[512,384]{1,0:T(8,128)(2,1)S(1)} %copy-done.3), custom_call_target="tpu_custom_call" | custom-call | flops 2000000000 | bytes 1000000 | tf_op jit(solution)/shard_map/pallas_call | solution.py:398
  68.1 2.8 %shard_map.122 = (f32[384]{0:T(512)}, f32[384,1152]{1,0:T(8,128)}, f32[384,384]{1,0:T(8,128)}) custom-call(s32[2]{0:T(128)S(1)} %pad_add_fusion.place, bf16[192,384]{1,0:T(8,128)(2,1)S(1)} %add_convert_fusion.1.refs_0_, bf16[192,384]{1,0:T(8,128)(2,1)S(1)} %collective-permute-done.12.refs_1_, bf16[192,384]{1,0:T(8,128)(2,1)S(1)} %collective-permute-done.13.refs_2_, ...), custom_call_target="tpu_custom_call" | custom-call | flops 1000000000 | bytes 1000000 | tf_op jit(solution)/shard_map/pallas_call | solution.py:398
  (56 shorter events, 2.3 us)
Async XLA Ops:
  0.6 15.0 %collective-permute-start.2 = (bf16[2,16,16,384]{3,2,1,0:T(8,128)(2,1)}, bf16[2,16,16,384]{3,2,1,0:T(8,128)(2,1)S(1)}, u32[]{:S(2)}, u32[]{:S(2)}) collective-permute-start(bf16[2,16,16,384]{3,2,1,0:T(8,128)(2,1)} %param.8), channel_id=1, source_target_pairs={{2,0},{0,2},{3,1},{1,3},{6,4},{4,6},{7,5},{5,7},{10,8},{8,10},{11,... | collective-permute-start | bytes 1179656 | tf_op jit(solution)/shard_map/ppermute | solution.py:415
  2.4 10.8 %collective-permute-start.1 = (bf16[272,384]{1,0:T(8,128)(2,1)S(1)}, bf16[272,384]{1,0:T(8,128)(2,1)S(1)}, u32[]{:S(2)}, u32[]{:S(2)}) collective-permute-start(bf16[272,384]{1,0:T(8,128)(2,1)S(1)} %fusion.1), channel_id=1, source_target_pairs={{4,0},{8,4},{12,8},{0,12},{5,1},{9,5},{13,9},{1,13},{6,2},{10,6},{... | collective-permute-start | bytes 626696 | tf_op jit(solution)/shard_map/ppermute | solution.py:415
  7.3 7.2 %copy-start.5 = (s32[2,16,16]{2,1,0:T(8,128)S(1)}, s32[2,16,16]{2,1,0:T(8,128)}, u32[]{:S(2)}) copy-start(s32[2,16,16]{2,1,0:T(8,128)} %inner_flags.1) | copy-start | bytes 6148
  13.2 2.4 %copy-start.4 = (bf16[272,384]{1,0:T(8,128)(2,1)}, bf16[272,384]{1,0:T(8,128)(2,1)S(1)}, u32[]{:S(2)}) copy-start(bf16[272,384]{1,0:T(8,128)(2,1)S(1)} %collective-permute-done.1.rows_far) | copy-start | bytes 626692
  14.1 1.6 %collective-permute-start.3 = (bf16[144,384]{1,0:T(8,128)(2,1)S(1)}, bf16[144,384]{1,0:T(8,128)(2,1)S(1)}, u32[]{:S(2)}, u32[]{:S(2)}) collective-permute-start(bf16[144,384]{1,0:T(8,128)(2,1)S(1)} %pad_maximum_fusion.1), channel_id=1, source_target_pairs={{2,0},{0,2},{3,1},{1,3},{6,4},{4,6},{7,5},{5,7},{10,8},{8,10},{11,... | collective-permute-start | bytes 331784 | tf_op jit(solution)/shard_map/ppermute | solution.py:415
  14.4 1.2 %collective-permute-start = (s32[2,16,16]{2,1,0:T(8,128)S(1)}, s32[2,16,16]{2,1,0:T(8,128)S(1)}, u32[]{:S(2)}, u32[]{:S(2)}) collective-permute-start(s32[2,16,16]{2,1,0:T(8,128)S(1)} %copy-done.5), channel_id=1, source_target_pairs={{2,0},{0,2},{3,1},{1,3},{6,4},{4,6},{7,5},{5,7},{10,8},{8,10},{11,... | collective-permute-start | bytes 6152 | tf_op jit(solution)/shard_map/ppermute | solution.py:415
  32.2 2.3 %collective-permute-start.7 = (bf16[768,384]{1,0:T(8,128)(2,1)}, bf16[768,384]{1,0:T(8,128)(2,1)S(1)}, u32[]{:S(2)}, u32[]{:S(2)}) collective-permute-start(bf16[768,384]{1,0:T(8,128)(2,1)} %get-tuple-element.31), channel_id=1, source_target_pairs={{0,2},{2,0},{1,3},{3,1},{4,6},{6,4},{5,7},{7,5},{8,10},{10,8},{9,1... | collective-permute-start | bytes 1769480 | tf_op jit(solution)/shard_map/ppermute | solution.py:439
  33.6 8.2 %copy-start.7 = (bf16[256,384]{1,0:T(8,128)(2,1)S(1)}, bf16[256,384]{1,0:T(8,128)(2,1)}, u32[]{:S(2)}) copy-start(bf16[256,384]{1,0:T(8,128)(2,1)} %get-tuple-element.28) | copy-start | bytes 589828
  33.7 8.0 %collective-permute-start.4 = (bf16[256,384]{1,0:T(8,128)(2,1)S(1)}, bf16[256,384]{1,0:T(8,128)(2,1)S(1)}, u32[]{:S(2)}, u32[]{:S(2)}) collective-permute-start(bf16[256,384]{1,0:T(8,128)(2,1)S(1)} %copy-done.8), channel_id=1, source_target_pairs={{12,0},{0,4},{4,8},{8,12},{13,1},{1,5},{5,9},{9,13},{14,2},{2,6},{... | collective-permute-start | bytes 589832 | tf_op jit(solution)/shard_map/ppermute | solution.py:415
  34.6 31.1 %copy-start.2 = (s32[2]{0:T(128)S(1)}, s32[2]{0:T(128)}, u32[]{:S(2)}) copy-start(s32[2]{0:T(128)} %shift.3) | copy-start | bytes 28
  34.7 31.1 %copy-start.3 = (bf16[512,384]{1,0:T(8,128)(2,1)S(1)}, bf16[512,384]{1,0:T(8,128)(2,1)}, u32[]{:S(2)}) copy-start(bf16[512,384]{1,0:T(8,128)(2,1)} %get-tuple-element.29.kept_far) | copy-start | bytes 1179652
  34.7 9.5 %collective-permute-start.8 = (bf16[192,384]{1,0:T(8,128)(2,1)S(1)}, bf16[192,384]{1,0:T(8,128)(2,1)S(1)}, u32[]{:S(2)}, u32[]{:S(2)}) collective-permute-start(bf16[192,384]{1,0:T(8,128)(2,1)S(1)} %get-tuple-element.35), channel_id=1, source_target_pairs={{0,4},{4,0},{8,12},{12,8},{1,5},{5,1},{9,13},{13,9},{2,6},{6,2},{1... | collective-permute-start | bytes 442376 | tf_op jit(solution)/shard_map/ppermute | solution.py:439
  34.8 9.4 %collective-permute-start.9 = (bf16[192,384]{1,0:T(8,128)(2,1)S(1)}, bf16[192,384]{1,0:T(8,128)(2,1)S(1)}, u32[]{:S(2)}, u32[]{:S(2)}) collective-permute-start(bf16[192,384]{1,0:T(8,128)(2,1)S(1)} %get-tuple-element.36), channel_id=1, source_target_pairs={{0,1},{1,0},{2,3},{3,2},{4,5},{5,4},{6,7},{7,6},{8,9},{9,8},{10,11... | collective-permute-start | bytes 442376 | tf_op jit(solution)/shard_map/ppermute | solution.py:439
  41.8 5.3 %collective-permute-start.10 = (bf16[192,384]{1,0:T(8,128)(2,1)S(1)}, bf16[192,384]{1,0:T(8,128)(2,1)S(1)}, u32[]{:S(2)}, u32[]{:S(2)}) collective-permute-start(bf16[192,384]{1,0:T(8,128)(2,1)S(1)} %fusion.2), channel_id=1, source_target_pairs={{0,5},{1,4},{4,1},{5,0},{8,13},{9,12},{12,9},{13,8},{2,7},{3,6},{6... | collective-permute-start | bytes 442376 | tf_op jit(solution)/shard_map/ppermute | solution.py:439
  41.9 17.0 %collective-permute-start.5 = (bf16[256,384]{1,0:T(8,128)(2,1)S(1)}, bf16[256,384]{1,0:T(8,128)(2,1)S(1)}, u32[]{:S(2)}, u32[]{:S(2)}) collective-permute-start(bf16[256,384]{1,0:T(8,128)(2,1)S(1)} %copy-done.7), channel_id=1, source_target_pairs={{2,0},{0,2},{3,1},{1,3},{6,4},{4,6},{7,5},{5,7},{10,8},{8,10},{11,... | collective-permute-start | bytes 589832 | tf_op jit(solution)/shard_map/ppermute | solution.py:415
  47.2 8.8 %collective-permute-start.11 = (bf16[192,384]{1,0:T(8,128)(2,1)S(1)}, bf16[192,384]{1,0:T(8,128)(2,1)S(1)}, u32[]{:S(2)}, u32[]{:S(2)}) collective-permute-start(bf16[192,384]{1,0:T(8,128)(2,1)S(1)} %add_convert_fusion.2), channel_id=1, source_target_pairs={{0,8},{4,12},{8,0},{12,4},{1,9},{5,13},{9,1},{13,5},{2,10},{6,14},... | collective-permute-start | bytes 442376 | tf_op jit(solution)/shard_map/ppermute | solution.py:439
  49.2 9.6 %collective-permute-start.6 = (bf16[128,384]{1,0:T(8,128)(2,1)S(1)}, bf16[128,384]{1,0:T(8,128)(2,1)S(1)}, u32[]{:S(2)}, u32[]{:S(2)}) collective-permute-start(bf16[128,384]{1,0:T(8,128)(2,1)S(1)} %slice_bitcast_fusion), channel_id=1, source_target_pairs={{2,0},{0,2},{3,1},{1,3},{6,4},{4,6},{7,5},{5,7},{10,8},{8,10},{11,... | collective-permute-start | bytes 294920 | tf_op jit(solution)/shard_map/ppermute | solution.py:415
  56.1 5.3 %collective-permute-start.12 = (bf16[192,384]{1,0:T(8,128)(2,1)S(1)}, bf16[192,384]{1,0:T(8,128)(2,1)S(1)}, u32[]{:S(2)}, u32[]{:S(2)}) collective-permute-start(bf16[192,384]{1,0:T(8,128)(2,1)S(1)} %add_convert_fusion.1.refs_0_), channel_id=1, source_target_pairs={{0,4},{4,0},{8,12},{12,8},{1,5},{5,1},{9,13},{13,9},{2,6},{6,2},{1... | collective-permute-start | bytes 442376 | tf_op jit(solution)/shard_map/ppermute | solution.py:439
  56.3 7.6 %collective-permute-start.13 = (bf16[192,384]{1,0:T(8,128)(2,1)S(1)}, bf16[192,384]{1,0:T(8,128)(2,1)S(1)}, u32[]{:S(2)}, u32[]{:S(2)}) collective-permute-start(bf16[192,384]{1,0:T(8,128)(2,1)S(1)} %add_convert_fusion.1.refs_0_), channel_id=1, source_target_pairs={{0,1},{1,0},{2,3},{3,2},{4,5},{5,4},{6,7},{7,6},{8,9},{9,8},{10,11... | collective-permute-start | bytes 442376 | tf_op jit(solution)/shard_map/ppermute | solution.py:439
  56.3 9.4 %collective-permute-start.14 = (bf16[192,384]{1,0:T(8,128)(2,1)S(1)}, bf16[192,384]{1,0:T(8,128)(2,1)S(1)}, u32[]{:S(2)}, u32[]{:S(2)}) collective-permute-start(bf16[192,384]{1,0:T(8,128)(2,1)S(1)} %add_convert_fusion.1.refs_0_), channel_id=1, source_target_pairs={{0,5},{1,4},{4,1},{5,0},{8,13},{9,12},{12,9},{13,8},{2,7},{3,6},{6... | collective-permute-start | bytes 442376 | tf_op jit(solution)/shard_map/ppermute | solution.py:439
  58.9 9.2 %collective-permute-start.15 = (bf16[192,384]{1,0:T(8,128)(2,1)S(1)}, bf16[192,384]{1,0:T(8,128)(2,1)S(1)}, u32[]{:S(2)}, u32[]{:S(2)}) collective-permute-start(bf16[192,384]{1,0:T(8,128)(2,1)S(1)} %add_convert_fusion.1.refs_0_), channel_id=1, source_target_pairs={{0,2},{2,0},{1,3},{3,1},{4,6},{6,4},{5,7},{7,5},{8,10},{10,8},{9,1... | collective-permute-start | bytes 442376 | tf_op jit(solution)/shard_map/ppermute | solution.py:439
  61.4 6.7 %collective-permute-start.16 = (bf16[192,384]{1,0:T(8,128)(2,1)S(1)}, bf16[192,384]{1,0:T(8,128)(2,1)S(1)}, u32[]{:S(2)}, u32[]{:S(2)}) collective-permute-start(bf16[192,384]{1,0:T(8,128)(2,1)S(1)} %collective-permute-done.12.refs_1_), channel_id=1, source_target_pairs={{0,2},{2,0},{1,3},{3,1},{4,6},{6,4},{5,7},{7,5},{8,10},{10,8},{9,1... | collective-permute-start | bytes 442376 | tf_op jit(solution)/shard_map/ppermute | solution.py:439
  64.0 4.1 %collective-permute-start.17 = (bf16[192,384]{1,0:T(8,128)(2,1)S(1)}, bf16[192,384]{1,0:T(8,128)(2,1)S(1)}, u32[]{:S(2)}, u32[]{:S(2)}) collective-permute-start(bf16[192,384]{1,0:T(8,128)(2,1)S(1)} %collective-permute-done.13.refs_2_), channel_id=1, source_target_pairs={{0,2},{2,0},{1,3},{3,1},{4,6},{6,4},{5,7},{7,5},{8,10},{10,8},{9,1... | collective-permute-start | bytes 442376 | tf_op jit(solution)/shard_map/ppermute | solution.py:439
  65.8 2.4 %collective-permute-start.18 = (bf16[192,384]{1,0:T(8,128)(2,1)S(1)}, bf16[192,384]{1,0:T(8,128)(2,1)S(1)}, u32[]{:S(2)}, u32[]{:S(2)}) collective-permute-start(bf16[192,384]{1,0:T(8,128)(2,1)S(1)} %collective-permute-done.14.refs_3_), channel_id=1, source_target_pairs={{0,2},{2,0},{1,3},{3,1},{4,6},{6,4},{5,7},{7,5},{8,10},{10,8},{9,1... | collective-permute-start | bytes 442376 | tf_op jit(solution)/shard_map/ppermute | solution.py:439
  (6 other events, 8.2 us)

commit v10 on v9

--- a/solution.py
+++ b/solution.py
@@ -443,15 +443,13 @@
     return sum(piece.astype(f32) for piece in pieces).astype(bf16)
 
 
-def sum_quarter(keep, send, below):
+def sum_quarter(keep, send):
     kept = lax.optimization_barrier(keep.astype(f32))
     block = add_up(kept, swapped(send, CORE))
     share = block.shape[0] // 4
     mine = quarter_index()
     pick = lambda array, place: lax.dynamic_slice_in_dim(array, place * share, share, 0)
-    late = pick(lax.optimization_barrier(block), mine ^ 3) + below[:share] * 0
-    pieces = [pick(block, mine ^ 1), pick(block, mine ^ 2), late]
-    arrived = [swapped(piece, *group) for piece, group in zip(pieces, GROUPS)]
+    arrived = [swapped(pick(block, mine ^ k), *GROUPS[k - 1]) for k in (1, 2, 3)]
     return add_up(pick(block, mine), *arrived)
 
 
@@ -514,10 +512,11 @@
         micros=3,
         limit=62,
     )
+    zeros = lax.optimization_barrier(blank + blank)
     corner_message = jnp.concatenate(
         [
             rows[: 2 * RIM * SIDE].reshape(2 * RIM, SIDE, width)[:, :RIM].reshape(-1, width),
-            rows[2 * RIM * SIDE :] + blank,
+            rows[2 * RIM * SIDE :] + zeros,
         ],
         0,
     )
@@ -576,7 +575,7 @@
     across = passed_along(
         below.reshape(2 * RIM, SIDE, width)[:, RIM:].reshape(-1, width), "sx", 1
     )
-    quarter = sum_quarter(keep, send, below)
+    quarter = sum_quarter(keep, send)
     (field_grad,) = local_call(
         place_kernel,
         [wide(TOKENS)],

time: 71.9 us -> 71.3 us (level)
  waiting for transfers between devices: 15.9 us -> 15 us
    ppermute x7, waiting for transfers between devices: 6.61 us -> 3.67 us  [passed_along(): lax.ppermute(block, axis, [((i - distance) % count, i) for i in range(cou...]
    ppermute x12, waiting for transfers between devices: 9.27 us -> 11.3 us  [swapped(): return lax.ppermute(block, axes, route)]
    ppermute x12, starting transfers between devices: 13.3 us -> 15.4 us  [swapped(): return lax.ppermute(block, axes, route)]
    ppermute x7, starting transfers between devices: 9.1 us -> 7.78 us  [passed_along(): lax.ppermute(block, axis, [((i - distance) % count, i) for i in range(cou...]
  transfers between devices with their start and end apart: 19 -> 19, of which waited for: 6 -> 8; matrix products, arithmetic and copies ran while one was open for 6% -> 6% of each run, Pallas kernels for 12% -> 12%
where the time goes in v10:
time: 71.3 us; the launch traced here: 70.9 us
  Pallas kernels  26.8 us (38%)
  starting transfers between devices  23.1 us (32%)
  waiting for transfers between devices  15 us (21%)
  other arithmetic  3.07 us (4%)
  local copies, waits for them, and re-layouts  1.84 us (3%)
  between operations  1.04 us (1%)
    pallas_call x4, Pallas kernels, local_call(): pl.pallas_call(kernel, out_shape=[jax.ShapeDtypeStruct(shape, dtype) for...  26.8 us
    ppermute x12, starting transfers between devices, swapped(): return lax.ppermute(block, axes, route)  15.4 us
    ppermute x12, waiting for transfers between devices, swapped(): return lax.ppermute(block, axes, route)  11.3 us
    ppermute x7, starting transfers between devices, passed_along(): lax.ppermute(block, axis, [((i - distance) % count, i) for i in range(cou...  7.78 us
    ppermute x7, waiting for transfers between devices, passed_along(): lax.ppermute(block, axis, [((i - distance) % count, i) for i in range(cou...  3.67 us
  transfers between devices with their start and end apart: 19, of which 8 were waited for; matrix products, arithmetic and copies ran while one was open for 6% of the time, Pallas kernels for 12%

profile of v10, /device:TPU:1, one launch (start us, length us, event | category | flops | bytes accessed | tf_op | source)
XLA Modules:
  0.0 70.9 jit_solution(14619304501219509424)
XLA Ops:
  0.8 0.9 %slice.19 = bf16[2,8,16,384]{3,2,1,0:T(8,128)(2,1)S(1)} slice(bf16[2,16,16,384]{3,2,1,0:T(8,128)(2,1)} %param.8), slice={[0:2], [0:8], [0:16], [0:384]} | slice | bytes 393216 | tf_op jit(solution)/shard_map/slice | solution.py:486
  2.4 4.8 %collective-permute-start.1 = (bf16[272,384]{1,0:T(8,128)(2,1)S(1)}, bf16[272,384]{1,0:T(8,128)(2,1)S(1)}, u32[]{:S(2)}, u32[]{:S(2)}) collective-permute-start(bf16[272,384]{1,0:T(8,128)(2,1)S(1)} %fusion.1), channel_id=1, source_target_pairs={{4,0},{8,4},{12,8},{0,12},{5,1},{9,5},{13,9},{1,13},{6,2},{10,6},{... | collective-permute-start | bytes 626696 | tf_op jit(solution)/shard_map/ppermute | solution.py:415
  7.3 6.0 %shard_map.119 = (bf16[16,384]{1,0:T(8,128)(2,1)}, f32[6,256,256]{2,1,0:T(8,128)}, f32[6,256,256]{2,1,0:T(8,128)}, f32[6,256,256]{2,1,0:T(8,128)}, bf16[384,512]{1,0:T(8,128)(2,1)}, /*index=5*/bf16[1152,384]{1,0:T(8,128)(2,1)}) custom-call(f32[6,2883]{1,0:T(8,128)} %position_bias.1, bf16[512,384]{1,0:T(8,128)(2,1)} %bitcast.20, ...), custom_call_target="tpu_custom_call" | custom-call | flops 3000000000 | bytes 1000000 | tf_op jit(solution)/shard_map/pallas_call | solution.py:398
  13.2 0.8 %add.42 = bf16[16,384]{1,0:T(8,128)(2,1)S(1)} add(bf16[16,384]{1,0:T(8,128)(2,1)} %get-tuple-element.20, bf16[16,384]{1,0:T(8,128)(2,1)} %get-tuple-element.20) | non-fusion elementwise | flops 6144 | bytes 36864 | tf_op jit(solution)/shard_map/add | solution.py:515
  14.7 1.0 %collective-permute-done.col_flags = s32[2,16,16]{2,1,0:T(8,128)S(1)} collective-permute-done((s32[2,16,16]{2,1,0:T(8,128)S(1)}, s32[2,16,16]{2,1,0:T(8,128)S(1)}, u32[]{:S(2)}, u32[]{:S(2)}) %collective-permute-start) | collective-permute-done | bytes 2080 | tf_op jit(solution)/shard_map/ppermute | solution.py:415
  16.5 15.8 %shard_map.120 = (bf16[768,384]{1,0:T(8,128)(2,1)}, bf16[768,384]{1,0:T(8,128)(2,1)}, bf16[512,384]{1,0:T(8,128)(2,1)}, bf16[512,384]{1,0:T(8,128)(2,1)}, bf16[2...) custom-call(s32[2]{0:T(128)} %shift.3, s32[1]{0:T(128)} %bitcast.core, s32[2,16,16]{2,1,0:T(8,128)} %inner_flags.1, ...), custom_call_target="tpu_custom_call" | custom-call | flops 12000000000 | bytes 1000000 | tf_op jit(solution)/shard_map/pallas_call | solution.py:398
  32.5 1.1 %convert_element_type.40 = f32[768,384]{1,0:T(8,128)S(1)} convert(bf16[768,384]{1,0:T(8,128)(2,1)} %get-tuple-element.30) | non-fusion elementwise | flops 294912 | bytes 1769472 | tf_op jit(solution)/shard_map/convert_element_type | solution.py:447
  33.7 0.8 %collective-permute-done.7 = bf16[768,384]{1,0:T(8,128)(2,1)S(1)} collective-permute-done((bf16[768,384]{1,0:T(8,128)(2,1)}, bf16[768,384]{1,0:T(8,128)(2,1)S(1)}, u32[]{:S(2)}, u32[]{:S(2)}) %collective-permute-start.7) | collective-permute-done | bytes 589856 | tf_op jit(solution)/shard_map/ppermute | solution.py:439
  34.9 2.4 %collective-permute-start.8 = (bf16[192,384]{1,0:T(8,128)(2,1)S(1)}, bf16[192,384]{1,0:T(8,128)(2,1)S(1)}, u32[]{:S(2)}, u32[]{:S(2)}) collective-permute-start(bf16[192,384]{1,0:T(8,128)(2,1)S(1)} %get-tuple-element.35), channel_id=1, source_target_pairs={{0,4},{4,0},{8,12},{12,8},{1,5},{5,1},{9,13},{13,9},{2,6},{6,2},{1... | collective-permute-start | bytes 442376 | tf_op jit(solution)/shard_map/ppermute | solution.py:439
  37.6 1.0 %collective-permute-start.5 = (bf16[256,384]{1,0:T(8,128)(2,1)S(1)}, bf16[256,384]{1,0:T(8,128)(2,1)S(1)}, u32[]{:S(2)}, u32[]{:S(2)}) collective-permute-start(bf16[256,384]{1,0:T(8,128)(2,1)S(1)} %copy-done.7), channel_id=1, source_target_pairs={{2,0},{0,2},{3,1},{1,3},{6,4},{4,6},{7,5},{5,7},{10,8},{8,10},{11,... | collective-permute-start | bytes 589832 | tf_op jit(solution)/shard_map/ppermute | solution.py:415
  38.7 2.3 %collective-permute-done.10 = bf16[192,384]{1,0:T(8,128)(2,1)S(1)} collective-permute-done((bf16[192,384]{1,0:T(8,128)(2,1)S(1)}, bf16[192,384]{1,0:T(8,128)(2,1)S(1)}, u32[]{:S(2)}, u32[]{:S(2)}) %collective-permute-start.10) | collective-permute-done | bytes 147488 | tf_op jit(solution)/shard_map/ppermute | solution.py:439
  41.0 3.2 %collective-permute-done.8 = bf16[192,384]{1,0:T(8,128)(2,1)S(1)} collective-permute-done((bf16[192,384]{1,0:T(8,128)(2,1)S(1)}, bf16[192,384]{1,0:T(8,128)(2,1)S(1)}, u32[]{:S(2)}, u32[]{:S(2)}) %collective-permute-start.8) | collective-permute-done | bytes 147488 | tf_op jit(solution)/shard_map/ppermute | solution.py:439
  44.7 1.2 %collective-permute-start.11 = (bf16[192,384]{1,0:T(8,128)(2,1)S(1)}, bf16[192,384]{1,0:T(8,128)(2,1)S(1)}, u32[]{:S(2)}, u32[]{:S(2)}) collective-permute-start(bf16[192,384]{1,0:T(8,128)(2,1)S(1)} %add_convert_fusion.2), channel_id=1, source_target_pairs={{0,8},{4,12},{8,0},{12,4},{1,9},{5,13},{9,1},{13,5},{2,10},{6,14},... | collective-permute-start | bytes 442376 | tf_op jit(solution)/shard_map/ppermute | solution.py:439
  46.0 2.7 %collective-permute-done.4 = bf16[256,384]{1,0:T(8,128)(2,1)S(1)} collective-permute-done((bf16[256,384]{1,0:T(8,128)(2,1)S(1)}, bf16[256,384]{1,0:T(8,128)(2,1)S(1)}, u32[]{:S(2)}, u32[]{:S(2)}) %collective-permute-start.4) | collective-permute-done | bytes 196640 | tf_op jit(solution)/shard_map/ppermute | solution.py:415
  48.7 1.1 %collective-permute-start.6 = (bf16[128,384]{1,0:T(8,128)(2,1)S(1)}, bf16[128,384]{1,0:T(8,128)(2,1)S(1)}, u32[]{:S(2)}, u32[]{:S(2)}) collective-permute-start(bf16[128,384]{1,0:T(8,128)(2,1)S(1)} %slice_bitcast_fusion), channel_id=1, source_target_pairs={{2,0},{0,2},{3,1},{1,3},{6,4},{4,6},{7,5},{5,7},{10,8},{8,10},{11,... | collective-permute-start | bytes 294920 | tf_op jit(solution)/shard_map/ppermute | solution.py:415
  49.8 4.0 %collective-permute-done.11 = bf16[192,384]{1,0:T(8,128)(2,1)S(1)} collective-permute-done((bf16[192,384]{1,0:T(8,128)(2,1)S(1)}, bf16[192,384]{1,0:T(8,128)(2,1)S(1)}, u32[]{:S(2)}, u32[]{:S(2)}) %collective-permute-start.11) | collective-permute-done | bytes 147488 | tf_op jit(solution)/shard_map/ppermute | solution.py:439
  53.9 2.6 %collective-permute-start.13 = (bf16[192,384]{1,0:T(8,128)(2,1)S(1)}, bf16[192,384]{1,0:T(8,128)(2,1)S(1)}, u32[]{:S(2)}, u32[]{:S(2)}) collective-permute-start(bf16[192,384]{1,0:T(8,128)(2,1)S(1)} %add_convert_fusion.1.refs_0_), channel_id=1, source_target_pairs={{0,1},{1,0},{2,3},{3,2},{4,5},{5,4},{6,7},{7,6},{8,9},{9,8},{10,11... | collective-permute-start | bytes 442376 | tf_op jit(solution)/shard_map/ppermute | solution.py:439
  56.5 1.1 %collective-permute-start.14 = (bf16[192,384]{1,0:T(8,128)(2,1)S(1)}, bf16[192,384]{1,0:T(8,128)(2,1)S(1)}, u32[]{:S(2)}, u32[]{:S(2)}) collective-permute-start(bf16[192,384]{1,0:T(8,128)(2,1)S(1)} %add_convert_fusion.1.refs_0_), channel_id=1, source_target_pairs={{0,5},{1,4},{4,1},{5,0},{8,13},{9,12},{12,9},{13,8},{2,7},{3,6},{6... | collective-permute-start | bytes 442376 | tf_op jit(solution)/shard_map/ppermute | solution.py:439
  57.8 1.7 %collective-permute-start.15 = (bf16[192,384]{1,0:T(8,128)(2,1)S(1)}, bf16[192,384]{1,0:T(8,128)(2,1)S(1)}, u32[]{:S(2)}, u32[]{:S(2)}) collective-permute-start(bf16[192,384]{1,0:T(8,128)(2,1)S(1)} %add_convert_fusion.1.refs_0_), channel_id=1, source_target_pairs={{0,2},{2,0},{1,3},{3,1},{4,6},{6,4},{5,7},{7,5},{8,10},{10,8},{9,1... | collective-permute-start | bytes 442376 | tf_op jit(solution)/shard_map/ppermute | solution.py:439
  59.5 2.8 %collective-permute-start.16 = (bf16[192,384]{1,0:T(8,128)(2,1)S(1)}, bf16[192,384]{1,0:T(8,128)(2,1)S(1)}, u32[]{:S(2)}, u32[]{:S(2)}) collective-permute-start(bf16[192,384]{1,0:T(8,128)(2,1)S(1)} %collective-permute-done.12.refs_1_), channel_id=1, source_target_pairs={{0,2},{2,0},{1,3},{3,1},{4,6},{6,4},{5,7},{7,5},{8,10},{10,8},{9,1... | collective-permute-start | bytes 442376 | tf_op jit(solution)/shard_map/ppermute | solution.py:439
  62.3 1.5 %collective-permute-start.17 = (bf16[192,384]{1,0:T(8,128)(2,1)S(1)}, bf16[192,384]{1,0:T(8,128)(2,1)S(1)}, u32[]{:S(2)}, u32[]{:S(2)}) collective-permute-start(bf16[192,384]{1,0:T(8,128)(2,1)S(1)} %collective-permute-done.13.refs_2_), channel_id=1, source_target_pairs={{0,2},{2,0},{1,3},{3,1},{4,6},{6,4},{5,7},{7,5},{8,10},{10,8},{9,1... | collective-permute-start | bytes 442376 | tf_op jit(solution)/shard_map/ppermute | solution.py:439
  64.3 1.3 %collective-permute-start.18 = (bf16[192,384]{1,0:T(8,128)(2,1)S(1)}, bf16[192,384]{1,0:T(8,128)(2,1)S(1)}, u32[]{:S(2)}, u32[]{:S(2)}) collective-permute-start(bf16[192,384]{1,0:T(8,128)(2,1)S(1)} %collective-permute-done.14.refs_3_), channel_id=1, source_target_pairs={{0,2},{2,0},{1,3},{3,1},{4,6},{6,4},{5,7},{7,5},{8,10},{10,8},{9,1... | collective-permute-start | bytes 442376 | tf_op jit(solution)/shard_map/ppermute | solution.py:439
  65.6 2.3 %shard_map.121 = bf16[512,384]{1,0:T(8,128)(2,1)} custom-call(s32[2]{0:T(128)S(1)} %copy-done.2, bf16[640,384]{1,0:T(8,128)(2,1)S(1)} %pad_maximum_fusion.halo, bf16[512,384]{1,0:T(8,128)(2,1)S(1)} %copy-done.3), custom_call_target="tpu_custom_call" | custom-call | flops 2000000000 | bytes 1000000 | tf_op jit(solution)/shard_map/pallas_call | solution.py:398
  68.0 2.8 %shard_map.122 = (f32[384]{0:T(512)}, f32[384,1152]{1,0:T(8,128)}, f32[384,384]{1,0:T(8,128)}) custom-call(s32[2]{0:T(128)S(1)} %pad_add_fusion.place, bf16[192,384]{1,0:T(8,128)(2,1)S(1)} %add_convert_fusion.1.refs_0_, bf16[192,384]{1,0:T(8,128)(2,1)S(1)} %collective-permute-done.12.refs_1_, bf16[192,384]{1,0:T(8,128)(2,1)S(1)} %collective-permute-done.13.refs_2_, ...), custom_call_target="tpu_custom_call" | custom-call | flops 1000000000 | bytes 1000000 | tf_op jit(solution)/shard_map/pallas_call | solution.py:398
  (56 shorter events, 4.4 us)
Async XLA Ops:
  0.6 15.1 %collective-permute-start.2 = (bf16[2,16,16,384]{3,2,1,0:T(8,128)(2,1)}, bf16[2,16,16,384]{3,2,1,0:T(8,128)(2,1)S(1)}, u32[]{:S(2)}, u32[]{:S(2)}) collective-permute-start(bf16[2,16,16,384]{3,2,1,0:T(8,128)(2,1)} %param.8), channel_id=1, source_target_pairs={{2,0},{0,2},{3,1},{1,3},{6,4},{4,6},{7,5},{5,7},{10,8},{8,10},{11,... | collective-permute-start | bytes 1179656 | tf_op jit(solution)/shard_map/ppermute | solution.py:415
  2.4 11.6 %collective-permute-start.1 = (bf16[272,384]{1,0:T(8,128)(2,1)S(1)}, bf16[272,384]{1,0:T(8,128)(2,1)S(1)}, u32[]{:S(2)}, u32[]{:S(2)}) collective-permute-start(bf16[272,384]{1,0:T(8,128)(2,1)S(1)} %fusion.1), channel_id=1, source_target_pairs={{4,0},{8,4},{12,8},{0,12},{5,1},{9,5},{13,9},{1,13},{6,2},{10,6},{... | collective-permute-start | bytes 626696 | tf_op jit(solution)/shard_map/ppermute | solution.py:415
  7.3 7.2 %copy-start.5 = (s32[2,16,16]{2,1,0:T(8,128)S(1)}, s32[2,16,16]{2,1,0:T(8,128)}, u32[]{:S(2)}) copy-start(s32[2,16,16]{2,1,0:T(8,128)} %inner_flags.1) | copy-start | bytes 6148
  14.1 1.6 %collective-permute-start.3 = (bf16[144,384]{1,0:T(8,128)(2,1)S(1)}, bf16[144,384]{1,0:T(8,128)(2,1)S(1)}, u32[]{:S(2)}, u32[]{:S(2)}) collective-permute-start(bf16[144,384]{1,0:T(8,128)(2,1)S(1)} %pad_maximum_fusion.1), channel_id=1, source_target_pairs={{2,0},{0,2},{3,1},{1,3},{6,4},{4,6},{7,5},{5,7},{10,8},{8,10},{11,... | collective-permute-start | bytes 331784 | tf_op jit(solution)/shard_map/ppermute | solution.py:415
  14.5 1.2 %collective-permute-start = (s32[2,16,16]{2,1,0:T(8,128)S(1)}, s32[2,16,16]{2,1,0:T(8,128)S(1)}, u32[]{:S(2)}, u32[]{:S(2)}) collective-permute-start(s32[2,16,16]{2,1,0:T(8,128)S(1)} %copy-done.5), channel_id=1, source_target_pairs={{2,0},{0,2},{3,1},{1,3},{6,4},{4,6},{7,5},{5,7},{10,8},{8,10},{11,... | collective-permute-start | bytes 6152 | tf_op jit(solution)/shard_map/ppermute | solution.py:415
  32.3 2.3 %collective-permute-start.7 = (bf16[768,384]{1,0:T(8,128)(2,1)}, bf16[768,384]{1,0:T(8,128)(2,1)S(1)}, u32[]{:S(2)}, u32[]{:S(2)}) collective-permute-start(bf16[768,384]{1,0:T(8,128)(2,1)} %get-tuple-element.31), channel_id=1, source_target_pairs={{0,2},{2,0},{1,3},{3,1},{4,6},{6,4},{5,7},{7,5},{8,10},{10,8},{9,1... | collective-permute-start | bytes 1769480 | tf_op jit(solution)/shard_map/ppermute | solution.py:439
  33.7 3.8 %copy-start.8 = (bf16[256,384]{1,0:T(8,128)(2,1)S(1)}, bf16[256,384]{1,0:T(8,128)(2,1)}, u32[]{:S(2)}) copy-start(bf16[256,384]{1,0:T(8,128)(2,1)} %get-tuple-element.27) | copy-start | bytes 589828
  33.7 3.9 %copy-start.7 = (bf16[256,384]{1,0:T(8,128)(2,1)S(1)}, bf16[256,384]{1,0:T(8,128)(2,1)}, u32[]{:S(2)}) copy-start(bf16[256,384]{1,0:T(8,128)(2,1)} %get-tuple-element.28) | copy-start | bytes 589828
  34.7 30.9 %copy-start.2 = (s32[2]{0:T(128)S(1)}, s32[2]{0:T(128)}, u32[]{:S(2)}) copy-start(s32[2]{0:T(128)} %shift.3) | copy-start | bytes 28
  34.7 30.9 %copy-start.3 = (bf16[512,384]{1,0:T(8,128)(2,1)S(1)}, bf16[512,384]{1,0:T(8,128)(2,1)}, u32[]{:S(2)}) copy-start(bf16[512,384]{1,0:T(8,128)(2,1)} %get-tuple-element.29.kept_far) | copy-start | bytes 1179652
  34.8 6.2 %collective-permute-start.10 = (bf16[192,384]{1,0:T(8,128)(2,1)S(1)}, bf16[192,384]{1,0:T(8,128)(2,1)S(1)}, u32[]{:S(2)}, u32[]{:S(2)}) collective-permute-start(bf16[192,384]{1,0:T(8,128)(2,1)S(1)} %get-tuple-element.36), channel_id=1, source_target_pairs={{0,5},{1,4},{4,1},{5,0},{8,13},{9,12},{12,9},{13,8},{2,7},{3,6},{6... | collective-permute-start | bytes 442376 | tf_op jit(solution)/shard_map/ppermute | solution.py:439
  34.9 9.4 %collective-permute-start.8 = (bf16[192,384]{1,0:T(8,128)(2,1)S(1)}, bf16[192,384]{1,0:T(8,128)(2,1)S(1)}, u32[]{:S(2)}, u32[]{:S(2)}) collective-permute-start(bf16[192,384]{1,0:T(8,128)(2,1)S(1)} %get-tuple-element.35), channel_id=1, source_target_pairs={{0,4},{4,0},{8,12},{12,8},{1,5},{5,1},{9,13},{13,9},{2,6},{6,2},{1... | collective-permute-start | bytes 442376 | tf_op jit(solution)/shard_map/ppermute | solution.py:439
  37.2 7.4 %collective-permute-start.9 = (bf16[192,384]{1,0:T(8,128)(2,1)S(1)}, bf16[192,384]{1,0:T(8,128)(2,1)S(1)}, u32[]{:S(2)}, u32[]{:S(2)}) collective-permute-start(bf16[192,384]{1,0:T(8,128)(2,1)S(1)} %get-tuple-element.37), channel_id=1, source_target_pairs={{0,1},{1,0},{2,3},{3,2},{4,5},{5,4},{6,7},{7,6},{8,9},{9,8},{10,11... | collective-permute-start | bytes 442376 | tf_op jit(solution)/shard_map/ppermute | solution.py:439
  37.5 11.2 %collective-permute-start.4 = (bf16[256,384]{1,0:T(8,128)(2,1)S(1)}, bf16[256,384]{1,0:T(8,128)(2,1)S(1)}, u32[]{:S(2)}, u32[]{:S(2)}) collective-permute-start(bf16[256,384]{1,0:T(8,128)(2,1)S(1)} %copy-done.8), channel_id=1, source_target_pairs={{12,0},{0,4},{4,8},{8,12},{13,1},{1,5},{5,9},{9,13},{14,2},{2,6},{... | collective-permute-start | bytes 589832 | tf_op jit(solution)/shard_map/ppermute | solution.py:415
  37.6 20.1 %collective-permute-start.5 = (bf16[256,384]{1,0:T(8,128)(2,1)S(1)}, bf16[256,384]{1,0:T(8,128)(2,1)S(1)}, u32[]{:S(2)}, u32[]{:S(2)}) collective-permute-start(bf16[256,384]{1,0:T(8,128)(2,1)S(1)} %copy-done.7), channel_id=1, source_target_pairs={{2,0},{0,2},{3,1},{1,3},{6,4},{4,6},{7,5},{5,7},{10,8},{8,10},{11,... | collective-permute-start | bytes 589832 | tf_op jit(solution)/shard_map/ppermute | solution.py:415
  44.7 9.0 %collective-permute-start.11 = (bf16[192,384]{1,0:T(8,128)(2,1)S(1)}, bf16[192,384]{1,0:T(8,128)(2,1)S(1)}, u32[]{:S(2)}, u32[]{:S(2)}) collective-permute-start(bf16[192,384]{1,0:T(8,128)(2,1)S(1)} %add_convert_fusion.2), channel_id=1, source_target_pairs={{0,8},{4,12},{8,0},{12,4},{1,9},{5,13},{9,1},{13,5},{2,10},{6,14},... | collective-permute-start | bytes 442376 | tf_op jit(solution)/shard_map/ppermute | solution.py:439
  48.7 9.1 %collective-permute-start.6 = (bf16[128,384]{1,0:T(8,128)(2,1)S(1)}, bf16[128,384]{1,0:T(8,128)(2,1)S(1)}, u32[]{:S(2)}, u32[]{:S(2)}) collective-permute-start(bf16[128,384]{1,0:T(8,128)(2,1)S(1)} %slice_bitcast_fusion), channel_id=1, source_target_pairs={{2,0},{0,2},{3,1},{1,3},{6,4},{4,6},{7,5},{5,7},{10,8},{8,10},{11,... | collective-permute-start | bytes 294920 | tf_op jit(solution)/shard_map/ppermute | solution.py:415
  53.8 5.7 %collective-permute-start.12 = (bf16[192,384]{1,0:T(8,128)(2,1)S(1)}, bf16[192,384]{1,0:T(8,128)(2,1)S(1)}, u32[]{:S(2)}, u32[]{:S(2)}) collective-permute-start(bf16[192,384]{1,0:T(8,128)(2,1)S(1)} %add_convert_fusion.1.refs_0_), channel_id=1, source_target_pairs={{0,4},{4,0},{8,12},{12,8},{1,5},{5,1},{9,13},{13,9},{2,6},{6,2},{1... | collective-permute-start | bytes 442376 | tf_op jit(solution)/shard_map/ppermute | solution.py:439
  53.9 8.4 %collective-permute-start.13 = (bf16[192,384]{1,0:T(8,128)(2,1)S(1)}, bf16[192,384]{1,0:T(8,128)(2,1)S(1)}, u32[]{:S(2)}, u32[]{:S(2)}) collective-permute-start(bf16[192,384]{1,0:T(8,128)(2,1)S(1)} %add_convert_fusion.1.refs_0_), channel_id=1, source_target_pairs={{0,1},{1,0},{2,3},{3,2},{4,5},{5,4},{6,7},{7,6},{8,9},{9,8},{10,11... | collective-permute-start | bytes 442376 | tf_op jit(solution)/shard_map/ppermute | solution.py:439
  56.5 7.7 %collective-permute-start.14 = (bf16[192,384]{1,0:T(8,128)(2,1)S(1)}, bf16[192,384]{1,0:T(8,128)(2,1)S(1)}, u32[]{:S(2)}, u32[]{:S(2)}) collective-permute-start(bf16[192,384]{1,0:T(8,128)(2,1)S(1)} %add_convert_fusion.1.refs_0_), channel_id=1, source_target_pairs={{0,5},{1,4},{4,1},{5,0},{8,13},{9,12},{12,9},{13,8},{2,7},{3,6},{6... | collective-permute-start | bytes 442376 | tf_op jit(solution)/shard_map/ppermute | solution.py:439
  57.8 10.1 %collective-permute-start.15 = (bf16[192,384]{1,0:T(8,128)(2,1)S(1)}, bf16[192,384]{1,0:T(8,128)(2,1)S(1)}, u32[]{:S(2)}, u32[]{:S(2)}) collective-permute-start(bf16[192,384]{1,0:T(8,128)(2,1)S(1)} %add_convert_fusion.1.refs_0_), channel_id=1, source_target_pairs={{0,2},{2,0},{1,3},{3,1},{4,6},{6,4},{5,7},{7,5},{8,10},{10,8},{9,1... | collective-permute-start | bytes 442376 | tf_op jit(solution)/shard_map/ppermute | solution.py:439
  59.5 8.4 %collective-permute-start.16 = (bf16[192,384]{1,0:T(8,128)(2,1)S(1)}, bf16[192,384]{1,0:T(8,128)(2,1)S(1)}, u32[]{:S(2)}, u32[]{:S(2)}) collective-permute-start(bf16[192,384]{1,0:T(8,128)(2,1)S(1)} %collective-permute-done.12.refs_1_), channel_id=1, source_target_pairs={{0,2},{2,0},{1,3},{3,1},{4,6},{6,4},{5,7},{7,5},{8,10},{10,8},{9,1... | collective-permute-start | bytes 442376 | tf_op jit(solution)/shard_map/ppermute | solution.py:439
  62.3 5.6 %collective-permute-start.17 = (bf16[192,384]{1,0:T(8,128)(2,1)S(1)}, bf16[192,384]{1,0:T(8,128)(2,1)S(1)}, u32[]{:S(2)}, u32[]{:S(2)}) collective-permute-start(bf16[192,384]{1,0:T(8,128)(2,1)S(1)} %collective-permute-done.13.refs_2_), channel_id=1, source_target_pairs={{0,2},{2,0},{1,3},{3,1},{4,6},{6,4},{5,7},{7,5},{8,10},{10,8},{9,1... | collective-permute-start | bytes 442376 | tf_op jit(solution)/shard_map/ppermute | solution.py:439
  64.3 3.7 %collective-permute-start.18 = (bf16[192,384]{1,0:T(8,128)(2,1)S(1)}, bf16[192,384]{1,0:T(8,128)(2,1)S(1)}, u32[]{:S(2)}, u32[]{:S(2)}) collective-permute-start(bf16[192,384]{1,0:T(8,128)(2,1)S(1)} %collective-permute-done.14.refs_3_), channel_id=1, source_target_pairs={{0,2},{2,0},{1,3},{3,1},{4,6},{6,4},{5,7},{7,5},{8,10},{10,8},{9,1... | collective-permute-start | bytes 442376 | tf_op jit(solution)/shard_map/ppermute | solution.py:439
  (6 other events, 8.4 us)
